TPU v7x, 32 devices: a whole 2x2x4 slice. The times are simulated.
32 devices in a mesh: segment: 4 (over y, x), mp: 2 (over core), dp: 4 (over z).
Axes of the slice: x: 2, y: 2, z: 4, core: 2. Of those that a mesh axis runs over, the one named last changes fastest.
Arguments:
- text_rows: bfloat16 [4, 512, 1024], P(None, 'dp'), may hold values from -6 to 6
- durations: int32 [4, 4, 128], P(None, 'dp'), may hold values from 1 to 16, 512 in all within a row
- unit_targets: int32 [4, 2048], P(None, 'dp'), may hold values from 0 to 9999
- w_in: bfloat16 [4, 1024, 8192], P('segment', None, 'mp'), may hold values from -0.1875 to 0.1875
- w_out: bfloat16 [4, 8192, 1024], P('segment', 'mp'), may hold values from -0.0625 to 0.0625
- w_unit: bfloat16 [1024, 10240], P(None, ('segment', 'mp')), as said below
Outputs:
- loss: float32 [4], P('dp')
- grad_in: float32 [4, 1024, 8192], P('segment', 'dp', 'mp')
- grad_out: float32 [4, 8192, 1024], P('segment', 'mp', 'dp')
- grad_unit: float32 [1024, 10240], P('dp', ('segment', 'mp'))
Inputs may be any that keep to these rules, and one draw needn't show every extreme that they name: Within each micro-batch and each index of dp the 128 durations sum to exactly 512, and one of them equals 16. `w_unit`: entries of order 3 / sqrt(1024) in most columns, some columns much larger.
All inputs are finite; a program needn't handle non-finite values.
Results may differ from a plain program's by a relative error of at most 0.035.
Values may be sent and summed in bfloat16 or wider, within the bound.
No kernel may reach another device: no remote copies, remote signals or barrier semaphores. Data moves between devices by JAX's collectives and lax.ppermute only.
A program may use at most 256 MiB of HBM per device.

v0:
```python
import jax
import jax.numpy as jnp
from jax import lax
from jax.sharding import PartitionSpec as P


def shifted(block, axis, distance):
    devices = range(lax.axis_size(axis))
    route = [(i - distance, i) for i in devices if i - distance in devices]
    return lax.ppermute(block, axis, route)


def broadcast(x, axis, root):
    mine = lax.axis_index(axis) == root
    return lax.psum(jnp.where(mine, x, jnp.zeros_like(x)), axis)


def gelu_parts(pre_vals):
    coeff = 0.7978845608
    inner = coeff * (pre_vals + 0.044715 * pre_vals * pre_vals * pre_vals)
    tanh_val = jnp.tanh(inner)
    value = 0.5 * pre_vals * (1.0 + tanh_val)
    slope = 0.5 * (1.0 + tanh_val) + 0.5 * pre_vals * (1.0 - tanh_val * tanh_val) * coeff * (
        1.0 + 3.0 * 0.044715 * pre_vals * pre_vals
    )
    return (value, slope)


def row_scale(rows_in):
    floats = rows_in.astype(jnp.float32)
    return lax.rsqrt(jnp.mean(floats * floats, axis=-1, keepdims=True) + 1e-06)


def norm_back(rows_in, grads):
    scale = row_scale(rows_in)
    normal = rows_in.astype(jnp.float32) * scale
    return scale * (grads - normal * jnp.mean(grads * normal, axis=-1, keepdims=True))


def section(rows_in, first):
    normed = (rows_in.astype(jnp.float32) * row_scale(rows_in)).astype(jnp.bfloat16)
    pre_vals = jnp.dot(normed, first, preferred_element_type=jnp.float32)
    value, slope = gelu_parts(pre_vals)
    return (normed, value.astype(jnp.bfloat16), slope)


def finish_forward(pieces, summed):
    return (pieces[0].astype(jnp.float32) + summed).astype(jnp.bfloat16)


def finish_backward(pieces, summed):
    return (pieces[0].astype(jnp.float32) + norm_back(pieces[1], summed)).astype(jnp.bfloat16)


def reduce_rows(partial_value, pieces, finisher):
    summed = lax.psum(partial_value, "mp")
    return finisher(pieces, summed)


def on_device(text_rows, durations, unit_targets, w_in, w_out, w_unit):
    micro_count, row_count, width = text_rows.shape
    segments = lax.axis_size("segment")
    segment_at = lax.axis_index("segment")
    first = w_in[0]
    second = w_out[0]
    clocks = micro_count + segments - 1
    stash = jnp.zeros((micro_count, row_count, width), jnp.bfloat16)
    final_rows = jnp.zeros((micro_count, row_count, width), jnp.bfloat16)
    outgoing = jnp.zeros((row_count, width), jnp.bfloat16)
    for clock in range(clocks):
        if clock > 0:
            incoming = shifted(outgoing, "segment", 1)
        else:
            incoming = jnp.zeros((row_count, width), jnp.bfloat16)
        rows_in = jnp.where(segment_at == 0, text_rows[min(clock, micro_count - 1)], incoming)
        batch_at = clock - segment_at
        is_live = (batch_at >= 0) & (batch_at < micro_count)
        slot_at = jnp.clip(batch_at, 0, micro_count - 1)
        stash = jnp.where(
            is_live, lax.dynamic_update_index_in_dim(stash, rows_in, slot_at, 0), stash
        )
        normed, hidden, slope = section(rows_in, first)
        partial_value = jnp.dot(hidden, second, preferred_element_type=jnp.float32)
        outgoing = reduce_rows(partial_value, (rows_in,), finish_forward)
        is_last = is_live & (segment_at == segments - 1)
        final_rows = jnp.where(
            is_last, lax.dynamic_update_index_in_dim(final_rows, outgoing, slot_at, 0), final_rows
        )
    final_rows = broadcast(final_rows, "segment", segments - 1)
    vocab_part = w_unit.shape[1]
    vocab_start = lax.axis_index(("segment", "mp")) * vocab_part
    final_norm = (final_rows.astype(jnp.float32) * row_scale(final_rows)).astype(jnp.bfloat16)
    logits = jnp.einsum("mrd,dv->mrv", final_norm, w_unit, preferred_element_type=jnp.float32)
    lengths = durations[:, 0, :]
    unit_count = unit_targets.shape[1]
    ends = jnp.cumsum(lengths, axis=-1)
    positions = jnp.arange(unit_count, dtype=jnp.int32)
    row_local = jnp.sum((ends[:, None, :] <= positions[None, :, None]).astype(jnp.int32), axis=-1)
    row_onehot = (
        row_local[:, :, None] == jnp.arange(row_count, dtype=jnp.int32)[None, None, :]
    ).astype(jnp.bfloat16)
    vocab_ids = vocab_start + jnp.arange(vocab_part, dtype=jnp.int32)
    target_hits = (unit_targets[:, :, None] == vocab_ids[None, None, :]).astype(jnp.bfloat16)
    counts = jnp.einsum("mur,muv->mrv", row_onehot, target_hits, preferred_element_type=jnp.float32)
    local_peak = jnp.max(logits, axis=-1)
    target_local = jnp.sum(counts * logits, axis=-1)
    peak = lax.pmax(local_peak, ("segment", "mp"))
    total, target_sum = lax.psum(
        (jnp.sum(jnp.exp(logits - peak[..., None]), axis=-1), target_local), ("segment", "mp")
    )
    lse = peak + jnp.log(total)
    denom = float(micro_count * unit_count * lax.axis_size("dp"))
    length_f = lengths.astype(jnp.float32)
    loss_local = jnp.sum(length_f * lse - target_sum)
    loss = (loss_local / denom)[None]
    dlogits = ((length_f[..., None] * jnp.exp(logits - lse[..., None]) - counts) / denom).astype(
        jnp.bfloat16
    )
    grad_unit = jnp.einsum("mrd,mrv->dv", final_norm, dlogits, preferred_element_type=jnp.float32)
    norm_part = jnp.einsum("mrv,dv->mrd", dlogits, w_unit, preferred_element_type=jnp.float32)
    norm_share = lax.psum_scatter(
        norm_part, ("segment", "mp"), scatter_dimension=2, tiled=True
    ).astype(jnp.bfloat16)
    dnorm = lax.all_gather(norm_share, ("segment", "mp"), axis=2, tiled=True)
    grad_final = norm_back(final_rows, dnorm.astype(jnp.float32)).astype(jnp.bfloat16)
    grad_first = jnp.zeros(first.shape, jnp.float32)
    grad_second = jnp.zeros(second.shape, jnp.float32)
    going_back = jnp.zeros((row_count, width), jnp.bfloat16)
    for clock in range(clocks):
        if clock > 0:
            arriving = shifted(going_back, "segment", -1)
        else:
            arriving = jnp.zeros((row_count, width), jnp.bfloat16)
        grad_rows = jnp.where(
            segment_at == segments - 1, grad_final[min(clock, micro_count - 1)], arriving
        )
        batch_at = clock - (segments - 1 - segment_at)
        is_live = (batch_at >= 0) & (batch_at < micro_count)
        slot_at = jnp.clip(batch_at, 0, micro_count - 1)
        rows_in = lax.dynamic_index_in_dim(stash, slot_at, 0, keepdims=False)
        normed, hidden, slope = section(rows_in, first)
        live_f = is_live.astype(jnp.float32)
        grad_second = grad_second + live_f * jnp.dot(
            hidden.T, grad_rows, preferred_element_type=jnp.float32
        )
        dhidden = jnp.dot(grad_rows, second.T, preferred_element_type=jnp.float32)
        dpre = (dhidden * slope).astype(jnp.bfloat16)
        grad_first = grad_first + live_f * jnp.dot(
            normed.T, dpre, preferred_element_type=jnp.float32
        )
        dnormed = jnp.dot(dpre, first.T, preferred_element_type=jnp.float32)
        going_back = reduce_rows(dnormed, (grad_rows, rows_in), finish_backward)
    sum_first, sum_second, sum_unit = (
        lax.psum_scatter(grad_first, "dp", scatter_dimension=0, tiled=True),
        lax.psum_scatter(grad_second, "dp", scatter_dimension=1, tiled=True),
        lax.psum_scatter(grad_unit, "dp", scatter_dimension=0, tiled=True),
    )
    return (loss, sum_first[None], sum_second[None], sum_unit)


def solution(mesh):
    placed = (
        P(None, "dp", None),
        P(None, "dp", None),
        P(None, "dp"),
        P("segment", None, "mp"),
        P("segment", "mp", None),
        P(None, ("segment", "mp")),
    )
    return jax.shard_map(
        on_device,
        mesh=mesh,
        in_specs=placed,
        out_specs=(
            P("dp"),
            P("segment", "dp", "mp"),
            P("segment", "mp", "dp"),
            P("dp", ("segment", "mp")),
        ),
        check_vma=False,
    )
```

profile of v0, /device:TPU:11, one launch (start us, length us, event | category | flops | bytes accessed | tf_op | source)
XLA Modules:
  0.0 1385.6 jit_solution(13689626649133818569)
XLA Ops:
  17.9 20.7 %all-reduce.16.cloned.1.call-done = f32[128,1024]{1,0:T(8,128)} async-done(((f32[128,1024]{1,0:T(8,128)}), f32[128,1024]{1,0:T(8,128)}) %all-reduce.16.cloned.1.call-update) | async-done | bytes 524304 | tf_op jit(solution)/shard_map/psum | solution.py:56
  62.4 20.8 %all-reduce.18.cloned.1.call-done = f32[128,1024]{1,0:T(8,128)} async-done(((f32[128,1024]{1,0:T(8,128)}), f32[128,1024]{1,0:T(8,128)}) %all-reduce.18.cloned.1.call-update) | async-done | bytes 524304 | tf_op jit(solution)/shard_map/psum | solution.py:56
  106.1 20.8 %all-reduce.20.cloned.1.call-done = f32[128,1024]{1,0:T(8,128)} async-done(((f32[128,1024]{1,0:T(8,128)}), f32[128,1024]{1,0:T(8,128)}) %all-reduce.20.cloned.1.call-update) | async-done | bytes 524304 | tf_op jit(solution)/shard_map/psum | solution.py:56
  149.8 20.8 %all-reduce.22.cloned.1.call-done = f32[128,1024]{1,0:T(8,128)} async-done(((f32[128,1024]{1,0:T(8,128)}), f32[128,1024]{1,0:T(8,128)}) %all-reduce.22.cloned.1.call-update) | async-done | bytes 524304 | tf_op jit(solution)/shard_map/psum | solution.py:56
  193.4 20.8 %all-reduce.24.cloned.1.call-done = f32[128,1024]{1,0:T(8,128)} async-done(((f32[128,1024]{1,0:T(8,128)}), f32[128,1024]{1,0:T(8,128)}) %all-reduce.24.cloned.1.call-update) | async-done | bytes 524304 | tf_op jit(solution)/shard_map/psum | solution.py:56
  237.1 20.8 %all-reduce.26.cloned.1.call-done = f32[128,1024]{1,0:T(8,128)} async-done(((f32[128,1024]{1,0:T(8,128)}), f32[128,1024]{1,0:T(8,128)}) %all-reduce.26.cloned.1.call-update) | async-done | bytes 524304 | tf_op jit(solution)/shard_map/psum | solution.py:56
  281.2 20.3 %all-reduce.28.cloned.1.call-done = f32[128,1024]{1,0:T(8,128)} async-done(((f32[128,1024]{1,0:T(8,128)}), f32[128,1024]{1,0:T(8,128)}) %all-reduce.28.cloned.1.call-update) | async-done | bytes 524304 | tf_op jit(solution)/shard_map/psum | solution.py:56
  305.3 53.6 %all-reduce.30.cloned.1.call-done = bf16[4,128,1024]{2,1,0:T(8,128)(2,1)} async-done(((bf16[4,128,1024]{2,1,0:T(8,128)(2,1)}), bf16[4,128,1024]{2,1,0:T(8,128)(2,1)}) %all-reduce.30.cloned.1.call-update) | async-done | bytes 1048592 | tf_op jit(solution)/shard_map/psum | solution.py:15
  364.8 11.3 pmax.7
  381.1 11.8 all-reduce
  400.7 42.7 %reduce-scatter.5.cloned.1.call-done = f32[4,128,128]{2,1,0:T(8,128)} async-done(((f32[4,128,1024]{2,1,0:T(8,128)}), f32[4,128,128]{2,1,0:T(8,128)}) %reduce-scatter.5.cloned.1.call-update) | async-done | bytes 262160 | tf_op jit(solution)/shard_map/reduce_scatter | solution.py:121
  452.5 17.4 %all-gather.2.cloned.1.call-done = bf16[4,128,1024]{2,1,0:T(8,128)(2,1)} async-done(((bf16[4,128,128]{2,1,0:T(8,128)(2,1)}), bf16[4,128,1024]{2,1,0:T(8,128)(2,1)}) %all-gather.2.cloned.1.call-update) | async-done | bytes 1048592 | tf_op jit(solution)/shard_map/all_gather | solution.py:124
  485.5 19.1 %all-reduce.32.cloned.1.call-done = f32[128,1024]{1,0:T(8,128)} async-done(((f32[128,1024]{1,0:T(8,128)}), f32[128,1024]{1,0:T(8,128)}) %all-reduce.32.cloned.1.call-update) | async-done | bytes 524304 | tf_op jit(solution)/shard_map/psum | solution.py:56
  527.2 19.9 %all-reduce.34.cloned.1.call-done = f32[128,1024]{1,0:T(8,128)} async-done(((f32[128,1024]{1,0:T(8,128)}), f32[128,1024]{1,0:T(8,128)}) %all-reduce.34.cloned.1.call-update) | async-done | bytes 524304 | tf_op jit(solution)/shard_map/psum | solution.py:56
  569.1 19.9 %all-reduce.36.cloned.1.call-done = f32[128,1024]{1,0:T(8,128)} async-done(((f32[128,1024]{1,0:T(8,128)}), f32[128,1024]{1,0:T(8,128)}) %all-reduce.36.cloned.1.call-update) | async-done | bytes 524304 | tf_op jit(solution)/shard_map/psum | solution.py:56
  611.1 19.9 %all-reduce.38.cloned.1.call-done = f32[128,1024]{1,0:T(8,128)} async-done(((f32[128,1024]{1,0:T(8,128)}), f32[128,1024]{1,0:T(8,128)}) %all-reduce.38.cloned.1.call-update) | async-done | bytes 524304 | tf_op jit(solution)/shard_map/psum | solution.py:56
  653.1 19.9 %all-reduce.40.cloned.1.call-done = f32[128,1024]{1,0:T(8,128)} async-done(((f32[128,1024]{1,0:T(8,128)}), f32[128,1024]{1,0:T(8,128)}) %all-reduce.40.cloned.1.call-update) | async-done | bytes 524304 | tf_op jit(solution)/shard_map/psum | solution.py:56
  764.7 40.5 %multiply_add_fusion = f32[4096,1024]{1,0:T(8,128)} fusion(f32[4096,1024]{1,0:T(8,128)} %fusion.213, f32[4096,1024]{1,0:T(8,128)} %fusion.212, f32[4096,1024]{1,0:T(8,128)} %fusion.211, f32[4096,1024]{1,0:T(8,128)} %fusion.210, f32[4096,1024]{1,0:T(8,128)} %fusion.209, f32[4096,1024]{1,0:T(8,128)} %fusion.208, f32[]{:T(128)S(6)} %convert_element_type.474, ...), kind=kOutput, calls=%fused_computation | convolution fusion | flops 1133117440 | bytes 120061984 | tf_op jit(solution)/shard_map/dot_general | solution.py:143
  815.7 9.8 fusion.394
  843.9 9.3 fusion.400
  853.2 9.6 fusion.402
  866.5 39.5 %multiply_add_fusion.1 = f32[1024,4096]{1,0:T(8,128)} fusion(f32[1024,4096]{1,0:T(8,128)} %fusion.402, f32[1024,4096]{1,0:T(8,128)} %fusion.400, f32[1024,4096]{1,0:T(8,128)} %fusion.398, f32[1024,4096]{1,0:T(8,128)} %fusion.396, f32[1024,4096]{1,0:T(8,128)} %fusion.394, f32[1024,4096]{1,0:T(8,128)} %fusion.392, bf16[128,4096]{1,0:T(8,128)(2,1)S(1)} %fusion.93, ...), kind=kOutput, calls=%fused_computation.1 | convolution fusion | flops 1128660992 | bytes 118751776 | tf_op jit(solution)/shard_map/dot_general | solution.py:148
  906.9 186.5 %reduce-scatter.9.cloned.1.call-done = f32[4096,256]{1,0:T(8,128)} async-done(((f32[4096,1024]{1,0:T(8,128)}), f32[4096,256]{1,0:T(8,128)}) %reduce-scatter.9.cloned.1.call-update) | async-done | bytes 4194320 | tf_op jit(solution)/shard_map/reduce_scatter | solution.py:155
  1093.3 284.1 %reduce-scatter.7.cloned.1.call-done = f32[256,4096]{1,0:T(8,128)} async-done(((f32[1024,4096]{1,0:T(8,128)}), f32[256,4096]{1,0:T(8,128)}) %reduce-scatter.7.cloned.1.call-update) | async-done | bytes 4194320 | tf_op jit(solution)/shard_map/reduce_scatter | solution.py:154
  (314 shorter events, 408.1 us)
Async XLA Ops:
  7.2 31.4 %all-reduce.16.cloned.1.call-start = ((), (), s32[]{:S(2)}) async-start(), calls=%async_computation.4 | async-start | bytes 1048576 | tf_op jit(solution)/shard_map/psum | solution.py:56
  17.8 65.5 %all-reduce.18.cloned.1.call-start = ((), (), s32[]{:S(2)}) async-start(), calls=%async_computation.5 | async-start | bytes 1048576 | tf_op jit(solution)/shard_map/psum | solution.py:56
  62.4 64.5 %all-reduce.20.cloned.1.call-start = ((), (), s32[]{:S(2)}) async-start(), calls=%async_computation.6 | async-start | bytes 1048576 | tf_op jit(solution)/shard_map/psum | solution.py:56
  106.1 64.5 %all-reduce.22.cloned.1.call-start = ((), (), s32[]{:S(2)}) async-start(), calls=%async_computation.7 | async-start | bytes 1048576 | tf_op jit(solution)/shard_map/psum | solution.py:56
  149.7 64.5 %all-reduce.24.cloned.1.call-start = ((), (), s32[]{:S(2)}) async-start(), calls=%async_computation.8 | async-start | bytes 1048576 | tf_op jit(solution)/shard_map/psum | solution.py:56
  193.4 64.5 %all-reduce.26.cloned.1.call-start = ((), (), s32[]{:S(2)}) async-start(), calls=%async_computation.9 | async-start | bytes 1048576 | tf_op jit(solution)/shard_map/psum | solution.py:56
  237.1 64.5 %all-reduce.28.cloned.1.call-start = ((), (), s32[]{:S(2)}) async-start(), calls=%async_computation.10 | async-start | bytes 1048576 | tf_op jit(solution)/shard_map/psum | solution.py:56
  280.7 78.2 %all-reduce.30.cloned.1.call-start = ((), (), s32[]{:S(2)}) async-start(), calls=%async_computation.11 | async-start | bytes 2097152 | tf_op jit(solution)/shard_map/psum | solution.py:15
  304.6 138.9 %reduce-scatter.5.cloned.1.call-start = ((), (), s32[]{:S(2)}) async-start(), calls=%async_computation.12 | async-start | bytes 2359296 | tf_op jit(solution)/shard_map/reduce_scatter | solution.py:121
  400.7 69.1 %all-gather.2.cloned.1.call-start = ((), (), s32[]{:S(2)}) async-start(), calls=%async_computation.13 | async-start | bytes 1179648 | tf_op jit(solution)/shard_map/all_gather | solution.py:124
  445.1 59.5 %all-reduce.32.cloned.1.call-start = ((), (), s32[]{:S(2)}) async-start(), calls=%async_computation.14 | async-start | bytes 1048576 | tf_op jit(solution)/shard_map/psum | solution.py:56
  485.4 61.7 %all-reduce.34.cloned.1.call-start = ((), (), s32[]{:S(2)}) async-start(), calls=%async_computation.15 | async-start | bytes 1048576 | tf_op jit(solution)/shard_map/psum | solution.py:56
  508.0 10.7 collective-permute-start.6
  527.1 62.0 %all-reduce.36.cloned.1.call-start = ((), (), s32[]{:S(2)}) async-start(), calls=%async_computation.16 | async-start | bytes 1048576 | tf_op jit(solution)/shard_map/psum | solution.py:56
  549.9 10.7 collective-permute-start.7
  569.1 62.0 %all-reduce.38.cloned.1.call-start = ((), (), s32[]{:S(2)}) async-start(), calls=%async_computation.17 | async-start | bytes 1048576 | tf_op jit(solution)/shard_map/psum | solution.py:56
  591.9 10.7 collective-permute-start.8
  611.1 61.9 %all-reduce.40.cloned.1.call-start = ((), (), s32[]{:S(2)}) async-start(), calls=%async_computation.18 | async-start | bytes 1048576 | tf_op jit(solution)/shard_map/psum | solution.py:56
  633.9 10.7 collective-permute-start.9
  653.0 99.4 %all-reduce.42.cloned.1.call-start = ((), (), s32[]{:S(2)}) async-start(), calls=%async_computation.19 | async-start | bytes 1048576 | tf_op jit(solution)/shard_map/psum | solution.py:56
  675.9 10.7 collective-permute-start.10
  695.7 211.1 %reduce-scatter.11.cloned.1.call-start = ((), (), s32[]{:S(2)}) async-start(), calls=%async_computation.22 | async-start | bytes 6553600 | tf_op jit(solution)/shard_map/reduce_scatter | solution.py:156
  699.7 393.6 %reduce-scatter.9.cloned.1.call-start = ((), (), s32[]{:S(2)}) async-start(), calls=%async_computation.21 | async-start | bytes 20971520 | tf_op jit(solution)/shard_map/reduce_scatter | solution.py:155
  805.2 572.2 %reduce-scatter.7.cloned.1.call-start = ((), (), s32[]{:S(2)}) async-start(), calls=%async_computation.20 | async-start | bytes 20971520 | tf_op jit(solution)/shard_map/reduce_scatter | solution.py:154
  (69 other events, 1569.1 us)
Sparse Core Ops, SparseCore 0:
  17.9 20.5 all-reduce.15
  62.5 20.7 all-reduce.17
  106.2 20.7 all-reduce.19
  149.8 20.7 all-reduce.21
  193.5 20.7 all-reduce.23
  237.2 20.6 all-reduce.25
  280.8 20.6 all-reduce.27
  305.5 53.3 all-reduce.29
  400.8 42.6 reduce-scatter.4
  445.8 24.0 all-gather.1
  485.5 19.0 all-reduce.31
  527.2 19.8 all-reduce.33
  569.2 19.8 all-reduce.35
  611.2 19.8 all-reduce.37
  653.2 19.7 all-reduce.39
  695.9 19.7 all-reduce.41
  718.4 94.2 reduce-scatter.10
  815.5 277.8 reduce-scatter.8
  1096.4 281.0 reduce-scatter.6
where the time goes:
time: 1400 us; the launch traced here: 1390 us
  waiting for transfers between devices  882 us (63%)
  matrix products  356 us (25%)
  other arithmetic  58.6 us (4%)
  starting transfers between devices  35 us (2%)
  blocking collectives  23.1 us (2%)
  between operations  17.5 us (1%)
    reduce_scatter x1, waiting for transfers between devices, on_device(): lax.psum_scatter(grad_first, 'dp', scatter_dimension=0, tiled=True)  284 us
    psum x13, waiting for transfers between devices, reduce_rows(): summed = lax.psum(partial_value, 'mp')  244 us
    reduce_scatter x1, waiting for transfers between devices, on_device(): lax.psum_scatter(grad_second, 'dp', scatter_dimension=1, tiled=True)  186 us
    dot_general x7, matrix products, on_device(): jnp.dot(normed.T, dpre, preferred_element_type=jnp.float32)  95.9 us
    dot_general x7, matrix products, on_device(): jnp.dot(hidden.T, grad_rows, preferred_element_type=jnp.float32)  91.5 us
    dot_general x7, matrix products, on_device(): partial_value = jnp.dot(hidden, second, preferred_element_type=jnp.float32)  64.4 us
    psum x1, waiting for transfers between devices, broadcast(): return lax.psum(jnp.where(mine, x, jnp.zeros_like(x)), axis)  53.6 us
    ppermute x12, waiting for transfers between devices, shifted(): return lax.ppermute(block, axis, route)  53.1 us
  transfers between devices with their start and end apart: 31, of which 29 were waited for; matrix products, arithmetic and copies ran while one was open for 17% of the time, Pallas kernels for 0%

commit v1 on v0

v1 whole, which is shorter than its diff:
```python
import jax
import jax.numpy as jnp
from jax import lax
from jax.sharding import PartitionSpec as P

CHUNKS = 4


def shifted(block, axis, distance):
    devices = range(lax.axis_size(axis))
    route = [(i - distance, i) for i in devices if i - distance in devices]
    return lax.ppermute(block, axis, route)


def gelu_parts(pre_vals):
    coeff = 0.7978845608
    inner = coeff * (pre_vals + 0.044715 * pre_vals * pre_vals * pre_vals)
    tanh_val = jnp.tanh(inner)
    value = 0.5 * pre_vals * (1.0 + tanh_val)
    slope = 0.5 * (1.0 + tanh_val) + 0.5 * pre_vals * (1.0 - tanh_val * tanh_val) * coeff * (
        1.0 + 3.0 * 0.044715 * pre_vals * pre_vals
    )
    return (value, slope)


def row_scale(rows_in):
    floats = rows_in.astype(jnp.float32)
    return lax.rsqrt(jnp.mean(floats * floats, axis=-1, keepdims=True) + 1e-06)


def normalised(rows_in):
    return (rows_in.astype(jnp.float32) * row_scale(rows_in)).astype(jnp.bfloat16)


def norm_back(rows_in, grads):
    scale = row_scale(rows_in)
    normal = rows_in.astype(jnp.float32) * scale
    return scale * (grads - normal * jnp.mean(grads * normal, axis=-1, keepdims=True))


def dot(a, b):
    return jnp.dot(a, b, preferred_element_type=jnp.float32)


def dot_t(a, b):
    return lax.dot_general(a, b, (((1,), (1,)), ((), ())), preferred_element_type=jnp.float32)


def t_dot(a, b):
    return lax.dot_general(a, b, (((0,), (0,)), ((), ())), preferred_element_type=jnp.float32)


def mp_sum(partial_value):
    if lax.axis_size("mp") != 2:
        return lax.psum(partial_value, "mp")
    mine = partial_value.astype(jnp.bfloat16)
    other = lax.ppermute(mine, "mp", [(0, 1), (1, 0)])
    return mine.astype(jnp.float32) + other.astype(jnp.float32)


def mp_stats(stats):
    if lax.axis_size("mp") != 2:
        return lax.all_gather(stats, "mp")
    other = lax.ppermute(stats, "mp", [(0, 1), (1, 0)])
    return jnp.stack([stats, other])


def unit_counts(ends, targets, ids):
    positions = jnp.arange(targets.shape[1], dtype=jnp.int32)
    row_local = jnp.sum((ends[:, None, :] <= positions[None, :, None]).astype(jnp.int32), axis=-1)
    rows = jnp.arange(ends.shape[1], dtype=jnp.int32)
    row_onehot = (row_local[:, :, None] == rows[None, None, :]).astype(jnp.bfloat16)
    hits = (targets[:, :, None] == ids[None, None, :]).astype(jnp.bfloat16)
    counts = jnp.einsum("mur,muv->mrv", row_onehot, hits, preferred_element_type=jnp.float32)
    return counts.astype(jnp.bfloat16)


def pick(options, index):
    chosen = None
    for at, option in options:
        chosen = option if chosen is None else jnp.where(index == at, option, chosen)
    return chosen


def on_device(text_rows, durations, unit_targets, w_in, w_out, w_unit):
    micro, row_count, width = text_rows.shape
    segments = lax.axis_size("segment")
    mp_size = lax.axis_size("mp")
    dp_size = lax.axis_size("dp")
    seg = lax.axis_index("segment")
    mp_at = lax.axis_index("mp")
    dp_at = lax.axis_index("dp")
    is_last = seg == segments - 1
    first = w_in[0]
    second = w_out[0]
    chunks = CHUNKS
    rows = micro * row_count // chunks
    text = text_rows.reshape(chunks, rows, width)
    vocab_part = w_unit.shape[1]
    unit_count = unit_targets.shape[1]
    denom = float(micro * unit_count * dp_size)
    lengths = durations[:, 0, :]
    length_f = lengths.astype(jnp.float32).reshape(chunks, rows, 1)
    ends = jnp.cumsum(lengths, axis=-1)

    w_head = lax.all_gather(w_unit, "segment", axis=1, tiled=True)
    part_ids = jnp.arange(vocab_part, dtype=jnp.int32)
    shard_ids = (jnp.arange(segments, dtype=jnp.int32) * mp_size + mp_at) * vocab_part
    head_ids = (shard_ids[:, None] + part_ids[None, :]).reshape(-1)
    head_counts = unit_counts(ends, unit_targets, head_ids).reshape(chunks, rows, -1)

    def forward(rows_in):
        value, _ = gelu_parts(dot(normalised(rows_in), first))
        summed = mp_sum(dot(value.astype(jnp.bfloat16), second))
        return (rows_in.astype(jnp.float32) + summed).astype(jnp.bfloat16)

    def head(final_rows, at):
        counts = head_counts[at].astype(jnp.float32)
        logits = dot(normalised(final_rows), w_head)
        peak = jnp.max(logits, axis=-1)
        total = jnp.sum(jnp.exp(logits - peak[:, None]), axis=-1)
        target = jnp.sum(counts * logits, axis=-1)
        stats = mp_stats(jnp.stack([peak, total, target]))
        top = jnp.max(stats[:, 0], axis=0)
        lse = top + jnp.log(jnp.sum(stats[:, 1] * jnp.exp(stats[:, 0] - top[None]), axis=0))
        loss_rows = length_f[at][:, 0] * lse - jnp.sum(stats[:, 2], axis=0)
        dlogits = (length_f[at] * jnp.exp(logits - lse[:, None]) - counts) / denom
        dnorm = mp_sum(dot_t(dlogits.astype(jnp.bfloat16), w_head)).astype(jnp.bfloat16)
        grad = norm_back(final_rows, dnorm.astype(jnp.float32)).astype(jnp.bfloat16)
        return lse, jnp.sum(loss_rows), grad

    def backward(rows_in, grad_rows):
        _, slope = gelu_parts(dot(normalised(rows_in), first))
        dpre = (dot_t(grad_rows, second) * slope).astype(jnp.bfloat16)
        summed = mp_sum(dot_t(dpre, first))
        return (grad_rows.astype(jnp.float32) + norm_back(rows_in, summed)).astype(jnp.bfloat16)

    inputs, all_inputs, all_grads = [], [], []
    finals, lses, losses = [], [], []
    outgoing = going_back = None
    for clock in range(2 * segments + chunks - 1):
        f_out = b_out = None
        if clock < segments + chunks - 1:
            own = text[min(clock, chunks - 1)]
            rows_in = own
            if clock > 0:
                rows_in = jnp.where(seg == 0, own, shifted(outgoing, "segment", 1))
            inputs.append(rows_in)
            all_inputs.append(lax.all_gather(rows_in, "dp"))
            f_out = forward(rows_in)
        if clock >= segments:
            at = clock - segments
            grad_rows = None
            if clock > segments:
                grad_rows = shifted(going_back, "segment", -1)
            if at < chunks:
                finals.append(outgoing)
                lse, loss_part, grad_final = head(outgoing, at)
                lses.append(lse)
                losses.append(loss_part)
                grad_rows = (
                    grad_final if grad_rows is None else jnp.where(is_last, grad_final, grad_rows)
                )
            options = []
            for other in range(segments):
                stage = clock - 2 * segments + 1 + 2 * other
                if 0 <= stage < len(inputs):
                    options.append((other, inputs[stage]))
            all_grads.append(lax.all_gather(grad_rows, "dp"))
            if clock < 2 * segments + chunks - 2:
                b_out = backward(pick(options, seg), grad_rows)
        outgoing, going_back = f_out, b_out

    final_rows = jnp.stack(finals)
    lse_rows = jnp.stack(lses)
    loss_sum = sum(losses)
    final_rows, lse_rows, loss_sum = lax.psum(
        (
            jnp.where(is_last, final_rows, jnp.zeros_like(final_rows)),
            jnp.where(is_last, lse_rows, 0.0),
            jnp.where(is_last, loss_sum, 0.0),
        ),
        "segment",
    )
    loss = (loss_sum / denom)[None]
    final_norm = normalised(final_rows).reshape(micro * row_count, width)
    own_ids = (seg * mp_size + mp_at) * vocab_part + part_ids
    own_counts = unit_counts(ends, unit_targets, own_ids).reshape(micro * row_count, vocab_part)
    own_logits = dot(final_norm, w_unit)
    own_length = length_f.reshape(-1, 1)
    own_exp = jnp.exp(own_logits - lse_rows.reshape(-1, 1))
    own_dlogits = ((own_length * own_exp - own_counts.astype(jnp.float32)) / denom).astype(
        jnp.bfloat16
    )
    grad_unit = t_dot(final_norm, own_dlogits)
    sum_unit = lax.psum_scatter(grad_unit, "dp", scatter_dimension=0, tiled=True)

    x_all = lax.dynamic_slice_in_dim(jnp.stack(all_inputs), seg, chunks, 0)
    g_all = lax.dynamic_slice_in_dim(jnp.stack(all_grads), segments - 1 - seg, chunks, 0)
    x_all = x_all.reshape(-1, width)
    g_all = g_all.reshape(-1, width)
    n_all = normalised(x_all)
    value, slope = gelu_parts(dot(n_all, first))
    dpre = (dot_t(g_all, second) * slope).astype(jnp.bfloat16)
    share = width // dp_size
    n_share = lax.dynamic_slice_in_dim(n_all, dp_at * share, share, 1)
    g_share = lax.dynamic_slice_in_dim(g_all, dp_at * share, share, 1)
    sum_first = t_dot(n_share, dpre)
    sum_second = t_dot(value.astype(jnp.bfloat16), g_share)
    return (loss, sum_first[None], sum_second[None], sum_unit)


def solution(mesh):
    placed = (
        P(None, "dp", None),
        P(None, "dp", None),
        P(None, "dp"),
        P("segment", None, "mp"),
        P("segment", "mp", None),
        P(None, ("segment", "mp")),
    )
    return jax.shard_map(
        on_device,
        mesh=mesh,
        in_specs=placed,
        out_specs=(
            P("dp"),
            P("segment", "dp", "mp"),
            P("segment", "mp", "dp"),
            P("dp", ("segment", "mp")),
        ),
        check_vma=False,
    )
```

time: 1400 us -> 709 us (0.51)
  waiting for transfers between devices: 882 us -> 192 us
  local copies, waits for them, and re-layouts: 13.6 us -> 42.3 us
  matrix products: 356 us -> 328 us
  starting transfers between devices: 35 us -> 55 us
  blocking collectives: 23.1 us -> 8.67 us
    reduce_scatter x3 -> x0, waiting for transfers between devices: 513 us -> none  [the longest x1 284 us: on_device(): lax.psum_scatter(grad_first, 'dp', scatter_dimension=0, tiled=True)]
    psum x14 -> x1, waiting for transfers between devices: 298 us -> 0.02 us  [on_device(): lax.psum((jnp.where(is_last, final_rows, jnp.zeros_like(final_rows)), jnp...]
    all_gather x1 -> x15, waiting for transfers between devices: 17.4 us -> 77.8 us  [the longest x7 48.9 us: on_device(): all_grads.append(lax.all_gather(grad_rows, 'dp'))]
    reduce_scatter x1, waiting for transfers between devices: 0.02 us -> 29.4 us  [on_device(): lax.psum_scatter(grad_unit, 'dp', scatter_dimension=0, tiled=True)]
    dot_general x45 -> x33, matrix products: 356 us -> 328 us  [the longest x18 135 us: dot(): return jnp.dot(a, b, preferred_element_type=jnp.float32)]
    ppermute x12, waiting for transfers between devices: 53.1 us -> 79.1 us  [shifted(): return lax.ppermute(block, axis, route)]
    select_n x20 -> x4, other arithmetic: 27.9 us -> 4.91 us  [the longest x3 3.76 us: on_device(): jnp.where(is_last, grad_final, grad_rows)]
    unnamed x124 -> x116, local copies, waits for them, and re-layouts: 11.4 us -> 33.3 us
  transfers between devices with their start and end apart: 31 -> 50, of which waited for: 29 -> 22; matrix products, arithmetic and copies ran while one was open for 17% -> 59% of each run, Pallas kernels for 0% -> 0%
where the time goes in v1:
time: 709 us; the launch traced here: 699 us
  matrix products  328 us (46%)
  waiting for transfers between devices  192 us (27%)
  starting transfers between devices  55 us (8%)
  other arithmetic  53.1 us (7%)
  local copies, waits for them, and re-layouts  42.3 us (6%)
  between operations  19.8 us (3%)
  blocking collectives  8.67 us (1%)
    dot_general x18, matrix products, dot(): return jnp.dot(a, b, preferred_element_type=jnp.float32)  135 us
    dot_general x10, matrix products, dot_t(): lax.dot_general(a, b, (((1,), (1,)), ((), ())), preferred_element_type=jn...  113 us
    ppermute x12, waiting for transfers between devices, shifted(): return lax.ppermute(block, axis, route)  79.1 us
    dot_general x3, matrix products, t_dot(): lax.dot_general(a, b, (((0,), (0,)), ((), ())), preferred_element_type=jn...  67 us
    all_gather x7, waiting for transfers between devices, on_device(): all_grads.append(lax.all_gather(grad_rows, 'dp'))  48.9 us
    ppermute x12, starting transfers between devices, shifted(): return lax.ppermute(block, axis, route)  37.9 us
    unnamed x116, local copies, waits for them, and re-layouts  33.3 us
    reduce_scatter x1, waiting for transfers between devices, on_device(): lax.psum_scatter(grad_unit, 'dp', scatter_dimension=0, tiled=True)  29.4 us
  transfers between devices with their start and end apart: 50, of which 22 were waited for; matrix products, arithmetic and copies ran while one was open for 59% of the time, Pallas kernels for 0%

profile of v1, /device:TPU:11, one launch (start us, length us, event | category | flops | bytes accessed | tf_op | source)
XLA Modules:
  0.0 698.9 jit_solution(10654775302443204258)
XLA Ops:
  52.5 8.6 %fusion.269 = bf16[128,1024]{1,0:T(8,128)(2,1)S(1)} fusion(bf16[1,4096,1024]{2,1,0:T(8,128)(2,1)} %param.10, bf16[1,1024,4096]{2,1,0:T(8,128)(2,1)} %param.9, bf16[128,1024]{1,0:T(8,128)(2,1)} %get-tuple-element.47, f32[128]{0:T(128)S(1)} %add_rsqrt_fusion.16), kind=kOutput, calls=%fused_computation.253 | convolution fusion | flops 2152726528 | bytes 17302016 | tf_op jit(solution)/shard_map/dot_general | solution.py:42
  79.7 9.5 %fusion.81 = bf16[4,128,5120]{2,1,0:T(8,128)(2,1)} fusion(s32[5120]{0:T(1024)S(1)} %add.552, s32[4,512]{1,0:T(4,128)S(1)} %copy-done.49, s32[4,512]{1,0:T(4,128)S(1)} %convert_reduce_fusion), kind=kOutput, calls=%fused_computation.86 | convolution fusion | flops 2697723904 | bytes 5279744 | tf_op jit(solution)/shard_map/mur,muv->mrv/dot_general | solution.py:74
  134.5 11.0 %fusion.278 = bf16[128,1024]{1,0:T(8,128)(2,1)S(1)} fusion(bf16[1,4096,1024]{2,1,0:T(8,128)(2,1)} %param.10, bf16[1,1024,4096]{2,1,0:T(8,128)(2,1)} %param.9, bf16[128,1024]{1,0:T(8,128)(2,1)S(1)} %get-tuple-element.23, f32[128]{0:T(128)S(1)} %add_rsqrt_fusion.11), kind=kOutput, calls=%fused_computation.256 | convolution fusion | flops 2152726528 | bytes 17302016 | tf_op jit(solution)/shard_map/dot_general | solution.py:42
  161.1 11.4 %collective-permute-done.14 = bf16[128,1024]{1,0:T(8,128)(2,1)S(1)} collective-permute-done((bf16[128,1024]{1,0:T(8,128)(2,1)S(1)}, bf16[128,1024]{1,0:T(8,128)(2,1)S(1)}, u32[]{:S(2)}, u32[]{:S(2)}) %collective-permute-start.14) | collective-permute-done | bytes 262176 | tf_op jit(solution)/shard_map/ppermute | solution.py:12
  172.9 9.1 %fusion.281 = bf16[128,1024]{1,0:T(8,128)(2,1)} fusion(bf16[1,4096,1024]{2,1,0:T(8,128)(2,1)} %param.10, bf16[1,1024,4096]{2,1,0:T(8,128)(2,1)} %param.9, bf16[128,1024]{1,0:T(8,128)(2,1)S(1)} %get-tuple-element.20, f32[128]{0:T(128)S(1)} %add_rsqrt_fusion.9), kind=kOutput, calls=%fused_computation.257 | convolution fusion | flops 2152726528 | bytes 17302016 | tf_op jit(solution)/shard_map/dot_general | solution.py:42
  209.3 28.9 %all-gather.29.cloned.1.call-done = bf16[1024,5120]{1,0:T(8,128)(2,1)} async-done(((bf16[1024,1280]{1,0:T(8,128)(2,1)}), bf16[1024,5120]{1,0:T(8,128)(2,1)}) %all-gather.29.cloned.1.call-update) | async-done | bytes 10485776 | tf_op jit(solution)/shard_map/all_gather | solution.py:106
  258.2 8.9 %fusion.284 = bf16[128,1024]{1,0:T(8,128)(2,1)S(1)} fusion(bf16[1024,5120]{1,0:T(8,128)(2,1)} %all-gather.29.cloned.1.call-done, f32[128,5120]{1,0:T(8,128)} %copy-done.3, f32[128]{0:T(128)S(1)} %get-tuple-element.34, f32[128]{0:T(128)S(1)} %get-tuple-element.69, bf16[4,128,5120]{2,1,0:T(8,128)(2,1)} %fusion.81), kind=kOutput, calls=%fused_computation.258 | convolution fusion | flops 1346240512 | bytes 14681088 | tf_op jit(solution)/shard_map/dot_general | solution.py:46
  274.6 13.5 %fusion.245 = bf16[128,1024]{1,0:T(8,128)(2,1)} fusion(bf16[1,1024,4096]{2,1,0:T(8,128)(2,1)} %param.9, bf16[128,1024]{1,0:T(8,128)(2,1)} %fusion.360, bf16[1,4096,1024]{2,1,0:T(8,128)(2,1)} %param.10, f32[128,4096]{1,0:T(8,128)} %fusion.65), kind=kOutput, calls=%fused_computation.245 | convolution fusion | flops 2157576192 | bytes 19398656 | tf_op jit(solution)/shard_map/dot_general | solution.py:46
  288.4 9.7 %fusion.287 = bf16[128,1024]{1,0:T(8,128)(2,1)} fusion(bf16[1024,5120]{1,0:T(8,128)(2,1)} %all-gather.29.cloned.1.call-done, f32[128,5120]{1,0:T(8,128)} %copy-done.2, f32[128]{0:T(128)S(1)} %get-tuple-element.35, f32[128]{0:T(128)S(1)} %get-tuple-element.68, bf16[4,128,5120]{2,1,0:T(8,128)(2,1)} %fusion.81), kind=kOutput, calls=%fused_computation.259 | convolution fusion | flops 1346240512 | bytes 14681088 | tf_op jit(solution)/shard_map/dot_general | solution.py:46
  304.5 12.4 %collective-permute-done.20 = bf16[128,1024]{1,0:T(8,128)(2,1)S(1)} collective-permute-done((bf16[128,1024]{1,0:T(8,128)(2,1)S(1)}, bf16[128,1024]{1,0:T(8,128)(2,1)S(1)}, u32[]{:S(2)}, u32[]{:S(2)}) %collective-permute-start.20) | collective-permute-done | bytes 262176 | tf_op jit(solution)/shard_map/ppermute | solution.py:12
  318.2 13.3 %fusion.248 = bf16[128,1024]{1,0:T(8,128)(2,1)} fusion(bf16[1,1024,4096]{2,1,0:T(8,128)(2,1)} %param.9, bf16[128,1024]{1,0:T(8,128)(2,1)S(1)} %fusion.443, bf16[1,4096,1024]{2,1,0:T(8,128)(2,1)} %param.10, f32[128,4096]{1,0:T(8,128)} %fusion.61), kind=kOutput, calls=%fused_computation.246 | convolution fusion | flops 2157576192 | bytes 19398656 | tf_op jit(solution)/shard_map/dot_general | solution.py:46
  332.9 9.0 %fusion.290 = bf16[128,1024]{1,0:T(8,128)(2,1)S(1)} fusion(bf16[1024,5120]{1,0:T(8,128)(2,1)} %all-gather.29.cloned.1.call-done, f32[128,5120]{1,0:T(8,128)} %copy-done.1, f32[128]{0:T(128)S(1)} %get-tuple-element.36, f32[128]{0:T(128)S(1)} %get-tuple-element.67, bf16[4,128,5120]{2,1,0:T(8,128)(2,1)} %fusion.81), kind=kOutput, calls=%fused_computation.260 | convolution fusion | flops 1346240512 | bytes 14681088 | tf_op jit(solution)/shard_map/dot_general | solution.py:46
  348.1 12.7 %collective-permute-done.23 = bf16[128,1024]{1,0:T(8,128)(2,1)S(1)} collective-permute-done((bf16[128,1024]{1,0:T(8,128)(2,1)}, bf16[128,1024]{1,0:T(8,128)(2,1)S(1)}, u32[]{:S(2)}, u32[]{:S(2)}) %collective-permute-start.23) | collective-permute-done | bytes 262176 | tf_op jit(solution)/shard_map/ppermute | solution.py:12
  362.1 13.3 %fusion.251 = bf16[128,1024]{1,0:T(8,128)(2,1)} fusion(bf16[1,1024,4096]{2,1,0:T(8,128)(2,1)} %param.9, bf16[128,1024]{1,0:T(8,128)(2,1)S(1)} %fusion.442, bf16[1,4096,1024]{2,1,0:T(8,128)(2,1)} %param.10, f32[128,4096]{1,0:T(8,128)} %fusion.57), kind=kOutput, calls=%fused_computation.247 | convolution fusion | flops 2157576192 | bytes 19398656 | tf_op jit(solution)/shard_map/dot_general | solution.py:46
  399.2 12.1 %fusion.254 = bf16[128,1024]{1,0:T(8,128)(2,1)S(1)} fusion(bf16[1,1024,4096]{2,1,0:T(8,128)(2,1)} %param.9, bf16[128,1024]{1,0:T(8,128)(2,1)S(1)} %fusion.441, bf16[1,4096,1024]{2,1,0:T(8,128)(2,1)} %param.10, f32[128,4096]{1,0:T(8,128)S(1)} %copy-done.39), kind=kOutput, calls=%fused_computation.248 | convolution fusion | flops 2157576192 | bytes 19398656 | tf_op jit(solution)/shard_map/dot_general | solution.py:46
  428.5 12.8 %fusion.257 = bf16[128,1024]{1,0:T(8,128)(2,1)S(1)} fusion(bf16[1,1024,4096]{2,1,0:T(8,128)(2,1)} %param.9, bf16[128,1024]{1,0:T(8,128)(2,1)S(1)} %collective-permute-done.28, bf16[1,4096,1024]{2,1,0:T(8,128)(2,1)} %param.10, f32[128,4096]{1,0:T(8,128)} %fusion.49), kind=kOutput, calls=%fused_computation.249 | convolution fusion | flops 2157576192 | bytes 19398656 | tf_op jit(solution)/shard_map/dot_general | solution.py:46
  457.1 12.2 %fusion.260 = bf16[128,1024]{1,0:T(8,128)(2,1)S(1)} fusion(bf16[1,1024,4096]{2,1,0:T(8,128)(2,1)} %param.9, bf16[128,1024]{1,0:T(8,128)(2,1)S(1)} %collective-permute-done.30, bf16[1,4096,1024]{2,1,0:T(8,128)(2,1)} %param.10, f32[128,4096]{1,0:T(8,128)S(1)} %copy-done.38), kind=kOutput, calls=%fused_computation.250 | convolution fusion | flops 2157576192 | bytes 19398656 | tf_op jit(solution)/shard_map/dot_general | solution.py:46
  477.6 25.0 %fusion.41 = f32[2048,4096]{1,0:T(8,128)} fusion(bf16[2048,1024]{1,0:T(8,128)(2,1)} %bitcast.366, bf16[1,1024,4096]{2,1,0:T(8,128)(2,1)} %param.9), kind=kOutput, calls=%fused_computation.44 | convolution fusion | flops 17179869184 | bytes 46137344 | tf_op jit(solution)/shard_map/dot_general | solution.py:42
  515.4 8.7 %all-reduce = (f32[]{:T(128)}, f32[512]{0:T(512)S(1)}) all-reduce(f32[]{:T(128)S(6)} %select_n.131, f32[512]{0:T(512)S(1)} %fusion.485), channel_id=1, replica_groups=mesh['segment'=4,'mp'=2,'dp'=4] {'segment'}, use_global_device_ids=true, to_apply=%region_41.42 | all-reduce | flops 513 | bytes 4104 | tf_op jit(solution)/shard_map/psum | solution.py:177
  543.4 21.7 %all-gather.55.cloned.1.call-done = bf16[512,1024]{1,0:T(8,128)(2,1)} async-done(((bf16[128,1024]{1,0:T(8,128)(2,1)}), bf16[512,1024]{1,0:T(8,128)(2,1)}) %all-gather.55.cloned.1.call-update) | async-done | bytes 1048592 | tf_op jit(solution)/shard_map/all_gather | solution.py:169
  567.3 27.2 %all-gather.57.cloned.1.call-done = bf16[512,1024]{1,0:T(8,128)(2,1)} async-done(((bf16[128,1024]{1,0:T(8,128)(2,1)}), bf16[512,1024]{1,0:T(8,128)(2,1)}) %all-gather.57.cloned.1.call-update) | async-done | bytes 1048592 | tf_op jit(solution)/shard_map/all_gather | solution.py:169
  601.5 19.1 %fusion.84 = f32[1,4096,256]{2,1,0:T(8,128)} fusion(f32[2048,4096]{1,0:T(8,128)} %fusion.41, bf16[2048,1024]{1,0:T(8,128)(2,1)S(1)} %bitcast.367, s32[]{:T(128)S(6)} %select_n.133), kind=kOutput, calls=%fused_computation.87 | convolution fusion | flops 4370464768 | bytes 38797316 | tf_op jit(solution)/shard_map/dot_general | solution.py:50
  620.6 40.8 %convolution_bitcast_fusion = f32[1,256,4096]{2,1,0:T(8,128)} fusion(f32[2048,4096]{1,0:T(8,128)} %fusion.41, bf16[2048,1024]{1,0:T(8,128)(2,1)} %bitcast.368, bf16[1,4096,1024]{2,1,0:T(8,128)(2,1)} %param.10, bf16[2048,256]{1,0:T(8,128)(2,1)S(1)} %copy-done.40), kind=kOutput, calls=%fused_computation.88 | convolution fusion | flops 21634220032 | bytes 51380224 | tf_op jit(solution)/shard_map/dot_general | solution.py:50
  661.4 29.4 %reduce-scatter.2.cloned.1.call-done = f32[256,1280]{1,0:T(8,128)} async-done(((f32[1024,1280]{1,0:T(8,128)}), f32[256,1280]{1,0:T(8,128)}) %reduce-scatter.2.cloned.1.call-update) | async-done | bytes 1310736 | tf_op jit(solution)/shard_map/reduce_scatter | solution.py:196
  (348 shorter events, 299.0 us)
Async XLA Ops:
  7.2 114.1 %all-gather.31.cloned.1.call-start = ((), (), s32[]{:S(2)}) async-start(), calls=%async_computation.2 | async-start | bytes 1310720 | tf_op jit(solution)/shard_map/all_gather | solution.py:149
  8.9 143.4 %all-gather.33.cloned.1.call-start = ((), (), s32[]{:S(2)}) async-start(), calls=%async_computation.5 | async-start | bytes 1310720 | tf_op jit(solution)/shard_map/all_gather | solution.py:149
  31.0 158.1 %all-gather.35.cloned.1.call-start = ((), (), s32[]{:S(2)}) async-start(), calls=%async_computation.6 | async-start | bytes 1310720 | tf_op jit(solution)/shard_map/all_gather | solution.py:149
  52.4 154.7 %all-gather.37.cloned.1.call-start = ((), (), s32[]{:S(2)}) async-start(), calls=%async_computation.7 | async-start | bytes 1310720 | tf_op jit(solution)/shard_map/all_gather | solution.py:149
  74.6 163.6 %all-gather.29.cloned.1.call-start = ((), (), s32[]{:S(2)}) async-start(), calls=%async_computation.1 | async-start | bytes 13107200 | tf_op jit(solution)/shard_map/all_gather | solution.py:106
  75.2 337.5 %all-gather.39.cloned.1.call-start = ((), (), s32[]{:S(2)}) async-start(), calls=%async_computation.8 | async-start | bytes 1310720 | tf_op jit(solution)/shard_map/all_gather | solution.py:149
  100.4 11.3 %collective-permute-start.8 = (bf16[128,1024]{1,0:T(8,128)(2,1)S(1)}, bf16[128,1024]{1,0:T(8,128)(2,1)S(1)}, u32[]{:S(2)}, u32[]{:S(2)}) collective-permute-start(bf16[128,1024]{1,0:T(8,128)(2,1)S(1)} %get-tuple-element.39), channel_id=1, source_target_pairs={{0,8},{8,16},{16,24},{1,9},{9,17},{17,25},{2,10},{10,18},{18,26},{... | collective-permute-start | bytes 786440 | tf_op jit(solution)/shard_map/ppermute | solution.py:12
  128.4 286.5 %all-gather.41.cloned.1.call-start = ((), (), s32[]{:S(2)}) async-start(), calls=%async_computation.9 | async-start | bytes 1310720 | tf_op jit(solution)/shard_map/all_gather | solution.py:149
  156.8 15.7 %collective-permute-start.14 = (bf16[128,1024]{1,0:T(8,128)(2,1)S(1)}, bf16[128,1024]{1,0:T(8,128)(2,1)S(1)}, u32[]{:S(2)}, u32[]{:S(2)}) collective-permute-start(bf16[128,1024]{1,0:T(8,128)(2,1)S(1)} %get-tuple-element.53), channel_id=1, source_target_pairs={{0,8},{8,16},{16,24},{1,9},{9,17},{17,25},{2,10},{10,18},{18,26},{... | collective-permute-start | bytes 786440 | tf_op jit(solution)/shard_map/ppermute | solution.py:12
  161.0 258.7 %all-reduce.3.cloned.1.call-start = ((), (), s32[]{:S(2)}) async-start(), calls=%async_computation.3 | async-start | bytes 2097152 | tf_op jit(solution)/shard_map/psum | solution.py:177
  194.6 248.8 %all-gather.43.cloned.1.call-start = ((), (), s32[]{:S(2)}) async-start(), calls=%async_computation.10 | async-start | bytes 1310720 | tf_op jit(solution)/shard_map/all_gather | solution.py:149
  200.7 331.3 %all-gather.45.cloned.1.call-start = ((), (), s32[]{:S(2)}) async-start(), calls=%async_computation.11 | async-start | bytes 1310720 | tf_op jit(solution)/shard_map/all_gather | solution.py:169
  298.4 235.9 %all-gather.47.cloned.1.call-start = ((), (), s32[]{:S(2)}) async-start(), calls=%async_computation.12 | async-start | bytes 1310720 | tf_op jit(solution)/shard_map/all_gather | solution.py:169
  301.1 15.8 %collective-permute-start.20 = (bf16[128,1024]{1,0:T(8,128)(2,1)S(1)}, bf16[128,1024]{1,0:T(8,128)(2,1)S(1)}, u32[]{:S(2)}, u32[]{:S(2)}) collective-permute-start(bf16[128,1024]{1,0:T(8,128)(2,1)S(1)} %fusion.368), channel_id=1, source_target_pairs={{8,0},{16,8},{24,16},{9,1},{17,9},{25,17},{10,2},{18,10},{26,18},{... | collective-permute-start | bytes 786440 | tf_op jit(solution)/shard_map/ppermute | solution.py:12
  345.2 15.6 %collective-permute-start.23 = (bf16[128,1024]{1,0:T(8,128)(2,1)}, bf16[128,1024]{1,0:T(8,128)(2,1)S(1)}, u32[]{:S(2)}, u32[]{:S(2)}) collective-permute-start(bf16[128,1024]{1,0:T(8,128)(2,1)} %fusion.377), channel_id=1, source_target_pairs={{8,0},{16,8},{24,16},{9,1},{17,9},{25,17},{10,2},{18,10},{26,18},{... | collective-permute-start | bytes 786440 | tf_op jit(solution)/shard_map/ppermute | solution.py:12
  347.8 188.7 %all-gather.49.cloned.1.call-start = ((), (), s32[]{:S(2)}) async-start(), calls=%async_computation.13 | async-start | bytes 1310720 | tf_op jit(solution)/shard_map/all_gather | solution.py:169
  390.0 148.8 %all-gather.51.cloned.1.call-start = ((), (), s32[]{:S(2)}) async-start(), calls=%async_computation.14 | async-start | bytes 1310720 | tf_op jit(solution)/shard_map/all_gather | solution.py:169
  417.8 10.7 %collective-permute-start.28 = (bf16[128,1024]{1,0:T(8,128)(2,1)S(1)}, bf16[128,1024]{1,0:T(8,128)(2,1)S(1)}, u32[]{:S(2)}, u32[]{:S(2)}) collective-permute-start(bf16[128,1024]{1,0:T(8,128)(2,1)S(1)} %fusion.392), channel_id=1, source_target_pairs={{8,0},{16,8},{24,16},{9,1},{17,9},{25,17},{10,2},{18,10},{26,18},{... | collective-permute-start | bytes 786440 | tf_op jit(solution)/shard_map/ppermute | solution.py:12
  421.3 119.8 %all-gather.53.cloned.1.call-start = ((), (), s32[]{:S(2)}) async-start(), calls=%async_computation.15 | async-start | bytes 1310720 | tf_op jit(solution)/shard_map/all_gather | solution.py:169
  446.2 10.8 %collective-permute-start.30 = (bf16[128,1024]{1,0:T(8,128)(2,1)S(1)}, bf16[128,1024]{1,0:T(8,128)(2,1)S(1)}, u32[]{:S(2)}, u32[]{:S(2)}) collective-permute-start(bf16[128,1024]{1,0:T(8,128)(2,1)S(1)} %fusion.398), channel_id=1, source_target_pairs={{8,0},{16,8},{24,16},{9,1},{17,9},{25,17},{10,2},{18,10},{26,18},{... | collective-permute-start | bytes 786440 | tf_op jit(solution)/shard_map/ppermute | solution.py:12
  451.6 113.5 %all-gather.55.cloned.1.call-start = ((), (), s32[]{:S(2)}) async-start(), calls=%async_computation.16 | async-start | bytes 1310720 | tf_op jit(solution)/shard_map/all_gather | solution.py:169
  475.1 119.4 %all-gather.57.cloned.1.call-start = ((), (), s32[]{:S(2)}) async-start(), calls=%async_computation.17 | async-start | bytes 1310720 | tf_op jit(solution)/shard_map/all_gather | solution.py:169
  475.7 26.9 %collective-permute-start.32 = (bf16[128,1024]{1,0:T(8,128)(2,1)S(1)}, bf16[128,1024]{1,0:T(8,128)(2,1)S(1)}, u32[]{:S(2)}, u32[]{:S(2)}) collective-permute-start(bf16[128,1024]{1,0:T(8,128)(2,1)S(1)} %fusion.404), channel_id=1, source_target_pairs={{8,0},{16,8},{24,16},{9,1},{17,9},{25,17},{10,2},{18,10},{26,18},{... | collective-permute-start | bytes 786440 | tf_op jit(solution)/shard_map/ppermute | solution.py:12
  503.4 187.5 %reduce-scatter.2.cloned.1.call-start = ((), (), s32[]{:S(2)}) async-start(), calls=%async_computation.4 | async-start | bytes 6553600 | tf_op jit(solution)/shard_map/reduce_scatter | solution.py:196
  (78 other events, 870.7 us)
Sparse Core Ops, SparseCore 0:
  9.6 28.8 all-gather.30
  40.6 27.4 all-gather.32
  70.2 27.4 all-gather.34
  99.0 27.4 all-gather.36
  128.2 109.9 all-gather.28
  239.7 27.6 all-gather.38
  268.9 27.4 all-gather.40
  299.5 62.8 all-reduce.2
  364.0 27.4 all-gather.42
  392.9 27.4 all-gather.44
  421.9 27.4 all-gather.46
  450.8 27.4 all-gather.48
  479.8 27.4 all-gather.50
  508.7 27.4 all-gather.52
  537.6 27.4 all-gather.54
  567.1 27.4 all-gather.56
  597.2 93.5 reduce-scatter.1

commit v2 on v1

v2 whole, which is shorter than its diff:
```python
import functools
import jax
import jax.numpy as jnp
from jax import lax
from jax.experimental import pallas as pl
from jax.experimental.pallas import tpu as pltpu
from jax.sharding import PartitionSpec as P

CHUNKS = 4
BF16 = jnp.bfloat16
F32 = jnp.float32
MIB = 1024 * 1024


def shifted(block, axis, distance):
    devices = range(lax.axis_size(axis))
    route = [(i - distance, i) for i in devices if i - distance in devices]
    return lax.ppermute(block, axis, route)


def swapped(block):
    return lax.ppermute(block, "mp", [(0, 1), (1, 0)])


def gelu_parts(pre_vals):
    coeff = 0.7978845608
    square = pre_vals * pre_vals
    inner = coeff * pre_vals * (1.0 + 0.044715 * square)
    half = 0.5 * (1.0 + jnp.tanh(inner))
    value = pre_vals * half
    slope = half + 2.0 * value * (1.0 - half) * coeff * (1.0 + 3.0 * 0.044715 * square)
    return (value, slope)


def row_scale(rows_in):
    floats = rows_in.astype(F32)
    return lax.rsqrt(jnp.mean(floats * floats, axis=-1, keepdims=True) + 1e-06)


def normalised(rows_in):
    return (rows_in.astype(F32) * row_scale(rows_in)).astype(BF16)


def norm_back(rows_in, grads):
    scale = row_scale(rows_in)
    normal = rows_in.astype(F32) * scale
    return scale * (grads - normal * jnp.mean(grads * normal, axis=-1, keepdims=True))


def dot(a, b):
    return jnp.dot(a, b, preferred_element_type=F32)


def dot_t(a, b):
    return lax.dot_general(a, b, (((1,), (1,)), ((), ())), preferred_element_type=F32)


def t_dot(a, b):
    return lax.dot_general(a, b, (((0,), (0,)), ((), ())), preferred_element_type=F32)


def tile_of(size, most):
    if size <= most:
        return size
    return max(t for t in range(128, most + 1, 128) if size % t == 0)


def params(limit):
    return pltpu.CompilerParams(vmem_limit_bytes=limit * MIB)


def added(refs):
    total = refs[0][...].astype(F32)
    for ref in refs[1:]:
        total = total + ref[...].astype(F32)
    return total


def chosen(index, candidates):
    value = candidates[0][1]
    for at, option in candidates[1:]:
        value = jnp.where(index == at, option, value)
    return value


def forward_kernel(where, own, arrived, w_in, w_out, rows_out, part, normed, total):
    step = pl.program_id(0)

    @pl.when(step == 0)
    def _():
        rows = jnp.where(where[0] == 0, own[...], arrived[...])
        rows_out[...] = rows
        normed[...] = normalised(rows)
        total[...] = jnp.zeros_like(total)

    value, _ = gelu_parts(dot(normed[...], w_in[...]))
    total[...] += dot(value.astype(BF16), w_out[...])

    @pl.when(step == pl.num_programs(0) - 1)
    def _():
        part[...] = total[...].astype(part.dtype)


def forward_section(where, own, arrived, w_in, w_out, part_type):
    rows, width = own.shape
    hidden = w_in.shape[1]
    tile = tile_of(hidden, 512)
    whole = pl.BlockSpec((rows, width), lambda j, s: (0, 0))
    return pl.pallas_call(
        forward_kernel,
        grid_spec=pltpu.PrefetchScalarGridSpec(
            num_scalar_prefetch=1,
            grid=(hidden // tile,),
            in_specs=[
                whole,
                whole,
                pl.BlockSpec((width, tile), lambda j, s: (0, j)),
                pl.BlockSpec((tile, width), lambda j, s: (j, 0)),
            ],
            out_specs=[whole, whole],
            scratch_shapes=[pltpu.VMEM((rows, width), BF16), pltpu.VMEM((rows, width), F32)],
        ),
        out_shape=[
            jax.ShapeDtypeStruct((rows, width), BF16),
            jax.ShapeDtypeStruct((rows, width), part_type),
        ],
        compiler_params=params(32),
        cost_estimate=pl.CostEstimate(
            flops=4 * rows * width * hidden,
            bytes_accessed=4 * width * hidden,
            transcendentals=rows * hidden,
        ),
        name="section_forward",
    )(where, own, arrived, w_in, w_out)


def finish_forward_kernel(*refs):
    refs[-1][...] = added(refs[:-1]).astype(BF16)


def finish_forward(rows, pieces):
    return pl.pallas_call(
        finish_forward_kernel,
        out_shape=jax.ShapeDtypeStruct(rows.shape, BF16),
        compiler_params=params(16),
        name="finish_forward",
    )(rows, *pieces)


def finish_backward_kernel(rows, grads, *refs):
    summed = added(refs[:-1])
    refs[-1][...] = (grads[...].astype(F32) + norm_back(rows[...], summed)).astype(BF16)


def finish_backward(rows, grads, pieces):
    return pl.pallas_call(
        finish_backward_kernel,
        out_shape=jax.ShapeDtypeStruct(rows.shape, BF16),
        compiler_params=params(16),
        name="finish_backward",
    )(rows, grads, *pieces)


def backward_kernel(owners, pieces, last, has_arrived, where, *refs):
    stashed, refs = refs[: len(owners)], refs[len(owners) :]
    final = None
    if pieces:
        final, parts, refs = refs[0], refs[1 : 1 + pieces], refs[1 + pieces :]
    if has_arrived:
        arrived, refs = refs[0], refs[1:]
    w_in, w_out, rows_out, grads_out, part, normed, total = refs
    step = pl.program_id(0)

    @pl.when(step == 0)
    def _():
        rows = chosen(where[0], [(at, ref[...]) for at, ref in zip(owners, stashed)])
        grads = None
        if pieces:
            dnorm = added(parts).astype(BF16).astype(F32)
            grads = norm_back(final[...], dnorm).astype(BF16)
        if has_arrived:
            grads = arrived[...] if grads is None else jnp.where(where[0] == last, grads, arrived[...])
        rows_out[...] = rows
        grads_out[...] = grads
        normed[...] = normalised(rows)
        total[...] = jnp.zeros_like(total)

    _, slope = gelu_parts(dot(normed[...], w_in[...]))
    dpre = (dot_t(grads_out[...], w_out[...]) * slope).astype(BF16)
    total[...] += dot_t(dpre, w_in[...])

    @pl.when(step == pl.num_programs(0) - 1)
    def _():
        part[...] = total[...].astype(part.dtype)


def backward_section(where, last, options, final, parts, arrived, w_in, w_out, part_type):
    width, hidden = w_in.shape
    rows = options[0][1].shape[0]
    tile = tile_of(hidden, 512)
    whole = pl.BlockSpec((rows, width), lambda j, s: (0, 0))
    operands = [option for _, option in options]
    if parts:
        operands += [final, *parts]
    if arrived is not None:
        operands.append(arrived)
    body = functools.partial(
        backward_kernel, tuple(at for at, _ in options), len(parts), last, arrived is not None
    )
    return pl.pallas_call(
        body,
        grid_spec=pltpu.PrefetchScalarGridSpec(
            num_scalar_prefetch=1,
            grid=(hidden // tile,),
            in_specs=[whole] * len(operands)
            + [
                pl.BlockSpec((width, tile), lambda j, s: (0, j)),
                pl.BlockSpec((tile, width), lambda j, s: (j, 0)),
            ],
            out_specs=[whole, whole, whole],
            scratch_shapes=[pltpu.VMEM((rows, width), BF16), pltpu.VMEM((rows, width), F32)],
        ),
        out_shape=[
            jax.ShapeDtypeStruct((rows, width), BF16),
            jax.ShapeDtypeStruct((rows, width), BF16),
            jax.ShapeDtypeStruct((rows, width), part_type),
        ],
        compiler_params=params(32),
        cost_estimate=pl.CostEstimate(
            flops=6 * rows * width * hidden,
            bytes_accessed=4 * width * hidden,
            transcendentals=rows * hidden,
        ),
        name="section_backward",
    )(where, *operands, w_in, w_out)


def lane_fill(columns, shape):
    lane = lax.broadcasted_iota(jnp.int32, shape, 1)
    filled = jnp.zeros(shape, F32)
    for at, column in enumerate(columns):
        filled = jnp.where(lane == at, column, filled)
    return filled


def logits_kernel(final, w_head, counts, logits, stats, normed, peak, total, target):
    step = pl.program_id(0)

    @pl.when(step == 0)
    def _():
        normed[...] = normalised(final[...])
        peak[...] = jnp.full_like(peak, -jnp.inf)
        total[...] = jnp.zeros_like(total)
        target[...] = jnp.zeros_like(target)

    values = dot(normed[...], w_head[...])
    logits[...] = values
    higher = jnp.maximum(peak[...], jnp.max(values, axis=-1, keepdims=True))
    total[...] = total[...] * jnp.exp(peak[...] - higher) + jnp.sum(
        jnp.exp(values - higher), axis=-1, keepdims=True
    )
    peak[...] = higher
    target[...] += jnp.sum(counts[...].astype(F32) * values, axis=-1, keepdims=True)

    @pl.when(step == pl.num_programs(0) - 1)
    def _():
        stats[...] = lane_fill([peak[...], total[...], target[...]], stats.shape)


def head_logits(final, w_head, counts, at):
    rows, width = final.shape
    vocab = w_head.shape[1]
    tile = tile_of(vocab, 1024)
    return pl.pallas_call(
        logits_kernel,
        grid=(vocab // tile,),
        in_specs=[
            pl.BlockSpec((rows, width), lambda j: (0, 0)),
            pl.BlockSpec((width, tile), lambda j: (0, j)),
            pl.BlockSpec((None, rows, tile), lambda j: (at, 0, j)),
        ],
        out_specs=[
            pl.BlockSpec((rows, tile), lambda j: (0, j)),
            pl.BlockSpec((rows, 128), lambda j: (0, 0)),
        ],
        out_shape=[
            jax.ShapeDtypeStruct((rows, vocab), F32),
            jax.ShapeDtypeStruct((rows, 128), F32),
        ],
        scratch_shapes=[pltpu.VMEM((rows, width), BF16)] + [pltpu.VMEM((rows, 1), F32)] * 3,
        compiler_params=params(32),
        cost_estimate=pl.CostEstimate(
            flops=2 * rows * width * vocab,
            bytes_accessed=2 * width * vocab + 6 * rows * vocab,
            transcendentals=rows * vocab,
        ),
        name="head_logits",
    )(final, w_head, counts)


def head_grads_kernel(shards, denom, *refs):
    stats, refs = refs[:shards], refs[shards:]
    lengths, logits, counts, w_head, part, results, lse, total = refs
    step = pl.program_id(0)

    @pl.when(step == 0)
    def _():
        tables = [ref[...] for ref in stats]
        top = tables[0][:, 0:1]
        for table in tables[1:]:
            top = jnp.maximum(top, table[:, 0:1])
        mass = sum(table[:, 1:2] * jnp.exp(table[:, 0:1] - top) for table in tables)
        target = sum(table[:, 2:3] for table in tables)
        lse[...] = top + jnp.log(mass)
        results[...] = lane_fill([lse[...], lengths[...] * lse[...] - target], results.shape)
        total[...] = jnp.zeros_like(total)

    exped = lengths[...] * jnp.exp(logits[...] - lse[...])
    dlogits = ((exped - counts[...].astype(F32)) / denom).astype(BF16)
    total[...] += dot_t(dlogits, w_head[...])

    @pl.when(step == pl.num_programs(0) - 1)
    def _():
        part[...] = total[...].astype(part.dtype)


def head_grads(stats, lengths, logits, counts, at, w_head, denom, part_type):
    rows, vocab = logits.shape
    width = w_head.shape[0]
    tile = tile_of(vocab, 1024)
    return pl.pallas_call(
        functools.partial(head_grads_kernel, len(stats), denom),
        grid=(vocab // tile,),
        in_specs=[pl.BlockSpec((rows, 128), lambda j: (0, 0))] * len(stats)
        + [
            pl.BlockSpec((None, rows, 1), lambda j: (at, 0, 0)),
            pl.BlockSpec((rows, tile), lambda j: (0, j)),
            pl.BlockSpec((None, rows, tile), lambda j: (at, 0, j)),
            pl.BlockSpec((width, tile), lambda j: (0, j)),
        ],
        out_specs=[
            pl.BlockSpec((rows, width), lambda j: (0, 0)),
            pl.BlockSpec((rows, 128), lambda j: (0, 0)),
        ],
        out_shape=[
            jax.ShapeDtypeStruct((rows, width), part_type),
            jax.ShapeDtypeStruct((rows, 128), F32),
        ],
        scratch_shapes=[pltpu.VMEM((rows, 1), F32), pltpu.VMEM((rows, width), F32)],
        compiler_params=params(32),
        cost_estimate=pl.CostEstimate(
            flops=2 * rows * width * vocab,
            bytes_accessed=2 * width * vocab + 6 * rows * vocab,
            transcendentals=rows * vocab,
        ),
        name="head_grads",
    )(*stats, lengths, logits, counts, w_head)


def weight_kernel(blocks, adding, share, where, *refs):
    x_refs, refs = refs[:blocks], refs[blocks:]
    g_refs, refs = refs[:blocks], refs[blocks:]
    w_in, w_out, refs = refs[0], refs[1], refs[2:]
    if adding:
        old_first, old_second, refs = refs[0], refs[1], refs[2:]
    first, second, normed, grads, normed_t, grads_t = refs
    count = x_refs[0].shape[0]

    @pl.when(pl.program_id(0) == 0)
    def _():
        columns = pl.ds(pl.multiple_of(where[0] * share, share), share)
        for at in range(blocks):
            place = pl.ds(at * count, count)
            normed[place, :] = normalised(x_refs[at][...])
            grads[place, :] = g_refs[at][...]
        normed_t[...] = normed[:, columns].astype(F32).T.astype(BF16)
        grads_t[...] = grads[:, columns].astype(F32).T.astype(BF16)

    total_first = old_first[...] if adding else None
    total_second = None
    rows = normed.shape[0]
    part = min(256, rows)
    for at in range(rows // part):
        place = pl.ds(at * part, part)
        value, slope = gelu_parts(dot(normed[place, :], w_in[...]))
        dpre = (dot_t(grads[place, :], w_out[...]) * slope).astype(BF16)
        now_first = dot(normed_t[:, place], dpre)
        now_second = dot(grads_t[:, place], value.astype(BF16))
        total_first = now_first if total_first is None else total_first + now_first
        total_second = now_second if total_second is None else total_second + now_second
    first[...] = total_first
    total_second = total_second.T
    second[...] = old_second[...] + total_second if adding else total_second


def weight_grads(where, x_parts, g_parts, w_in, w_out, old, share):
    width, hidden = w_in.shape
    tile = tile_of(hidden, 512)
    blocks = len(g_parts)
    count = g_parts[0].shape[0]
    rows = blocks * count
    in_specs = [
        pl.BlockSpec((None, None, count, width), index) for _, index in x_parts
    ]
    in_specs += [pl.BlockSpec((count, width), lambda j, s: (0, 0))] * blocks
    in_specs += [
        pl.BlockSpec((width, tile), lambda j, s: (0, j)),
        pl.BlockSpec((tile, width), lambda j, s: (j, 0)),
    ]
    grad_specs = [
        pl.BlockSpec((share, tile), lambda j, s: (0, j)),
        pl.BlockSpec((tile, share), lambda j, s: (j, 0)),
    ]
    adding = old is not None
    aliases = {}
    if adding:
        in_specs += grad_specs
        aliases = {1 + 2 * blocks + 2: 0, 1 + 2 * blocks + 3: 1}
    return pl.pallas_call(
        functools.partial(weight_kernel, blocks, adding, share),
        grid_spec=pltpu.PrefetchScalarGridSpec(
            num_scalar_prefetch=1,
            grid=(hidden // tile,),
            in_specs=in_specs,
            out_specs=grad_specs,
            scratch_shapes=[
                pltpu.VMEM((rows, width), BF16),
                pltpu.VMEM((rows, width), BF16),
                pltpu.VMEM((share, rows), BF16),
                pltpu.VMEM((share, rows), BF16),
            ],
        ),
        out_shape=[
            jax.ShapeDtypeStruct((share, hidden), F32),
            jax.ShapeDtypeStruct((hidden, share), F32),
        ],
        input_output_aliases=aliases,
        compiler_params=params(48),
        cost_estimate=pl.CostEstimate(
            flops=4 * rows * (width + share) * hidden,
            bytes_accessed=4 * width * hidden + 16 * share * hidden,
            transcendentals=rows * hidden,
        ),
        name="weight_grads",
    )(where, *[x for x, _ in x_parts], *g_parts, w_in, w_out, *(old or ()))


def unit_counts(ends, targets, ids):
    positions = jnp.arange(targets.shape[1], dtype=jnp.int32)
    row_local = jnp.sum((ends[:, None, :] <= positions[None, :, None]).astype(jnp.int32), axis=-1)
    rows = jnp.arange(ends.shape[1], dtype=jnp.int32)
    row_onehot = (row_local[:, :, None] == rows[None, None, :]).astype(BF16)
    hits = (targets[:, :, None] == ids[None, None, :]).astype(BF16)
    counts = jnp.einsum("mur,muv->mrv", row_onehot, hits, preferred_element_type=F32)
    return counts.astype(BF16)


def on_device(text_rows, durations, unit_targets, w_in, w_out, w_unit):
    micro, row_count, width = text_rows.shape
    segments = lax.axis_size("segment")
    mp_size = lax.axis_size("mp")
    dp_size = lax.axis_size("dp")
    seg = lax.axis_index("segment")
    mp_at = lax.axis_index("mp")
    dp_at = lax.axis_index("dp")
    last = segments - 1
    is_last = seg == last
    seg_ref = seg.astype(jnp.int32)[None]
    dp_ref = dp_at.astype(jnp.int32)[None]
    pair = mp_size == 2
    part_type = BF16 if pair else F32
    first = w_in[0]
    second = w_out[0]
    chunks = CHUNKS
    rows = micro * row_count // chunks
    text = [t for t in text_rows.reshape(chunks, rows, width)]
    vocab_part = w_unit.shape[1]
    unit_count = unit_targets.shape[1]
    denom = float(micro * unit_count * dp_size)
    lengths = durations[:, 0, :]
    length_f = lengths.astype(F32).reshape(chunks, rows, 1)
    ends = jnp.cumsum(lengths, axis=-1)

    w_head = lax.all_gather(w_unit, "segment", axis=1, tiled=True)
    part_ids = jnp.arange(vocab_part, dtype=jnp.int32)
    shard_ids = (jnp.arange(segments, dtype=jnp.int32) * mp_size + mp_at) * vocab_part
    head_ids = (shard_ids[:, None] + part_ids[None, :]).reshape(-1)
    head_counts = unit_counts(ends, unit_targets, head_ids).reshape(chunks, rows, -1)
    own_ids = (seg * mp_size + mp_at) * vocab_part + part_ids
    own_counts = unit_counts(ends, unit_targets, own_ids).reshape(micro * row_count, vocab_part)

    def mp_pieces(part):
        if pair:
            return [part, swapped(part)]
        return [lax.psum(part, "mp")]

    def mp_tables(stats):
        if pair:
            return [stats, swapped(stats)]
        return [t for t in lax.all_gather(stats, "mp")]

    def my_half(block):
        if not pair:
            return block
        half = rows // 2
        return lax.dynamic_slice_in_dim(block, mp_at * half, half, 0)

    def other_half(block):
        half = rows // 2
        return lax.dynamic_slice_in_dim(block, (1 - mp_at) * half, half, 0)

    def gather_grads(block):
        if not pair:
            return [t for t in lax.all_gather(block, "dp")]
        mine = my_half(block)
        own = [mine]
        theirs = [other_half(block)]
        for distance in range(1, dp_size):
            route = [(i, (i + distance) % dp_size) for i in range(dp_size)]
            came = lax.ppermute(mine, "dp", route)
            own.append(came)
            theirs.append(swapped(came))
        return own + theirs

    stash, grads, finals, results, sent = [], [], [], [], []
    sums = None
    x_mine = x_theirs = None
    outgoing = going_back = None

    def x_parts(at):
        if not pair:
            return [
                (x_mine, lambda j, s, k=k: (k, at, 0, 0)) for k in range(dp_size)
            ]
        return [
            (source, lambda j, s, k=k: (lax.rem(s[0] + dp_size - k, dp_size), at, 0, 0))
            for source in (x_mine, x_theirs)
            for k in range(dp_size)
        ]

    for clock in range(2 * segments + chunks - 1):
        f_out = b_out = None
        if clock < segments + chunks - 1:
            own = text[min(clock, chunks - 1)]
            arrived = own if clock == 0 else shifted(outgoing, "segment", 1)
            rows_in, part = forward_section(seg_ref, own, arrived, first, second, part_type)
            stash.append(rows_in)
            f_out = finish_forward(rows_in, mp_pieces(part))
        if clock >= segments:
            at = clock - segments
            arrived = None if at == 0 else shifted(going_back, "segment", -1)
            parts = []
            if at < chunks:
                finals.append(outgoing)
                sent.append(
                    [lax.ppermute(outgoing, "segment", [(last, to)]) for to in range(last)]
                )
                logits, stats = head_logits(outgoing, w_head, head_counts, at)
                part, result = head_grads(
                    mp_tables(stats), length_f, logits, head_counts, at, w_head, denom, part_type
                )
                results.append(result[:, 0:2])
                parts = mp_pieces(part)
            options = []
            for other in range(segments):
                stage = clock - 2 * segments + 1 + 2 * other
                if 0 <= stage < len(stash):
                    options.append((other, stash[stage]))
            rows_in, grad_rows, part = backward_section(
                seg_ref, last, options, outgoing, parts, arrived, first, second, part_type
            )
            grads.append(grad_rows)
            if clock < 2 * segments + chunks - 2:
                b_out = finish_backward(rows_in, grad_rows, mp_pieces(part))
        if clock == segments + chunks - 2:
            x_half = jnp.stack(
                [
                    chosen(seg, [(s, my_half(stash[b + s])) for s in range(segments)])
                    for b in range(chunks)
                ]
            )
            x_mine = lax.all_gather(x_half, "dp")
            x_theirs = swapped(x_mine) if pair else None
        if clock >= 2 * segments - 1:
            at = clock - 2 * segments + 1
            block = chosen(seg, [(s, grads[at + last - s]) for s in range(segments)])
            sums = weight_grads(
                dp_ref, x_parts(at), gather_grads(block), first, second, sums, width // dp_size
            )
        outgoing, going_back = f_out, b_out

    results = lax.all_gather(jnp.stack(results), "segment")[last]
    loss = (jnp.sum(results[:, :, 1]) / denom)[None]
    final_rows = jnp.concatenate(
        [
            chosen(seg, [(last, finals[b])] + [(to, sent[b][to]) for to in range(last)])
            for b in range(chunks)
        ]
    )
    final_norm = normalised(final_rows)
    own_logits = dot(final_norm, w_unit)
    own_exp = jnp.exp(own_logits - results[:, :, 0].reshape(-1, 1))
    own_dlogits = (
        (length_f.reshape(-1, 1) * own_exp - own_counts.astype(F32)) / denom
    ).astype(BF16)
    grad_unit = t_dot(final_norm, own_dlogits).astype(BF16)
    sum_unit = lax.psum_scatter(grad_unit, "dp", scatter_dimension=0, tiled=True).astype(F32)
    return (loss, sums[0][None], sums[1][None], sum_unit)


def solution(mesh):
    placed = (
        P(None, "dp", None),
        P(None, "dp", None),
        P(None, "dp"),
        P("segment", None, "mp"),
        P("segment", "mp", None),
        P(None, ("segment", "mp")),
    )
    return jax.shard_map(
        on_device,
        mesh=mesh,
        in_specs=placed,
        out_specs=(
            P("dp"),
            P("segment", "dp", "mp"),
            P("segment", "mp", "dp"),
            P("dp", ("segment", "mp")),
        ),
        check_vma=False,
    )
```

time: 709 us -> 644 us (0.908)
  matrix products: 328 us -> 19.7 us
  Pallas kernels: 0 us -> 251 us
  waiting for transfers between devices: 192 us -> 109 us
  local copies, waits for them, and re-layouts: 42.3 us -> 114 us
  starting transfers between devices: 55 us -> 108 us
  other arithmetic: 53.1 us -> 8.12 us
    dot_general x33 -> x3, matrix products: 328 us -> 19.7 us  [the longest x2 12.7 us: unit_counts(): jnp.einsum('mur,muv->mrv', row_onehot, hits, preferred_element_type=F32)]
    pallas_call x0 -> x39, Pallas kernels: none -> 251 us  [the longest x4 84 us: weight_grads(): pl.pallas_call(functools.partial(weight_kernel, blocks, adding, share), g...]
    unnamed x116 -> x204, local copies, waits for them, and re-layouts: 33.3 us -> 113 us
    all_gather x14 -> x1, waiting for transfers between devices: 48.9 us -> 0.03 us  [on_device(): x_mine = lax.all_gather(x_half, 'dp')]
    ppermute x21 -> x58, starting transfers between devices: 14.9 us -> 60.7 us  [the longest x34 34.8 us: swapped(): return lax.ppermute(block, 'mp', [(0, 1), (1, 0)])]
    ppermute x21 -> x58, waiting for transfers between devices: 5.08 us -> 48.4 us  [the longest x12 40.3 us: gather_grads(): came = lax.ppermute(mine, 'dp', route)]
    reduce_scatter x1, waiting for transfers between devices: 29.4 us -> 0.01 us  [on_device(): lax.psum_scatter(grad_unit, 'dp', scatter_dimension=0, tiled=True)]
    all_gather x1, waiting for transfers between devices: 28.9 us -> 0.02 us  [on_device(): w_head = lax.all_gather(w_unit, 'segment', axis=1, tiled=True)]
  transfers between devices with their start and end apart: 50 -> 73, of which waited for: 22 -> 23; matrix products, arithmetic and copies ran while one was open for 59% -> 4% of each run, Pallas kernels for 0% -> 40%
where the time goes in v2:
time: 644 us; the launch traced here: 634 us
  Pallas kernels  251 us (39%)
  local copies, waits for them, and re-layouts  114 us (18%)
  waiting for transfers between devices  109 us (17%)
  starting transfers between devices  108 us (17%)
  matrix products  19.7 us (3%)
  between operations  19.1 us (3%)
  other arithmetic  8.12 us (1%)
    unnamed x204, local copies, waits for them, and re-layouts  113 us
    pallas_call x4, Pallas kernels, weight_grads(): pl.pallas_call(functools.partial(weight_kernel, blocks, adding, share), g...  84 us
    pallas_call x7, Pallas kernels, backward_section(): pl.pallas_call(body, grid_spec=pltpu.PrefetchScalarGridSpec(num_scalar_pr...  70.5 us
    ppermute x12, waiting for transfers between devices, shifted(): return lax.ppermute(block, axis, route)  59.4 us
    ppermute x12, starting transfers between devices, shifted(): return lax.ppermute(block, axis, route)  47 us
    pallas_call x7, Pallas kernels, forward_section(): pl.pallas_call(forward_kernel, grid_spec=pltpu.PrefetchScalarGridSpec(num...  42.6 us
    ppermute x12, waiting for transfers between devices, gather_grads(): came = lax.ppermute(mine, 'dp', route)  40.3 us
    ppermute x34, starting transfers between devices, swapped(): return lax.ppermute(block, 'mp', [(0, 1), (1, 0)])  34.8 us
  transfers between devices with their start and end apart: 73, of which 23 were waited for; matrix products, arithmetic and copies ran while one was open for 4% of the time, Pallas kernels for 40%

profile of v2, /device:TPU:11, one launch (start us, length us, event | category | flops | bytes accessed | tf_op | source)
XLA Modules:
  0.0 634.0 jit_solution(6641643143762316162)
XLA Ops:
  27.1 12.5 %collective-permute-done.1.arrived = bf16[128,1024]{1,0:T(8,128)(2,1)S(1)} collective-permute-done((bf16[128,1024]{1,0:T(8,128)(2,1)S(1)}, bf16[128,1024]{1,0:T(8,128)(2,1)S(1)}, u32[]{:S(2)}, u32[]{:S(2)}) %collective-permute-start.1) | collective-permute-done | bytes 262176 | tf_op jit(solution)/shard_map/ppermute | solution.py:18
  55.3 7.3 %collective-permute-done.3.arrived = bf16[128,1024]{1,0:T(8,128)(2,1)S(1)} collective-permute-done((bf16[128,1024]{1,0:T(8,128)(2,1)S(1)}, bf16[128,1024]{1,0:T(8,128)(2,1)S(1)}, u32[]{:S(2)}, u32[]{:S(2)}) %collective-permute-start.3) | collective-permute-done | bytes 262176 | tf_op jit(solution)/shard_map/ppermute | solution.py:18
  74.5 11.6 %collective-permute-done.5.arrived = bf16[128,1024]{1,0:T(8,128)(2,1)S(1)} collective-permute-done((bf16[128,1024]{1,0:T(8,128)(2,1)S(1)}, bf16[128,1024]{1,0:T(8,128)(2,1)S(1)}, u32[]{:S(2)}, u32[]{:S(2)}) %collective-permute-start.5) | collective-permute-done | bytes 262176 | tf_op jit(solution)/shard_map/ppermute | solution.py:18
  99.4 11.4 %collective-permute-done.8.arrived = bf16[128,1024]{1,0:T(8,128)(2,1)S(1)} collective-permute-done((bf16[128,1024]{1,0:T(8,128)(2,1)S(1)}, bf16[128,1024]{1,0:T(8,128)(2,1)S(1)}, u32[]{:S(2)}, u32[]{:S(2)}) %collective-permute-start.8) | collective-permute-done | bytes 262176 | tf_op jit(solution)/shard_map/ppermute | solution.py:18
  131.0 9.6 %fusion.6.counts.refs_4_ = bf16[4,128,5120]{2,1,0:T(8,128)(2,1)} fusion(s32[5120]{0:T(1024)S(1)} %add.89, s32[4,512]{1,0:T(4,128)S(1)} %copy-done.94, s32[4,512]{1,0:T(4,128)S(1)} %convert_reduce_fusion), kind=kOutput, calls=%fused_computation.6 | convolution fusion | flops 2697723904 | bytes 5279744 | tf_op jit(solution)/shard_map/mur,muv->mrv/dot_general | solution.py:454
  188.4 10.3 %section_backward.7 = (bf16[128,1024]{1,0:T(8,128)(2,1)S(1)}, bf16[128,1024]{1,0:T(8,128)(2,1)S(1)}, bf16[128,1024]{1,0:T(8,128)(2,1)}) custom-call(s32[1]{0:T(128)} %bitcast.where, bf16[128,1024]{1,0:T(8,128)(2,1)S(1)} %copy-done.41, bf16[128,1024]{1,0:T(8,128)(2,1)S(1)} %get-tuple-element.67.refs_0_.refs_1_, bf16[128,1024]{1,0:T(8,128)(2,1)S(1)} %copy-done.47, ...), custom_call_target="tpu_custom_call" | custom-call | flops 3221225472 | bytes 16777216 | tf_op jit(solution)/shard_map/section_backward/pallas_call | solution.py:210
  220.6 6.4 %head_grads.5 = (bf16[128,1024]{1,0:T(8,128)(2,1)S(1)}, f32[128,128]{1,0:T(8,128)S(1)}) custom-call(f32[128,128]{1,0:T(8,128)} %get-tuple-element.74.refs_0_, f32[128,128]{1,0:T(8,128)S(1)} %collective-permute-done.10.refs_1_, f32[4,128,1]{2,1,0:T(8,128)S(1)} %copy.30.refs_2_, f32[128,5120]{1,0:T(8,128)S(1)} %copy-done.56, ...), custom_call_target="tpu_custom_call" | custom-call | flops 1342177280 | bytes 14417920 | tf_op jit(solution)/shard_map/head_grads/pallas_call | solution.py:331
  237.1 7.4 %section_forward.13 = (bf16[128,1024]{1,0:T(8,128)(2,1)S(1)}, bf16[128,1024]{1,0:T(8,128)(2,1)}) custom-call(s32[1]{0:T(128)} %bitcast.where, bf16[128,1024]{1,0:T(8,128)(2,1)S(1)} %get-tuple-element.120.own, bf16[128,1024]{1,0:T(8,128)(2,1)} %collective-permute-done.14.arrived, bf16[1024,4096]{1,0:T(8,128)(2,1)S(1)} %bitcast.54, bf16[4096,1024]{1,0:T(8,128)(2,1)S(1)} %bitcast.74), custom_call_target="tpu_custom_call" | custom-call | flops 2147483648 | bytes 16777216 | tf_op jit(solution)/shard_map/section_forward/pallas_call | solution.py:109
  252.5 10.6 %section_backward.8 = (bf16[128,1024]{1,0:T(8,128)(2,1)S(1)}, bf16[128,1024]{1,0:T(8,128)(2,1)S(1)}, bf16[128,1024]{1,0:T(8,128)(2,1)S(1)}) custom-call(s32[1]{0:T(128)} %bitcast.where, bf16[128,1024]{1,0:T(8,128)(2,1)S(1)} %copy-done.50, bf16[128,1024]{1,0:T(8,128)(2,1)S(1)} %copy-done.34, bf16[128,1024]{1,0:T(8,128)(2,1)S(1)} %copy-done.39, ...), custom_call_target="tpu_custom_call" | custom-call | flops 3221225472 | bytes 16777216 | tf_op jit(solution)/shard_map/section_backward/pallas_call | solution.py:210
  273.5 6.3 %head_grads.6 = (bf16[128,1024]{1,0:T(8,128)(2,1)}, f32[128,128]{1,0:T(8,128)S(1)}) custom-call(f32[128,128]{1,0:T(8,128)S(1)} %get-tuple-element.79.refs_0_, f32[128,128]{1,0:T(8,128)S(1)} %collective-permute-done.13.refs_1_, f32[4,128,1]{2,1,0:T(8,128)S(1)} %copy.30.refs_2_, f32[128,5120]{1,0:T(8,128)S(1)} %get-tuple-element.80.refs_3_, ...), custom_call_target="tpu_custom_call" | custom-call | flops 1342177280 | bytes 14417920 | tf_op jit(solution)/shard_map/head_grads/pallas_call | solution.py:331
  298.4 11.5 %section_backward.9 = (bf16[128,1024]{1,0:T(8,128)(2,1)S(1)}, bf16[128,1024]{1,0:T(8,128)(2,1)S(1)}, bf16[128,1024]{1,0:T(8,128)(2,1)}) custom-call(s32[1]{0:T(128)} %bitcast.where, bf16[128,1024]{1,0:T(8,128)(2,1)S(1)} %copy-done.42, bf16[128,1024]{1,0:T(8,128)(2,1)S(1)} %get-tuple-element.67.refs_0_.refs_1_, bf16[128,1024]{1,0:T(8,128)(2,1)S(1)} %copy-done.37, ...), custom_call_target="tpu_custom_call" | custom-call | flops 3221225472 | bytes 16777216 | tf_op jit(solution)/shard_map/section_backward/pallas_call | solution.py:210
  362.4 9.5 %section_backward.10 = (bf16[128,1024]{1,0:T(8,128)(2,1)S(1)}, bf16[128,1024]{1,0:T(8,128)(2,1)S(1)}, bf16[128,1024]{1,0:T(8,128)(2,1)S(1)}) custom-call(s32[1]{0:T(128)} %bitcast.where, bf16[128,1024]{1,0:T(8,128)(2,1)S(1)} %copy-done.50, bf16[128,1024]{1,0:T(8,128)(2,1)S(1)} %copy-done.34, bf16[128,1024]{1,0:T(8,128)(2,1)S(1)} %copy-done.39, ...), custom_call_target="tpu_custom_call" | custom-call | flops 3221225472 | bytes 16777216 | tf_op jit(solution)/shard_map/section_backward/pallas_call | solution.py:210
  374.4 9.3 %collective-permute-start.29 = (bf16[128,1024]{1,0:T(8,128)(2,1)S(1)}, bf16[128,1024]{1,0:T(8,128)(2,1)S(1)}, u32[]{:S(2)}, u32[]{:S(2)}) collective-permute-start(bf16[128,1024]{1,0:T(8,128)(2,1)S(1)} %finish_backward.9), channel_id=1, source_target_pairs={{8,0},{16,8},{24,16},{9,1},{17,9},{25,17},{10,2},{18,10},{26,18},{... | collective-permute-start | bytes 786440 | tf_op jit(solution)/shard_map/ppermute | solution.py:18
  396.2 9.3 %section_backward.11 = (bf16[128,1024]{1,0:T(8,128)(2,1)S(1)}, bf16[128,1024]{1,0:T(8,128)(2,1)S(1)}, bf16[128,1024]{1,0:T(8,128)(2,1)S(1)}) custom-call(s32[1]{0:T(128)} %bitcast.where, bf16[128,1024]{1,0:T(8,128)(2,1)S(1)} %copy-done.42, bf16[128,1024]{1,0:T(8,128)(2,1)S(1)} %get-tuple-element.67.refs_0_.refs_1_, bf16[128,1024]{1,0:T(8,128)(2,1)S(1)} %copy-done.37, ...), custom_call_target="tpu_custom_call" | custom-call | flops 3221225472 | bytes 16777216 | tf_op jit(solution)/shard_map/section_backward/pallas_call | solution.py:210
  412.0 6.3 collective-permute-done.31.refs_3_
  418.3 9.2 %section_backward.12 = (bf16[128,1024]{1,0:T(8,128)(2,1)S(1)}, bf16[128,1024]{1,0:T(8,128)(2,1)S(1)}, bf16[128,1024]{1,0:T(8,128)(2,1)S(1)}) custom-call(s32[1]{0:T(128)} %bitcast.where, bf16[128,1024]{1,0:T(8,128)(2,1)S(1)} %copy-done.34, bf16[128,1024]{1,0:T(8,128)(2,1)S(1)} %copy-done.39, bf16[128,1024]{1,0:T(8,128)(2,1)S(1)} %get-tuple-element.82.refs_0_.refs_3_.refs_2_, ...), custom_call_target="tpu_custom_call" | custom-call | flops 3221225472 | bytes 16777216 | tf_op jit(solution)/shard_map/section_backward/pallas_call | solution.py:210
  438.4 6.9 %convolution_convert_fusion = bf16[1024,1280]{1,0:T(8,128)(2,1)} fusion(bf16[1024,1280]{1,0:T(8,128)(2,1)} %param.11, bf16[512,1280]{1,0:T(8,128)(2,1)} %bitcast.104, f32[512]{0:T(512)S(1)} %bitcast.103, f32[512]{0:T(512)S(1)} %bitcast.101, f32[512]{0:T(512)S(1)} %add_rsqrt_fusion, bf16[128,1024]{1,0:T(8,128)(2,1)} %copy-done.86, ...), kind=kOutput, calls=%fused_computation.9 | convolution fusion | flops 2700083200 | bytes 7608320 | tf_op jit(solution)/shard_map/dot_general | solution.py:59
  452.1 10.1 %section_backward.13 = (bf16[128,1024]{1,0:T(8,128)(2,1)}, bf16[128,1024]{1,0:T(8,128)(2,1)S(1)}, bf16[128,1024]{1,0:T(8,128)(2,1)}) custom-call(s32[1]{0:T(128)} %bitcast.where, bf16[128,1024]{1,0:T(8,128)(2,1)S(1)} %get-tuple-element.67.refs_0_.refs_1_, bf16[128,1024]{1,0:T(8,128)(2,1)S(1)} %copy-done.37, ...), custom_call_target="tpu_custom_call" | custom-call | flops 3221225472 | bytes 16777216 | tf_op jit(solution)/shard_map/section_backward/pallas_call | solution.py:210
  472.8 13.1 %collective-permute-done.53.refs_10_ = bf16[64,1024]{1,0:T(8,128)(2,1)} collective-permute-done((bf16[64,1024]{1,0:T(8,128)(2,1)S(1)}, bf16[64,1024]{1,0:T(8,128)(2,1)}, u32[]{:S(2)}, u32[]{:S(2)}) %collective-permute-start.53) | collective-permute-done | bytes 131104 | tf_op jit(solution)/shard_map/ppermute | solution.py:520
  485.9 10.2 %collective-permute-done.54.refs_11_ = bf16[64,1024]{1,0:T(8,128)(2,1)} collective-permute-done((bf16[64,1024]{1,0:T(8,128)(2,1)S(1)}, bf16[64,1024]{1,0:T(8,128)(2,1)}, u32[]{:S(2)}, u32[]{:S(2)}) %collective-permute-start.54) | collective-permute-done | bytes 131104 | tf_op jit(solution)/shard_map/ppermute | solution.py:520
  531.8 20.7 %weight_grads.4 = (f32[256,4096]{1,0:T(8,128)}, f32[4096,256]{1,0:T(8,128)}) custom-call(s32[1]{0:T(128)} %bitcast.14.where, bf16[4,4,64,1024]{3,2,1,0:T(8,128)(2,1)S(1)} %bitcast.82, bf16[4,4,64,1024]{3,2,1,0:T(8,128)(2,1)S(1)} %bitcast.83, bf16[4,4,64,1024]{3,2,1,0:T(8,128)(2,1)S(1)} %bitcast.84, bf16[4,4,64,1024]{3,2,1,0:T(8,128)(2,1)S(1)} %bitcast.85, ...), custom_call_target="tpu_custom_call" | custom-call | flops 10737418240 | bytes 33554432 | tf_op jit(solution)/shard_map/weight_grads/pallas_call | solution.py:419
  558.8 21.1 %weight_grads.5 = (f32[256,4096]{1,0:T(8,128)}, f32[4096,256]{1,0:T(8,128)}) custom-call(s32[1]{0:T(128)} %bitcast.14.where, bf16[4,4,64,1024]{3,2,1,0:T(8,128)(2,1)S(1)} %bitcast.86, bf16[4,4,64,1024]{3,2,1,0:T(8,128)(2,1)S(1)} %bitcast.87, bf16[4,4,64,1024]{3,2,1,0:T(8,128)(2,1)S(1)} %bitcast.88, ...), custom_call_target="tpu_custom_call", output_to_operand_aliasing={{0}: (19, {}), {1}: (20, {})} | custom-call | flops 10737418240 | bytes 33554432 | tf_op jit(solution)/shard_map/weight_grads/pallas_call | solution.py:419
  580.5 21.1 %weight_grads.6 = (f32[256,4096]{1,0:T(8,128)}, f32[4096,256]{1,0:T(8,128)}) custom-call(s32[1]{0:T(128)} %bitcast.14.where, bf16[4,4,64,1024]{3,2,1,0:T(8,128)(2,1)S(1)} %bitcast.90, bf16[4,4,64,1024]{3,2,1,0:T(8,128)(2,1)S(1)} %bitcast.91, bf16[4,4,64,1024]{3,2,1,0:T(8,128)(2,1)S(1)} %bitcast.92, ...), custom_call_target="tpu_custom_call", output_to_operand_aliasing={{0}: (19, {}), {1}: (20, {})} | custom-call | flops 10737418240 | bytes 33554432 | tf_op jit(solution)/shard_map/weight_grads/pallas_call | solution.py:419
  601.6 21.1 %weight_grads.7 = (f32[256,4096]{1,0:T(8,128)}, f32[4096,256]{1,0:T(8,128)}) custom-call(s32[1]{0:T(128)} %bitcast.14.where, bf16[4,4,64,1024]{3,2,1,0:T(8,128)(2,1)S(1)} %bitcast.94, bf16[4,4,64,1024]{3,2,1,0:T(8,128)(2,1)S(1)} %bitcast.95, bf16[4,4,64,1024]{3,2,1,0:T(8,128)(2,1)S(1)} %bitcast.96, ...), custom_call_target="tpu_custom_call", output_to_operand_aliasing={{0}: (19, {}), {1}: (20, {})} | custom-call | flops 10737418240 | bytes 33554432 | tf_op jit(solution)/shard_map/weight_grads/pallas_call | solution.py:419
  (405 shorter events, 342.0 us)
Async XLA Ops:
  8.0 132.8 %all-gather.5.cloned.1.call-start = ((), (), s32[]{:S(2)}) async-start(), calls=%async_computation.1 | async-start | bytes 13107200 | tf_op jit(solution)/shard_map/all_gather | solution.py:484
  8.7 375.3 %all-gather.7.cloned.1.call-start = ((), (), s32[]{:S(2)}) async-start(), calls=%async_computation.3 | async-start | bytes 2621440 | tf_op jit(solution)/shard_map/all_gather | solution.py:582
  126.0 28.5 %collective-permute-start.11 = (bf16[128,1024]{1,0:T(8,128)(2,1)S(1)}, bf16[128,1024]{1,0:T(8,128)(2,1)S(1)}, u32[]{:S(2)}, u32[]{:S(2)}) collective-permute-start(bf16[128,1024]{1,0:T(8,128)(2,1)S(1)} %finish_forward.11.final.refs_3_), channel_id=1, source_target_pairs={{0,8},{8,16},{16,24},{1,9},{9,17},{17,25},{2,10},{10,18},{18,26},{... | collective-permute-start | bytes 786440 | tf_op jit(solution)/shard_map/ppermute | solution.py:18
  182.6 51.1 %collective-permute-start.14 = (bf16[128,1024]{1,0:T(8,128)(2,1)}, bf16[128,1024]{1,0:T(8,128)(2,1)}, u32[]{:S(2)}, u32[]{:S(2)}) collective-permute-start(bf16[128,1024]{1,0:T(8,128)(2,1)} %finish_forward.12.final.refs_3_), channel_id=1, source_target_pairs={{0,8},{8,16},{16,24},{1,9},{9,17},{17,25},{2,10},{10,18},{18,26},{... | collective-permute-start | bytes 786440 | tf_op jit(solution)/shard_map/ppermute | solution.py:18
  199.4 28.1 %collective-permute-start.22 = (bf16[128,1024]{1,0:T(8,128)(2,1)}, bf16[128,1024]{1,0:T(8,128)(2,1)}, u32[]{:S(2)}, u32[]{:S(2)}) collective-permute-start(bf16[128,1024]{1,0:T(8,128)(2,1)} %get-tuple-element.93.refs_0_), channel_id=1, source_target_pairs={{0,4},{4,0},{1,5},{5,1},{2,6},{6,2},{3,7},{7,3},{8,12},{12,8},{9,1... | collective-permute-start | bytes 786440 | tf_op jit(solution)/shard_map/ppermute | solution.py:22
  245.7 377.1 %reduce-scatter.2.cloned.1.call-start = ((), (), s32[]{:S(2)}) async-start(), calls=%async_computation.2 | async-start | bytes 3276800 | tf_op jit(solution)/shard_map/reduce_scatter | solution.py:607
  283.0 42.0 %collective-permute-start.58 = (bf16[128,1024]{1,0:T(8,128)(2,1)S(1)}, bf16[128,1024]{1,0:T(8,128)(2,1)S(1)}, u32[]{:S(2)}, u32[]{:S(2)}) collective-permute-start(bf16[128,1024]{1,0:T(8,128)(2,1)S(1)} %copy-done.48), channel_id=1, source_target_pairs={{24,16},{25,17},{26,18},{27,19},{28,20},{29,21},{30,22},{31,23}} | collective-permute-start | bytes 786440 | tf_op jit(solution)/shard_map/ppermute | solution.py:556
  283.7 62.8 %collective-permute-start.59 = (bf16[128,1024]{1,0:T(8,128)(2,1)S(1)}, bf16[128,1024]{1,0:T(8,128)(2,1)}, u32[]{:S(2)}, u32[]{:S(2)}) collective-permute-start(bf16[128,1024]{1,0:T(8,128)(2,1)S(1)} %copy-done.48), channel_id=1, source_target_pairs={{24,8},{25,9},{26,10},{27,11},{28,12},{29,13},{30,14},{31,15}} | collective-permute-start | bytes 786440 | tf_op jit(solution)/shard_map/ppermute | solution.py:556
  285.0 62.1 %collective-permute-start.60 = (bf16[128,1024]{1,0:T(8,128)(2,1)S(1)}, bf16[128,1024]{1,0:T(8,128)(2,1)}, u32[]{:S(2)}, u32[]{:S(2)}) collective-permute-start(bf16[128,1024]{1,0:T(8,128)(2,1)S(1)} %copy-done.48), channel_id=1, source_target_pairs={{24,0},{25,1},{26,2},{27,3},{28,4},{29,5},{30,6},{31,7}} | collective-permute-start | bytes 786440 | tf_op jit(solution)/shard_map/ppermute | solution.py:556
  287.5 60.1 %collective-permute-start.61 = (bf16[128,1024]{1,0:T(8,128)(2,1)S(1)}, bf16[128,1024]{1,0:T(8,128)(2,1)}, u32[]{:S(2)}, u32[]{:S(2)}) collective-permute-start(bf16[128,1024]{1,0:T(8,128)(2,1)S(1)} %copy-done.45), channel_id=1, source_target_pairs={{24,16},{25,17},{26,18},{27,19},{28,20},{29,21},{30,22},{31,23}} | collective-permute-start | bytes 786440 | tf_op jit(solution)/shard_map/ppermute | solution.py:556
  384.0 83.1 %collective-permute-start.17 = (bf16[4,4,64,1024]{3,2,1,0:T(8,128)(2,1)}, bf16[4,4,64,1024]{3,2,1,0:T(8,128)(2,1)}, u32[]{:S(2)}, u32[]{:S(2)}) collective-permute-start(bf16[4,4,64,1024]{3,2,1,0:T(8,128)(2,1)} %bitcast.81), channel_id=1, source_target_pairs={{0,4},{4,0},{1,5},{5,1},{2,6},{6,2},{3,7},{7,3},{8,12},{12,8},{9,1... | collective-permute-start | bytes 6291464 | tf_op jit(solution)/shard_map/ppermute | solution.py:22
  465.6 30.5 %collective-permute-start.54 = (bf16[64,1024]{1,0:T(8,128)(2,1)S(1)}, bf16[64,1024]{1,0:T(8,128)(2,1)}, u32[]{:S(2)}, u32[]{:S(2)}) collective-permute-start(bf16[64,1024]{1,0:T(8,128)(2,1)S(1)} %get-tuple-element.131.refs_8_), channel_id=1, source_target_pairs={{0,3},{1,0},{2,1},{3,2},{4,7},{5,4},{6,5},{7,6},{8,11},{9,8},{10,9... | collective-permute-start | bytes 393224 | tf_op jit(solution)/shard_map/ppermute | solution.py:520
  466.8 33.5 %collective-permute-start.46 = (bf16[64,1024]{1,0:T(8,128)(2,1)S(1)}, bf16[64,1024]{1,0:T(8,128)(2,1)S(1)}, u32[]{:S(2)}, u32[]{:S(2)}) collective-permute-start(bf16[64,1024]{1,0:T(8,128)(2,1)S(1)} %get-tuple-element.133.refs_8_), channel_id=1, source_target_pairs={{0,1},{1,2},{2,3},{3,0},{4,5},{5,6},{6,7},{7,4},{8,9},{9,10},{10,1... | collective-permute-start | bytes 393224 | tf_op jit(solution)/shard_map/ppermute | solution.py:520
  467.2 45.4 %collective-permute-start.47 = (bf16[64,1024]{1,0:T(8,128)(2,1)S(1)}, bf16[64,1024]{1,0:T(8,128)(2,1)S(1)}, u32[]{:S(2)}, u32[]{:S(2)}) collective-permute-start(bf16[64,1024]{1,0:T(8,128)(2,1)S(1)} %get-tuple-element.133.refs_8_), channel_id=1, source_target_pairs={{0,2},{1,3},{2,0},{3,1},{4,6},{5,7},{6,4},{7,5},{8,10},{9,11},{10,... | collective-permute-start | bytes 393224 | tf_op jit(solution)/shard_map/ppermute | solution.py:520
  471.4 50.6 %collective-permute-start.48 = (bf16[64,1024]{1,0:T(8,128)(2,1)S(1)}, bf16[64,1024]{1,0:T(8,128)(2,1)S(1)}, u32[]{:S(2)}, u32[]{:S(2)}) collective-permute-start(bf16[64,1024]{1,0:T(8,128)(2,1)S(1)} %get-tuple-element.133.refs_8_), channel_id=1, source_target_pairs={{0,3},{1,0},{2,1},{3,2},{4,7},{5,4},{6,5},{7,6},{8,11},{9,8},{10,9... | collective-permute-start | bytes 393224 | tf_op jit(solution)/shard_map/ppermute | solution.py:520
  485.9 38.9 %collective-permute-start.40 = (bf16[64,1024]{1,0:T(8,128)(2,1)S(1)}, bf16[64,1024]{1,0:T(8,128)(2,1)S(1)}, u32[]{:S(2)}, u32[]{:S(2)}) collective-permute-start(bf16[64,1024]{1,0:T(8,128)(2,1)S(1)} %get-tuple-element.135.refs_8_), channel_id=1, source_target_pairs={{0,1},{1,2},{2,3},{3,0},{4,5},{5,6},{6,7},{7,4},{8,9},{9,10},{10,1... | collective-permute-start | bytes 393224 | tf_op jit(solution)/shard_map/ppermute | solution.py:520
  496.1 30.3 %collective-permute-start.41 = (bf16[64,1024]{1,0:T(8,128)(2,1)S(1)}, bf16[64,1024]{1,0:T(8,128)(2,1)S(1)}, u32[]{:S(2)}, u32[]{:S(2)}) collective-permute-start(bf16[64,1024]{1,0:T(8,128)(2,1)S(1)} %get-tuple-element.135.refs_8_), channel_id=1, source_target_pairs={{0,2},{1,3},{2,0},{3,1},{4,6},{5,7},{6,4},{7,5},{8,10},{9,11},{10,... | collective-permute-start | bytes 393224 | tf_op jit(solution)/shard_map/ppermute | solution.py:520
  500.3 26.5 %collective-permute-start.55 = (bf16[64,1024]{1,0:T(8,128)(2,1)}, bf16[64,1024]{1,0:T(8,128)(2,1)}, u32[]{:S(2)}, u32[]{:S(2)}) collective-permute-start(bf16[64,1024]{1,0:T(8,128)(2,1)} %collective-permute-done.52.refs_9_), channel_id=1, source_target_pairs={{0,4},{4,0},{1,5},{5,1},{2,6},{6,2},{3,7},{7,3},{8,12},{12,8},{9,1... | collective-permute-start | bytes 393224 | tf_op jit(solution)/shard_map/ppermute | solution.py:22
  524.9 27.6 %collective-permute-start.42 = (bf16[64,1024]{1,0:T(8,128)(2,1)S(1)}, bf16[64,1024]{1,0:T(8,128)(2,1)S(1)}, u32[]{:S(2)}, u32[]{:S(2)}) collective-permute-start(bf16[64,1024]{1,0:T(8,128)(2,1)S(1)} %get-tuple-element.135.refs_8_), channel_id=1, source_target_pairs={{0,3},{1,0},{2,1},{3,2},{4,7},{5,4},{6,5},{7,6},{8,11},{9,8},{10,9... | collective-permute-start | bytes 393224 | tf_op jit(solution)/shard_map/ppermute | solution.py:520
  526.5 29.2 %collective-permute-start.34 = (bf16[64,1024]{1,0:T(8,128)(2,1)S(1)}, bf16[64,1024]{1,0:T(8,128)(2,1)S(1)}, u32[]{:S(2)}, u32[]{:S(2)}) collective-permute-start(bf16[64,1024]{1,0:T(8,128)(2,1)S(1)} %get-tuple-element.137.refs_8_), channel_id=1, source_target_pairs={{0,1},{1,2},{2,3},{3,0},{4,5},{5,6},{6,7},{7,4},{8,9},{9,10},{10,1... | collective-permute-start | bytes 393224 | tf_op jit(solution)/shard_map/ppermute | solution.py:520
  526.8 30.9 %collective-permute-start.49 = (bf16[64,1024]{1,0:T(8,128)(2,1)S(1)}, bf16[64,1024]{1,0:T(8,128)(2,1)S(1)}, u32[]{:S(2)}, u32[]{:S(2)}) collective-permute-start(bf16[64,1024]{1,0:T(8,128)(2,1)S(1)} %collective-permute-done.46.refs_9_), channel_id=1, source_target_pairs={{0,4},{4,0},{1,5},{5,1},{2,6},{6,2},{3,7},{7,3},{8,12},{12,8},{9,1... | collective-permute-start | bytes 393224 | tf_op jit(solution)/shard_map/ppermute | solution.py:22
  531.3 27.0 %collective-permute-start.50 = (bf16[64,1024]{1,0:T(8,128)(2,1)S(1)}, bf16[64,1024]{1,0:T(8,128)(2,1)S(1)}, u32[]{:S(2)}, u32[]{:S(2)}) collective-permute-start(bf16[64,1024]{1,0:T(8,128)(2,1)S(1)} %collective-permute-done.47.refs_10_), channel_id=1, source_target_pairs={{0,4},{4,0},{1,5},{5,1},{2,6},{6,2},{3,7},{7,3},{8,12},{12,8},{9,1... | collective-permute-start | bytes 393224 | tf_op jit(solution)/shard_map/ppermute | solution.py:22
  531.4 27.0 %collective-permute-start.51 = (bf16[64,1024]{1,0:T(8,128)(2,1)S(1)}, bf16[64,1024]{1,0:T(8,128)(2,1)S(1)}, u32[]{:S(2)}, u32[]{:S(2)}) collective-permute-start(bf16[64,1024]{1,0:T(8,128)(2,1)S(1)} %collective-permute-done.48.refs_11_), channel_id=1, source_target_pairs={{0,4},{4,0},{1,5},{5,1},{2,6},{6,2},{3,7},{7,3},{8,12},{12,8},{9,1... | collective-permute-start | bytes 393224 | tf_op jit(solution)/shard_map/ppermute | solution.py:22
  552.5 27.3 %collective-permute-start.35 = (bf16[64,1024]{1,0:T(8,128)(2,1)S(1)}, bf16[64,1024]{1,0:T(8,128)(2,1)S(1)}, u32[]{:S(2)}, u32[]{:S(2)}) collective-permute-start(bf16[64,1024]{1,0:T(8,128)(2,1)S(1)} %get-tuple-element.137.refs_8_), channel_id=1, source_target_pairs={{0,2},{1,3},{2,0},{3,1},{4,6},{5,7},{6,4},{7,5},{8,10},{9,11},{10,... | collective-permute-start | bytes 393224 | tf_op jit(solution)/shard_map/ppermute | solution.py:520
  (151 other events, 1698.3 us)
Sparse Core Ops, SparseCore 0:
  10.7 125.3 all-gather.4
Sparse Core Ops, SparseCore 1:
  245.8 43.7 all-gather.6
  445.4 85.0 reduce-scatter.1

commit v3 on v2

v3 whole, which is shorter than its diff:
```python
import functools
import jax
import jax.numpy as jnp
from jax import lax
from jax.experimental import pallas as pl
from jax.experimental.pallas import tpu as pltpu
from jax.sharding import PartitionSpec as P

CHUNKS = 2
VMEM_MIB = 60
BF16 = jnp.bfloat16
F32 = jnp.float32
MIB = 1024 * 1024


def shifted(block, axis, distance):
    devices = range(lax.axis_size(axis))
    route = [(i - distance, i) for i in devices if i - distance in devices]
    return lax.ppermute(block, axis, route)


def swapped(block):
    return lax.ppermute(block, "mp", [(0, 1), (1, 0)])


def gelu_parts(pre_vals):
    coeff = 0.7978845608
    square = pre_vals * pre_vals
    inner = coeff * pre_vals * (1.0 + 0.044715 * square)
    half = 0.5 * (1.0 + jnp.tanh(inner))
    value = pre_vals * half
    slope = half + 2.0 * value * (1.0 - half) * coeff * (1.0 + 3.0 * 0.044715 * square)
    return (value, slope)


def row_scale(rows_in):
    floats = rows_in.astype(F32)
    return lax.rsqrt(jnp.mean(floats * floats, axis=-1, keepdims=True) + 1e-06)


def normalised(rows_in):
    return (rows_in.astype(F32) * row_scale(rows_in)).astype(BF16)


def norm_back(rows_in, grads):
    scale = row_scale(rows_in)
    normal = rows_in.astype(F32) * scale
    return scale * (grads - normal * jnp.mean(grads * normal, axis=-1, keepdims=True))


def dot(a, b):
    return jnp.dot(a, b, preferred_element_type=F32)


def dot_t(a, b):
    return lax.dot_general(a, b, (((1,), (1,)), ((), ())), preferred_element_type=F32)


def t_dot(a, b):
    return lax.dot_general(a, b, (((0,), (0,)), ((), ())), preferred_element_type=F32)


def tile_of(size, most):
    if size <= most:
        return size
    return max(t for t in range(128, most + 1, 128) if size % t == 0)


def params(limit):
    return pltpu.CompilerParams(vmem_limit_bytes=limit * MIB)


def added(refs):
    total = refs[0][...].astype(F32)
    for ref in refs[1:]:
        total = total + ref[...].astype(F32)
    return total


def chosen(index, candidates):
    value = candidates[0][1]
    for at, option in candidates[1:]:
        value = jnp.where(index == at, option, value)
    return value


def gathered(halves, place):
    if len(halves) == 1:
        return halves[0][...]
    mine, theirs = (half[...] for half in halves)
    first = jnp.where(place == 0, mine, theirs)
    second = jnp.where(place == 0, theirs, mine)
    return jnp.concatenate([first, second], axis=0)


def part_of(block, place, parts):
    rows = block.shape[0] // parts
    if parts == 1:
        return block[...]
    return block[pl.ds(pl.multiple_of(place * rows, rows), rows), :]


def whole_spec(shape):
    return pl.BlockSpec(shape, lambda *_: (0,) * len(shape))


def emit_parts(total, place, keep, send):
    if send is None:
        keep[...] = total[...]
        return
    keep[...] = part_of(total, place, 2)
    send[...] = part_of(total, 1 - place, 2).astype(send.dtype)


def forward_kernel(halves, where, own, *refs):
    arrived, refs = refs[:halves], refs[halves:]
    w_in, w_out, rows_out, mine_out, keep, *send, whole, normed, total = refs
    step = pl.program_id(0)

    @pl.when(step == 0)
    def _():
        rows = jnp.where(where[0] == 0, own[...], gathered(arrived, where[1]))
        rows_out[...] = rows
        whole[...] = rows
        mine_out[...] = part_of(whole, where[1], halves)
        normed[...] = normalised(rows)
        total[...] = jnp.zeros_like(total)

    value, _ = gelu_parts(dot(normed[...], w_in[...]))
    total[...] += dot(value.astype(BF16), w_out[...])

    @pl.when(step == pl.num_programs(0) - 1)
    def _():
        emit_parts(total, where[1], keep, send[0] if send else None)


def forward_section(where, own, arrived, w_in, w_out):
    rows, width = own.shape
    hidden = w_in.shape[1]
    tile = tile_of(hidden, 512)
    halves = len(arrived)
    full, part = (rows, width), (rows // halves, width)
    shapes = [(full, BF16), (part, BF16), (part, F32)] + [(part, BF16)] * (halves - 1)
    return pl.pallas_call(
        functools.partial(forward_kernel, halves),
        grid_spec=pltpu.PrefetchScalarGridSpec(
            num_scalar_prefetch=1,
            grid=(hidden // tile,),
            in_specs=[
                whole_spec(full),
                *[whole_spec(part)] * halves,
                pl.BlockSpec((width, tile), lambda j, s: (0, j)),
                pl.BlockSpec((tile, width), lambda j, s: (j, 0)),
            ],
            out_specs=[whole_spec(shape) for shape, _ in shapes],
            scratch_shapes=[pltpu.VMEM(full, BF16), pltpu.VMEM(full, BF16), pltpu.VMEM(full, F32)],
        ),
        out_shape=[jax.ShapeDtypeStruct(*shape) for shape in shapes],
        compiler_params=params(VMEM_MIB),
        cost_estimate=pl.CostEstimate(
            flops=4 * rows * width * hidden,
            bytes_accessed=4 * width * hidden,
            transcendentals=rows * hidden,
        ),
        name="section_forward",
    )(where, own, *arrived, w_in, w_out)


def finish_forward_kernel(*refs):
    refs[-1][...] = added(refs[:-1]).astype(BF16)


def finish_forward(rows, pieces):
    return pl.pallas_call(
        finish_forward_kernel,
        out_shape=jax.ShapeDtypeStruct(rows.shape, BF16),
        compiler_params=params(VMEM_MIB),
        name="finish_forward",
    )(rows, *pieces)


def finish_backward_kernel(rows, grads, *refs):
    summed = added(refs[:-1])
    refs[-1][...] = (grads[...].astype(F32) + norm_back(rows[...], summed)).astype(BF16)


def finish_backward(rows, grads, pieces):
    return pl.pallas_call(
        finish_backward_kernel,
        out_shape=jax.ShapeDtypeStruct(rows.shape, BF16),
        compiler_params=params(VMEM_MIB),
        name="finish_backward",
    )(rows, grads, *pieces)


def backward_kernel(owners, halves, pieces, last, has_arrived, where, *refs):
    stashed, refs = refs[: len(owners)], refs[len(owners) :]
    if pieces:
        final, refs = refs[:halves], refs[halves:]
        parts, refs = refs[:pieces], refs[pieces:]
    if has_arrived:
        arrived, refs = refs[:halves], refs[halves:]
    w_in, w_out, mine_rows, mine_grads, keep, *send, rows, grads, normed, total = refs
    step = pl.program_id(0)

    @pl.when(step == 0)
    def _():
        rows[...] = chosen(where[0], [(at, ref[...]) for at, ref in zip(owners, stashed)])
        here = None
        if pieces:
            dnorm = added(parts).astype(BF16).astype(F32)
            here = norm_back(gathered(final, where[1]), dnorm).astype(BF16)
        if has_arrived:
            came = gathered(arrived, where[1])
            here = came if here is None else jnp.where(where[0] == last, here, came)
        grads[...] = here
        mine_rows[...] = part_of(rows, where[1], halves)
        mine_grads[...] = part_of(grads, where[1], halves)
        normed[...] = normalised(rows[...])
        total[...] = jnp.zeros_like(total)

    _, slope = gelu_parts(dot(normed[...], w_in[...]))
    dpre = (dot_t(grads[...], w_out[...]) * slope).astype(BF16)
    total[...] += dot_t(dpre, w_in[...])

    @pl.when(step == pl.num_programs(0) - 1)
    def _():
        emit_parts(total, where[1], keep, send[0] if send else None)


def backward_section(where, last, halves, options, final, parts, arrived, w_in, w_out):
    width, hidden = w_in.shape
    rows = options[0][1].shape[0]
    tile = tile_of(hidden, 512)
    full, part = (rows, width), (rows // halves, width)
    operands = [option for _, option in options]
    specs = [whole_spec(full)] * len(options)
    if parts:
        operands += [*final, *parts]
        specs += [whole_spec(part)] * halves + [whole_spec(full)] * len(parts)
    if arrived is not None:
        operands += arrived
        specs += [whole_spec(part)] * halves
    body = functools.partial(
        backward_kernel,
        tuple(at for at, _ in options),
        halves,
        len(parts),
        last,
        arrived is not None,
    )
    shapes = [(part, BF16), (part, BF16), (part, F32)] + [(part, BF16)] * (halves - 1)
    return pl.pallas_call(
        body,
        grid_spec=pltpu.PrefetchScalarGridSpec(
            num_scalar_prefetch=1,
            grid=(hidden // tile,),
            in_specs=specs
            + [
                pl.BlockSpec((width, tile), lambda j, s: (0, j)),
                pl.BlockSpec((tile, width), lambda j, s: (j, 0)),
            ],
            out_specs=[whole_spec(shape) for shape, _ in shapes],
            scratch_shapes=[pltpu.VMEM(full, BF16)] * 3 + [pltpu.VMEM(full, F32)],
        ),
        out_shape=[jax.ShapeDtypeStruct(*shape) for shape in shapes],
        compiler_params=params(VMEM_MIB),
        cost_estimate=pl.CostEstimate(
            flops=6 * rows * width * hidden,
            bytes_accessed=4 * width * hidden,
            transcendentals=rows * hidden,
        ),
        name="section_backward",
    )(where, *operands, w_in, w_out)


def lane_fill(columns, shape):
    lane = lax.broadcasted_iota(jnp.int32, shape, 1)
    filled = jnp.zeros(shape, F32)
    for at, column in enumerate(columns):
        filled = jnp.where(lane == at, column, filled)
    return filled


def shard_specs(count, width, tile, tiles):
    def index(shard, i, t):
        before, after = i < shard, i > shard
        return (0, jnp.where(before, 0, jnp.where(after, tiles - 1, t)))

    return [
        pl.BlockSpec((width, tile), lambda i, t, s, k=k: index(k, i, t)) for k in range(count)
    ]


def logits_kernel(halves, where, *refs):
    final, refs = refs[:halves], refs[halves:]
    *shards, counts, logits, stats, normed, peak, total, target = refs
    shard, step = pl.program_id(0), pl.program_id(1)
    is_first = (shard == 0) & (step == 0)
    is_end = (shard == pl.num_programs(0) - 1) & (step == pl.num_programs(1) - 1)

    @pl.when(is_first)
    def _():
        normed[...] = normalised(gathered(final, where[1]))
        peak[...] = jnp.full_like(peak, -jnp.inf)
        total[...] = jnp.zeros_like(total)
        target[...] = jnp.zeros_like(target)

    for at, w_part in enumerate(shards):

        @pl.when(shard == at)
        def _(w_part=w_part):
            values = dot(normed[...], w_part[...])
            logits[...] = values
            higher = jnp.maximum(peak[...], jnp.max(values, axis=-1, keepdims=True))
            total[...] = total[...] * jnp.exp(peak[...] - higher) + jnp.sum(
                jnp.exp(values - higher), axis=-1, keepdims=True
            )
            peak[...] = higher
            target[...] += jnp.sum(counts[...].astype(F32) * values, axis=-1, keepdims=True)

    @pl.when(is_end)
    def _():
        stats[...] = lane_fill([peak[...], total[...], target[...]], stats.shape)


def head_logits(where, final, shards, counts, at):
    halves = len(final)
    half, width = final[0].shape
    rows = half * halves
    vocab = shards[0].shape[1]
    tile = tile_of(vocab, 640)
    tiles = vocab // tile
    return pl.pallas_call(
        functools.partial(logits_kernel, halves),
        grid_spec=pltpu.PrefetchScalarGridSpec(
            num_scalar_prefetch=1,
            grid=(len(shards), tiles),
            in_specs=[
                *[whole_spec((half, width))] * halves,
                *shard_specs(len(shards), width, tile, tiles),
                pl.BlockSpec((None, None, rows, tile), lambda i, t, s: (i, at, 0, t)),
            ],
            out_specs=[
                pl.BlockSpec((None, rows, tile), lambda i, t, s: (i, 0, t)),
                whole_spec((rows, 128)),
            ],
            scratch_shapes=[pltpu.VMEM((rows, width), BF16)] + [pltpu.VMEM((rows, 1), F32)] * 3,
        ),
        out_shape=[
            jax.ShapeDtypeStruct((len(shards), rows, vocab), F32),
            jax.ShapeDtypeStruct((rows, 128), F32),
        ],
        compiler_params=params(VMEM_MIB),
        cost_estimate=pl.CostEstimate(
            flops=2 * rows * width * vocab * len(shards),
            bytes_accessed=(2 * width + 6 * rows) * vocab * len(shards),
            transcendentals=rows * vocab * len(shards),
        ),
        name="head_logits",
    )(where, *final, *shards, counts)


def head_grads_kernel(tables, denom, where, *refs):
    stats, refs = refs[:tables], refs[tables:]
    lengths, logits, counts, *shards, part, results, lse, total = refs
    shard, step = pl.program_id(0), pl.program_id(1)
    is_first = (shard == 0) & (step == 0)
    is_end = (shard == pl.num_programs(0) - 1) & (step == pl.num_programs(1) - 1)

    @pl.when(is_first)
    def _():
        values = [ref[...] for ref in stats]
        top = values[0][:, 0:1]
        for table in values[1:]:
            top = jnp.maximum(top, table[:, 0:1])
        mass = sum(table[:, 1:2] * jnp.exp(table[:, 0:1] - top) for table in values)
        target = sum(table[:, 2:3] for table in values)
        lse[...] = top + jnp.log(mass)
        results[...] = lane_fill([lse[...], lengths[...] * lse[...] - target], results.shape)
        total[...] = jnp.zeros_like(total)

    for at, w_part in enumerate(shards):

        @pl.when(shard == at)
        def _(w_part=w_part):
            exped = lengths[...] * jnp.exp(logits[...] - lse[...])
            dlogits = ((exped - counts[...].astype(F32)) / denom).astype(BF16)
            total[...] += dot_t(dlogits, w_part[...])

    @pl.when(is_end)
    def _():
        part[...] = total[...].astype(part.dtype)


def head_grads(where, stats, lengths, logits, counts, at, shards, denom, part_type):
    count, rows, vocab = logits.shape
    width = shards[0].shape[0]
    tile = tile_of(vocab, 640)
    tiles = vocab // tile
    return pl.pallas_call(
        functools.partial(head_grads_kernel, len(stats), denom),
        grid_spec=pltpu.PrefetchScalarGridSpec(
            num_scalar_prefetch=1,
            grid=(count, tiles),
            in_specs=[whole_spec((rows, 128))] * len(stats)
            + [
                pl.BlockSpec((None, rows, 1), lambda i, t, s: (at, 0, 0)),
                pl.BlockSpec((None, rows, tile), lambda i, t, s: (i, 0, t)),
                pl.BlockSpec((None, None, rows, tile), lambda i, t, s: (i, at, 0, t)),
                *shard_specs(count, width, tile, tiles),
            ],
            out_specs=[whole_spec((rows, width)), whole_spec((rows, 128))],
            scratch_shapes=[pltpu.VMEM((rows, 1), F32), pltpu.VMEM((rows, width), F32)],
        ),
        out_shape=[
            jax.ShapeDtypeStruct((rows, width), part_type),
            jax.ShapeDtypeStruct((rows, 128), F32),
        ],
        compiler_params=params(VMEM_MIB),
        cost_estimate=pl.CostEstimate(
            flops=2 * rows * width * vocab * count,
            bytes_accessed=(2 * width + 6 * rows) * vocab * count,
            transcendentals=rows * vocab * count,
        ),
        name="head_grads",
    )(where, *stats, lengths, logits, counts, *shards)


def weight_kernel(blocks, adding, share, where, *refs):
    x_refs, refs = refs[:blocks], refs[blocks:]
    g_refs, refs = refs[:blocks], refs[blocks:]
    w_in, w_out, refs = refs[0], refs[1], refs[2:]
    if adding:
        old_first, old_second, refs = refs[0], refs[1], refs[2:]
    first, second, normed, grads, normed_t, grads_t = refs
    count = x_refs[0].shape[0]

    @pl.when(pl.program_id(0) == 0)
    def _():
        columns = pl.ds(pl.multiple_of(where[0] * share, share), share)
        for at in range(blocks):
            place = pl.ds(at * count, count)
            normed[place, :] = normalised(x_refs[at][...])
            grads[place, :] = g_refs[at][...]
        normed_t[...] = normed[:, columns].astype(F32).T.astype(BF16)
        grads_t[...] = grads[:, columns].astype(F32).T.astype(BF16)

    total_first = old_first[...] if adding else None
    total_second = None
    rows = normed.shape[0]
    part = min(256, rows)
    for at in range(rows // part):
        place = pl.ds(at * part, part)
        value, slope = gelu_parts(dot(normed[place, :], w_in[...]))
        dpre = (dot_t(grads[place, :], w_out[...]) * slope).astype(BF16)
        now_first = dot(normed_t[:, place], dpre)
        now_second = dot(grads_t[:, place], value.astype(BF16))
        total_first = now_first if total_first is None else total_first + now_first
        total_second = now_second if total_second is None else total_second + now_second
    first[...] = total_first
    total_second = total_second.T
    second[...] = old_second[...] + total_second if adding else total_second


def weight_grads(where, x_parts, g_parts, w_in, w_out, old, share):
    width, hidden = w_in.shape
    tile = tile_of(hidden, 512)
    blocks = len(g_parts)
    count = g_parts[0].shape[0]
    rows = blocks * count
    in_specs = [
        pl.BlockSpec((None, None, count, width), index) for _, index in x_parts
    ]
    in_specs += [pl.BlockSpec((count, width), lambda j, s: (0, 0))] * blocks
    in_specs += [
        pl.BlockSpec((width, tile), lambda j, s: (0, j)),
        pl.BlockSpec((tile, width), lambda j, s: (j, 0)),
    ]
    grad_specs = [
        pl.BlockSpec((share, tile), lambda j, s: (0, j)),
        pl.BlockSpec((tile, share), lambda j, s: (j, 0)),
    ]
    adding = old is not None
    aliases = {}
    if adding:
        in_specs += grad_specs
        aliases = {1 + 2 * blocks + 2: 0, 1 + 2 * blocks + 3: 1}
    return pl.pallas_call(
        functools.partial(weight_kernel, blocks, adding, share),
        grid_spec=pltpu.PrefetchScalarGridSpec(
            num_scalar_prefetch=1,
            grid=(hidden // tile,),
            in_specs=in_specs,
            out_specs=grad_specs,
            scratch_shapes=[
                pltpu.VMEM((rows, width), BF16),
                pltpu.VMEM((rows, width), BF16),
                pltpu.VMEM((share, rows), BF16),
                pltpu.VMEM((share, rows), BF16),
            ],
        ),
        out_shape=[
            jax.ShapeDtypeStruct((share, hidden), F32),
            jax.ShapeDtypeStruct((hidden, share), F32),
        ],
        input_output_aliases=aliases,
        compiler_params=params(VMEM_MIB),
        cost_estimate=pl.CostEstimate(
            flops=4 * rows * (width + share) * hidden,
            bytes_accessed=4 * width * hidden + 16 * share * hidden,
            transcendentals=rows * hidden,
        ),
        name="weight_grads",
    )(where, *[x for x, _ in x_parts], *g_parts, w_in, w_out, *(old or ()))


def unit_counts(ends, targets, ids):
    positions = jnp.arange(targets.shape[1], dtype=jnp.int32)
    row_local = jnp.sum((ends[:, None, :] <= positions[None, :, None]).astype(jnp.int32), axis=-1)
    rows = jnp.arange(ends.shape[1], dtype=jnp.int32)
    row_onehot = (row_local[:, :, None] == rows[None, None, :]).astype(BF16)
    hits = (targets[:, :, None] == ids[None, None, :]).astype(BF16)
    counts = jnp.einsum("mur,muv->mrv", row_onehot, hits, preferred_element_type=F32)
    return counts.astype(BF16)


def on_device(text_rows, durations, unit_targets, w_in, w_out, w_unit):
    micro, row_count, width = text_rows.shape
    segments = lax.axis_size("segment")
    mp_size = lax.axis_size("mp")
    dp_size = lax.axis_size("dp")
    seg = lax.axis_index("segment").astype(jnp.int32)
    mp_at = lax.axis_index("mp").astype(jnp.int32)
    dp_at = lax.axis_index("dp").astype(jnp.int32)
    last = segments - 1
    pair = mp_size == 2
    halves = 2 if pair else 1
    part_type = BF16 if pair else F32
    where = jnp.stack([seg, mp_at])
    first = w_in[0]
    second = w_out[0]
    chunks = CHUNKS
    rows = micro * row_count // chunks
    text = [t for t in text_rows.reshape(chunks, rows, width)]
    vocab_part = w_unit.shape[1]
    unit_count = unit_targets.shape[1]
    denom = float(micro * unit_count * dp_size)
    lengths = durations[:, 0, :]
    length_f = lengths.astype(F32).reshape(chunks, rows, 1)
    ends = jnp.cumsum(lengths, axis=-1)

    shards = [w_unit] + [lax.ppermute(w_unit, "segment", [(j, last)]) for j in range(last)]
    part_ids = jnp.arange(vocab_part, dtype=jnp.int32)
    head_counts = jnp.stack(
        [
            unit_counts(ends, unit_targets, (j * mp_size + mp_at) * vocab_part + part_ids)
            for j in [last, *range(last)]
        ]
    ).reshape(segments, chunks, rows, vocab_part)
    own_ids = (seg * mp_size + mp_at) * vocab_part + part_ids
    own_counts = unit_counts(ends, unit_targets, own_ids).reshape(micro * row_count, vocab_part)

    def both(part):
        return [part, swapped(part)] if pair else [part]

    def reduced(keep, send):
        return [keep, swapped(send[0])] if pair else [lax.psum(keep, "mp")]

    def mp_pieces(part):
        return [part, swapped(part)] if pair else [lax.psum(part, "mp")]

    def mp_tables(stats):
        if pair:
            return [stats, swapped(stats)]
        return [t for t in lax.all_gather(stats, "mp")]

    def gather_grads(mine, theirs):
        if not pair:
            return [t for t in lax.all_gather(mine, "dp")]
        own, other = [mine], [theirs]
        for distance in range(1, dp_size):
            route = [(i, (i + distance) % dp_size) for i in range(dp_size)]
            came = lax.ppermute(mine, "dp", route)
            own.append(came)
            other.append(swapped(came))
        return own + other

    stash, x_halves, grads, finals, results, sent = [], [], [], [], [], []
    sums = None
    x_mine = x_theirs = None
    f_hop = b_hop = None

    def x_parts(at):
        if not pair:
            return [(x_mine, lambda j, s, k=k: (k, at, 0, 0)) for k in range(dp_size)]
        return [
            (source, lambda j, s, k=k: (lax.rem(s[0] + dp_size - k, dp_size), at, 0, 0))
            for source in (x_mine, x_theirs)
            for k in range(dp_size)
        ]

    clocks = 2 * segments + chunks - 1
    for clock in range(clocks):
        f_out = b_out = None
        if clock < segments + chunks - 1:
            own = text[min(clock, chunks - 1)]
            arrived = [own[: rows // halves]] * halves
            if clock > 0:
                arrived = both(shifted(f_hop, "segment", 1))
            rows_in, mine, keep, *send = forward_section(where, own, arrived, first, second)
            stash.append(rows_in)
            x_halves.append(mine)
            f_out = finish_forward(mine, reduced(keep, send))
        if clock >= segments:
            at = clock - segments
            arrived = None if at == 0 else both(shifted(b_hop, "segment", -1))
            if clock < clocks - 1:
                parts = []
                final = None
                if at < chunks:
                    final = both(f_hop)
                    finals.append(final)
                    sent.append(
                        [lax.ppermute(f_hop, "segment", [(last, to)]) for to in range(last)]
                    )
                    logits, stats = head_logits(where, final, shards, head_counts, at)
                    part, result = head_grads(
                        where,
                        mp_tables(stats),
                        length_f,
                        logits,
                        head_counts,
                        at,
                        shards,
                        denom,
                        part_type,
                    )
                    results.append(result[:, 0:2])
                    parts = mp_pieces(part)
                options = []
                for other in range(segments):
                    stage = clock - 2 * segments + 1 + 2 * other
                    if 0 <= stage < len(stash):
                        options.append((other, stash[stage]))
                mine, g_mine, keep, *send = backward_section(
                    where, last, halves, options, final, parts, arrived, first, second
                )
                grads.append(g_mine)
                b_out = finish_backward(mine, g_mine, reduced(keep, send))
            else:
                grads.append(arrived[0])
        if clock == segments + chunks - 2:
            x_half = jnp.stack(
                [
                    chosen(seg, [(s, x_halves[b + s]) for s in range(segments)])
                    for b in range(chunks)
                ]
            )
            x_mine = lax.all_gather(x_half, "dp")
            x_theirs = swapped(x_mine) if pair else None
        if clock >= 2 * segments - 1:
            at = clock - 2 * segments + 1
            mine = chosen(seg, [(s, grads[at + last - s]) for s in range(segments)])
            theirs = swapped(mine) if pair else None
            sums = weight_grads(
                dp_at[None],
                x_parts(at),
                gather_grads(mine, theirs),
                first,
                second,
                sums,
                width // dp_size,
            )
        f_hop, b_hop = f_out, b_out

    results = jnp.stack(results)
    results = chosen(
        seg,
        [(last, results)]
        + [(to, lax.ppermute(results, "segment", [(last, to)])) for to in range(last)],
    )
    loss = (jnp.sum(results[:, :, 1]) / denom)[None]
    final_rows = []
    for b in range(chunks):
        mine = chosen(seg, [(last, finals[b][0])] + [(to, sent[b][to]) for to in range(last)])
        pieces = both(mine)
        if pair:
            pieces = [
                jnp.where(mp_at == 0, pieces[0], pieces[1]),
                jnp.where(mp_at == 0, pieces[1], pieces[0]),
            ]
        final_rows += pieces
    final_norm = normalised(jnp.concatenate(final_rows))
    own_logits = dot(final_norm, w_unit)
    own_exp = jnp.exp(own_logits - results[:, :, 0].reshape(-1, 1))
    own_dlogits = (
        (length_f.reshape(-1, 1) * own_exp - own_counts.astype(F32)) / denom
    ).astype(BF16)
    grad_unit = t_dot(final_norm, own_dlogits).astype(BF16)
    sum_unit = lax.psum_scatter(grad_unit, "dp", scatter_dimension=0, tiled=True).astype(F32)
    return (loss, sums[0][None], sums[1][None], sum_unit)


def solution(mesh):
    placed = (
        P(None, "dp", None),
        P(None, "dp", None),
        P(None, "dp"),
        P("segment", None, "mp"),
        P("segment", "mp", None),
        P(None, ("segment", "mp")),
    )
    return jax.shard_map(
        on_device,
        mesh=mesh,
        in_specs=placed,
        out_specs=(
            P("dp"),
            P("segment", "dp", "mp"),
            P("segment", "mp", "dp"),
            P("dp", ("segment", "mp")),
        ),
        check_vma=False,
    )
```

time: 644 us -> 602 us (0.935)
  local copies, waits for them, and re-layouts: 114 us -> 19.8 us
  waiting for transfers between devices: 109 us -> 152 us
  Pallas kernels: 251 us -> 282 us
  starting transfers between devices: 108 us -> 86.7 us
    unnamed x204 -> x124, local copies, waits for them, and re-layouts: 113 us -> 14.7 us
    pallas_call x11 -> x7, Pallas kernels: 64.2 us -> 97.2 us  [the longest x5 68.9 us: forward_section(): pl.pallas_call(functools.partial(forward_kernel, halves), grid_spec=pltpu...]
    ppermute x12 -> x6, waiting for transfers between devices: 40.3 us -> 66 us  [gather_grads(): came = lax.ppermute(mine, 'dp', route)]
    ppermute x12, waiting for transfers between devices: 0.03 us -> 22.9 us  [the longest x3 13.2 us: on_device(): lax.ppermute(w_unit, 'segment', [(j, last)])]
    ppermute x12 -> x8, starting transfers between devices: 47 us -> 33.2 us  [shifted(): return lax.ppermute(block, axis, route)]
    pallas_call x7 -> x4, Pallas kernels: 70.5 us -> 62.3 us  [backward_section(): pl.pallas_call(body, grid_spec=pltpu.PrefetchScalarGridSpec(num_scalar_pr...]
    pallas_call x4 -> x2, Pallas kernels: 84 us -> 76.2 us  [weight_grads(): pl.pallas_call(functools.partial(weight_kernel, blocks, adding, share), g...]
    pallas_call x7 -> x5, Pallas kernels: 2.42 us -> 9.87 us  [finish_forward(): pl.pallas_call(finish_forward_kernel, out_shape=jax.ShapeDtypeStruct(rows...]
  transfers between devices with their start and end apart: 73 -> 61, of which waited for: 23 -> 23; matrix products, arithmetic and copies ran while one was open for 4% -> 5% of each run, Pallas kernels for 40% -> 42%
where the time goes in v3:
time: 602 us; the launch traced here: 590 us
  Pallas kernels  282 us (47%)
  waiting for transfers between devices  152 us (25%)
  starting transfers between devices  86.7 us (14%)
  matrix products  21.9 us (4%)
  local copies, waits for them, and re-layouts  19.8 us (3%)
  between operations  17 us (3%)
  other arithmetic  11.4 us (2%)
    pallas_call x2, Pallas kernels, weight_grads(): pl.pallas_call(functools.partial(weight_kernel, blocks, adding, share), g...  76.2 us
    pallas_call x5, Pallas kernels, forward_section(): pl.pallas_call(functools.partial(forward_kernel, halves), grid_spec=pltpu...  68.9 us
    ppermute x6, waiting for transfers between devices, gather_grads(): came = lax.ppermute(mine, 'dp', route)  66 us
    pallas_call x4, Pallas kernels, backward_section(): pl.pallas_call(body, grid_spec=pltpu.PrefetchScalarGridSpec(num_scalar_pr...  62.3 us
    ppermute x8, waiting for transfers between devices, shifted(): return lax.ppermute(block, axis, route)  53.2 us
    ppermute x8, starting transfers between devices, shifted(): return lax.ppermute(block, axis, route)  33.2 us
    ppermute x33, starting transfers between devices, swapped(): return lax.ppermute(block, 'mp', [(0, 1), (1, 0)])  30.5 us
    pallas_call x2, Pallas kernels, head_logits(): pl.pallas_call(functools.partial(logits_kernel, halves), grid_spec=pltpu....  28.3 us
  transfers between devices with their start and end apart: 61, of which 23 were waited for; matrix products, arithmetic and copies ran while one was open for 5% of the time, Pallas kernels for 42%

profile of v3, /device:TPU:11, one launch (start us, length us, event | category | flops | bytes accessed | tf_op | source)
XLA Modules:
  0.0 590.5 jit_solution(6382974373006694808)
XLA Ops:
  11.7 14.2 %section_forward.5 = (bf16[256,1024]{1,0:T(8,128)(2,1)}, bf16[128,1024]{1,0:T(8,128)(2,1)}, f32[128,1024]{1,0:T(8,128)}, bf16[128,1024]{1,0:T(8,128)(2,1)}) custom-call(s32[2]{0:T(128)} %pad_add_fusion.where, bf16[256,1024]{1,0:T(8,128)(2,1)} %bitcast.57, bf16[128,1024]{1,0:T(8,128)(2,1)} %slice_bitcast_fusion.refs_0_.refs_1_, ...), custom_call_target="tpu_custom_call" | custom-call | flops 4294967296 | bytes 16777216 | tf_op jit(solution)/shard_map/section_forward/pallas_call | solution.py:144
  33.7 6.5 %collective-permute-done.1.refs_0_ = bf16[128,1024]{1,0:T(8,128)(2,1)S(1)} collective-permute-done((bf16[128,1024]{1,0:T(8,128)(2,1)}, bf16[128,1024]{1,0:T(8,128)(2,1)S(1)}, u32[]{:S(2)}, u32[]{:S(2)}) %collective-permute-start.1) | collective-permute-done | bytes 262176 | tf_op jit(solution)/shard_map/ppermute | solution.py:19
  43.3 13.8 %section_forward.6 = (bf16[256,1024]{1,0:T(8,128)(2,1)}, bf16[128,1024]{1,0:T(8,128)(2,1)}, f32[128,1024]{1,0:T(8,128)}, bf16[128,1024]{1,0:T(8,128)(2,1)}) custom-call(s32[2]{0:T(128)} %pad_add_fusion.where, bf16[256,1024]{1,0:T(8,128)(2,1)} %bitcast.53, bf16[128,1024]{1,0:T(8,128)(2,1)} %copy-done.22, bf16[128,1024]{1,0:T(8,128)(2,1)} %copy-done.24, ...), custom_call_target="tpu_custom_call" | custom-call | flops 4294967296 | bytes 16777216 | tf_op jit(solution)/shard_map/section_forward/pallas_call | solution.py:144
  81.7 13.6 %section_forward.7 = (bf16[256,1024]{1,0:T(8,128)(2,1)}, bf16[128,1024]{1,0:T(8,128)(2,1)}, f32[128,1024]{1,0:T(8,128)}, bf16[128,1024]{1,0:T(8,128)(2,1)}) custom-call(s32[2]{0:T(128)} %pad_add_fusion.where, bf16[256,1024]{1,0:T(8,128)(2,1)} %bitcast.54, bf16[128,1024]{1,0:T(8,128)(2,1)} %copy-done.18, bf16[128,1024]{1,0:T(8,128)(2,1)} %copy-done.20, ...), custom_call_target="tpu_custom_call" | custom-call | flops 4294967296 | bytes 16777216 | tf_op jit(solution)/shard_map/section_forward/pallas_call | solution.py:144
  108.4 30.9 %collective-permute-done.7.refs_0_ = bf16[128,1024]{1,0:T(8,128)(2,1)S(1)} collective-permute-done((bf16[128,1024]{1,0:T(8,128)(2,1)}, bf16[128,1024]{1,0:T(8,128)(2,1)S(1)}, u32[]{:S(2)}, u32[]{:S(2)}) %collective-permute-start.7) | collective-permute-done | bytes 262176 | tf_op jit(solution)/shard_map/ppermute | solution.py:19
  144.0 13.7 %section_forward.8 = (bf16[256,1024]{1,0:T(8,128)(2,1)}, bf16[128,1024]{1,0:T(8,128)(2,1)}, f32[128,1024]{1,0:T(8,128)}, bf16[128,1024]{1,0:T(8,128)(2,1)}) custom-call(s32[2]{0:T(128)} %pad_add_fusion.where, bf16[256,1024]{1,0:T(8,128)(2,1)} %bitcast.55, bf16[128,1024]{1,0:T(8,128)(2,1)} %copy-done.19, bf16[128,1024]{1,0:T(8,128)(2,1)} %copy-done.23, ...), custom_call_target="tpu_custom_call" | custom-call | flops 4294967296 | bytes 16777216 | tf_op jit(solution)/shard_map/section_forward/pallas_call | solution.py:144
  175.9 13.2 %collective-permute-done.12.refs_4_.refs_7_ = bf16[1024,1280]{1,0:T(8,128)(2,1)} collective-permute-done((bf16[1024,1280]{1,0:T(8,128)(2,1)S(1)}, bf16[1024,1280]{1,0:T(8,128)(2,1)}, u32[]{:S(2)}, u32[]{:S(2)}) %collective-permute-start.12) | collective-permute-done | bytes 2621472 | tf_op jit(solution)/shard_map/ppermute | solution.py:553
  189.9 14.1 %head_logits.2 = (f32[4,256,1280]{2,1,0:T(8,128)}, f32[256,128]{1,0:T(8,128)}) custom-call(s32[2]{0:T(128)} %pad_add_fusion.where, bf16[128,1024]{1,0:T(8,128)(2,1)} %finish_forward.8.refs_0_.refs_2_, bf16[128,1024]{1,0:T(8,128)(2,1)} %copy-done.16, bf16[1024,1280]{1,0:T(8,128)(2,1)} %refs_5_.3, bf16[1024,1280]{1,0:T(8,128)(2,1)} %collective-permute-done.11.refs_3_.refs_6_, ...), custom_call_target="tpu_custom_call" | custom-call | flops 2684354560 | bytes 18350080 | tf_op jit(solution)/shard_map/head_logits/pallas_call | solution.py:334
  206.2 13.5 %head_grads.2 = (bf16[256,1024]{1,0:T(8,128)(2,1)}, f32[256,128]{1,0:T(8,128)}) custom-call(s32[2]{0:T(128)} %pad_add_fusion.where, f32[256,128]{1,0:T(8,128)} %get-tuple-element.64.refs_0_, f32[256,128]{1,0:T(8,128)} %copy-done.36, f32[2,256,1]{2,1,0:T(8,128)} %convert_element_type.91.refs_2_, f32[4,256,1280]{2,1,0:T(8,128)} %get-tuple-element.65.refs_3_, ...), custom_call_target="tpu_custom_call" | custom-call | flops 2684354560 | bytes 18350080 | tf_op jit(solution)/shard_map/head_grads/pallas_call | solution.py:401
  220.9 13.6 %section_forward.9 = (bf16[256,1024]{1,0:T(8,128)(2,1)}, bf16[128,1024]{1,0:T(8,128)(2,1)}, f32[128,1024]{1,0:T(8,128)}, bf16[128,1024]{1,0:T(8,128)(2,1)}) custom-call(s32[2]{0:T(128)} %pad_add_fusion.where, bf16[256,1024]{1,0:T(8,128)(2,1)} %bitcast.56, bf16[128,1024]{1,0:T(8,128)(2,1)} %copy-done.17, bf16[128,1024]{1,0:T(8,128)(2,1)} %copy-done.21, ...), custom_call_target="tpu_custom_call" | custom-call | flops 4294967296 | bytes 16777216 | tf_op jit(solution)/shard_map/section_forward/pallas_call | solution.py:144
  239.9 15.8 %section_backward.4 = (bf16[128,1024]{1,0:T(8,128)(2,1)}, bf16[128,1024]{1,0:T(8,128)(2,1)}, f32[128,1024]{1,0:T(8,128)}, bf16[128,1024]{1,0:T(8,128)(2,1)}) custom-call(s32[2]{0:T(128)} %pad_add_fusion.where, bf16[256,1024]{1,0:T(8,128)(2,1)} %get-tuple-element.77.refs_0_, bf16[256,1024]{1,0:T(8,128)(2,1)} %get-tuple-element.78.refs_1_, ...), custom_call_target="tpu_custom_call" | custom-call | flops 6442450944 | bytes 16777216 | tf_op jit(solution)/shard_map/section_backward/pallas_call | solution.py:253
  256.8 14.3 %head_logits.3 = (f32[4,256,1280]{2,1,0:T(8,128)}, f32[256,128]{1,0:T(8,128)}) custom-call(s32[2]{0:T(128)} %pad_add_fusion.where, bf16[128,1024]{1,0:T(8,128)(2,1)} %finish_forward.9.refs_0_.refs_3_, bf16[128,1024]{1,0:T(8,128)(2,1)} %copy-done.15, bf16[1024,1280]{1,0:T(8,128)(2,1)} %refs_5_.3, bf16[1024,1280]{1,0:T(8,128)(2,1)} %collective-permute-done.11.refs_3_.refs_6_, ...), custom_call_target="tpu_custom_call" | custom-call | flops 2684354560 | bytes 18350080 | tf_op jit(solution)/shard_map/head_logits/pallas_call | solution.py:334
  276.7 13.6 %head_grads.3 = (bf16[256,1024]{1,0:T(8,128)(2,1)}, f32[256,128]{1,0:T(8,128)}) custom-call(s32[2]{0:T(128)} %pad_add_fusion.where, f32[256,128]{1,0:T(8,128)} %get-tuple-element.70.refs_0_, f32[256,128]{1,0:T(8,128)} %copy-done.35, f32[2,256,1]{2,1,0:T(8,128)} %convert_element_type.91.refs_2_, f32[4,256,1280]{2,1,0:T(8,128)} %get-tuple-element.71.refs_3_, ...), custom_call_target="tpu_custom_call" | custom-call | flops 2684354560 | bytes 18350080 | tf_op jit(solution)/shard_map/head_grads/pallas_call | solution.py:401
  293.5 9.7 %collective-permute-done.52 = bf16[128,1024]{1,0:T(8,128)(2,1)S(1)} collective-permute-done((bf16[128,1024]{1,0:T(8,128)(2,1)S(1)}, bf16[128,1024]{1,0:T(8,128)(2,1)S(1)}, u32[]{:S(2)}, u32[]{:S(2)}) %collective-permute-start.52) | collective-permute-done | bytes 262176 | tf_op jit(solution)/shard_map/ppermute | solution.py:625
  305.0 16.3 %section_backward.5 = (bf16[128,1024]{1,0:T(8,128)(2,1)}, bf16[128,1024]{1,0:T(8,128)(2,1)}, f32[128,1024]{1,0:T(8,128)}, bf16[128,1024]{1,0:T(8,128)(2,1)}) custom-call(s32[2]{0:T(128)} %pad_add_fusion.where, bf16[256,1024]{1,0:T(8,128)(2,1)} %get-tuple-element.73.refs_0_, bf16[256,1024]{1,0:T(8,128)(2,1)} %get-tuple-element.74.refs_1_, ...), custom_call_target="tpu_custom_call" | custom-call | flops 6442450944 | bytes 16777216 | tf_op jit(solution)/shard_map/section_backward/pallas_call | solution.py:253
  326.0 7.4 %collective-permute-start.30 = (bf16[128,1024]{1,0:T(8,128)(2,1)}, bf16[128,1024]{1,0:T(8,128)(2,1)S(1)}, u32[]{:S(2)}, u32[]{:S(2)}) collective-permute-start(bf16[128,1024]{1,0:T(8,128)(2,1)} %finish_backward.5), channel_id=1, source_target_pairs={{8,0},{16,8},{24,16},{9,1},{17,9},{25,17},{10,2},{18,10},{26,18},{... | collective-permute-start | bytes 786440 | tf_op jit(solution)/shard_map/ppermute | solution.py:19
  343.9 15.2 %section_backward.6 = (bf16[128,1024]{1,0:T(8,128)(2,1)}, bf16[128,1024]{1,0:T(8,128)(2,1)}, f32[128,1024]{1,0:T(8,128)}, bf16[128,1024]{1,0:T(8,128)(2,1)}) custom-call(s32[2]{0:T(128)} %pad_add_fusion.where, bf16[256,1024]{1,0:T(8,128)(2,1)} %get-tuple-element.77.refs_0_, bf16[256,1024]{1,0:T(8,128)(2,1)} %get-tuple-element.78.refs_1_, ...), custom_call_target="tpu_custom_call" | custom-call | flops 6442450944 | bytes 16777216 | tf_op jit(solution)/shard_map/section_backward/pallas_call | solution.py:253
  378.7 15.1 %section_backward.7 = (bf16[128,1024]{1,0:T(8,128)(2,1)}, bf16[128,1024]{1,0:T(8,128)(2,1)}, f32[128,1024]{1,0:T(8,128)}, bf16[128,1024]{1,0:T(8,128)(2,1)}) custom-call(s32[2]{0:T(128)} %pad_add_fusion.where, bf16[256,1024]{1,0:T(8,128)(2,1)} %get-tuple-element.73.refs_0_, bf16[256,1024]{1,0:T(8,128)(2,1)} %get-tuple-element.74.refs_1_, ...), custom_call_target="tpu_custom_call" | custom-call | flops 6442450944 | bytes 16777216 | tf_op jit(solution)/shard_map/section_backward/pallas_call | solution.py:253
  418.7 25.5 %collective-permute-done.38.refs_10_ = bf16[128,1024]{1,0:T(8,128)(2,1)S(1)} collective-permute-done((bf16[128,1024]{1,0:T(8,128)(2,1)S(1)}, bf16[128,1024]{1,0:T(8,128)(2,1)S(1)}, u32[]{:S(2)}, u32[]{:S(2)}) %collective-permute-start.38) | collective-permute-done | bytes 262176 | tf_op jit(solution)/shard_map/ppermute | solution.py:584
  444.9 27.0 %collective-permute-done.39.refs_11_ = bf16[128,1024]{1,0:T(8,128)(2,1)S(1)} collective-permute-done((bf16[128,1024]{1,0:T(8,128)(2,1)S(1)}, bf16[128,1024]{1,0:T(8,128)(2,1)S(1)}, u32[]{:S(2)}, u32[]{:S(2)}) %collective-permute-start.39) | collective-permute-done | bytes 262176 | tf_op jit(solution)/shard_map/ppermute | solution.py:584
  473.0 12.5 %collective-permute-start.48 = (bf16[128,1024]{1,0:T(8,128)(2,1)S(1)}, bf16[128,1024]{1,0:T(8,128)(2,1)S(1)}, u32[]{:S(2)}, u32[]{:S(2)}) collective-permute-start(bf16[128,1024]{1,0:T(8,128)(2,1)S(1)} %collective-permute-done.44.refs_9_), channel_id=1, source_target_pairs={{0,4},{4,0},{1,5},{5,1},{2,6},{6,2},{3,7},{7,3},{8,12},{12,8},{9,1... | collective-permute-start | bytes 786440 | tf_op jit(solution)/shard_map/ppermute | solution.py:23
  485.5 7.0 %collective-permute-done.45.refs_10_ = bf16[128,1024]{1,0:T(8,128)(2,1)S(1)} collective-permute-done((bf16[128,1024]{1,0:T(8,128)(2,1)S(1)}, bf16[128,1024]{1,0:T(8,128)(2,1)S(1)}, u32[]{:S(2)}, u32[]{:S(2)}) %collective-permute-start.45) | collective-permute-done | bytes 262176 | tf_op jit(solution)/shard_map/ppermute | solution.py:584
  502.6 37.0 %weight_grads.2 = (f32[256,4096]{1,0:T(8,128)}, f32[4096,256]{1,0:T(8,128)}) custom-call(s32[1]{0:T(128)} %bitcast.15.where, bf16[4,2,128,1024]{3,2,1,0:T(8,128)(2,1)} %bitcast.66, bf16[4,2,128,1024]{3,2,1,0:T(8,128)(2,1)} %bitcast.67, bf16[4,2,128,1024]{3,2,1,0:T(8,128)(2,1)} %bitcast.68, bf16[4,2,128,1024]{3,2,1,0:T(8,128)(2,1)} %bitcast.69, ...), custom_call_target="tpu_custom_call" | custom-call | flops 21474836480 | bytes 33554432 | tf_op jit(solution)/shard_map/weight_grads/pallas_call | solution.py:489
  540.6 39.2 %weight_grads.3 = (f32[256,4096]{1,0:T(8,128)}, f32[4096,256]{1,0:T(8,128)}) custom-call(s32[1]{0:T(128)} %bitcast.15.where, bf16[4,2,128,1024]{3,2,1,0:T(8,128)(2,1)} %bitcast.70, bf16[4,2,128,1024]{3,2,1,0:T(8,128)(2,1)} %bitcast.71, bf16[4,2,128,1024]{3,2,1,0:T(8,128)(2,1)} %bitcast.72, ...), custom_call_target="tpu_custom_call", output_to_operand_aliasing={{0}: (19, {}), {1}: (20, {})} | custom-call | flops 21474836480 | bytes 33554432 | tf_op jit(solution)/shard_map/weight_grads/pallas_call | solution.py:489
  (285 shorter events, 170.9 us)
Async XLA Ops:
  7.2 387.3 %all-gather.3.cloned.1.call-start = ((), (), s32[]{:S(2)}) async-start(), calls=%async_computation.2 | async-start | bytes 2621440 | tf_op jit(solution)/shard_map/all_gather | solution.py:660
  72.3 103.6 %collective-permute-start.11 = (bf16[1024,1280]{1,0:T(8,128)(2,1)S(1)}, bf16[1024,1280]{1,0:T(8,128)(2,1)}, u32[]{:S(2)}, u32[]{:S(2)}) collective-permute-start(bf16[1024,1280]{1,0:T(8,128)(2,1)S(1)} %copy-done), channel_id=1, source_target_pairs={{0,24},{1,25},{2,26},{3,27},{4,28},{5,29},{6,30},{7,31}} | collective-permute-start | bytes 7864328 | tf_op jit(solution)/shard_map/ppermute | solution.py:553
  74.5 114.7 %collective-permute-start.12 = (bf16[1024,1280]{1,0:T(8,128)(2,1)S(1)}, bf16[1024,1280]{1,0:T(8,128)(2,1)}, u32[]{:S(2)}, u32[]{:S(2)}) collective-permute-start(bf16[1024,1280]{1,0:T(8,128)(2,1)S(1)} %copy-done), channel_id=1, source_target_pairs={{8,24},{9,25},{10,26},{11,27},{12,28},{13,29},{14,30},{15,31}} | collective-permute-start | bytes 7864328 | tf_op jit(solution)/shard_map/ppermute | solution.py:553
  78.2 110.9 %collective-permute-start.13 = (bf16[1024,1280]{1,0:T(8,128)(2,1)S(1)}, bf16[1024,1280]{1,0:T(8,128)(2,1)}, u32[]{:S(2)}, u32[]{:S(2)}) collective-permute-start(bf16[1024,1280]{1,0:T(8,128)(2,1)S(1)} %copy-done), channel_id=1, source_target_pairs={{16,24},{17,25},{18,26},{19,27},{20,28},{21,29},{22,30},{23,31}} | collective-permute-start | bytes 7864328 | tf_op jit(solution)/shard_map/ppermute | solution.py:553
  101.5 37.8 %collective-permute-start.7 = (bf16[128,1024]{1,0:T(8,128)(2,1)}, bf16[128,1024]{1,0:T(8,128)(2,1)S(1)}, u32[]{:S(2)}, u32[]{:S(2)}) collective-permute-start(bf16[128,1024]{1,0:T(8,128)(2,1)} %finish_forward.7), channel_id=1, source_target_pairs={{0,8},{8,16},{16,24},{1,9},{9,17},{17,25},{2,10},{10,18},{18,26},{... | collective-permute-start | bytes 786440 | tf_op jit(solution)/shard_map/ppermute | solution.py:19
  163.6 25.5 %collective-permute-start.10 = (bf16[128,1024]{1,0:T(8,128)(2,1)}, bf16[128,1024]{1,0:T(8,128)(2,1)S(1)}, u32[]{:S(2)}, u32[]{:S(2)}) collective-permute-start(bf16[128,1024]{1,0:T(8,128)(2,1)} %finish_forward.8.refs_0_.refs_2_), channel_id=1, source_target_pairs={{0,4},{4,0},{1,5},{5,1},{2,6},{6,2},{3,7},{7,3},{8,12},{12,8},{9,1... | collective-permute-start | bytes 786440 | tf_op jit(solution)/shard_map/ppermute | solution.py:23
  170.0 34.4 %collective-permute-start.15 = (bf16[128,1024]{1,0:T(8,128)(2,1)S(1)}, bf16[128,1024]{1,0:T(8,128)(2,1)S(1)}, u32[]{:S(2)}, u32[]{:S(2)}) collective-permute-start(bf16[128,1024]{1,0:T(8,128)(2,1)S(1)} %copy-done.3), channel_id=1, source_target_pairs={{0,8},{8,16},{16,24},{1,9},{9,17},{17,25},{2,10},{10,18},{18,26},{... | collective-permute-start | bytes 786440 | tf_op jit(solution)/shard_map/ppermute | solution.py:19
  303.3 37.1 %collective-permute-start.54 = (bf16[128,1024]{1,0:T(8,128)(2,1)S(1)}, bf16[128,1024]{1,0:T(8,128)(2,1)S(1)}, u32[]{:S(2)}, u32[]{:S(2)}) collective-permute-start(bf16[128,1024]{1,0:T(8,128)(2,1)S(1)} %select_select_fusion.1), channel_id=1, source_target_pairs={{0,4},{4,0},{1,5},{5,1},{2,6},{6,2},{3,7},{7,3},{8,12},{12,8},{9,1... | collective-permute-start | bytes 786440 | tf_op jit(solution)/shard_map/ppermute | solution.py:23
  334.3 245.5 %reduce-scatter.2.cloned.1.call-start = ((), (), s32[]{:S(2)}) async-start(), calls=%async_computation.1 | async-start | bytes 3276800 | tf_op jit(solution)/shard_map/reduce_scatter | solution.py:701
  340.4 24.0 %collective-permute-start.55 = (bf16[128,1024]{1,0:T(8,128)(2,1)S(1)}, bf16[128,1024]{1,0:T(8,128)(2,1)S(1)}, u32[]{:S(2)}, u32[]{:S(2)}) collective-permute-start(bf16[128,1024]{1,0:T(8,128)(2,1)S(1)} %copy-done.2), channel_id=1, source_target_pairs={{24,16},{25,17},{26,18},{27,19},{28,20},{29,21},{30,22},{31,23}} | collective-permute-start | bytes 786440 | tf_op jit(solution)/shard_map/ppermute | solution.py:625
  341.2 23.9 %collective-permute-start.56 = (bf16[128,1024]{1,0:T(8,128)(2,1)S(1)}, bf16[128,1024]{1,0:T(8,128)(2,1)S(1)}, u32[]{:S(2)}, u32[]{:S(2)}) collective-permute-start(bf16[128,1024]{1,0:T(8,128)(2,1)S(1)} %copy-done.2), channel_id=1, source_target_pairs={{24,8},{25,9},{26,10},{27,11},{28,12},{29,13},{30,14},{31,15}} | collective-permute-start | bytes 786440 | tf_op jit(solution)/shard_map/ppermute | solution.py:625
  342.5 26.6 %collective-permute-start.57 = (bf16[128,1024]{1,0:T(8,128)(2,1)S(1)}, bf16[128,1024]{1,0:T(8,128)(2,1)S(1)}, u32[]{:S(2)}, u32[]{:S(2)}) collective-permute-start(bf16[128,1024]{1,0:T(8,128)(2,1)S(1)} %copy-done.2), channel_id=1, source_target_pairs={{24,0},{25,1},{26,2},{27,3},{28,4},{29,5},{30,6},{31,7}} | collective-permute-start | bytes 786440 | tf_op jit(solution)/shard_map/ppermute | solution.py:625
  394.5 107.8 %collective-permute-start.23 = (bf16[4,2,128,1024]{3,2,1,0:T(8,128)(2,1)}, bf16[4,2,128,1024]{3,2,1,0:T(8,128)(2,1)}, u32[]{:S(2)}, u32[]{:S(2)}) collective-permute-start(bf16[4,2,128,1024]{3,2,1,0:T(8,128)(2,1)} %bitcast.65), channel_id=1, source_target_pairs={{0,4},{4,0},{1,5},{5,1},{2,6},{6,2},{3,7},{7,3},{8,12},{12,8},{9,1... | collective-permute-start | bytes 6291464 | tf_op jit(solution)/shard_map/ppermute | solution.py:23
  410.8 33.4 %collective-permute-start.38 = (bf16[128,1024]{1,0:T(8,128)(2,1)S(1)}, bf16[128,1024]{1,0:T(8,128)(2,1)S(1)}, u32[]{:S(2)}, u32[]{:S(2)}) collective-permute-start(bf16[128,1024]{1,0:T(8,128)(2,1)S(1)} %get-tuple-element.103.refs_8_), channel_id=1, source_target_pairs={{0,2},{1,3},{2,0},{3,1},{4,6},{5,7},{6,4},{7,5},{8,10},{9,11},{10,... | collective-permute-start | bytes 786440 | tf_op jit(solution)/shard_map/ppermute | solution.py:584
  411.9 60.0 %collective-permute-start.39 = (bf16[128,1024]{1,0:T(8,128)(2,1)S(1)}, bf16[128,1024]{1,0:T(8,128)(2,1)S(1)}, u32[]{:S(2)}, u32[]{:S(2)}) collective-permute-start(bf16[128,1024]{1,0:T(8,128)(2,1)S(1)} %get-tuple-element.103.refs_8_), channel_id=1, source_target_pairs={{0,3},{1,0},{2,1},{3,2},{4,7},{5,4},{6,5},{7,6},{8,11},{9,8},{10,9... | collective-permute-start | bytes 786440 | tf_op jit(solution)/shard_map/ppermute | solution.py:584
  413.3 59.7 %collective-permute-start.44 = (bf16[128,1024]{1,0:T(8,128)(2,1)S(1)}, bf16[128,1024]{1,0:T(8,128)(2,1)S(1)}, u32[]{:S(2)}, u32[]{:S(2)}) collective-permute-start(bf16[128,1024]{1,0:T(8,128)(2,1)S(1)} %get-tuple-element.102.refs_8_), channel_id=1, source_target_pairs={{0,1},{1,2},{2,3},{3,0},{4,5},{5,6},{6,7},{7,4},{8,9},{9,10},{10,1... | collective-permute-start | bytes 786440 | tf_op jit(solution)/shard_map/ppermute | solution.py:584
  416.4 76.1 %collective-permute-start.45 = (bf16[128,1024]{1,0:T(8,128)(2,1)S(1)}, bf16[128,1024]{1,0:T(8,128)(2,1)S(1)}, u32[]{:S(2)}, u32[]{:S(2)}) collective-permute-start(bf16[128,1024]{1,0:T(8,128)(2,1)S(1)} %get-tuple-element.102.refs_8_), channel_id=1, source_target_pairs={{0,2},{1,3},{2,0},{3,1},{4,6},{5,7},{6,4},{7,5},{8,10},{9,11},{10,... | collective-permute-start | bytes 786440 | tf_op jit(solution)/shard_map/ppermute | solution.py:584
  444.2 55.8 %collective-permute-start.46 = (bf16[128,1024]{1,0:T(8,128)(2,1)S(1)}, bf16[128,1024]{1,0:T(8,128)(2,1)S(1)}, u32[]{:S(2)}, u32[]{:S(2)}) collective-permute-start(bf16[128,1024]{1,0:T(8,128)(2,1)S(1)} %get-tuple-element.102.refs_8_), channel_id=1, source_target_pairs={{0,3},{1,0},{2,1},{3,2},{4,7},{5,4},{6,5},{7,6},{8,11},{9,8},{10,9... | collective-permute-start | bytes 786440 | tf_op jit(solution)/shard_map/ppermute | solution.py:584
  471.9 29.3 %collective-permute-start.47 = (bf16[128,1024]{1,0:T(8,128)(2,1)S(1)}, bf16[128,1024]{1,0:T(8,128)(2,1)S(1)}, u32[]{:S(2)}, u32[]{:S(2)}) collective-permute-start(bf16[128,1024]{1,0:T(8,128)(2,1)S(1)} %get-tuple-element.102.refs_8_), channel_id=1, source_target_pairs={{0,4},{4,0},{1,5},{5,1},{2,6},{6,2},{3,7},{7,3},{8,12},{12,8},{9,1... | collective-permute-start | bytes 786440 | tf_op jit(solution)/shard_map/ppermute | solution.py:23
  473.0 28.4 %collective-permute-start.48 = (bf16[128,1024]{1,0:T(8,128)(2,1)S(1)}, bf16[128,1024]{1,0:T(8,128)(2,1)S(1)}, u32[]{:S(2)}, u32[]{:S(2)}) collective-permute-start(bf16[128,1024]{1,0:T(8,128)(2,1)S(1)} %collective-permute-done.44.refs_9_), channel_id=1, source_target_pairs={{0,4},{4,0},{1,5},{5,1},{2,6},{6,2},{3,7},{7,3},{8,12},{12,8},{9,1... | collective-permute-start | bytes 786440 | tf_op jit(solution)/shard_map/ppermute | solution.py:23
  501.2 38.4 %collective-permute-start.40 = (bf16[128,1024]{1,0:T(8,128)(2,1)S(1)}, bf16[128,1024]{1,0:T(8,128)(2,1)S(1)}, u32[]{:S(2)}, u32[]{:S(2)}) collective-permute-start(bf16[128,1024]{1,0:T(8,128)(2,1)S(1)} %get-tuple-element.103.refs_8_), channel_id=1, source_target_pairs={{0,4},{4,0},{1,5},{5,1},{2,6},{6,2},{3,7},{7,3},{8,12},{12,8},{9,1... | collective-permute-start | bytes 786440 | tf_op jit(solution)/shard_map/ppermute | solution.py:23
  501.4 38.3 %collective-permute-start.41 = (bf16[128,1024]{1,0:T(8,128)(2,1)S(1)}, bf16[128,1024]{1,0:T(8,128)(2,1)S(1)}, u32[]{:S(2)}, u32[]{:S(2)}) collective-permute-start(bf16[128,1024]{1,0:T(8,128)(2,1)S(1)} %collective-permute-done.37.refs_9_), channel_id=1, source_target_pairs={{0,4},{4,0},{1,5},{5,1},{2,6},{6,2},{3,7},{7,3},{8,12},{12,8},{9,1... | collective-permute-start | bytes 786440 | tf_op jit(solution)/shard_map/ppermute | solution.py:23
  501.8 37.9 %collective-permute-start.42 = (bf16[128,1024]{1,0:T(8,128)(2,1)S(1)}, bf16[128,1024]{1,0:T(8,128)(2,1)S(1)}, u32[]{:S(2)}, u32[]{:S(2)}) collective-permute-start(bf16[128,1024]{1,0:T(8,128)(2,1)S(1)} %collective-permute-done.38.refs_10_), channel_id=1, source_target_pairs={{0,4},{4,0},{1,5},{5,1},{2,6},{6,2},{3,7},{7,3},{8,12},{12,8},{9,1... | collective-permute-start | bytes 786440 | tf_op jit(solution)/shard_map/ppermute | solution.py:23
  501.9 37.8 %collective-permute-start.43 = (bf16[128,1024]{1,0:T(8,128)(2,1)S(1)}, bf16[128,1024]{1,0:T(8,128)(2,1)}, u32[]{:S(2)}, u32[]{:S(2)}) collective-permute-start(bf16[128,1024]{1,0:T(8,128)(2,1)S(1)} %collective-permute-done.39.refs_11_), channel_id=1, source_target_pairs={{0,4},{4,0},{1,5},{5,1},{2,6},{6,2},{3,7},{7,3},{8,12},{12,8},{9,1... | collective-permute-start | bytes 786440 | tf_op jit(solution)/shard_map/ppermute | solution.py:23
  (99 other events, 1156.3 us)
Sparse Core Ops, SparseCore 0:
  334.4 44.0 all-gather.2
  407.2 92.7 reduce-scatter.1

commit v4 on v3

--- a/solution.py
+++ b/solution.py
@@ -7,7 +7,8 @@
 from jax.sharding import PartitionSpec as P
 
 CHUNKS = 2
-VMEM_MIB = 60
+VMEM_MIB = 58
+SMALL_MIB = 16
 BF16 = jnp.bfloat16
 F32 = jnp.float32
 MIB = 1024 * 1024
@@ -66,6 +67,18 @@
     return max(t for t in range(128, most + 1, 128) if size % t == 0)
 
 
+def pieces_of(size):
+    return [(at, min(256, size - at)) for at in range(0, size, 256)]
+
+
+def cost(flops, bytes_accessed, transcendentals):
+    return pl.CostEstimate(
+        flops=flops // 16,
+        bytes_accessed=bytes_accessed // 16,
+        transcendentals=transcendentals // 16,
+    )
+
+
 def params(limit):
     return pltpu.CompilerParams(vmem_limit_bytes=limit * MIB)
 
@@ -126,8 +139,11 @@
         normed[...] = normalised(rows)
         total[...] = jnp.zeros_like(total)
 
-    value, _ = gelu_parts(dot(normed[...], w_in[...]))
-    total[...] += dot(value.astype(BF16), w_out[...])
+    values = []
+    for at, size in pieces_of(w_in.shape[1]):
+        value, _ = gelu_parts(dot(normed[...], w_in[:, at : at + size]))
+        values.append(value.astype(BF16))
+    total[...] += dot(jnp.concatenate(values, axis=1), w_out[...])
 
     @pl.when(step == pl.num_programs(0) - 1)
     def _():
@@ -137,7 +153,7 @@
 def forward_section(where, own, arrived, w_in, w_out):
     rows, width = own.shape
     hidden = w_in.shape[1]
-    tile = tile_of(hidden, 512)
+    tile = tile_of(hidden, 1024)
     halves = len(arrived)
     full, part = (rows, width), (rows // halves, width)
     shapes = [(full, BF16), (part, BF16), (part, F32)] + [(part, BF16)] * (halves - 1)
@@ -157,7 +173,7 @@
         ),
         out_shape=[jax.ShapeDtypeStruct(*shape) for shape in shapes],
         compiler_params=params(VMEM_MIB),
-        cost_estimate=pl.CostEstimate(
+        cost_estimate=cost(
             flops=4 * rows * width * hidden,
             bytes_accessed=4 * width * hidden,
             transcendentals=rows * hidden,
@@ -174,7 +190,7 @@
     return pl.pallas_call(
         finish_forward_kernel,
         out_shape=jax.ShapeDtypeStruct(rows.shape, BF16),
-        compiler_params=params(VMEM_MIB),
+        compiler_params=params(SMALL_MIB),
         name="finish_forward",
     )(rows, *pieces)
 
@@ -188,7 +204,7 @@
     return pl.pallas_call(
         finish_backward_kernel,
         out_shape=jax.ShapeDtypeStruct(rows.shape, BF16),
-        compiler_params=params(VMEM_MIB),
+        compiler_params=params(SMALL_MIB),
         name="finish_backward",
     )(rows, grads, *pieces)
 
@@ -219,9 +235,11 @@
         normed[...] = normalised(rows[...])
         total[...] = jnp.zeros_like(total)
 
-    _, slope = gelu_parts(dot(normed[...], w_in[...]))
-    dpre = (dot_t(grads[...], w_out[...]) * slope).astype(BF16)
-    total[...] += dot_t(dpre, w_in[...])
+    dpres = []
+    for at, size in pieces_of(w_in.shape[1]):
+        _, slope = gelu_parts(dot(normed[...], w_in[:, at : at + size]))
+        dpres.append((dot_t(grads[...], w_out[at : at + size, :]) * slope).astype(BF16))
+    total[...] += dot_t(jnp.concatenate(dpres, axis=1), w_in[...])
 
     @pl.when(step == pl.num_programs(0) - 1)
     def _():
@@ -231,7 +249,7 @@
 def backward_section(where, last, halves, options, final, parts, arrived, w_in, w_out):
     width, hidden = w_in.shape
     rows = options[0][1].shape[0]
-    tile = tile_of(hidden, 512)
+    tile = tile_of(hidden, 1024)
     full, part = (rows, width), (rows // halves, width)
     operands = [option for _, option in options]
     specs = [whole_spec(full)] * len(options)
@@ -265,7 +283,7 @@
         ),
         out_shape=[jax.ShapeDtypeStruct(*shape) for shape in shapes],
         compiler_params=params(VMEM_MIB),
-        cost_estimate=pl.CostEstimate(
+        cost_estimate=cost(
             flops=6 * rows * width * hidden,
             bytes_accessed=4 * width * hidden,
             transcendentals=rows * hidden,
@@ -282,88 +300,110 @@
     return filled
 
 
-def shard_specs(count, width, tile, tiles):
+def shard_specs(count, shape, tiles, lead=()):
     def index(shard, i, t):
         before, after = i < shard, i > shard
-        return (0, jnp.where(before, 0, jnp.where(after, tiles - 1, t)))
-
-    return [
-        pl.BlockSpec((width, tile), lambda i, t, s, k=k: index(k, i, t)) for k in range(count)
-    ]
-
-
-def logits_kernel(halves, where, *refs):
+        return (*lead, 0, jnp.where(before, 0, jnp.where(after, tiles - 1, t)))
+
+    block = (None,) * len(lead) + shape
+    return [pl.BlockSpec(block, lambda i, t, s, k=k: index(k, i, t)) for k in range(count)]
+
+
+def logits_kernel(halves, count, where, *refs):
     final, refs = refs[:halves], refs[halves:]
-    *shards, counts, logits, stats, normed, peak, total, target = refs
+    shards, refs = refs[:count], refs[count:]
+    counts, refs = refs[:count], refs[count:]
+    logits, stats, normed, peak, total, target = refs
     shard, step = pl.program_id(0), pl.program_id(1)
     is_first = (shard == 0) & (step == 0)
     is_end = (shard == pl.num_programs(0) - 1) & (step == pl.num_programs(1) - 1)
+    lanes = peak.shape[1]
 
     @pl.when(is_first)
     def _():
         normed[...] = normalised(gathered(final, where[1]))
-        peak[...] = jnp.full_like(peak, -jnp.inf)
+        peak[...] = jnp.full_like(peak, -1e30)
         total[...] = jnp.zeros_like(total)
         target[...] = jnp.zeros_like(target)
 
-    for at, w_part in enumerate(shards):
+    for at in range(count):
 
         @pl.when(shard == at)
-        def _(w_part=w_part):
-            values = dot(normed[...], w_part[...])
-            logits[...] = values
-            higher = jnp.maximum(peak[...], jnp.max(values, axis=-1, keepdims=True))
-            total[...] = total[...] * jnp.exp(peak[...] - higher) + jnp.sum(
-                jnp.exp(values - higher), axis=-1, keepdims=True
-            )
+        def _(w_part=shards[at], hits=counts[at]):
+            columns = []
+            for start, size in pieces_of(w_part.shape[1]):
+                values = dot(normed[...], w_part[:, start : start + size])
+                logits[:, start : start + size] = values
+                counted = hits[:, start : start + size].astype(F32) * values
+                columns += [
+                    (values[:, c : c + lanes], counted[:, c : c + lanes])
+                    for c in range(0, size, lanes)
+                ]
+            higher = peak[...]
+            for values, _ in columns:
+                higher = jnp.maximum(higher, values)
+            mass = total[...] * jnp.exp(peak[...] - higher)
+            summed = target[...]
+            for values, counted in columns:
+                mass = mass + jnp.exp(values - higher)
+                summed = summed + counted
             peak[...] = higher
-            target[...] += jnp.sum(counts[...].astype(F32) * values, axis=-1, keepdims=True)
+            total[...] = mass
+            target[...] = summed
 
     @pl.when(is_end)
     def _():
-        stats[...] = lane_fill([peak[...], total[...], target[...]], stats.shape)
+        top = jnp.max(peak[...], axis=-1, keepdims=True)
+        mass = jnp.sum(total[...] * jnp.exp(peak[...] - top), axis=-1, keepdims=True)
+        summed = jnp.sum(target[...], axis=-1, keepdims=True)
+        stats[...] = lane_fill([top, mass, summed], stats.shape)
 
 
 def head_logits(where, final, shards, counts, at):
     halves = len(final)
+    count = len(shards)
     half, width = final[0].shape
     rows = half * halves
     vocab = shards[0].shape[1]
+    lanes = 128 if vocab % 128 == 0 else vocab
     tile = tile_of(vocab, 640)
     tiles = vocab // tile
     return pl.pallas_call(
-        functools.partial(logits_kernel, halves),
+        functools.partial(logits_kernel, halves, count),
         grid_spec=pltpu.PrefetchScalarGridSpec(
             num_scalar_prefetch=1,
-            grid=(len(shards), tiles),
+            grid=(count, tiles),
             in_specs=[
                 *[whole_spec((half, width))] * halves,
-                *shard_specs(len(shards), width, tile, tiles),
-                pl.BlockSpec((None, None, rows, tile), lambda i, t, s: (i, at, 0, t)),
+                *shard_specs(count, (width, tile), tiles),
+                *shard_specs(count, (rows, tile), tiles, (at,)),
             ],
             out_specs=[
                 pl.BlockSpec((None, rows, tile), lambda i, t, s: (i, 0, t)),
                 whole_spec((rows, 128)),
             ],
-            scratch_shapes=[pltpu.VMEM((rows, width), BF16)] + [pltpu.VMEM((rows, 1), F32)] * 3,
+            scratch_shapes=[pltpu.VMEM((rows, width), BF16)] + [pltpu.VMEM((rows, lanes), F32)] * 3,
         ),
         out_shape=[
-            jax.ShapeDtypeStruct((len(shards), rows, vocab), F32),
+            jax.ShapeDtypeStruct((count, rows, vocab), F32),
             jax.ShapeDtypeStruct((rows, 128), F32),
         ],
         compiler_params=params(VMEM_MIB),
-        cost_estimate=pl.CostEstimate(
-            flops=2 * rows * width * vocab * len(shards),
-            bytes_accessed=(2 * width + 6 * rows) * vocab * len(shards),
-            transcendentals=rows * vocab * len(shards),
+        cost_estimate=cost(
+            flops=2 * rows * width * vocab * count,
+            bytes_accessed=(2 * width + 6 * rows) * vocab * count,
+            transcendentals=rows * vocab * count,
         ),
         name="head_logits",
-    )(where, *final, *shards, counts)
-
-
-def head_grads_kernel(tables, denom, where, *refs):
+    )(where, *final, *shards, *counts)
+
+
+def head_grads_kernel(tables, count, denom, where, *refs):
     stats, refs = refs[:tables], refs[tables:]
-    lengths, logits, counts, *shards, part, results, lse, total = refs
+    lengths, logits, refs = refs[0], refs[1], refs[2:]
+    shards, refs = refs[:count], refs[count:]
+    counts, refs = refs[:count], refs[count:]
+    part, results, shift, total = refs
     shard, step = pl.program_id(0), pl.program_id(1)
     is_first = (shard == 0) & (step == 0)
     is_end = (shard == pl.num_programs(0) - 1) & (step == pl.num_programs(1) - 1)
@@ -376,17 +416,21 @@
             top = jnp.maximum(top, table[:, 0:1])
         mass = sum(table[:, 1:2] * jnp.exp(table[:, 0:1] - top) for table in values)
         target = sum(table[:, 2:3] for table in values)
-        lse[...] = top + jnp.log(mass)
-        results[...] = lane_fill([lse[...], lengths[...] * lse[...] - target], results.shape)
+        lse = top + jnp.log(mass)
+        shift[...] = lse - jnp.log(lengths[...] * (1.0 / denom))
+        results[...] = lane_fill([shift[...], lengths[...] * lse - target], results.shape)
         total[...] = jnp.zeros_like(total)
 
-    for at, w_part in enumerate(shards):
+    for at in range(count):
 
         @pl.when(shard == at)
-        def _(w_part=w_part):
-            exped = lengths[...] * jnp.exp(logits[...] - lse[...])
-            dlogits = ((exped - counts[...].astype(F32)) / denom).astype(BF16)
-            total[...] += dot_t(dlogits, w_part[...])
+        def _(w_part=shards[at], hits=counts[at]):
+            columns = []
+            for start, size in pieces_of(w_part.shape[1]):
+                exped = jnp.exp(logits[:, start : start + size] - shift[...])
+                counted = hits[:, start : start + size].astype(F32) * (1.0 / denom)
+                columns.append((exped - counted).astype(BF16))
+            total[...] += dot_t(jnp.concatenate(columns, axis=1), w_part[...])
 
     @pl.when(is_end)
     def _():
@@ -399,7 +443,7 @@
     tile = tile_of(vocab, 640)
     tiles = vocab // tile
     return pl.pallas_call(
-        functools.partial(head_grads_kernel, len(stats), denom),
+        functools.partial(head_grads_kernel, len(stats), count, denom),
         grid_spec=pltpu.PrefetchScalarGridSpec(
             num_scalar_prefetch=1,
             grid=(count, tiles),
@@ -407,8 +451,8 @@
             + [
                 pl.BlockSpec((None, rows, 1), lambda i, t, s: (at, 0, 0)),
                 pl.BlockSpec((None, rows, tile), lambda i, t, s: (i, 0, t)),
-                pl.BlockSpec((None, None, rows, tile), lambda i, t, s: (i, at, 0, t)),
-                *shard_specs(count, width, tile, tiles),
+                *shard_specs(count, (width, tile), tiles),
+                *shard_specs(count, (rows, tile), tiles, (at,)),
             ],
             out_specs=[whole_spec((rows, width)), whole_spec((rows, 128))],
             scratch_shapes=[pltpu.VMEM((rows, 1), F32), pltpu.VMEM((rows, width), F32)],
@@ -418,13 +462,75 @@
             jax.ShapeDtypeStruct((rows, 128), F32),
         ],
         compiler_params=params(VMEM_MIB),
-        cost_estimate=pl.CostEstimate(
+        cost_estimate=cost(
             flops=2 * rows * width * vocab * count,
             bytes_accessed=(2 * width + 6 * rows) * vocab * count,
             transcendentals=rows * vocab * count,
         ),
         name="head_grads",
-    )(where, *stats, lengths, logits, counts, *shards)
+    )(where, *stats, lengths, logits, *shards, *counts)
+
+
+def unit_kernel(blocks, tables, share, denom, where, *refs):
+    x_refs, refs = refs[: len(blocks)], refs[len(blocks) :]
+    shifts, refs = refs[:tables], refs[tables:]
+    counts, refs = refs[:tables], refs[tables:]
+    w_unit, grad, normed, normed_t = refs
+    half = x_refs[0].shape[0]
+    rows = normed.shape[0] // tables
+
+    @pl.when(pl.program_id(0) == 0)
+    def _():
+        for ref, (base, theirs) in zip(x_refs, blocks):
+            side = 0
+            if theirs is not None:
+                side = 1 - where[1] if theirs else where[1]
+            place = pl.ds(pl.multiple_of(base + side * half, half), half)
+            normed[place, :] = normalised(ref[...])
+        columns = pl.ds(pl.multiple_of(where[0] * share, share), share)
+        normed_t[...] = normed[:, columns].astype(F32).T.astype(BF16)
+
+    total = None
+    for k in range(tables):
+        place = pl.ds(k * rows, rows)
+        exped = jnp.exp(dot(normed[place, :], w_unit[...]) - shifts[k][...])
+        dlogits = (exped - counts[k][...].astype(F32) * (1.0 / denom)).astype(BF16)
+        now = dot(normed_t[:, place], dlogits)
+        total = now if total is None else total + now
+    grad[...] = total
+
+
+def unit_grads(where, x_parts, shifts, counts, w_unit, denom, share):
+    width, vocab = w_unit.shape
+    tile = tile_of(vocab, 256)
+    half = x_parts[0][0].shape[2]
+    rows = shifts[0].shape[0]
+    tables = len(shifts)
+    blocks = tuple(block for _, _, block in x_parts)
+    return pl.pallas_call(
+        functools.partial(unit_kernel, blocks, tables, share, denom),
+        grid_spec=pltpu.PrefetchScalarGridSpec(
+            num_scalar_prefetch=1,
+            grid=(vocab // tile,),
+            in_specs=[pl.BlockSpec((None, None, half, width), index) for _, index, _ in x_parts]
+            + [whole_spec((rows, 1))] * tables
+            + [pl.BlockSpec((rows, tile), lambda j, s: (0, j))] * tables
+            + [pl.BlockSpec((width, tile), lambda j, s: (0, j))],
+            out_specs=pl.BlockSpec((share, tile), lambda j, s: (0, j)),
+            scratch_shapes=[
+                pltpu.VMEM((rows * tables, width), BF16),
+                pltpu.VMEM((share, rows * tables), BF16),
+            ],
+        ),
+        out_shape=jax.ShapeDtypeStruct((share, vocab), F32),
+        compiler_params=params(VMEM_MIB),
+        cost_estimate=cost(
+            flops=2 * rows * tables * (width + share) * vocab,
+            bytes_accessed=2 * (width + rows * tables) * vocab,
+            transcendentals=rows * tables * vocab,
+        ),
+        name="unit_grads",
+    )(where, *[x for x, _, _ in x_parts], *shifts, *counts, w_unit)
 
 
 def weight_kernel(blocks, adding, share, where, *refs):
@@ -467,12 +573,10 @@
     width, hidden = w_in.shape
     tile = tile_of(hidden, 512)
     blocks = len(g_parts)
-    count = g_parts[0].shape[0]
+    count = g_parts[0][0].shape[1]
     rows = blocks * count
-    in_specs = [
-        pl.BlockSpec((None, None, count, width), index) for _, index in x_parts
-    ]
-    in_specs += [pl.BlockSpec((count, width), lambda j, s: (0, 0))] * blocks
+    in_specs = [pl.BlockSpec((None, None, count, width), index) for _, index in x_parts]
+    in_specs += [pl.BlockSpec((None, count, width), index) for _, index in g_parts]
     in_specs += [
         pl.BlockSpec((width, tile), lambda j, s: (0, j)),
         pl.BlockSpec((tile, width), lambda j, s: (j, 0)),
@@ -506,13 +610,13 @@
         ],
         input_output_aliases=aliases,
         compiler_params=params(VMEM_MIB),
-        cost_estimate=pl.CostEstimate(
+        cost_estimate=cost(
             flops=4 * rows * (width + share) * hidden,
             bytes_accessed=4 * width * hidden + 16 * share * hidden,
             transcendentals=rows * hidden,
         ),
         name="weight_grads",
-    )(where, *[x for x, _ in x_parts], *g_parts, w_in, w_out, *(old or ()))
+    )(where, *[x for x, _ in x_parts], *[g for g, _ in g_parts], w_in, w_out, *(old or ()))
 
 
 def unit_counts(ends, targets, ids):
@@ -552,14 +656,27 @@
 
     shards = [w_unit] + [lax.ppermute(w_unit, "segment", [(j, last)]) for j in range(last)]
     part_ids = jnp.arange(vocab_part, dtype=jnp.int32)
-    head_counts = jnp.stack(
-        [
-            unit_counts(ends, unit_targets, (j * mp_size + mp_at) * vocab_part + part_ids)
-            for j in [last, *range(last)]
-        ]
-    ).reshape(segments, chunks, rows, vocab_part)
+    head_counts = [
+        unit_counts(ends, unit_targets, (j * mp_size + mp_at) * vocab_part + part_ids).reshape(
+            chunks, rows, vocab_part
+        )
+        for j in [last, *range(last)]
+    ]
     own_ids = (seg * mp_size + mp_at) * vocab_part + part_ids
-    own_counts = unit_counts(ends, unit_targets, own_ids).reshape(micro * row_count, vocab_part)
+
+    def around(block):
+        came = [block]
+        for distance in range(1, dp_size):
+            route = [(i, (i + distance) % dp_size) for i in range(dp_size)]
+            came.append(lax.ppermute(block, "dp", route))
+        return came
+
+    own_counts = [
+        unit_counts(packed[:, unit_count:], packed[:, :unit_count], own_ids).reshape(
+            micro * row_count, vocab_part
+        )
+        for packed in around(jnp.concatenate([unit_targets, ends], axis=1))
+    ]
 
     def both(part):
         return [part, swapped(part)] if pair else [part]
@@ -575,29 +692,25 @@
             return [stats, swapped(stats)]
         return [t for t in lax.all_gather(stats, "mp")]
 
-    def gather_grads(mine, theirs):
-        if not pair:
-            return [t for t in lax.all_gather(mine, "dp")]
-        own, other = [mine], [theirs]
-        for distance in range(1, dp_size):
-            route = [(i, (i + distance) % dp_size) for i in range(dp_size)]
-            came = lax.ppermute(mine, "dp", route)
-            own.append(came)
-            other.append(swapped(came))
-        return own + other
+    def gathered_rows(mine):
+        came = lax.all_gather(mine, "dp")
+        return [came, swapped(came)] if pair else [came]
 
     stash, x_halves, grads, finals, results, sent = [], [], [], [], [], []
     sums = None
-    x_mine = x_theirs = None
+    x_gathered = None
     f_hop = b_hop = None
 
     def x_parts(at):
-        if not pair:
-            return [(x_mine, lambda j, s, k=k: (k, at, 0, 0)) for k in range(dp_size)]
         return [
-            (source, lambda j, s, k=k: (lax.rem(s[0] + dp_size - k, dp_size), at, 0, 0))
-            for source in (x_mine, x_theirs)
+            (source, lambda j, s, k=k: (k, at, 0, 0))
+            for source in x_gathered
             for k in range(dp_size)
+        ]
+
+    def g_parts(sources):
+        return [
+            (source, lambda j, s, k=k: (k, 0, 0)) for source in sources for k in range(dp_size)
         ]
 
     clocks = 2 * segments + chunks - 1
@@ -615,6 +728,18 @@
         if clock >= segments:
             at = clock - segments
             arrived = None if at == 0 else both(shifted(b_hop, "segment", -1))
+            if clock == segments + chunks:
+                unit_rows = gathered_rows(
+                    jnp.stack(
+                        [
+                            chosen(
+                                seg,
+                                [(last, finals[b][0])] + [(to, sent[b][to]) for to in range(last)],
+                            )
+                            for b in range(chunks)
+                        ]
+                    )
+                )
             if clock < clocks - 1:
                 parts = []
                 final = None
@@ -657,16 +782,14 @@
                     for b in range(chunks)
                 ]
             )
-            x_mine = lax.all_gather(x_half, "dp")
-            x_theirs = swapped(x_mine) if pair else None
+            x_gathered = gathered_rows(x_half)
         if clock >= 2 * segments - 1:
             at = clock - 2 * segments + 1
             mine = chosen(seg, [(s, grads[at + last - s]) for s in range(segments)])
-            theirs = swapped(mine) if pair else None
             sums = weight_grads(
                 dp_at[None],
                 x_parts(at),
-                gather_grads(mine, theirs),
+                g_parts(gathered_rows(mine)),
                 first,
                 second,
                 sums,
@@ -681,24 +804,20 @@
         + [(to, lax.ppermute(results, "segment", [(last, to)])) for to in range(last)],
     )
     loss = (jnp.sum(results[:, :, 1]) / denom)[None]
-    final_rows = []
-    for b in range(chunks):
-        mine = chosen(seg, [(last, finals[b][0])] + [(to, sent[b][to]) for to in range(last)])
-        pieces = both(mine)
-        if pair:
-            pieces = [
-                jnp.where(mp_at == 0, pieces[0], pieces[1]),
-                jnp.where(mp_at == 0, pieces[1], pieces[0]),
-            ]
-        final_rows += pieces
-    final_norm = normalised(jnp.concatenate(final_rows))
-    own_logits = dot(final_norm, w_unit)
-    own_exp = jnp.exp(own_logits - results[:, :, 0].reshape(-1, 1))
-    own_dlogits = (
-        (length_f.reshape(-1, 1) * own_exp - own_counts.astype(F32)) / denom
-    ).astype(BF16)
-    grad_unit = t_dot(final_norm, own_dlogits).astype(BF16)
-    sum_unit = lax.psum_scatter(grad_unit, "dp", scatter_dimension=0, tiled=True).astype(F32)
+    shifts = around(results[:, :, 0].reshape(-1, 1))
+    unit_parts = [
+        (
+            source,
+            lambda j, s, k=k, b=b: (lax.rem(s[0] + dp_size - k, dp_size), b, 0, 0),
+            ((k * chunks + b) * rows, bool(at) if pair else None),
+        )
+        for at, source in enumerate(unit_rows)
+        for k in range(dp_size)
+        for b in range(chunks)
+    ]
+    sum_unit = unit_grads(
+        jnp.stack([dp_at, mp_at]), unit_parts, shifts, own_counts, w_unit, denom, width // dp_size
+    )
     return (loss, sums[0][None], sums[1][None], sum_unit)
 
 

time: 602 us -> 652 us (1.083)
  the two profiles are of different devices: /device:TPU:11 before, /device:TPU:0 now
where the time goes in v4:
time: 652 us; the launch traced here: 643 us
  Pallas kernels  265 us (41%)
  waiting for transfers between devices  238 us (37%)
  starting transfers between devices  57.3 us (9%)
  local copies, waits for them, and re-layouts  33.4 us (5%)
  matrix products  25.4 us (4%)
  between operations  16.7 us (3%)
    pallas_call x2, Pallas kernels, weight_grads(): pl.pallas_call(functools.partial(weight_kernel, blocks, adding, share), g...  76.1 us
    ppermute x6, waiting for transfers between devices, on_device(): lax.ppermute(f_hop, 'segment', [(last, to)])  69.2 us
    ppermute x8, waiting for transfers between devices, shifted(): return lax.ppermute(block, axis, route)  59.7 us
    pallas_call x5, Pallas kernels, forward_section(): pl.pallas_call(functools.partial(forward_kernel, halves), grid_spec=pltpu...  58.5 us
    pallas_call x4, Pallas kernels, backward_section(): pl.pallas_call(body, grid_spec=pltpu.PrefetchScalarGridSpec(num_scalar_pr...  54.5 us
    all_gather x4, waiting for transfers between devices, gathered_rows(): came = lax.all_gather(mine, 'dp')  41.7 us
    pallas_call x2, Pallas kernels, head_grads(): pl.pallas_call(functools.partial(head_grads_kernel, len(stats), count, de...  28.5 us
    unnamed x126, local copies, waits for them, and re-layouts  28.3 us
  transfers between devices with their start and end apart: 56, of which 30 were waited for; matrix products, arithmetic and copies ran while one was open for 5% of the time, Pallas kernels for 28%

profile of v4, /device:TPU:0, one launch (start us, length us, event | category | flops | bytes accessed | tf_op | source)
XLA Modules:
  0.0 643.1 jit_solution(6757327724183629649)
XLA Ops:
  11.7 12.5 %section_forward.5 = (bf16[256,1024]{1,0:T(8,128)(2,1)}, bf16[128,1024]{1,0:T(8,128)(2,1)}, f32[128,1024]{1,0:T(8,128)}, bf16[128,1024]{1,0:T(8,128)(2,1)}) custom-call(s32[2]{0:T(128)} %pad_add_fusion.1.where, bf16[256,1024]{1,0:T(8,128)(2,1)} %bitcast.110, bf16[128,1024]{1,0:T(8,128)(2,1)} %slice_bitcast_fusion.refs_0_.refs_1_, ...), custom_call_target="tpu_custom_call" | custom-call | flops 268435456 | bytes 1048576 | tf_op jit(solution)/shard_map/section_forward/pallas_call | solution.py:160
  41.0 11.5 %section_forward.6 = (bf16[256,1024]{1,0:T(8,128)(2,1)}, bf16[128,1024]{1,0:T(8,128)(2,1)}, f32[128,1024]{1,0:T(8,128)}, bf16[128,1024]{1,0:T(8,128)(2,1)}) custom-call(s32[2]{0:T(128)} %pad_add_fusion.1.where, bf16[256,1024]{1,0:T(8,128)(2,1)} %bitcast.104, bf16[128,1024]{1,0:T(8,128)(2,1)} %copy-done.48, bf16[128,1024]{1,0:T(8,128)(2,1)} %copy-done.53, ...), custom_call_target="tpu_custom_call" | custom-call | flops 268435456 | bytes 1048576 | tf_op jit(solution)/shard_map/section_forward/pallas_call | solution.py:160
  68.8 11.5 %section_forward.7 = (bf16[256,1024]{1,0:T(8,128)(2,1)}, bf16[128,1024]{1,0:T(8,128)(2,1)}, f32[128,1024]{1,0:T(8,128)}, bf16[128,1024]{1,0:T(8,128)(2,1)}) custom-call(s32[2]{0:T(128)} %pad_add_fusion.1.where, bf16[256,1024]{1,0:T(8,128)(2,1)} %bitcast.105, bf16[128,1024]{1,0:T(8,128)(2,1)} %copy-done.49, bf16[128,1024]{1,0:T(8,128)(2,1)} %copy-done.54, ...), custom_call_target="tpu_custom_call" | custom-call | flops 268435456 | bytes 1048576 | tf_op jit(solution)/shard_map/section_forward/pallas_call | solution.py:160
  96.8 11.5 %section_forward.8 = (bf16[256,1024]{1,0:T(8,128)(2,1)}, bf16[128,1024]{1,0:T(8,128)(2,1)}, f32[128,1024]{1,0:T(8,128)}, bf16[128,1024]{1,0:T(8,128)(2,1)}) custom-call(s32[2]{0:T(128)} %pad_add_fusion.1.where, bf16[256,1024]{1,0:T(8,128)(2,1)} %bitcast.106, bf16[128,1024]{1,0:T(8,128)(2,1)} %copy-done.50, bf16[128,1024]{1,0:T(8,128)(2,1)} %copy-done.55, ...), custom_call_target="tpu_custom_call" | custom-call | flops 268435456 | bytes 1048576 | tf_op jit(solution)/shard_map/section_forward/pallas_call | solution.py:160
  135.8 11.5 %section_forward.9 = (bf16[256,1024]{1,0:T(8,128)(2,1)}, bf16[128,1024]{1,0:T(8,128)(2,1)}, f32[128,1024]{1,0:T(8,128)}, bf16[128,1024]{1,0:T(8,128)(2,1)}) custom-call(s32[2]{0:T(128)} %pad_add_fusion.1.where, bf16[256,1024]{1,0:T(8,128)(2,1)} %bitcast.107, bf16[128,1024]{1,0:T(8,128)(2,1)} %copy-done.42, bf16[128,1024]{1,0:T(8,128)(2,1)} %copy-done.43, ...), custom_call_target="tpu_custom_call" | custom-call | flops 268435456 | bytes 1048576 | tf_op jit(solution)/shard_map/section_forward/pallas_call | solution.py:160
  162.2 23.8 %collective-permute-done.11.refs_3_.refs_5_ = bf16[1024,1280]{1,0:T(8,128)(2,1)} collective-permute-done((bf16[1024,1280]{1,0:T(8,128)(2,1)S(1)}, bf16[1024,1280]{1,0:T(8,128)(2,1)}, u32[]{:S(2)}, u32[]{:S(2)}) %collective-permute-start.11) | collective-permute-done | bytes 2621472 | tf_op jit(solution)/shard_map/ppermute | solution.py:657
  186.8 13.5 %head_logits.2 = (f32[4,256,1280]{2,1,0:T(8,128)}, f32[256,128]{1,0:T(8,128)}) custom-call(s32[2]{0:T(128)} %pad_add_fusion.1.where, bf16[128,1024]{1,0:T(8,128)(2,1)} %copy-done, bf16[128,1024]{1,0:T(8,128)(2,1)} %copy-done.36, bf16[1024,1280]{1,0:T(8,128)(2,1)} %refs_24_.1, bf16[1024,1280]{1,0:T(8,128)(2,1)} %collective-permute-done.11.refs_3_.refs_5_, ...), custom_call_target="tpu_custom_call" | custom-call | flops 167772160 | bytes 1146880 | tf_op jit(solution)/shard_map/head_logits/pallas_call | solution.py:371
  202.5 14.2 %head_grads.2 = (bf16[256,1024]{1,0:T(8,128)(2,1)}, f32[256,128]{1,0:T(8,128)}) custom-call(s32[2]{0:T(128)} %pad_add_fusion.1.where, f32[256,128]{1,0:T(8,128)} %get-tuple-element.64.refs_0_, f32[256,128]{1,0:T(8,128)} %copy-done.57, f32[2,256,1]{2,1,0:T(8,128)} %convert_element_type.83.refs_2_, f32[4,256,1280]{2,1,0:T(8,128)} %get-tuple-element.65.refs_3_, ...), custom_call_target="tpu_custom_call" | custom-call | flops 167772160 | bytes 1146880 | tf_op jit(solution)/shard_map/head_grads/pallas_call | solution.py:445
  221.7 69.2 %collective-permute-done.41 = bf16[128,1024]{1,0:T(8,128)(2,1)S(1)} collective-permute-done((bf16[128,1024]{1,0:T(8,128)(2,1)S(1)}, bf16[128,1024]{1,0:T(8,128)(2,1)S(1)}, u32[]{:S(2)}, u32[]{:S(2)}) %collective-permute-start.41) | collective-permute-done | bytes 262176 | tf_op jit(solution)/shard_map/ppermute | solution.py:750
  293.5 13.9 %section_backward.4 = (bf16[128,1024]{1,0:T(8,128)(2,1)}, bf16[128,1024]{1,0:T(8,128)(2,1)}, f32[128,1024]{1,0:T(8,128)}, bf16[128,1024]{1,0:T(8,128)(2,1)}) custom-call(s32[2]{0:T(128)} %pad_add_fusion.1.where, bf16[256,1024]{1,0:T(8,128)(2,1)} %get-tuple-element.77.refs_0_, bf16[256,1024]{1,0:T(8,128)(2,1)} %get-tuple-element.78.refs_1_, ...), custom_call_target="tpu_custom_call" | custom-call | flops 402653184 | bytes 1048576 | tf_op jit(solution)/shard_map/section_backward/pallas_call | solution.py:271
  308.2 13.5 %head_logits.3 = (f32[4,256,1280]{2,1,0:T(8,128)}, f32[256,128]{1,0:T(8,128)}) custom-call(s32[2]{0:T(128)} %pad_add_fusion.1.where, bf16[128,1024]{1,0:T(8,128)(2,1)} %copy-done.2, bf16[128,1024]{1,0:T(8,128)(2,1)} %copy-done.35, bf16[1024,1280]{1,0:T(8,128)(2,1)} %refs_24_.1, bf16[1024,1280]{1,0:T(8,128)(2,1)} %collective-permute-done.11.refs_3_.refs_5_, ...), custom_call_target="tpu_custom_call" | custom-call | flops 167772160 | bytes 1146880 | tf_op jit(solution)/shard_map/head_logits/pallas_call | solution.py:371
  324.1 14.3 %head_grads.3 = (bf16[256,1024]{1,0:T(8,128)(2,1)}, f32[256,128]{1,0:T(8,128)}) custom-call(s32[2]{0:T(128)} %pad_add_fusion.1.where, f32[256,128]{1,0:T(8,128)} %get-tuple-element.70.refs_0_, f32[256,128]{1,0:T(8,128)} %copy-done.56, f32[2,256,1]{2,1,0:T(8,128)} %convert_element_type.83.refs_2_, f32[4,256,1280]{2,1,0:T(8,128)} %get-tuple-element.71.refs_3_, ...), custom_call_target="tpu_custom_call" | custom-call | flops 167772160 | bytes 1146880 | tf_op jit(solution)/shard_map/head_grads/pallas_call | solution.py:445
  351.6 14.3 %section_backward.5 = (bf16[128,1024]{1,0:T(8,128)(2,1)}, bf16[128,1024]{1,0:T(8,128)(2,1)}, f32[128,1024]{1,0:T(8,128)}, bf16[128,1024]{1,0:T(8,128)(2,1)}) custom-call(s32[2]{0:T(128)} %pad_add_fusion.1.where, bf16[256,1024]{1,0:T(8,128)(2,1)} %get-tuple-element.73.refs_0_, bf16[256,1024]{1,0:T(8,128)(2,1)} %get-tuple-element.74.refs_1_, ...), custom_call_target="tpu_custom_call" | custom-call | flops 402653184 | bytes 1048576 | tf_op jit(solution)/shard_map/section_backward/pallas_call | solution.py:271
  372.2 8.9 %collective-permute-done.30.refs_2_ = bf16[128,1024]{1,0:T(8,128)(2,1)S(1)} collective-permute-done((bf16[128,1024]{1,0:T(8,128)(2,1)S(1)}, bf16[128,1024]{1,0:T(8,128)(2,1)S(1)}, u32[]{:S(2)}, u32[]{:S(2)}) %collective-permute-start.30) | collective-permute-done | bytes 262176 | tf_op jit(solution)/shard_map/ppermute | solution.py:20
  383.3 13.1 %section_backward.6 = (bf16[128,1024]{1,0:T(8,128)(2,1)}, bf16[128,1024]{1,0:T(8,128)(2,1)}, f32[128,1024]{1,0:T(8,128)}, bf16[128,1024]{1,0:T(8,128)(2,1)}) custom-call(s32[2]{0:T(128)} %pad_add_fusion.1.where, bf16[256,1024]{1,0:T(8,128)(2,1)} %get-tuple-element.77.refs_0_, bf16[256,1024]{1,0:T(8,128)(2,1)} %get-tuple-element.78.refs_1_, ...), custom_call_target="tpu_custom_call" | custom-call | flops 402653184 | bytes 1048576 | tf_op jit(solution)/shard_map/section_backward/pallas_call | solution.py:271
  402.8 8.9 %collective-permute-done.33.refs_3_ = bf16[128,1024]{1,0:T(8,128)(2,1)S(1)} collective-permute-done((bf16[128,1024]{1,0:T(8,128)(2,1)S(1)}, bf16[128,1024]{1,0:T(8,128)(2,1)S(1)}, u32[]{:S(2)}, u32[]{:S(2)}) %collective-permute-start.33) | collective-permute-done | bytes 262176 | tf_op jit(solution)/shard_map/ppermute | solution.py:20
  414.0 13.2 %section_backward.7 = (bf16[128,1024]{1,0:T(8,128)(2,1)}, bf16[128,1024]{1,0:T(8,128)(2,1)}, f32[128,1024]{1,0:T(8,128)}, bf16[128,1024]{1,0:T(8,128)(2,1)}) custom-call(s32[2]{0:T(128)} %pad_add_fusion.1.where, bf16[256,1024]{1,0:T(8,128)(2,1)} %get-tuple-element.73.refs_0_, bf16[256,1024]{1,0:T(8,128)(2,1)} %get-tuple-element.74.refs_1_, ...), custom_call_target="tpu_custom_call" | custom-call | flops 402653184 | bytes 1048576 | tf_op jit(solution)/shard_map/section_backward/pallas_call | solution.py:271
  433.5 9.7 %collective-permute-done.36 = bf16[128,1024]{1,0:T(8,128)(2,1)S(1)} collective-permute-done((bf16[128,1024]{1,0:T(8,128)(2,1)S(1)}, bf16[128,1024]{1,0:T(8,128)(2,1)S(1)}, u32[]{:S(2)}, u32[]{:S(2)}) %collective-permute-start.36) | collective-permute-done | bytes 262176 | tf_op jit(solution)/shard_map/ppermute | solution.py:20
  461.6 12.2 %all-gather.11.cloned.1.call-done = bf16[512,1024]{1,0:T(8,128)(2,1)} async-done(((bf16[128,1024]{1,0:T(8,128)(2,1)}), bf16[512,1024]{1,0:T(8,128)(2,1)}) %all-gather.11.cloned.1.call-update) | async-done | bytes 1048592 | tf_op jit(solution)/shard_map/all_gather | solution.py:696
  473.8 29.5 %all-gather.13.cloned.1.call-done = bf16[512,1024]{1,0:T(8,128)(2,1)} async-done(((bf16[128,1024]{1,0:T(8,128)(2,1)}), bf16[512,1024]{1,0:T(8,128)(2,1)}) %all-gather.13.cloned.1.call-update) | async-done | bytes 1048592 | tf_op jit(solution)/shard_map/all_gather | solution.py:696
  515.1 13.1 %collective-permute-done.47.refs_18_ = f32[512,1]{1,0:T(8,128)S(1)} collective-permute-done((f32[512,1]{1,0:T(8,128)S(1)}, f32[512,1]{1,0:T(8,128)S(1)}, u32[]{:S(2)}, u32[]{:S(2)}) %collective-permute-start.47) | collective-permute-done | bytes 2080 | tf_op jit(solution)/shard_map/ppermute | solution.py:671
  537.2 19.4 %unit_grads.1 = f32[256,1280]{1,0:T(8,128)} custom-call(s32[2]{0:T(128)} %pad_add_fusion.2.where, bf16[4,2,128,1024]{3,2,1,0:T(8,128)(2,1)} %bitcast.70, bf16[4,2,128,1024]{3,2,1,0:T(8,128)(2,1)} %bitcast.71, bf16[4,2,128,1024]{3,2,1,0:T(8,128)(2,1)} %bitcast.72, bf16[4,2,128,1024]{3,2,1,0:T(8,128)(2,1)} %bitcast.73, bf16[4,2,128,1024]{3,2,1,0:T(8,128)(2,1)} %bitcast.74, ...), custom_call_target="tpu_custom_call" | custom-call | flops 419430400 | bytes 491520 | tf_op jit(solution)/shard_map/unit_grads/pallas_call | solution.py:510
  557.9 36.4 %weight_grads.2 = (f32[256,4096]{1,0:T(8,128)}, f32[4096,256]{1,0:T(8,128)}) custom-call(s32[1]{0:T(128)} %bitcast.15.where, bf16[4,2,128,1024]{3,2,1,0:T(8,128)(2,1)} %bitcast.61, bf16[4,2,128,1024]{3,2,1,0:T(8,128)(2,1)} %bitcast.62, bf16[4,2,128,1024]{3,2,1,0:T(8,128)(2,1)} %bitcast.63, bf16[4,2,128,1024]{3,2,1,0:T(8,128)(2,1)} %bitcast.64, ...), custom_call_target="tpu_custom_call" | custom-call | flops 1342177280 | bytes 2097152 | tf_op jit(solution)/shard_map/weight_grads/pallas_call | solution.py:593
  595.3 39.7 %weight_grads.3 = (f32[256,4096]{1,0:T(8,128)}, f32[4096,256]{1,0:T(8,128)}) custom-call(s32[1]{0:T(128)} %bitcast.15.where, bf16[4,2,128,1024]{3,2,1,0:T(8,128)(2,1)} %bitcast.65, bf16[4,2,128,1024]{3,2,1,0:T(8,128)(2,1)} %bitcast.66, bf16[4,2,128,1024]{3,2,1,0:T(8,128)(2,1)} %bitcast.67, ...), custom_call_target="tpu_custom_call", output_to_operand_aliasing={{0}: (19, {}), {1}: (20, {})} | custom-call | flops 1342177280 | bytes 2097152 | tf_op jit(solution)/shard_map/weight_grads/pallas_call | solution.py:593
  (288 shorter events, 187.2 us)
Async XLA Ops:
  7.2 445.7 %all-gather.9.cloned.1.call-start = ((), (), s32[]{:S(2)}) async-start(), calls=%async_computation | async-start | bytes 2621440 | tf_op jit(solution)/shard_map/all_gather | solution.py:696
  112.1 11.1 %collective-permute-start.15 = (bf16[128,1024]{1,0:T(8,128)(2,1)S(1)}, bf16[128,1024]{1,0:T(8,128)(2,1)S(1)}, u32[]{:S(2)}, u32[]{:S(2)}) collective-permute-start(bf16[128,1024]{1,0:T(8,128)(2,1)S(1)} %finish_forward.8.refs_0_.refs_2_), channel_id=1, source_target_pairs={{0,8},{8,16},{16,24},{1,9},{9,17},{17,25},{2,10},{10,18},{18,26},{... | collective-permute-start | bytes 786440 | tf_op jit(solution)/shard_map/ppermute | solution.py:20
  123.2 11.9 %collective-permute-start.16 = (bf16[128,1024]{1,0:T(8,128)(2,1)S(1)}, bf16[128,1024]{1,0:T(8,128)(2,1)S(1)}, u32[]{:S(2)}, u32[]{:S(2)}) collective-permute-start(bf16[128,1024]{1,0:T(8,128)(2,1)S(1)} %collective-permute-done.15.refs_0_), channel_id=1, source_target_pairs={{0,4},{4,0},{1,5},{5,1},{2,6},{6,2},{3,7},{7,3},{8,12},{12,8},{9,1... | collective-permute-start | bytes 786440 | tf_op jit(solution)/shard_map/ppermute | solution.py:24
  123.2 62.9 %collective-permute-start.11 = (bf16[1024,1280]{1,0:T(8,128)(2,1)S(1)}, bf16[1024,1280]{1,0:T(8,128)(2,1)}, u32[]{:S(2)}, u32[]{:S(2)}) collective-permute-start(bf16[1024,1280]{1,0:T(8,128)(2,1)S(1)} %copy-done.33), channel_id=1, source_target_pairs={{0,24},{1,25},{2,26},{3,27},{4,28},{5,29},{6,30},{7,31}} | collective-permute-start | bytes 7864328 | tf_op jit(solution)/shard_map/ppermute | solution.py:657
  130.8 55.3 %collective-permute-start.12 = (bf16[1024,1280]{1,0:T(8,128)(2,1)S(1)}, bf16[1024,1280]{1,0:T(8,128)(2,1)}, u32[]{:S(2)}, u32[]{:S(2)}) collective-permute-start(bf16[1024,1280]{1,0:T(8,128)(2,1)S(1)} %copy-done.33), channel_id=1, source_target_pairs={{8,24},{9,25},{10,26},{11,27},{12,28},{13,29},{14,30},{15,31}} | collective-permute-start | bytes 7864328 | tf_op jit(solution)/shard_map/ppermute | solution.py:657
  132.9 53.1 %collective-permute-start.13 = (bf16[1024,1280]{1,0:T(8,128)(2,1)S(1)}, bf16[1024,1280]{1,0:T(8,128)(2,1)}, u32[]{:S(2)}, u32[]{:S(2)}) collective-permute-start(bf16[1024,1280]{1,0:T(8,128)(2,1)S(1)} %copy-done.33), channel_id=1, source_target_pairs={{16,24},{17,25},{18,26},{19,27},{20,28},{21,29},{22,30},{23,31}} | collective-permute-start | bytes 7864328 | tf_op jit(solution)/shard_map/ppermute | solution.py:657
  148.3 304.6 %all-gather.15.cloned.1.call-start = ((), (), s32[]{:S(2)}) async-start(), calls=%async_computation.3 | async-start | bytes 2621440 | tf_op jit(solution)/shard_map/all_gather | solution.py:696
  158.8 27.2 %collective-permute-start.10 = (bf16[128,1024]{1,0:T(8,128)(2,1)S(1)}, bf16[128,1024]{1,0:T(8,128)(2,1)S(1)}, u32[]{:S(2)}, u32[]{:S(2)}) collective-permute-start(bf16[128,1024]{1,0:T(8,128)(2,1)S(1)} %finish_forward.8.refs_0_.refs_2_), channel_id=1, source_target_pairs={{0,4},{4,0},{1,5},{5,1},{2,6},{6,2},{3,7},{7,3},{8,12},{12,8},{9,1... | collective-permute-start | bytes 786440 | tf_op jit(solution)/shard_map/ppermute | solution.py:24
  216.8 75.9 %collective-permute-start.25 = (bf16[256,1024]{1,0:T(8,128)(2,1)}, bf16[256,1024]{1,0:T(8,128)(2,1)S(1)}, u32[]{:S(2)}, u32[]{:S(2)}) collective-permute-start(bf16[256,1024]{1,0:T(8,128)(2,1)} %get-tuple-element.79.refs_4_), channel_id=1, source_target_pairs={{0,4},{4,0},{1,5},{5,1},{2,6},{6,2},{3,7},{7,3},{8,12},{12,8},{9,1... | collective-permute-start | bytes 1572872 | tf_op jit(solution)/shard_map/ppermute | solution.py:24
  218.7 72.2 %collective-permute-start.41 = (bf16[128,1024]{1,0:T(8,128)(2,1)S(1)}, bf16[128,1024]{1,0:T(8,128)(2,1)S(1)}, u32[]{:S(2)}, u32[]{:S(2)}) collective-permute-start(bf16[128,1024]{1,0:T(8,128)(2,1)S(1)} %copy-done.1), channel_id=1, source_target_pairs={{24,0},{25,1},{26,2},{27,3},{28,4},{29,5},{30,6},{31,7}} | collective-permute-start | bytes 786440 | tf_op jit(solution)/shard_map/ppermute | solution.py:750
  220.1 87.3 %collective-permute-start.18 = (bf16[128,1024]{1,0:T(8,128)(2,1)S(1)}, bf16[128,1024]{1,0:T(8,128)(2,1)S(1)}, u32[]{:S(2)}, u32[]{:S(2)}) collective-permute-start(bf16[128,1024]{1,0:T(8,128)(2,1)S(1)} %finish_forward.9.refs_0_.refs_3_), channel_id=1, source_target_pairs={{0,4},{4,0},{1,5},{5,1},{2,6},{6,2},{3,7},{7,3},{8,12},{12,8},{9,1... | collective-permute-start | bytes 786440 | tf_op jit(solution)/shard_map/ppermute | solution.py:24
  220.3 101.9 %collective-permute-start.42 = (bf16[128,1024]{1,0:T(8,128)(2,1)S(1)}, bf16[128,1024]{1,0:T(8,128)(2,1)S(1)}, u32[]{:S(2)}, u32[]{:S(2)}) collective-permute-start(bf16[128,1024]{1,0:T(8,128)(2,1)S(1)} %finish_forward.9.refs_0_.refs_3_), channel_id=1, source_target_pairs={{24,16},{25,17},{26,18},{27,19},{28,20},{29,21},{30,22},{31,23}} | collective-permute-start | bytes 786440 | tf_op jit(solution)/shard_map/ppermute | solution.py:750
  221.0 101.3 %collective-permute-start.43 = (bf16[128,1024]{1,0:T(8,128)(2,1)S(1)}, bf16[128,1024]{1,0:T(8,128)(2,1)S(1)}, u32[]{:S(2)}, u32[]{:S(2)}) collective-permute-start(bf16[128,1024]{1,0:T(8,128)(2,1)S(1)} %finish_forward.9.refs_0_.refs_3_), channel_id=1, source_target_pairs={{24,8},{25,9},{26,10},{27,11},{28,12},{29,13},{30,14},{31,15}} | collective-permute-start | bytes 786440 | tf_op jit(solution)/shard_map/ppermute | solution.py:750
  290.9 31.4 %collective-permute-start.44 = (bf16[128,1024]{1,0:T(8,128)(2,1)S(1)}, bf16[128,1024]{1,0:T(8,128)(2,1)S(1)}, u32[]{:S(2)}, u32[]{:S(2)}) collective-permute-start(bf16[128,1024]{1,0:T(8,128)(2,1)S(1)} %finish_forward.9.refs_0_.refs_3_), channel_id=1, source_target_pairs={{24,0},{25,1},{26,2},{27,3},{28,4},{29,5},{30,6},{31,7}} | collective-permute-start | bytes 786440 | tf_op jit(solution)/shard_map/ppermute | solution.py:750
  307.4 31.4 %collective-permute-start.26 = (bf16[128,1024]{1,0:T(8,128)(2,1)}, bf16[128,1024]{1,0:T(8,128)(2,1)S(1)}, u32[]{:S(2)}, u32[]{:S(2)}) collective-permute-start(bf16[128,1024]{1,0:T(8,128)(2,1)} %get-tuple-element.83), channel_id=1, source_target_pairs={{0,4},{4,0},{1,5},{5,1},{2,6},{6,2},{3,7},{7,3},{8,12},{12,8},{9,1... | collective-permute-start | bytes 786440 | tf_op jit(solution)/shard_map/ppermute | solution.py:24
  323.2 150.6 %all-gather.11.cloned.1.call-start = ((), (), s32[]{:S(2)}) async-start(), calls=%async_computation.1 | async-start | bytes 1310720 | tf_op jit(solution)/shard_map/all_gather | solution.py:696
  444.1 59.2 %all-gather.13.cloned.1.call-start = ((), (), s32[]{:S(2)}) async-start(), calls=%async_computation.2 | async-start | bytes 1310720 | tf_op jit(solution)/shard_map/all_gather | solution.py:696
  452.9 103.7 %collective-permute-start.23 = (bf16[4,2,128,1024]{3,2,1,0:T(8,128)(2,1)}, bf16[4,2,128,1024]{3,2,1,0:T(8,128)(2,1)S(1)}, u32[]{:S(2)}, u32[]{:S(2)}) collective-permute-start(bf16[4,2,128,1024]{3,2,1,0:T(8,128)(2,1)} %bitcast.60), channel_id=1, source_target_pairs={{0,4},{4,0},{1,5},{5,1},{2,6},{6,2},{3,7},{7,3},{8,12},{12,8},{9,1... | collective-permute-start | bytes 6291464 | tf_op jit(solution)/shard_map/ppermute | solution.py:24
  452.9 84.3 %collective-permute-start.45 = (bf16[4,2,128,1024]{3,2,1,0:T(8,128)(2,1)}, bf16[4,2,128,1024]{3,2,1,0:T(8,128)(2,1)}, u32[]{:S(2)}, u32[]{:S(2)}) collective-permute-start(bf16[4,2,128,1024]{3,2,1,0:T(8,128)(2,1)} %bitcast.69), channel_id=1, source_target_pairs={{0,4},{4,0},{1,5},{5,1},{2,6},{6,2},{3,7},{7,3},{8,12},{12,8},{9,1... | collective-permute-start | bytes 6291464 | tf_op jit(solution)/shard_map/ppermute | solution.py:24
  458.6 15.3 %collective-permute-start.22 = (f32[2,256,2]{1,2,0:T(2,128)S(1)}, f32[2,256,2]{1,2,0:T(2,128)S(1)}, u32[]{:S(2)}, u32[]{:S(2)}) collective-permute-start(f32[2,256,2]{1,2,0:T(2,128)S(1)} %pad_maximum_fusion.2), channel_id=1, source_target_pairs={{24,0},{25,1},{26,2},{27,3},{28,4},{29,5},{30,6},{31,7}} | collective-permute-start | bytes 12296 | tf_op jit(solution)/shard_map/ppermute | solution.py:804
  460.2 43.8 %collective-permute-start.51 = (s32[4,640]{1,0:T(4,128)S(1)}, s32[4,640]{1,0:T(4,128)S(1)}, u32[]{:S(2)}, u32[]{:S(2)}) collective-permute-start(s32[4,640]{1,0:T(4,128)S(1)} %pad_add_fusion), channel_id=1, source_target_pairs={{0,3},{1,0},{2,1},{3,2},{4,7},{5,4},{6,5},{7,6},{8,11},{9,8},{10,9... | collective-permute-start | bytes 30728 | tf_op jit(solution)/shard_map/ppermute | solution.py:671
  473.8 120.5 %collective-permute-start.37 = (bf16[4,128,1024]{2,1,0:T(8,128)(2,1)}, bf16[4,128,1024]{2,1,0:T(8,128)(2,1)S(1)}, u32[]{:S(2)}, u32[]{:S(2)}) collective-permute-start(bf16[4,128,1024]{2,1,0:T(8,128)(2,1)} %bitcast.94), channel_id=1, source_target_pairs={{0,4},{4,0},{1,5},{5,1},{2,6},{6,2},{3,7},{7,3},{8,12},{12,8},{9,1... | collective-permute-start | bytes 3145736 | tf_op jit(solution)/shard_map/ppermute | solution.py:24
  503.3 53.4 %collective-permute-start.38 = (bf16[4,128,1024]{2,1,0:T(8,128)(2,1)}, bf16[4,128,1024]{2,1,0:T(8,128)(2,1)}, u32[]{:S(2)}, u32[]{:S(2)}) collective-permute-start(bf16[4,128,1024]{2,1,0:T(8,128)(2,1)} %bitcast.99), channel_id=1, source_target_pairs={{0,4},{4,0},{1,5},{5,1},{2,6},{6,2},{3,7},{7,3},{8,12},{12,8},{9,1... | collective-permute-start | bytes 3145736 | tf_op jit(solution)/shard_map/ppermute | solution.py:24
  514.6 13.5 %collective-permute-start.47 = (f32[512,1]{1,0:T(8,128)S(1)}, f32[512,1]{1,0:T(8,128)S(1)}, u32[]{:S(2)}, u32[]{:S(2)}) collective-permute-start(f32[512,1]{1,0:T(8,128)S(1)} %copy.33.refs_16_), channel_id=1, source_target_pairs={{0,2},{1,3},{2,0},{3,1},{4,6},{5,7},{6,4},{7,5},{8,10},{9,11},{10,... | collective-permute-start | bytes 6152 | tf_op jit(solution)/shard_map/ppermute | solution.py:671
  (95 other events, 691.5 us)
Sparse Core Ops, SparseCore 0:
  148.5 45.4 all-gather.8
  323.3 48.2 all-gather.14
  444.3 29.5 all-gather.10
  475.8 27.4 all-gather.12

commit v5 on v4

v5 whole, which is shorter than its diff:
```python
import functools
import jax
import jax.numpy as jnp
from jax import lax
from jax.experimental import pallas as pl
from jax.experimental.pallas import tpu as pltpu
from jax.sharding import PartitionSpec as P

CHUNKS = 2
VMEM_MIB = 58
BF16 = jnp.bfloat16
F32 = jnp.float32
MIB = 1024 * 1024


def shifted(block, axis, distance):
    devices = range(lax.axis_size(axis))
    route = [(i - distance, i) for i in devices if i - distance in devices]
    return lax.ppermute(block, axis, route)


def swapped(block):
    return lax.ppermute(block, "mp", [(0, 1), (1, 0)])


def gelu_parts(pre_vals):
    coeff = 0.7978845608
    square = pre_vals * pre_vals
    inner = coeff * pre_vals * (1.0 + 0.044715 * square)
    half = 0.5 * (1.0 + jnp.tanh(inner))
    value = pre_vals * half
    slope = half + 2.0 * value * (1.0 - half) * coeff * (1.0 + 3.0 * 0.044715 * square)
    return (value, slope)


def row_scale(rows_in):
    floats = rows_in.astype(F32)
    return lax.rsqrt(jnp.mean(floats * floats, axis=-1, keepdims=True) + 1e-06)


def normalised(rows_in):
    return (rows_in.astype(F32) * row_scale(rows_in)).astype(BF16)


def norm_back(rows_in, grads):
    scale = row_scale(rows_in)
    normal = rows_in.astype(F32) * scale
    return scale * (grads - normal * jnp.mean(grads * normal, axis=-1, keepdims=True))


def dot(a, b):
    return jnp.dot(a, b, preferred_element_type=F32)


def dot_t(a, b):
    return lax.dot_general(a, b, (((1,), (1,)), ((), ())), preferred_element_type=F32)


def t_dot(a, b):
    return lax.dot_general(a, b, (((0,), (0,)), ((), ())), preferred_element_type=F32)


def tile_of(size, most):
    if size <= most:
        return size
    return max(t for t in range(128, most + 1, 128) if size % t == 0)


def pieces_of(size):
    return [(at, min(256, size - at)) for at in range(0, size, 256)]


def cost(flops, bytes_accessed, transcendentals):
    return pl.CostEstimate(
        flops=flops,
        bytes_accessed=bytes_accessed,
        transcendentals=transcendentals,
    )


def params(limit):
    return pltpu.CompilerParams(vmem_limit_bytes=limit * MIB)


def chosen(index, candidates):
    value = candidates[0][1]
    for at, option in candidates[1:]:
        value = jnp.where(index == at, option, value)
    return value


def gathered(halves, place):
    if len(halves) == 1:
        return halves[0][...]
    mine, theirs = (half[...] for half in halves)
    first = jnp.where(place == 0, mine, theirs)
    second = jnp.where(place == 0, theirs, mine)
    return jnp.concatenate([first, second], axis=0)


def part_of(block, place, parts):
    rows = block.shape[0] // parts
    if parts == 1:
        return block[...]
    return block[pl.ds(pl.multiple_of(place * rows, rows), rows), :]


def whole_spec(shape):
    return pl.BlockSpec(shape, lambda *_: (0,) * len(shape))


def forward_kernel(halves, has_arrived, where, own, *refs):
    if has_arrived:
        arrived, refs = refs[:halves], refs[halves:]
    w_in, w_out, rows_out, mine_out, keep, *send, whole, normed, total = refs
    step = pl.program_id(0)

    @pl.when(step == 0)
    def _():
        rows = own[...]
        if has_arrived:
            rows = jnp.where(where[0] == 0, rows, gathered(arrived, where[1]))
        rows_out[...] = rows
        whole[...] = rows
        mine_out[...] = part_of(whole, where[1], halves)
        normed[...] = normalised(rows)
        total[...] = jnp.zeros_like(total)

    values = []
    for at, size in pieces_of(w_in.shape[1]):
        value, _ = gelu_parts(dot(normed[...], w_in[:, at : at + size]))
        values.append(value.astype(BF16))
    total[...] += dot(jnp.concatenate(values, axis=1), w_out[...])

    @pl.when(step == pl.num_programs(0) - 1)
    def _():
        if send:
            keep[...] = part_of(total, where[1], 2) + part_of(whole, where[1], 2).astype(F32)
            send[0][...] = part_of(total, 1 - where[1], 2).astype(send[0].dtype)
        else:
            keep[...] = total[...]


def forward_section(where, text, at, halves, arrived, w_in, w_out):
    _, rows, width = text.shape
    hidden = w_in.shape[1]
    tile = tile_of(hidden, 1024)
    full, part = (rows, width), (rows // halves, width)
    shapes = [(full, BF16), (part, BF16), (part, F32)] + [(part, BF16)] * (halves - 1)
    return pl.pallas_call(
        functools.partial(forward_kernel, halves, bool(arrived)),
        grid_spec=pltpu.PrefetchScalarGridSpec(
            num_scalar_prefetch=1,
            grid=(hidden // tile,),
            in_specs=[
                pl.BlockSpec((None, rows, width), lambda j, s: (at, 0, 0)),
                *[whole_spec(part)] * len(arrived),
                pl.BlockSpec((width, tile), lambda j, s: (0, j)),
                pl.BlockSpec((tile, width), lambda j, s: (j, 0)),
            ],
            out_specs=[whole_spec(shape) for shape, _ in shapes],
            scratch_shapes=[pltpu.VMEM(full, BF16), pltpu.VMEM(full, BF16), pltpu.VMEM(full, F32)],
        ),
        out_shape=[jax.ShapeDtypeStruct(*shape) for shape in shapes],
        compiler_params=params(VMEM_MIB),
        cost_estimate=cost(
            flops=4 * rows * width * hidden,
            bytes_accessed=4 * width * hidden,
            transcendentals=rows * hidden,
        ),
        name="section_forward",
    )(where, text, *arrived, w_in, w_out)


def total_of(pieces):
    total = pieces[0].astype(F32)
    for piece in pieces[1:]:
        total = total + piece.astype(F32)
    return total


def finish_backward(rows, grads, pieces):
    return (grads.astype(F32) + norm_back(rows, total_of(pieces))).astype(BF16)


def backward_kernel(owners, halves, where, *refs):
    stashed, refs = refs[: len(owners)], refs[len(owners) :]
    arrived, refs = refs[:halves], refs[halves:]
    w_in, w_out, mine_rows, keep, *send, rows, grads, normed, total = refs
    step = pl.program_id(0)

    @pl.when(step == 0)
    def _():
        rows[...] = chosen(where[0], [(at, ref[...]) for at, ref in zip(owners, stashed)])
        grads[...] = gathered(arrived, where[1])
        mine_rows[...] = part_of(rows, where[1], halves)
        normed[...] = normalised(rows[...])
        total[...] = jnp.zeros_like(total)

    dpres = []
    for at, size in pieces_of(w_in.shape[1]):
        _, slope = gelu_parts(dot(normed[...], w_in[:, at : at + size]))
        dpres.append((dot_t(grads[...], w_out[at : at + size, :]) * slope).astype(BF16))
    total[...] += dot_t(jnp.concatenate(dpres, axis=1), w_in[...])

    @pl.when(step == pl.num_programs(0) - 1)
    def _():
        if send:
            keep[...] = part_of(total, where[1], 2)
            send[0][...] = part_of(total, 1 - where[1], 2).astype(send[0].dtype)
        else:
            keep[...] = total[...]


def backward_section(where, halves, options, arrived, w_in, w_out):
    width, hidden = w_in.shape
    rows = options[0][1].shape[0]
    tile = tile_of(hidden, 1024)
    full, part = (rows, width), (rows // halves, width)
    shapes = [(part, BF16), (part, F32)] + [(part, BF16)] * (halves - 1)
    return pl.pallas_call(
        functools.partial(backward_kernel, tuple(at for at, _ in options), halves),
        grid_spec=pltpu.PrefetchScalarGridSpec(
            num_scalar_prefetch=1,
            grid=(hidden // tile,),
            in_specs=[whole_spec(full)] * len(options)
            + [whole_spec(part)] * halves
            + [
                pl.BlockSpec((width, tile), lambda j, s: (0, j)),
                pl.BlockSpec((tile, width), lambda j, s: (j, 0)),
            ],
            out_specs=[whole_spec(shape) for shape, _ in shapes],
            scratch_shapes=[pltpu.VMEM(full, BF16)] * 3 + [pltpu.VMEM(full, F32)],
        ),
        out_shape=[jax.ShapeDtypeStruct(*shape) for shape in shapes],
        compiler_params=params(VMEM_MIB),
        cost_estimate=cost(
            flops=6 * rows * width * hidden,
            bytes_accessed=4 * width * hidden,
            transcendentals=rows * hidden,
        ),
        name="section_backward",
    )(where, *[option for _, option in options], *arrived, w_in, w_out)


def lane_fill(columns, shape):
    lane = lax.broadcasted_iota(jnp.int32, shape, 1)
    filled = jnp.zeros(shape, F32)
    for at, column in enumerate(columns):
        filled = jnp.where(lane == at, column, filled)
    return filled


def logits_kernel(halves, where, *refs):
    final, refs = refs[:halves], refs[halves:]
    w_unit, counts, logits, stats, normed, peak, total, target = refs
    step = pl.program_id(0)
    lanes = peak.shape[1]

    @pl.when(step == 0)
    def _():
        normed[...] = normalised(gathered(final, where[1]))
        peak[...] = jnp.full_like(peak, -1e30)
        total[...] = jnp.zeros_like(total)
        target[...] = jnp.zeros_like(target)

    columns = []
    for start, size in pieces_of(w_unit.shape[1]):
        values = dot(normed[...], w_unit[:, start : start + size])
        logits[:, start : start + size] = values
        counted = counts[:, start : start + size].astype(F32) * values
        columns += [
            (values[:, c : c + lanes], counted[:, c : c + lanes]) for c in range(0, size, lanes)
        ]
    higher = peak[...]
    for values, _ in columns:
        higher = jnp.maximum(higher, values)
    mass = total[...] * jnp.exp(peak[...] - higher)
    summed = target[...]
    for values, counted in columns:
        mass = mass + jnp.exp(values - higher)
        summed = summed + counted
    peak[...] = higher
    total[...] = mass
    target[...] = summed

    @pl.when(step == pl.num_programs(0) - 1)
    def _():
        top = jnp.max(peak[...], axis=-1, keepdims=True)
        mass = jnp.sum(total[...] * jnp.exp(peak[...] - top), axis=-1, keepdims=True)
        summed = jnp.sum(target[...], axis=-1, keepdims=True)
        stats[...] = lane_fill([top, mass, summed], stats.shape)


def head_logits(where, final, w_unit, counts, at):
    halves = len(final)
    half, width = final[0].shape
    rows = half * halves
    vocab = w_unit.shape[1]
    lanes = 128 if vocab % 128 == 0 else vocab
    tile = tile_of(vocab, 640)
    return pl.pallas_call(
        functools.partial(logits_kernel, halves),
        grid_spec=pltpu.PrefetchScalarGridSpec(
            num_scalar_prefetch=1,
            grid=(vocab // tile,),
            in_specs=[
                *[whole_spec((half, width))] * halves,
                pl.BlockSpec((width, tile), lambda t, s: (0, t)),
                pl.BlockSpec((None, rows, tile), lambda t, s: (at, 0, t)),
            ],
            out_specs=[
                pl.BlockSpec((rows, tile), lambda t, s: (0, t)),
                whole_spec((rows, 128)),
            ],
            scratch_shapes=[pltpu.VMEM((rows, width), BF16)] + [pltpu.VMEM((rows, lanes), F32)] * 3,
        ),
        out_shape=[
            jax.ShapeDtypeStruct((rows, vocab), F32),
            jax.ShapeDtypeStruct((rows, 128), F32),
        ],
        compiler_params=params(VMEM_MIB),
        cost_estimate=cost(
            flops=2 * rows * width * vocab,
            bytes_accessed=(2 * width + 6 * rows) * vocab,
            transcendentals=rows * vocab,
        ),
        name="head_logits",
    )(where, *final, w_unit, counts)


def head_grads_kernel(denom, halves, where, *refs):
    stats, lengths, logits, counts, w_unit, keep, *send, results, shift, total = refs
    step = pl.program_id(0)

    @pl.when(step == 0)
    def _():
        values = [stats[at] for at in range(stats.shape[0])]
        top = values[0][:, 0:1]
        for table in values[1:]:
            top = jnp.maximum(top, table[:, 0:1])
        mass = sum(table[:, 1:2] * jnp.exp(table[:, 0:1] - top) for table in values)
        target = sum(table[:, 2:3] for table in values)
        lse = top + jnp.log(mass)
        shift[...] = lse - jnp.log(lengths[...] * (1.0 / denom))
        results[...] = lane_fill([shift[...], lengths[...] * lse - target], results.shape)
        total[...] = jnp.zeros_like(total)

    columns = []
    for start, size in pieces_of(w_unit.shape[1]):
        exped = jnp.exp(logits[:, start : start + size] - shift[...])
        counted = counts[:, start : start + size].astype(F32) * (1.0 / denom)
        columns.append((exped - counted).astype(BF16))
    total[...] += dot_t(jnp.concatenate(columns, axis=1), w_unit[...])

    @pl.when(step == pl.num_programs(0) - 1)
    def _():
        if send:
            keep[...] = part_of(total, where[1], 2)
            send[0][...] = part_of(total, 1 - where[1], 2).astype(send[0].dtype)
        else:
            keep[...] = total[...]


def head_grads(where, halves, stats, lengths, logits, counts, at, w_unit, denom):
    rows, vocab = logits.shape
    width = w_unit.shape[0]
    tile = tile_of(vocab, 640)
    part = (rows // halves, width)
    shapes = [(part, F32)] + [(part, BF16)] * (halves - 1) + [((rows, 128), F32)]
    return pl.pallas_call(
        functools.partial(head_grads_kernel, denom, halves),
        grid_spec=pltpu.PrefetchScalarGridSpec(
            num_scalar_prefetch=1,
            grid=(vocab // tile,),
            in_specs=[
                whole_spec(stats.shape),
                pl.BlockSpec((None, rows, 1), lambda t, s: (at, 0, 0)),
                pl.BlockSpec((rows, tile), lambda t, s: (0, t)),
                pl.BlockSpec((None, rows, tile), lambda t, s: (at, 0, t)),
                pl.BlockSpec((width, tile), lambda t, s: (0, t)),
            ],
            out_specs=[whole_spec(shape) for shape, _ in shapes],
            scratch_shapes=[pltpu.VMEM((rows, 1), F32), pltpu.VMEM((rows, width), F32)],
        ),
        out_shape=[jax.ShapeDtypeStruct(*shape) for shape in shapes],
        compiler_params=params(VMEM_MIB),
        cost_estimate=cost(
            flops=2 * rows * width * vocab,
            bytes_accessed=(2 * width + 6 * rows) * vocab,
            transcendentals=rows * vocab,
        ),
        name="head_grads",
    )(where, stats, lengths, logits, counts, w_unit)


def unit_kernel(blocks, tables, share, denom, where, *refs):
    x_refs, refs = refs[: len(blocks)], refs[len(blocks) :]
    shifts, refs = refs[:tables], refs[tables:]
    counts, refs = refs[:tables], refs[tables:]
    w_unit, grad, normed, normed_t = refs
    half = x_refs[0].shape[0]
    rows = normed.shape[0] // tables

    @pl.when(pl.program_id(0) == 0)
    def _():
        for ref, (base, theirs) in zip(x_refs, blocks):
            side = 0
            if theirs is not None:
                side = 1 - where[1] if theirs else where[1]
            place = pl.ds(pl.multiple_of(base + side * half, half), half)
            normed[place, :] = normalised(ref[...])
        columns = pl.ds(pl.multiple_of(where[0] * share, share), share)
        normed_t[...] = normed[:, columns].astype(F32).T.astype(BF16)

    logits = dot(normed[...], w_unit[...])
    dlogits = []
    for k in range(tables):
        exped = jnp.exp(logits[k * rows : (k + 1) * rows] - shifts[k][...])
        counted = counts[k][...].astype(F32) * (1.0 / denom)
        dlogits.append((exped - counted).astype(BF16))
    grad[...] = dot(normed_t[...], jnp.concatenate(dlogits, axis=0))


def unit_grads(where, x_parts, shifts, counts, w_unit, denom, share):
    width, vocab = w_unit.shape
    tile = tile_of(vocab, 256)
    half = x_parts[0][0].shape[2]
    rows = shifts[0].shape[0]
    tables = len(shifts)
    blocks = tuple(block for _, _, block in x_parts)
    return pl.pallas_call(
        functools.partial(unit_kernel, blocks, tables, share, denom),
        grid_spec=pltpu.PrefetchScalarGridSpec(
            num_scalar_prefetch=1,
            grid=(vocab // tile,),
            in_specs=[pl.BlockSpec((None, None, half, width), index) for _, index, _ in x_parts]
            + [whole_spec((rows, 1))] * tables
            + [pl.BlockSpec((rows, tile), lambda j, s: (0, j))] * tables
            + [pl.BlockSpec((width, tile), lambda j, s: (0, j))],
            out_specs=pl.BlockSpec((share, tile), lambda j, s: (0, j)),
            scratch_shapes=[
                pltpu.VMEM((rows * tables, width), BF16),
                pltpu.VMEM((share, rows * tables), BF16),
            ],
        ),
        out_shape=jax.ShapeDtypeStruct((share, vocab), F32),
        compiler_params=params(VMEM_MIB),
        cost_estimate=cost(
            flops=2 * rows * tables * (width + share) * vocab,
            bytes_accessed=2 * (width + rows * tables) * vocab,
            transcendentals=rows * tables * vocab,
        ),
        name="unit_grads",
    )(where, *[x for x, _, _ in x_parts], *shifts, *counts, w_unit)


def weight_kernel(blocks, adding, share, where, *refs):
    x_refs, refs = refs[:blocks], refs[blocks:]
    g_refs, refs = refs[:blocks], refs[blocks:]
    w_in, w_out, refs = refs[0], refs[1], refs[2:]
    if adding:
        old_first, old_second, refs = refs[0], refs[1], refs[2:]
    first, second, normed, grads, normed_t, grads_t = refs
    count = x_refs[0].shape[0]

    @pl.when(pl.program_id(0) == 0)
    def _():
        columns = pl.ds(pl.multiple_of(where[0] * share, share), share)
        for at in range(blocks):
            place = pl.ds(at * count, count)
            normed[place, :] = normalised(x_refs[at][...])
            grads[place, :] = g_refs[at][...]
        normed_t[...] = normed[:, columns].astype(F32).T.astype(BF16)
        grads_t[...] = grads[:, columns].astype(F32).T.astype(BF16)

    for at, size in pieces_of(w_in.shape[1]):
        value, slope = gelu_parts(dot(normed[...], w_in[:, at : at + size]))
        dpre = (dot_t(grads[...], w_out[at : at + size, :]) * slope).astype(BF16)
        now_first = dot(normed_t[...], dpre)
        now_second = dot(grads_t[...], value.astype(BF16)).T
        if adding:
            now_first = old_first[:, at : at + size] + now_first
            now_second = old_second[at : at + size, :] + now_second
        first[:, at : at + size] = now_first
        second[at : at + size, :] = now_second


def weight_grads(where, x_parts, g_parts, w_in, w_out, old, share):
    width, hidden = w_in.shape
    tile = tile_of(hidden, 512)
    blocks = len(g_parts)
    count = g_parts[0][0].shape[1]
    rows = blocks * count
    in_specs = [pl.BlockSpec((None, None, count, width), index) for _, index in x_parts]
    in_specs += [pl.BlockSpec((None, count, width), index) for _, index in g_parts]
    in_specs += [
        pl.BlockSpec((width, tile), lambda j, s: (0, j)),
        pl.BlockSpec((tile, width), lambda j, s: (j, 0)),
    ]
    grad_specs = [
        pl.BlockSpec((share, tile), lambda j, s: (0, j)),
        pl.BlockSpec((tile, share), lambda j, s: (j, 0)),
    ]
    adding = old is not None
    aliases = {}
    if adding:
        in_specs += grad_specs
        aliases = {1 + 2 * blocks + 2: 0, 1 + 2 * blocks + 3: 1}
    return pl.pallas_call(
        functools.partial(weight_kernel, blocks, adding, share),
        grid_spec=pltpu.PrefetchScalarGridSpec(
            num_scalar_prefetch=1,
            grid=(hidden // tile,),
            in_specs=in_specs,
            out_specs=grad_specs,
            scratch_shapes=[
                pltpu.VMEM((rows, width), BF16),
                pltpu.VMEM((rows, width), BF16),
                pltpu.VMEM((share, rows), BF16),
                pltpu.VMEM((share, rows), BF16),
            ],
        ),
        out_shape=[
            jax.ShapeDtypeStruct((share, hidden), F32),
            jax.ShapeDtypeStruct((hidden, share), F32),
        ],
        input_output_aliases=aliases,
        compiler_params=params(VMEM_MIB),
        cost_estimate=cost(
            flops=4 * rows * (width + share) * hidden,
            bytes_accessed=4 * width * hidden + 16 * share * hidden,
            transcendentals=rows * hidden,
        ),
        name="weight_grads",
    )(where, *[x for x, _ in x_parts], *[g for g, _ in g_parts], w_in, w_out, *(old or ()))


def unit_counts(ends, targets, ids):
    positions = jnp.arange(targets.shape[1], dtype=jnp.int32)
    row_local = jnp.sum((ends[:, None, :] <= positions[None, :, None]).astype(jnp.int32), axis=-1)
    rows = jnp.arange(ends.shape[1], dtype=jnp.int32)
    row_onehot = (row_local[:, :, None] == rows[None, None, :]).astype(BF16)
    hits = (targets[:, :, None] == ids[None, None, :]).astype(BF16)
    counts = jnp.einsum("mur,muv->mrv", row_onehot, hits, preferred_element_type=F32)
    return counts.astype(BF16)


def on_device(text_rows, durations, unit_targets, w_in, w_out, w_unit):
    micro, row_count, width = text_rows.shape
    segments = lax.axis_size("segment")
    mp_size = lax.axis_size("mp")
    dp_size = lax.axis_size("dp")
    seg = lax.axis_index("segment").astype(jnp.int32)
    mp_at = lax.axis_index("mp").astype(jnp.int32)
    dp_at = lax.axis_index("dp").astype(jnp.int32)
    last = segments - 1
    pair = mp_size == 2
    halves = 2 if pair else 1
    where = jnp.stack([seg, mp_at])
    first = w_in[0]
    second = w_out[0]
    chunks = CHUNKS
    rows = micro * row_count // chunks
    text = text_rows.reshape(chunks, rows, width)
    vocab_part = w_unit.shape[1]
    unit_count = unit_targets.shape[1]
    denom = float(micro * unit_count * dp_size)
    lengths = durations[:, 0, :]
    length_f = lengths.astype(F32).reshape(chunks, rows, 1)
    ends = jnp.cumsum(lengths, axis=-1)
    own_ids = (seg * mp_size + mp_at) * vocab_part + jnp.arange(vocab_part, dtype=jnp.int32)

    def around(block):
        came = [block]
        for distance in range(1, dp_size):
            route = [(i, (i + distance) % dp_size) for i in range(dp_size)]
            came.append(lax.ppermute(block, "dp", route))
        return came

    unit_hits = [
        unit_counts(packed[:, unit_count:], packed[:, :unit_count], own_ids)
        for packed in around(jnp.concatenate([unit_targets, ends], axis=1))
    ]
    head_counts = unit_hits[0].reshape(chunks, rows, vocab_part)
    unit_hits = [hits.reshape(micro * row_count, vocab_part) for hits in unit_hits]

    def both(part):
        return [part, swapped(part)] if pair else [part]

    def reduced(keep, send):
        return [keep, swapped(send[0])] if pair else [lax.psum(keep, "mp")]

    def gathered_rows(mine):
        came = lax.all_gather(mine, "dp")
        return [came, swapped(came)] if pair else [came]

    stash, x_halves, grads, finals, results = [], [], [], [], []
    sums = None
    x_gathered = None
    f_hop = b_hop = None

    def x_parts(at):
        return [
            (source, lambda j, s, k=k: (k, at, 0, 0))
            for source in x_gathered
            for k in range(dp_size)
        ]

    def g_parts(sources):
        return [
            (source, lambda j, s, k=k: (k, 0, 0)) for source in sources for k in range(dp_size)
        ]

    clocks = 2 * segments + chunks - 1
    for clock in range(clocks):
        f_out = b_out = None
        if clock < segments + chunks - 1:
            arrived = [] if clock == 0 else both(shifted(f_hop, "segment", 1))
            rows_in, mine, keep, *send = forward_section(
                where, text, min(clock, chunks - 1), halves, arrived, first, second
            )
            stash.append(rows_in)
            x_halves.append(mine)
            pieces = reduced(keep, send)
            f_out = total_of(pieces if pair else [mine, *pieces]).astype(BF16)
        if clock >= segments:
            at = clock - segments
            arrived = None if at == 0 else shifted(b_hop, "segment", -1)
            if at < chunks:
                final = chosen(
                    seg,
                    [(last, f_hop)]
                    + [(to, lax.ppermute(f_hop, "segment", [(last, to)])) for to in range(last)],
                )
                finals.append(final)
                logits, stats = head_logits(where, both(final), w_unit, head_counts, at)
                tables = lax.all_gather(stats[:, 0:3], ("segment", "mp"))
                keep, *send, result = head_grads(
                    where, halves, tables, length_f, logits, head_counts, at, w_unit, denom
                )
                results.append(result[:, 0:2])
                dnorm = total_of(reduced(keep, send)).astype(BF16)
                dnorm = total_of(
                    [dnorm]
                    + [lax.ppermute(dnorm, "segment", [(j, last)]) for j in range(last)]
                ).astype(BF16)
                grad_final = norm_back(final, dnorm.astype(F32)).astype(BF16)
                arrived = (
                    grad_final if arrived is None else jnp.where(seg == last, grad_final, arrived)
                )
            grads.append(arrived)
            if clock < clocks - 1:
                options = []
                for other in range(segments):
                    stage = clock - 2 * segments + 1 + 2 * other
                    if 0 <= stage < len(stash):
                        options.append((other, stash[stage]))
                mine, keep, *send = backward_section(
                    where, halves, options, both(arrived), first, second
                )
                b_out = finish_backward(mine, arrived, reduced(keep, send))
        if clock == segments + chunks - 2:
            x_half = jnp.stack(
                [
                    chosen(seg, [(s, x_halves[b + s]) for s in range(segments)])
                    for b in range(chunks)
                ]
            )
            x_gathered = gathered_rows(x_half)
        if clock == segments + chunks - 1:
            unit_rows = gathered_rows(jnp.stack(finals))
        if clock >= 2 * segments - 1:
            at = clock - 2 * segments + 1
            mine = chosen(seg, [(s, grads[at + last - s]) for s in range(segments)])
            sums = weight_grads(
                dp_at[None],
                x_parts(at),
                g_parts(gathered_rows(mine)),
                first,
                second,
                sums,
                width // dp_size,
            )
        f_hop, b_hop = f_out, b_out

    results = jnp.stack(results)
    loss = (jnp.sum(results[:, :, 1]) / denom)[None]
    shifts = around(results[:, :, 0].reshape(-1, 1))
    unit_parts = [
        (
            source,
            lambda j, s, k=k, b=b: (lax.rem(s[0] + dp_size - k, dp_size), b, 0, 0),
            ((k * chunks + b) * rows, bool(at) if pair else None),
        )
        for at, source in enumerate(unit_rows)
        for k in range(dp_size)
        for b in range(chunks)
    ]
    sum_unit = unit_grads(
        jnp.stack([dp_at, mp_at]), unit_parts, shifts, unit_hits, w_unit, denom, width // dp_size
    )
    return (loss, sums[0][None], sums[1][None], sum_unit)


def solution(mesh):
    placed = (
        P(None, "dp", None),
        P(None, "dp", None),
        P(None, "dp"),
        P("segment", None, "mp"),
        P("segment", "mp", None),
        P(None, ("segment", "mp")),
    )
    return jax.shard_map(
        on_device,
        mesh=mesh,
        in_specs=placed,
        out_specs=(
            P("dp"),
            P("segment", "dp", "mp"),
            P("segment", "mp", "dp"),
            P("dp", ("segment", "mp")),
        ),
        check_vma=False,
    )
```

time: 652 us -> 527 us (0.81)
  the two profiles are of different devices: /device:TPU:0 before, /device:TPU:11 now
where the time goes in v5:
time: 527 us; the launch traced here: 519 us
  Pallas kernels  225 us (43%)
  waiting for transfers between devices  121 us (23%)
  starting transfers between devices  74.6 us (14%)
  blocking collectives  29.1 us (6%)
  other arithmetic  28.9 us (5%)
  between operations  16.7 us (3%)
  matrix products  12.7 us (2%)
  local copies, waits for them, and re-layouts  10.9 us (2%)
    pallas_call x2, Pallas kernels, weight_grads(): pl.pallas_call(functools.partial(weight_kernel, blocks, adding, share), g...  74 us
    pallas_call x5, Pallas kernels, forward_section(): pl.pallas_call(functools.partial(forward_kernel, halves, bool(arrived)),...  60.4 us
    pallas_call x4, Pallas kernels, backward_section(): pl.pallas_call(functools.partial(backward_kernel, tuple((at for at, _ in...  53.6 us
    ppermute x8, waiting for transfers between devices, shifted(): return lax.ppermute(block, axis, route)  44.8 us
    all_gather x2, blocking collectives, on_device(): tables = lax.all_gather(stats[:, 0:3], ('segment', 'mp'))  29.1 us
    ppermute x8, starting transfers between devices, shifted(): return lax.ppermute(block, axis, route)  27.6 us
    all_gather x4, waiting for transfers between devices, gathered_rows(): came = lax.all_gather(mine, 'dp')  27.5 us
    ppermute x6, waiting for transfers between devices, around(): came.append(lax.ppermute(block, 'dp', route))  21.8 us
  transfers between devices with their start and end apart: 55, of which 29 were waited for; matrix products, arithmetic and copies ran while one was open for 7% of the time, Pallas kernels for 27%

profile of v5, /device:TPU:11, one launch (start us, length us, event | category | flops | bytes accessed | tf_op | source)
XLA Modules:
  0.0 518.8 jit_solution(11310648768322367979)
XLA Ops:
  7.8 12.0 %section_forward.5 = (bf16[256,1024]{1,0:T(8,128)(2,1)}, bf16[128,1024]{1,0:T(8,128)(2,1)}, f32[128,1024]{1,0:T(8,128)}, bf16[128,1024]{1,0:T(8,128)(2,1)}) custom-call(s32[2]{0:T(128)} %pad_add_fusion.1.where, bf16[2,256,1024]{2,1,0:T(8,128)(2,1)} %bitcast.70, bf16[1024,4096]{1,0:T(8,128)(2,1)} %bitcast.34, bf16[4096,1024]{1,0:T(8,128)(2,1)} %bitcast.45), custom_call_target="tpu_custom_call" | custom-call | flops 4294967296 | bytes 16777216 | tf_op jit(solution)/shard_map/section_forward/pallas_call | solution.py:150
  26.1 6.3 %collective-permute-done.1.refs_0_ = bf16[128,1024]{1,0:T(8,128)(2,1)S(1)} collective-permute-done((bf16[128,1024]{1,0:T(8,128)(2,1)S(1)}, bf16[128,1024]{1,0:T(8,128)(2,1)S(1)}, u32[]{:S(2)}, u32[]{:S(2)}) %collective-permute-start.1) | collective-permute-done | bytes 262176 | tf_op jit(solution)/shard_map/ppermute | solution.py:19
  35.5 12.1 %section_forward.6 = (bf16[256,1024]{1,0:T(8,128)(2,1)}, bf16[128,1024]{1,0:T(8,128)(2,1)}, f32[128,1024]{1,0:T(8,128)}, bf16[128,1024]{1,0:T(8,128)(2,1)}) custom-call(s32[2]{0:T(128)} %pad_add_fusion.1.where, bf16[2,256,1024]{2,1,0:T(8,128)(2,1)} %bitcast.71, bf16[128,1024]{1,0:T(8,128)(2,1)} %copy-done.22, bf16[128,1024]{1,0:T(8,128)(2,1)} %copy-done.25, ...), custom_call_target="tpu_custom_call" | custom-call | flops 4294967296 | bytes 16777216 | tf_op jit(solution)/shard_map/section_forward/pallas_call | solution.py:150
  62.9 12.1 %section_forward.7 = (bf16[256,1024]{1,0:T(8,128)(2,1)}, bf16[128,1024]{1,0:T(8,128)(2,1)}, f32[128,1024]{1,0:T(8,128)}, bf16[128,1024]{1,0:T(8,128)(2,1)}) custom-call(s32[2]{0:T(128)} %pad_add_fusion.1.where, bf16[2,256,1024]{2,1,0:T(8,128)(2,1)} %bitcast.72, bf16[128,1024]{1,0:T(8,128)(2,1)} %copy-done.23, bf16[128,1024]{1,0:T(8,128)(2,1)} %copy-done.26, ...), custom_call_target="tpu_custom_call" | custom-call | flops 4294967296 | bytes 16777216 | tf_op jit(solution)/shard_map/section_forward/pallas_call | solution.py:150
  91.2 12.1 %section_forward.8 = (bf16[256,1024]{1,0:T(8,128)(2,1)}, bf16[128,1024]{1,0:T(8,128)(2,1)}, f32[128,1024]{1,0:T(8,128)}, bf16[128,1024]{1,0:T(8,128)(2,1)}) custom-call(s32[2]{0:T(128)} %pad_add_fusion.1.where, bf16[2,256,1024]{2,1,0:T(8,128)(2,1)} %bitcast.73, bf16[128,1024]{1,0:T(8,128)(2,1)} %copy-done.24, bf16[128,1024]{1,0:T(8,128)(2,1)} %copy-done.27, ...), custom_call_target="tpu_custom_call" | custom-call | flops 4294967296 | bytes 16777216 | tf_op jit(solution)/shard_map/section_forward/pallas_call | solution.py:150
  123.5 12.1 %section_forward.9 = (bf16[256,1024]{1,0:T(8,128)(2,1)}, bf16[128,1024]{1,0:T(8,128)(2,1)}, f32[128,1024]{1,0:T(8,128)}, bf16[128,1024]{1,0:T(8,128)(2,1)}) custom-call(s32[2]{0:T(128)} %pad_add_fusion.1.where, bf16[2,256,1024]{2,1,0:T(8,128)(2,1)} %bitcast.74, bf16[128,1024]{1,0:T(8,128)(2,1)} %copy-done.17, bf16[128,1024]{1,0:T(8,128)(2,1)} %copy-done.19, ...), custom_call_target="tpu_custom_call" | custom-call | flops 4294967296 | bytes 16777216 | tf_op jit(solution)/shard_map/section_forward/pallas_call | solution.py:150
  144.4 15.6 %all-gather = f32[2048,3]{1,0:T(8,128)} all-gather(f32[256,3]{1,0:T(8,128)} %bitcast.82), channel_id=2, replica_groups=mesh['segment'=4,'mp'=2,'dp'=4] {'segment','mp'}, dimensions={0}, use_global_device_ids=true | all-gather | bytes 27648 | tf_op jit(solution)/shard_map/all_gather | solution.py:638
  159.9 5.8 %head_grads.2 = (f32[128,1024]{1,0:T(8,128)}, bf16[128,1024]{1,0:T(8,128)(2,1)}, f32[256,128]{1,0:T(8,128)}) custom-call(s32[2]{0:T(128)} %pad_add_fusion.1.where, f32[8,256,3]{2,1,0:T(8,128)} %bitcast.78, f32[2,256,1]{2,1,0:T(8,128)} %convert_element_type.245.refs_1_, f32[256,1280]{1,0:T(8,128)} %get-tuple-element.59.refs_2_, ...), custom_call_target="tpu_custom_call" | custom-call | flops 671088640 | bytes 4587520 | tf_op jit(solution)/shard_map/head_grads/pallas_call | solution.py:371
  178.8 7.8 %collective-permute-done.28 = bf16[128,1024]{1,0:T(8,128)(2,1)S(1)} collective-permute-done((bf16[128,1024]{1,0:T(8,128)(2,1)S(1)}, bf16[128,1024]{1,0:T(8,128)(2,1)S(1)}, u32[]{:S(2)}, u32[]{:S(2)}) %collective-permute-start.28) | collective-permute-done | bytes 262176 | tf_op jit(solution)/shard_map/ppermute | solution.py:646
  194.5 13.6 %all-gather.1 = f32[2048,3]{1,0:T(8,128)} all-gather(f32[256,3]{1,0:T(8,128)} %bitcast.83), channel_id=3, replica_groups=mesh['segment'=4,'mp'=2,'dp'=4] {'segment','mp'}, dimensions={0}, use_global_device_ids=true | all-gather | bytes 27648 | tf_op jit(solution)/shard_map/all_gather | solution.py:638
  208.1 5.7 %head_grads.3 = (f32[128,1024]{1,0:T(8,128)}, bf16[128,1024]{1,0:T(8,128)(2,1)}, f32[256,128]{1,0:T(8,128)}) custom-call(s32[2]{0:T(128)} %pad_add_fusion.1.where, f32[8,256,3]{2,1,0:T(8,128)} %bitcast.77, f32[2,256,1]{2,1,0:T(8,128)} %convert_element_type.245.refs_1_, f32[256,1280]{1,0:T(8,128)} %get-tuple-element.64.refs_2_, ...), custom_call_target="tpu_custom_call" | custom-call | flops 671088640 | bytes 4587520 | tf_op jit(solution)/shard_map/head_grads/pallas_call | solution.py:371
  214.6 14.1 %section_backward.4 = (bf16[128,1024]{1,0:T(8,128)(2,1)}, f32[128,1024]{1,0:T(8,128)}, bf16[128,1024]{1,0:T(8,128)(2,1)}) custom-call(s32[2]{0:T(128)} %pad_add_fusion.1.where, bf16[256,1024]{1,0:T(8,128)(2,1)} %get-tuple-element.75.refs_0_, bf16[256,1024]{1,0:T(8,128)(2,1)} %get-tuple-element.76.refs_1_, bf16[128,1024]{1,0:T(8,128)(2,1)} %copy-done.7, ...), custom_call_target="tpu_custom_call" | custom-call | flops 6442450944 | bytes 16777216 | tf_op jit(solution)/shard_map/section_backward/pallas_call | solution.py:221
  252.4 13.1 %section_backward.5 = (bf16[128,1024]{1,0:T(8,128)(2,1)}, f32[128,1024]{1,0:T(8,128)}, bf16[128,1024]{1,0:T(8,128)(2,1)}) custom-call(s32[2]{0:T(128)} %pad_add_fusion.1.where, bf16[256,1024]{1,0:T(8,128)(2,1)} %get-tuple-element.80.refs_0_, bf16[256,1024]{1,0:T(8,128)(2,1)} %get-tuple-element.81.refs_1_, bf16[256,1024]{1,0:T(8,128)(2,1)} %get-tuple-element.82.refs_2_, ...), custom_call_target="tpu_custom_call" | custom-call | flops 6442450944 | bytes 16777216 | tf_op jit(solution)/shard_map/section_backward/pallas_call | solution.py:221
  273.0 7.5 %collective-permute-done.35.refs_2_ = bf16[128,1024]{1,0:T(8,128)(2,1)S(1)} collective-permute-done((bf16[128,1024]{1,0:T(8,128)(2,1)S(1)}, bf16[128,1024]{1,0:T(8,128)(2,1)S(1)}, u32[]{:S(2)}, u32[]{:S(2)}) %collective-permute-start.35) | collective-permute-done | bytes 262176 | tf_op jit(solution)/shard_map/ppermute | solution.py:19
  283.6 13.2 %section_backward.6 = (bf16[128,1024]{1,0:T(8,128)(2,1)}, f32[128,1024]{1,0:T(8,128)}, bf16[128,1024]{1,0:T(8,128)(2,1)}) custom-call(s32[2]{0:T(128)} %pad_add_fusion.1.where, bf16[256,1024]{1,0:T(8,128)(2,1)} %get-tuple-element.75.refs_0_, bf16[256,1024]{1,0:T(8,128)(2,1)} %get-tuple-element.76.refs_1_, bf16[128,1024]{1,0:T(8,128)(2,1)} %copy-done.11, ...), custom_call_target="tpu_custom_call" | custom-call | flops 6442450944 | bytes 16777216 | tf_op jit(solution)/shard_map/section_backward/pallas_call | solution.py:221
  303.5 8.5 %collective-permute-done.38.refs_3_ = bf16[128,1024]{1,0:T(8,128)(2,1)S(1)} collective-permute-done((bf16[128,1024]{1,0:T(8,128)(2,1)S(1)}, bf16[128,1024]{1,0:T(8,128)(2,1)S(1)}, u32[]{:S(2)}, u32[]{:S(2)}) %collective-permute-start.38) | collective-permute-done | bytes 262176 | tf_op jit(solution)/shard_map/ppermute | solution.py:19
  315.0 13.2 %section_backward.7 = (bf16[128,1024]{1,0:T(8,128)(2,1)}, f32[128,1024]{1,0:T(8,128)}, bf16[128,1024]{1,0:T(8,128)(2,1)}) custom-call(s32[2]{0:T(128)} %pad_add_fusion.1.where, bf16[256,1024]{1,0:T(8,128)(2,1)} %get-tuple-element.80.refs_0_, bf16[256,1024]{1,0:T(8,128)(2,1)} %get-tuple-element.81.refs_1_, bf16[256,1024]{1,0:T(8,128)(2,1)} %get-tuple-element.82.refs_2_, ...), custom_call_target="tpu_custom_call" | custom-call | flops 6442450944 | bytes 16777216 | tf_op jit(solution)/shard_map/section_backward/pallas_call | solution.py:221
  334.8 8.4 %collective-permute-done.41 = bf16[128,1024]{1,0:T(8,128)(2,1)S(1)} collective-permute-done((bf16[128,1024]{1,0:T(8,128)(2,1)S(1)}, bf16[128,1024]{1,0:T(8,128)(2,1)S(1)}, u32[]{:S(2)}, u32[]{:S(2)}) %collective-permute-start.41) | collective-permute-done | bytes 262176 | tf_op jit(solution)/shard_map/ppermute | solution.py:19
  359.8 12.8 %all-gather.15.cloned.1.call-done = bf16[512,1024]{1,0:T(8,128)(2,1)} async-done(((bf16[128,1024]{1,0:T(8,128)(2,1)}), bf16[512,1024]{1,0:T(8,128)(2,1)}) %all-gather.15.cloned.1.call-update) | async-done | bytes 1048592 | tf_op jit(solution)/shard_map/all_gather | solution.py:595
  387.0 16.0 %collective-permute-done.46.refs_18_ = f32[512,1]{1,0:T(8,128)S(1)} collective-permute-done((f32[512,1]{1,0:T(8,128)S(1)}, f32[512,1]{1,0:T(8,128)S(1)}, u32[]{:S(2)}, u32[]{:S(2)}) %collective-permute-start.46) | collective-permute-done | bytes 2080 | tf_op jit(solution)/shard_map/ppermute | solution.py:578
  403.1 14.7 %all-gather.13.cloned.1.call-done = bf16[512,1024]{1,0:T(8,128)(2,1)} async-done(((bf16[128,1024]{1,0:T(8,128)(2,1)}), bf16[512,1024]{1,0:T(8,128)(2,1)}) %all-gather.13.cloned.1.call-update) | async-done | bytes 1048592 | tf_op jit(solution)/shard_map/all_gather | solution.py:595
  419.8 15.8 %unit_grads.1 = f32[256,1280]{1,0:T(8,128)} custom-call(s32[2]{0:T(128)} %pad_add_fusion.2.where, bf16[4,2,128,1024]{3,2,1,0:T(8,128)(2,1)} %bitcast.57, bf16[4,2,128,1024]{3,2,1,0:T(8,128)(2,1)} %bitcast.58, bf16[4,2,128,1024]{3,2,1,0:T(8,128)(2,1)} %bitcast.59, bf16[4,2,128,1024]{3,2,1,0:T(8,128)(2,1)} %bitcast.60, bf16[4,2,128,1024]{3,2,1,0:T(8,128)(2,1)} %bitcast.61, ...), custom_call_target="tpu_custom_call" | custom-call | flops 6710886400 | bytes 7864320 | tf_op jit(solution)/shard_map/unit_grads/pallas_call | solution.py:432
  435.6 36.3 %weight_grads.2 = (f32[256,4096]{1,0:T(8,128)}, f32[4096,256]{1,0:T(8,128)}) custom-call(s32[1]{0:T(128)} %bitcast.12.where, bf16[4,2,128,1024]{3,2,1,0:T(8,128)(2,1)} %bitcast.87, bf16[4,2,128,1024]{3,2,1,0:T(8,128)(2,1)} %bitcast.88, bf16[4,2,128,1024]{3,2,1,0:T(8,128)(2,1)} %bitcast.89, bf16[4,2,128,1024]{3,2,1,0:T(8,128)(2,1)} %bitcast.90, ...), custom_call_target="tpu_custom_call" | custom-call | flops 21474836480 | bytes 33554432 | tf_op jit(solution)/shard_map/weight_grads/pallas_call | solution.py:510
  473.0 37.6 %weight_grads.3 = (f32[256,4096]{1,0:T(8,128)}, f32[4096,256]{1,0:T(8,128)}) custom-call(s32[1]{0:T(128)} %bitcast.12.where, bf16[4,2,128,1024]{3,2,1,0:T(8,128)(2,1)} %bitcast.91, bf16[4,2,128,1024]{3,2,1,0:T(8,128)(2,1)} %bitcast.92, bf16[4,2,128,1024]{3,2,1,0:T(8,128)(2,1)} %bitcast.93, ...), custom_call_target="tpu_custom_call", output_to_operand_aliasing={{0}: (19, {}), {1}: (20, {})} | custom-call | flops 21474836480 | bytes 33554432 | tf_op jit(solution)/shard_map/weight_grads/pallas_call | solution.py:510
  (264 shorter events, 175.9 us)
Async XLA Ops:
  7.2 337.0 %all-gather.17.cloned.1.call-start = ((), (), s32[]{:S(2)}) async-start(), calls=%async_computation.3 | async-start | bytes 2621440 | tf_op jit(solution)/shard_map/all_gather | solution.py:595
  106.1 10.3 %collective-permute-start.14 = (bf16[128,1024]{1,0:T(8,128)(2,1)S(1)}, bf16[128,1024]{1,0:T(8,128)(2,1)S(1)}, u32[]{:S(2)}, u32[]{:S(2)}) collective-permute-start(bf16[128,1024]{1,0:T(8,128)(2,1)S(1)} %add_convert_fusion.5), channel_id=1, source_target_pairs={{0,8},{8,16},{16,24},{1,9},{9,17},{17,25},{2,10},{10,18},{18,26},{... | collective-permute-start | bytes 786440 | tf_op jit(solution)/shard_map/ppermute | solution.py:19
  121.2 17.6 %collective-permute-start.13 = (bf16[128,1024]{1,0:T(8,128)(2,1)S(1)}, bf16[128,1024]{1,0:T(8,128)(2,1)S(1)}, u32[]{:S(2)}, u32[]{:S(2)}) collective-permute-start(bf16[128,1024]{1,0:T(8,128)(2,1)S(1)} %get-tuple-element.103.refs_0_), channel_id=1, source_target_pairs={{0,4},{4,0},{1,5},{5,1},{2,6},{6,2},{3,7},{7,3},{8,12},{12,8},{9,1... | collective-permute-start | bytes 786440 | tf_op jit(solution)/shard_map/ppermute | solution.py:23
  135.6 30.3 %collective-permute-start.16 = (bf16[128,1024]{1,0:T(8,128)(2,1)}, bf16[128,1024]{1,0:T(8,128)(2,1)S(1)}, u32[]{:S(2)}, u32[]{:S(2)}) collective-permute-start(bf16[128,1024]{1,0:T(8,128)(2,1)} %get-tuple-element.62), channel_id=1, source_target_pairs={{0,4},{4,0},{1,5},{5,1},{2,6},{6,2},{3,7},{7,3},{8,12},{12,8},{9,1... | collective-permute-start | bytes 786440 | tf_op jit(solution)/shard_map/ppermute | solution.py:23
  170.5 16.1 %collective-permute-start.28 = (bf16[128,1024]{1,0:T(8,128)(2,1)S(1)}, bf16[128,1024]{1,0:T(8,128)(2,1)S(1)}, u32[]{:S(2)}, u32[]{:S(2)}) collective-permute-start(bf16[128,1024]{1,0:T(8,128)(2,1)S(1)} %add_convert_fusion.1), channel_id=1, source_target_pairs={{8,24},{9,25},{10,26},{11,27},{12,28},{13,29},{14,30},{15,31}} | collective-permute-start | bytes 786440 | tf_op jit(solution)/shard_map/ppermute | solution.py:646
  176.0 10.6 %collective-permute-start.27 = (bf16[128,1024]{1,0:T(8,128)(2,1)S(1)}, bf16[128,1024]{1,0:T(8,128)(2,1)S(1)}, u32[]{:S(2)}, u32[]{:S(2)}) collective-permute-start(bf16[128,1024]{1,0:T(8,128)(2,1)S(1)} %add_convert_fusion.1), channel_id=1, source_target_pairs={{0,24},{1,25},{2,26},{3,27},{4,28},{5,29},{6,30},{7,31}} | collective-permute-start | bytes 786440 | tf_op jit(solution)/shard_map/ppermute | solution.py:646
  177.0 11.8 %collective-permute-start.20 = (bf16[128,1024]{1,0:T(8,128)(2,1)S(1)}, bf16[128,1024]{1,0:T(8,128)(2,1)S(1)}, u32[]{:S(2)}, u32[]{:S(2)}) collective-permute-start(bf16[128,1024]{1,0:T(8,128)(2,1)S(1)} %get-tuple-element.99.refs_0_), channel_id=1, source_target_pairs={{0,4},{4,0},{1,5},{5,1},{2,6},{6,2},{3,7},{7,3},{8,12},{12,8},{9,1... | collective-permute-start | bytes 786440 | tf_op jit(solution)/shard_map/ppermute | solution.py:23
  178.8 172.9 %all-gather.11.cloned.1.call-start = ((), (), s32[]{:S(2)}) async-start(), calls=%async_computation | async-start | bytes 2621440 | tf_op jit(solution)/shard_map/all_gather | solution.py:595
  187.2 26.7 %collective-permute-start.30 = (bf16[128,1024]{1,0:T(8,128)(2,1)S(1)}, bf16[128,1024]{1,0:T(8,128)(2,1)S(1)}, u32[]{:S(2)}, u32[]{:S(2)}) collective-permute-start(bf16[128,1024]{1,0:T(8,128)(2,1)S(1)} %fusion.65.refs_2_), channel_id=1, source_target_pairs={{0,4},{4,0},{1,5},{5,1},{2,6},{6,2},{3,7},{7,3},{8,12},{12,8},{9,1... | collective-permute-start | bytes 786440 | tf_op jit(solution)/shard_map/ppermute | solution.py:23
  213.8 16.6 %collective-permute-start.22 = (bf16[128,1024]{1,0:T(8,128)(2,1)}, bf16[128,1024]{1,0:T(8,128)(2,1)S(1)}, u32[]{:S(2)}, u32[]{:S(2)}) collective-permute-start(bf16[128,1024]{1,0:T(8,128)(2,1)} %get-tuple-element.72), channel_id=1, source_target_pairs={{0,4},{4,0},{1,5},{5,1},{2,6},{6,2},{3,7},{7,3},{8,12},{12,8},{9,1... | collective-permute-start | bytes 786440 | tf_op jit(solution)/shard_map/ppermute | solution.py:23
  230.4 12.0 %collective-permute-start.25 = (bf16[128,1024]{1,0:T(8,128)(2,1)S(1)}, bf16[128,1024]{1,0:T(8,128)(2,1)S(1)}, u32[]{:S(2)}, u32[]{:S(2)}) collective-permute-start(bf16[128,1024]{1,0:T(8,128)(2,1)S(1)} %add_convert_fusion.3), channel_id=1, source_target_pairs={{16,24},{17,25},{18,26},{19,27},{20,28},{21,29},{22,30},{23,31}} | collective-permute-start | bytes 786440 | tf_op jit(solution)/shard_map/ppermute | solution.py:646
  231.1 15.4 %collective-permute-start.24 = (bf16[128,1024]{1,0:T(8,128)(2,1)S(1)}, bf16[128,1024]{1,0:T(8,128)(2,1)S(1)}, u32[]{:S(2)}, u32[]{:S(2)}) collective-permute-start(bf16[128,1024]{1,0:T(8,128)(2,1)S(1)} %add_convert_fusion.3), channel_id=1, source_target_pairs={{8,24},{9,25},{10,26},{11,27},{12,28},{13,29},{14,30},{15,31}} | collective-permute-start | bytes 786440 | tf_op jit(solution)/shard_map/ppermute | solution.py:646
  235.4 11.2 %collective-permute-start.23 = (bf16[128,1024]{1,0:T(8,128)(2,1)S(1)}, bf16[128,1024]{1,0:T(8,128)(2,1)S(1)}, u32[]{:S(2)}, u32[]{:S(2)}) collective-permute-start(bf16[128,1024]{1,0:T(8,128)(2,1)S(1)} %add_convert_fusion.3), channel_id=1, source_target_pairs={{0,24},{1,25},{2,26},{3,27},{4,28},{5,29},{6,30},{7,31}} | collective-permute-start | bytes 786440 | tf_op jit(solution)/shard_map/ppermute | solution.py:646
  270.2 10.3 %collective-permute-start.35 = (bf16[128,1024]{1,0:T(8,128)(2,1)S(1)}, bf16[128,1024]{1,0:T(8,128)(2,1)S(1)}, u32[]{:S(2)}, u32[]{:S(2)}) collective-permute-start(bf16[128,1024]{1,0:T(8,128)(2,1)S(1)} %fusion.52), channel_id=1, source_target_pairs={{8,0},{16,8},{24,16},{9,1},{17,9},{25,17},{10,2},{18,10},{26,18},{... | collective-permute-start | bytes 786440 | tf_op jit(solution)/shard_map/ppermute | solution.py:19
  282.7 89.9 %all-gather.15.cloned.1.call-start = ((), (), s32[]{:S(2)}) async-start(), calls=%async_computation.2 | async-start | bytes 1310720 | tf_op jit(solution)/shard_map/all_gather | solution.py:595
  301.4 10.6 %collective-permute-start.38 = (bf16[128,1024]{1,0:T(8,128)(2,1)S(1)}, bf16[128,1024]{1,0:T(8,128)(2,1)S(1)}, u32[]{:S(2)}, u32[]{:S(2)}) collective-permute-start(bf16[128,1024]{1,0:T(8,128)(2,1)S(1)} %fusion.47), channel_id=1, source_target_pairs={{8,0},{16,8},{24,16},{9,1},{17,9},{25,17},{10,2},{18,10},{26,18},{... | collective-permute-start | bytes 786440 | tf_op jit(solution)/shard_map/ppermute | solution.py:19
  332.9 10.3 %collective-permute-start.41 = (bf16[128,1024]{1,0:T(8,128)(2,1)S(1)}, bf16[128,1024]{1,0:T(8,128)(2,1)S(1)}, u32[]{:S(2)}, u32[]{:S(2)}) collective-permute-start(bf16[128,1024]{1,0:T(8,128)(2,1)S(1)} %fusion.42), channel_id=1, source_target_pairs={{8,0},{16,8},{24,16},{9,1},{17,9},{25,17},{10,2},{18,10},{26,18},{... | collective-permute-start | bytes 786440 | tf_op jit(solution)/shard_map/ppermute | solution.py:19
  344.1 73.7 %all-gather.13.cloned.1.call-start = ((), (), s32[]{:S(2)}) async-start(), calls=%async_computation.1 | async-start | bytes 1310720 | tf_op jit(solution)/shard_map/all_gather | solution.py:595
  344.1 74.3 %collective-permute-start.44 = (bf16[4,2,128,1024]{3,2,1,0:T(8,128)(2,1)}, bf16[4,2,128,1024]{3,2,1,0:T(8,128)(2,1)S(1)}, u32[]{:S(2)}, u32[]{:S(2)}) collective-permute-start(bf16[4,2,128,1024]{3,2,1,0:T(8,128)(2,1)} %bitcast.56), channel_id=1, source_target_pairs={{0,4},{4,0},{1,5},{5,1},{2,6},{6,2},{3,7},{7,3},{8,12},{12,8},{9,1... | collective-permute-start | bytes 6291464 | tf_op jit(solution)/shard_map/ppermute | solution.py:23
  351.7 84.0 %collective-permute-start.21 = (bf16[4,2,128,1024]{3,2,1,0:T(8,128)(2,1)}, bf16[4,2,128,1024]{3,2,1,0:T(8,128)(2,1)}, u32[]{:S(2)}, u32[]{:S(2)}) collective-permute-start(bf16[4,2,128,1024]{3,2,1,0:T(8,128)(2,1)} %bitcast.86), channel_id=1, source_target_pairs={{0,4},{4,0},{1,5},{5,1},{2,6},{6,2},{3,7},{7,3},{8,12},{12,8},{9,1... | collective-permute-start | bytes 6291464 | tf_op jit(solution)/shard_map/ppermute | solution.py:23
  372.6 63.0 %collective-permute-start.43 = (bf16[4,128,1024]{2,1,0:T(8,128)(2,1)}, bf16[4,128,1024]{2,1,0:T(8,128)(2,1)}, u32[]{:S(2)}, u32[]{:S(2)}) collective-permute-start(bf16[4,128,1024]{2,1,0:T(8,128)(2,1)} %bitcast.95), channel_id=1, source_target_pairs={{0,4},{4,0},{1,5},{5,1},{2,6},{6,2},{3,7},{7,3},{8,12},{12,8},{9,1... | collective-permute-start | bytes 3145736 | tf_op jit(solution)/shard_map/ppermute | solution.py:23
  375.0 28.1 %collective-permute-start.46 = (f32[512,1]{1,0:T(8,128)S(1)}, f32[512,1]{1,0:T(8,128)S(1)}, u32[]{:S(2)}, u32[]{:S(2)}) collective-permute-start(f32[512,1]{1,0:T(8,128)S(1)} %copy.33.refs_16_), channel_id=1, source_target_pairs={{0,2},{1,3},{2,0},{3,1},{4,6},{5,7},{6,4},{7,5},{8,10},{9,11},{10,... | collective-permute-start | bytes 6152 | tf_op jit(solution)/shard_map/ppermute | solution.py:578
  382.2 36.2 %collective-permute-start.45 = (f32[512,1]{1,0:T(8,128)S(1)}, f32[512,1]{1,0:T(8,128)S(1)}, u32[]{:S(2)}, u32[]{:S(2)}) collective-permute-start(f32[512,1]{1,0:T(8,128)S(1)} %copy.33.refs_16_), channel_id=1, source_target_pairs={{0,1},{1,2},{2,3},{3,0},{4,5},{5,6},{6,7},{7,4},{8,9},{9,10},{10,1... | collective-permute-start | bytes 6152 | tf_op jit(solution)/shard_map/ppermute | solution.py:578
  417.8 54.2 %collective-permute-start.42 = (bf16[4,128,1024]{2,1,0:T(8,128)(2,1)}, bf16[4,128,1024]{2,1,0:T(8,128)(2,1)S(1)}, u32[]{:S(2)}, u32[]{:S(2)}) collective-permute-start(bf16[4,128,1024]{2,1,0:T(8,128)(2,1)} %bitcast.100), channel_id=1, source_target_pairs={{0,4},{4,0},{1,5},{5,1},{2,6},{6,2},{3,7},{7,3},{8,12},{12,8},{9,1... | collective-permute-start | bytes 3145736 | tf_op jit(solution)/shard_map/ppermute | solution.py:23
  (75 other events, 541.5 us)
Sparse Core Ops, SparseCore 0:
  178.9 47.9 all-gather.16
  282.8 43.7 all-gather.10
  344.2 28.3 all-gather.14
  374.0 43.6 all-gather.12

commit v6 on v5

--- a/solution.py
+++ b/solution.py
@@ -25,11 +25,13 @@
 
 def gelu_parts(pre_vals):
     coeff = 0.7978845608
-    square = pre_vals * pre_vals
-    inner = coeff * pre_vals * (1.0 + 0.044715 * square)
-    half = 0.5 * (1.0 + jnp.tanh(inner))
-    value = pre_vals * half
-    slope = half + 2.0 * value * (1.0 - half) * coeff * (1.0 + 3.0 * 0.044715 * square)
+    pre = pre_vals.astype(BF16)
+    square = pre * pre
+    inner = pre * (square * BF16(coeff * 0.044715) + BF16(coeff))
+    half = jnp.tanh(inner) * BF16(0.5) + BF16(0.5)
+    value = pre * half
+    bend = square * BF16(6.0 * coeff * 0.044715) + BF16(2.0 * coeff)
+    slope = half + value * (BF16(1.0) - half) * bend
     return (value, slope)
 
 
@@ -109,9 +111,11 @@
     return pl.BlockSpec(shape, lambda *_: (0,) * len(shape))
 
 
-def forward_kernel(halves, has_arrived, where, own, *refs):
+def forward_kernel(halves, has_arrived, ties, where, own, *refs):
+    refs = refs[ties:]
     if has_arrived:
         arrived, refs = refs[:halves], refs[halves:]
+    live = where[2] == 1
     w_in, w_out, rows_out, mine_out, keep, *send, whole, normed, total = refs
     step = pl.program_id(0)
 
@@ -126,11 +130,13 @@
         normed[...] = normalised(rows)
         total[...] = jnp.zeros_like(total)
 
-    values = []
-    for at, size in pieces_of(w_in.shape[1]):
-        value, _ = gelu_parts(dot(normed[...], w_in[:, at : at + size]))
-        values.append(value.astype(BF16))
-    total[...] += dot(jnp.concatenate(values, axis=1), w_out[...])
+    @pl.when(live)
+    def _():
+        values = []
+        for at, size in pieces_of(w_in.shape[1]):
+            value, _ = gelu_parts(dot(normed[...], w_in[:, at : at + size]))
+            values.append(value)
+        total[...] += dot(jnp.concatenate(values, axis=1), w_out[...])
 
     @pl.when(step == pl.num_programs(0) - 1)
     def _():
@@ -141,22 +147,23 @@
             keep[...] = total[...]
 
 
-def forward_section(where, text, at, halves, arrived, w_in, w_out):
+def forward_section(where, text, at, halves, arrived, w_in, w_out, ties):
     _, rows, width = text.shape
     hidden = w_in.shape[1]
     tile = tile_of(hidden, 1024)
     full, part = (rows, width), (rows // halves, width)
     shapes = [(full, BF16), (part, BF16), (part, F32)] + [(part, BF16)] * (halves - 1)
     return pl.pallas_call(
-        functools.partial(forward_kernel, halves, bool(arrived)),
+        functools.partial(forward_kernel, halves, bool(arrived), len(ties)),
         grid_spec=pltpu.PrefetchScalarGridSpec(
             num_scalar_prefetch=1,
             grid=(hidden // tile,),
             in_specs=[
                 pl.BlockSpec((None, rows, width), lambda j, s: (at, 0, 0)),
+                *[pl.BlockSpec(memory_space=pl.ANY)] * len(ties),
                 *[whole_spec(part)] * len(arrived),
-                pl.BlockSpec((width, tile), lambda j, s: (0, j)),
-                pl.BlockSpec((tile, width), lambda j, s: (j, 0)),
+                pl.BlockSpec((width, tile), lambda j, s: (0, j * s[2])),
+                pl.BlockSpec((tile, width), lambda j, s: (j * s[2], 0)),
             ],
             out_specs=[whole_spec(shape) for shape, _ in shapes],
             scratch_shapes=[pltpu.VMEM(full, BF16), pltpu.VMEM(full, BF16), pltpu.VMEM(full, F32)],
@@ -169,7 +176,7 @@
             transcendentals=rows * hidden,
         ),
         name="section_forward",
-    )(where, text, *arrived, w_in, w_out)
+    )(where, text, *ties, *arrived, w_in, w_out)
 
 
 def total_of(pieces):
@@ -183,7 +190,9 @@
     return (grads.astype(F32) + norm_back(rows, total_of(pieces))).astype(BF16)
 
 
-def backward_kernel(owners, halves, where, *refs):
+def backward_kernel(owners, halves, ties, where, *refs):
+    refs = refs[ties:]
+    live = where[2] == 1
     stashed, refs = refs[: len(owners)], refs[len(owners) :]
     arrived, refs = refs[:halves], refs[halves:]
     w_in, w_out, mine_rows, keep, *send, rows, grads, normed, total = refs
@@ -197,11 +206,13 @@
         normed[...] = normalised(rows[...])
         total[...] = jnp.zeros_like(total)
 
-    dpres = []
-    for at, size in pieces_of(w_in.shape[1]):
-        _, slope = gelu_parts(dot(normed[...], w_in[:, at : at + size]))
-        dpres.append((dot_t(grads[...], w_out[at : at + size, :]) * slope).astype(BF16))
-    total[...] += dot_t(jnp.concatenate(dpres, axis=1), w_in[...])
+    @pl.when(live)
+    def _():
+        dpres = []
+        for at, size in pieces_of(w_in.shape[1]):
+            _, slope = gelu_parts(dot(normed[...], w_in[:, at : at + size]))
+            dpres.append(dot_t(grads[...], w_out[at : at + size, :]).astype(BF16) * slope)
+        total[...] += dot_t(jnp.concatenate(dpres, axis=1), w_in[...])
 
     @pl.when(step == pl.num_programs(0) - 1)
     def _():
@@ -212,22 +223,23 @@
             keep[...] = total[...]
 
 
-def backward_section(where, halves, options, arrived, w_in, w_out):
+def backward_section(where, halves, options, arrived, w_in, w_out, ties):
     width, hidden = w_in.shape
     rows = options[0][1].shape[0]
     tile = tile_of(hidden, 1024)
     full, part = (rows, width), (rows // halves, width)
     shapes = [(part, BF16), (part, F32)] + [(part, BF16)] * (halves - 1)
     return pl.pallas_call(
-        functools.partial(backward_kernel, tuple(at for at, _ in options), halves),
+        functools.partial(backward_kernel, tuple(at for at, _ in options), halves, len(ties)),
         grid_spec=pltpu.PrefetchScalarGridSpec(
             num_scalar_prefetch=1,
             grid=(hidden // tile,),
-            in_specs=[whole_spec(full)] * len(options)
+            in_specs=[pl.BlockSpec(memory_space=pl.ANY)] * len(ties)
+            + [whole_spec(full)] * len(options)
             + [whole_spec(part)] * halves
             + [
-                pl.BlockSpec((width, tile), lambda j, s: (0, j)),
-                pl.BlockSpec((tile, width), lambda j, s: (j, 0)),
+                pl.BlockSpec((width, tile), lambda j, s: (0, j * s[2])),
+                pl.BlockSpec((tile, width), lambda j, s: (j * s[2], 0)),
             ],
             out_specs=[whole_spec(shape) for shape, _ in shapes],
             scratch_shapes=[pltpu.VMEM(full, BF16)] * 3 + [pltpu.VMEM(full, F32)],
@@ -240,15 +252,20 @@
             transcendentals=rows * hidden,
         ),
         name="section_backward",
-    )(where, *[option for _, option in options], *arrived, w_in, w_out)
-
-
-def lane_fill(columns, shape):
-    lane = lax.broadcasted_iota(jnp.int32, shape, 1)
-    filled = jnp.zeros(shape, F32)
-    for at, column in enumerate(columns):
-        filled = jnp.where(lane == at, column, filled)
-    return filled
+    )(where, *ties, *[option for _, option in options], *arrived, w_in, w_out)
+
+
+def row_table(rows):
+    pad = jnp.zeros((8 - len(rows), rows[0].shape[1]), F32)
+    return jnp.concatenate([*rows, pad], axis=0)
+
+
+def as_row(column):
+    return jnp.broadcast_to(column, (column.shape[0], 128)).T[0:1, :]
+
+
+def as_columns(row):
+    return jnp.broadcast_to(row, (128, row.shape[1])).T
 
 
 def logits_kernel(halves, where, *refs):
@@ -289,7 +306,7 @@
         top = jnp.max(peak[...], axis=-1, keepdims=True)
         mass = jnp.sum(total[...] * jnp.exp(peak[...] - top), axis=-1, keepdims=True)
         summed = jnp.sum(target[...], axis=-1, keepdims=True)
-        stats[...] = lane_fill([top, mass, summed], stats.shape)
+        stats[...] = row_table([as_row(top), as_row(mass), as_row(summed)])
 
 
 def head_logits(where, final, w_unit, counts, at):
@@ -311,13 +328,13 @@
             ],
             out_specs=[
                 pl.BlockSpec((rows, tile), lambda t, s: (0, t)),
-                whole_spec((rows, 128)),
+                whole_spec((8, rows)),
             ],
             scratch_shapes=[pltpu.VMEM((rows, width), BF16)] + [pltpu.VMEM((rows, lanes), F32)] * 3,
         ),
         out_shape=[
             jax.ShapeDtypeStruct((rows, vocab), F32),
-            jax.ShapeDtypeStruct((rows, 128), F32),
+            jax.ShapeDtypeStruct((8, rows), F32),
         ],
         compiler_params=params(VMEM_MIB),
         cost_estimate=cost(
@@ -329,26 +346,28 @@
     )(where, *final, w_unit, counts)
 
 
-def head_grads_kernel(denom, halves, where, *refs):
-    stats, lengths, logits, counts, w_unit, keep, *send, results, shift, total = refs
+def head_grads_kernel(denom, halves, tables, where, *refs):
+    stats, refs = refs[:tables], refs[tables:]
+    lengths, logits, counts, w_unit, keep, *send, results, shift, total = refs
     step = pl.program_id(0)
 
     @pl.when(step == 0)
     def _():
-        values = [stats[at] for at in range(stats.shape[0])]
-        top = values[0][:, 0:1]
+        values = [ref[...] for ref in stats]
+        top = values[0][0:1, :]
         for table in values[1:]:
-            top = jnp.maximum(top, table[:, 0:1])
-        mass = sum(table[:, 1:2] * jnp.exp(table[:, 0:1] - top) for table in values)
-        target = sum(table[:, 2:3] for table in values)
+            top = jnp.maximum(top, table[0:1, :])
+        mass = sum(table[1:2, :] * jnp.exp(table[0:1, :] - top) for table in values)
+        target = sum(table[2:3, :] for table in values)
         lse = top + jnp.log(mass)
-        shift[...] = lse - jnp.log(lengths[...] * (1.0 / denom))
-        results[...] = lane_fill([shift[...], lengths[...] * lse - target], results.shape)
+        moved = lse - jnp.log(lengths[...] * (1.0 / denom))
+        shift[...] = as_columns(moved)
+        results[...] = row_table([moved, lengths[...] * lse - target])
         total[...] = jnp.zeros_like(total)
 
     columns = []
     for start, size in pieces_of(w_unit.shape[1]):
-        exped = jnp.exp(logits[:, start : start + size] - shift[...])
+        exped = jnp.exp(logits[:, start : start + size] - shift[:, 0:1])
         counted = counts[:, start : start + size].astype(F32) * (1.0 / denom)
         columns.append((exped - counted).astype(BF16))
     total[...] += dot_t(jnp.concatenate(columns, axis=1), w_unit[...])
@@ -367,21 +386,21 @@
     width = w_unit.shape[0]
     tile = tile_of(vocab, 640)
     part = (rows // halves, width)
-    shapes = [(part, F32)] + [(part, BF16)] * (halves - 1) + [((rows, 128), F32)]
+    shapes = [(part, F32)] + [(part, BF16)] * (halves - 1) + [((8, rows), F32)]
     return pl.pallas_call(
-        functools.partial(head_grads_kernel, denom, halves),
+        functools.partial(head_grads_kernel, denom, halves, len(stats)),
         grid_spec=pltpu.PrefetchScalarGridSpec(
             num_scalar_prefetch=1,
             grid=(vocab // tile,),
             in_specs=[
-                whole_spec(stats.shape),
-                pl.BlockSpec((None, rows, 1), lambda t, s: (at, 0, 0)),
+                *[whole_spec((8, rows))] * len(stats),
+                pl.BlockSpec((None, 1, rows), lambda t, s: (at, 0, 0)),
                 pl.BlockSpec((rows, tile), lambda t, s: (0, t)),
                 pl.BlockSpec((None, rows, tile), lambda t, s: (at, 0, t)),
                 pl.BlockSpec((width, tile), lambda t, s: (0, t)),
             ],
             out_specs=[whole_spec(shape) for shape, _ in shapes],
-            scratch_shapes=[pltpu.VMEM((rows, 1), F32), pltpu.VMEM((rows, width), F32)],
+            scratch_shapes=[pltpu.VMEM((rows, 128), F32), pltpu.VMEM((rows, width), F32)],
         ),
         out_shape=[jax.ShapeDtypeStruct(*shape) for shape in shapes],
         compiler_params=params(VMEM_MIB),
@@ -391,14 +410,14 @@
             transcendentals=rows * vocab,
         ),
         name="head_grads",
-    )(where, stats, lengths, logits, counts, w_unit)
+    )(where, *stats, lengths, logits, counts, w_unit)
 
 
 def unit_kernel(blocks, tables, share, denom, where, *refs):
     x_refs, refs = refs[: len(blocks)], refs[len(blocks) :]
     shifts, refs = refs[:tables], refs[tables:]
     counts, refs = refs[:tables], refs[tables:]
-    w_unit, grad, normed, normed_t = refs
+    w_unit, grad, normed, normed_t, *columns_of = refs
     half = x_refs[0].shape[0]
     rows = normed.shape[0] // tables
 
@@ -412,11 +431,13 @@
             normed[place, :] = normalised(ref[...])
         columns = pl.ds(pl.multiple_of(where[0] * share, share), share)
         normed_t[...] = normed[:, columns].astype(F32).T.astype(BF16)
+        for shift, column in zip(shifts, columns_of):
+            column[...] = as_columns(shift[...])
 
     logits = dot(normed[...], w_unit[...])
     dlogits = []
     for k in range(tables):
-        exped = jnp.exp(logits[k * rows : (k + 1) * rows] - shifts[k][...])
+        exped = jnp.exp(logits[k * rows : (k + 1) * rows] - columns_of[k][:, 0:1])
         counted = counts[k][...].astype(F32) * (1.0 / denom)
         dlogits.append((exped - counted).astype(BF16))
     grad[...] = dot(normed_t[...], jnp.concatenate(dlogits, axis=0))
@@ -426,7 +447,7 @@
     width, vocab = w_unit.shape
     tile = tile_of(vocab, 256)
     half = x_parts[0][0].shape[2]
-    rows = shifts[0].shape[0]
+    rows = shifts[0].shape[1]
     tables = len(shifts)
     blocks = tuple(block for _, _, block in x_parts)
     return pl.pallas_call(
@@ -435,13 +456,14 @@
             num_scalar_prefetch=1,
             grid=(vocab // tile,),
             in_specs=[pl.BlockSpec((None, None, half, width), index) for _, index, _ in x_parts]
-            + [whole_spec((rows, 1))] * tables
+            + [whole_spec((1, rows))] * tables
             + [pl.BlockSpec((rows, tile), lambda j, s: (0, j))] * tables
             + [pl.BlockSpec((width, tile), lambda j, s: (0, j))],
             out_specs=pl.BlockSpec((share, tile), lambda j, s: (0, j)),
             scratch_shapes=[
                 pltpu.VMEM((rows * tables, width), BF16),
                 pltpu.VMEM((share, rows * tables), BF16),
+                *[pltpu.VMEM((rows, 128), F32)] * tables,
             ],
         ),
         out_shape=jax.ShapeDtypeStruct((share, vocab), F32),
@@ -476,9 +498,9 @@
 
     for at, size in pieces_of(w_in.shape[1]):
         value, slope = gelu_parts(dot(normed[...], w_in[:, at : at + size]))
-        dpre = (dot_t(grads[...], w_out[at : at + size, :]) * slope).astype(BF16)
+        dpre = dot_t(grads[...], w_out[at : at + size, :]).astype(BF16) * slope
         now_first = dot(normed_t[...], dpre)
-        now_second = dot(grads_t[...], value.astype(BF16)).T
+        now_second = dot(grads_t[...], value).T
         if adding:
             now_first = old_first[:, at : at + size] + now_first
             now_second = old_second[at : at + size, :] + now_second
@@ -557,17 +579,20 @@
     last = segments - 1
     pair = mp_size == 2
     halves = 2 if pair else 1
-    where = jnp.stack([seg, mp_at])
+    chunks = CHUNKS
+    def place(live_at):
+        live = (live_at >= 0) & (live_at < chunks)
+        return jnp.stack([seg, mp_at, jnp.asarray(live, jnp.int32)])
+
     first = w_in[0]
     second = w_out[0]
-    chunks = CHUNKS
     rows = micro * row_count // chunks
     text = text_rows.reshape(chunks, rows, width)
     vocab_part = w_unit.shape[1]
     unit_count = unit_targets.shape[1]
     denom = float(micro * unit_count * dp_size)
     lengths = durations[:, 0, :]
-    length_f = lengths.astype(F32).reshape(chunks, rows, 1)
+    length_f = lengths.astype(F32).reshape(chunks, 1, rows)
     ends = jnp.cumsum(lengths, axis=-1)
     own_ids = (seg * mp_size + mp_at) * vocab_part + jnp.arange(vocab_part, dtype=jnp.int32)
 
@@ -595,51 +620,80 @@
         came = lax.all_gather(mine, "dp")
         return [came, swapped(came)] if pair else [came]
 
+    def all_tables(table):
+        if not pair:
+            return [t for t in lax.all_gather(table, ("segment", "mp"))]
+        count = segments * mp_size
+        return [table] + [
+            lax.ppermute(table, ("segment", "mp"), [(i, (i + k) % count) for i in range(count)])
+            for k in range(1, count)
+        ]
+
     stash, x_halves, grads, finals, results = [], [], [], [], []
     sums = None
     x_gathered = None
     f_hop = b_hop = None
 
-    def x_parts(at):
+    def x_parts(at, side):
         return [
-            (source, lambda j, s, k=k: (k, at, 0, 0))
-            for source in x_gathered
-            for k in range(dp_size)
-        ]
-
-    def g_parts(sources):
-        return [
-            (source, lambda j, s, k=k: (k, 0, 0)) for source in sources for k in range(dp_size)
+            (x_gathered[side], lambda j, s, k=k: (k, at, 0, 0)) for k in range(dp_size)
         ]
 
     clocks = 2 * segments + chunks - 1
     for clock in range(clocks):
         f_out = b_out = None
+        f_ties, b_ties = [], []
+        head_at = clock - segments
+        if 0 <= head_at < chunks:
+            final = chosen(
+                seg,
+                [(last, f_hop)]
+                + [(to, lax.ppermute(f_hop, "segment", [(last, to)])) for to in range(last)],
+            )
+            finals.append(final)
+            logits, stats = head_logits(place(0), both(final), w_unit, head_counts, head_at)
+            f_ties = [logits]
         if clock < segments + chunks - 1:
             arrived = [] if clock == 0 else both(shifted(f_hop, "segment", 1))
+            if clock == segments - 1:
+                f_ties = unit_hits
             rows_in, mine, keep, *send = forward_section(
-                where, text, min(clock, chunks - 1), halves, arrived, first, second
+                place(clock - seg),
+                text,
+                min(clock, chunks - 1),
+                halves,
+                arrived,
+                first,
+                second,
+                f_ties,
             )
             stash.append(rows_in)
             x_halves.append(mine)
             pieces = reduced(keep, send)
             f_out = total_of(pieces if pair else [mine, *pieces]).astype(BF16)
+        if clock == segments + chunks - 2:
+            x_half = jnp.stack(
+                [
+                    chosen(seg, [(s, x_halves[b + s]) for s in range(segments)])
+                    for b in range(chunks)
+                ]
+            )
+            x_gathered = gathered_rows(x_half)
         if clock >= segments:
-            at = clock - segments
-            arrived = None if at == 0 else shifted(b_hop, "segment", -1)
-            if at < chunks:
-                final = chosen(
-                    seg,
-                    [(last, f_hop)]
-                    + [(to, lax.ppermute(f_hop, "segment", [(last, to)])) for to in range(last)],
+            arrived = None if head_at == 0 else shifted(b_hop, "segment", -1)
+            if head_at < chunks:
+                keep, *send, result = head_grads(
+                    place(0),
+                    halves,
+                    all_tables(stats),
+                    length_f,
+                    logits,
+                    head_counts,
+                    head_at,
+                    w_unit,
+                    denom,
                 )
-                finals.append(final)
-                logits, stats = head_logits(where, both(final), w_unit, head_counts, at)
-                tables = lax.all_gather(stats[:, 0:3], ("segment", "mp"))
-                keep, *send, result = head_grads(
-                    where, halves, tables, length_f, logits, head_counts, at, w_unit, denom
-                )
-                results.append(result[:, 0:2])
+                results.append(result)
                 dnorm = total_of(reduced(keep, send)).astype(BF16)
                 dnorm = total_of(
                     [dnorm]
@@ -649,6 +703,11 @@
                 arrived = (
                     grad_final if arrived is None else jnp.where(seg == last, grad_final, arrived)
                 )
+                if head_at == chunks - 1:
+                    unit_rows = gathered_rows(jnp.stack(finals))
+                    shifts = around(
+                        jnp.concatenate([result[0:1, :] for result in results], axis=1)
+                    )
             grads.append(arrived)
             if clock < clocks - 1:
                 options = []
@@ -656,37 +715,36 @@
                     stage = clock - 2 * segments + 1 + 2 * other
                     if 0 <= stage < len(stash):
                         options.append((other, stash[stage]))
+                if clock == clocks - 3:
+                    b_ties = [*shifts, *x_gathered]
+                if clock == clocks - 2:
+                    b_ties = unit_rows
                 mine, keep, *send = backward_section(
-                    where, halves, options, both(arrived), first, second
+                    place(head_at - last + seg),
+                    halves,
+                    options,
+                    both(arrived),
+                    first,
+                    second,
+                    b_ties,
                 )
                 b_out = finish_backward(mine, arrived, reduced(keep, send))
-        if clock == segments + chunks - 2:
-            x_half = jnp.stack(
-                [
-                    chosen(seg, [(s, x_halves[b + s]) for s in range(segments)])
-                    for b in range(chunks)
-                ]
-            )
-            x_gathered = gathered_rows(x_half)
-        if clock == segments + chunks - 1:
-            unit_rows = gathered_rows(jnp.stack(finals))
         if clock >= 2 * segments - 1:
             at = clock - 2 * segments + 1
             mine = chosen(seg, [(s, grads[at + last - s]) for s in range(segments)])
-            sums = weight_grads(
-                dp_at[None],
-                x_parts(at),
-                g_parts(gathered_rows(mine)),
-                first,
-                second,
-                sums,
-                width // dp_size,
-            )
+            for side, source in enumerate(gathered_rows(mine)):
+                sums = weight_grads(
+                    dp_at[None],
+                    x_parts(at, side),
+                    [(source, lambda j, s, k=k: (k, 0, 0)) for k in range(dp_size)],
+                    first,
+                    second,
+                    sums,
+                    width // dp_size,
+                )
         f_hop, b_hop = f_out, b_out
 
-    results = jnp.stack(results)
-    loss = (jnp.sum(results[:, :, 1]) / denom)[None]
-    shifts = around(results[:, :, 0].reshape(-1, 1))
+    loss = (sum(jnp.sum(result[1, :]) for result in results) / denom)[None]
     unit_parts = [
         (
             source,

time: 527 us -> 489 us (0.928)
  Pallas kernels: 225 us -> 186 us
  blocking collectives: 29.1 us -> 0 us
  starting transfers between devices: 74.6 us -> 97.4 us
    all_gather x2 -> x0, blocking collectives: 29.1 us -> none  [on_device(): tables = lax.all_gather(stats[:, 0:3], ('segment', 'mp'))]
    pallas_call x7, Pallas kernels: 71.8 us -> 46.2 us  [the longest x5 36.5 us: forward_section(): pl.pallas_call(functools.partial(forward_kernel, halves, bool(arrived), l...]
    ppermute x0 -> x14, starting transfers between devices: none -> 22.2 us  [all_tables(): lax.ppermute(table, ('segment', 'mp'), [(i, (i + k) % count) for i in ran...]
    ppermute x6, waiting for transfers between devices: 21.8 us -> 0.2 us  [around(): came.append(lax.ppermute(block, 'dp', route))]
    pallas_call x4, Pallas kernels: 53.6 us -> 35.4 us  [backward_section(): pl.pallas_call(functools.partial(backward_kernel, tuple((at for at, _ in...]
    all_gather x4, waiting for transfers between devices: 27.5 us -> 39.4 us  [gathered_rows(): came = lax.all_gather(mine, 'dp')]
    ppermute x6, starting transfers between devices: 12.5 us -> 19.6 us  [on_device(): lax.ppermute(dnorm, 'segment', [(j, last)])]
    ppermute x0 -> x14, waiting for transfers between devices: none -> 5.65 us  [all_tables(): lax.ppermute(table, ('segment', 'mp'), [(i, (i + k) % count) for i in ran...]
  transfers between devices with their start and end apart: 55 -> 69, of which waited for: 29 -> 27; matrix products, arithmetic and copies ran while one was open for 7% -> 7% of each run, Pallas kernels for 27% -> 27%
where the time goes in v6:
time: 489 us; the launch traced here: 480 us
  Pallas kernels  186 us (38%)
  waiting for transfers between devices  125 us (26%)
  starting transfers between devices  97.4 us (20%)
  other arithmetic  32.1 us (7%)
  between operations  17.3 us (4%)
  matrix products  12.8 us (3%)
  local copies, waits for them, and re-layouts  10.4 us (2%)
    pallas_call x4, Pallas kernels, weight_grads(): pl.pallas_call(functools.partial(weight_kernel, blocks, adding, share), g...  78.4 us
    ppermute x8, waiting for transfers between devices, shifted(): return lax.ppermute(block, axis, route)  49.4 us
    all_gather x4, waiting for transfers between devices, gathered_rows(): came = lax.all_gather(mine, 'dp')  39.4 us
    pallas_call x5, Pallas kernels, forward_section(): pl.pallas_call(functools.partial(forward_kernel, halves, bool(arrived), l...  36.5 us
    pallas_call x4, Pallas kernels, backward_section(): pl.pallas_call(functools.partial(backward_kernel, tuple((at for at, _ in...  35.4 us
    ppermute x8, starting transfers between devices, shifted(): return lax.ppermute(block, axis, route)  26.1 us
    ppermute x14, starting transfers between devices, all_tables(): lax.ppermute(table, ('segment', 'mp'), [(i, (i + k) % count) for i in ran...  22.2 us
    ppermute x6, starting transfers between devices, on_device(): lax.ppermute(dnorm, 'segment', [(j, last)])  19.6 us
  transfers between devices with their start and end apart: 69, of which 27 were waited for; matrix products, arithmetic and copies ran while one was open for 7% of the time, Pallas kernels for 27%

profile of v6, /device:TPU:11, one launch (start us, length us, event | category | flops | bytes accessed | tf_op | source)
XLA Modules:
  0.0 480.2 jit_solution(15733678828140828427)
XLA Ops:
  19.6 10.9 %collective-permute-done.4.refs_0_ = bf16[128,1024]{1,0:T(8,128)(2,1)S(1)} collective-permute-done((bf16[128,1024]{1,0:T(8,128)(2,1)S(1)}, bf16[128,1024]{1,0:T(8,128)(2,1)S(1)}, u32[]{:S(2)}, u32[]{:S(2)}) %collective-permute-start.4) | collective-permute-done | bytes 262176 | tf_op jit(solution)/shard_map/ppermute | solution.py:19
  33.2 11.0 %section_forward.6 = (bf16[256,1024]{1,0:T(8,128)(2,1)}, bf16[128,1024]{1,0:T(8,128)(2,1)}, f32[128,1024]{1,0:T(8,128)}, bf16[128,1024]{1,0:T(8,128)(2,1)}) custom-call(s32[3]{0:T(128)} %get-tuple-element.127.where, bf16[2,256,1024]{2,1,0:T(8,128)(2,1)} %bitcast.78, bf16[128,1024]{1,0:T(8,128)(2,1)} %copy-done.23, bf16[128,1024]{1,0:T(8,128)(2,1)} %copy-done.24, ...), custom_call_target="tpu_custom_call" | custom-call | flops 4294967296 | bytes 16777216 | tf_op jit(solution)/shard_map/section_forward/pallas_call | solution.py:156
  61.7 10.9 %section_forward.7 = (bf16[256,1024]{1,0:T(8,128)(2,1)}, bf16[128,1024]{1,0:T(8,128)(2,1)}, f32[128,1024]{1,0:T(8,128)}, bf16[128,1024]{1,0:T(8,128)(2,1)}) custom-call(s32[3]{0:T(128)} %get-tuple-element.128.where, bf16[2,256,1024]{2,1,0:T(8,128)(2,1)} %bitcast.79, bf16[128,1024]{1,0:T(8,128)(2,1)} %copy-done.17, bf16[128,1024]{1,0:T(8,128)(2,1)} %copy-done.21, ...), custom_call_target="tpu_custom_call" | custom-call | flops 4294967296 | bytes 16777216 | tf_op jit(solution)/shard_map/section_forward/pallas_call | solution.py:156
  101.6 9.8 %collective-permute-start.24 = (bf16[128,1024]{1,0:T(8,128)(2,1)S(1)}, bf16[128,1024]{1,0:T(8,128)(2,1)S(1)}, u32[]{:S(2)}, u32[]{:S(2)}) collective-permute-start(bf16[128,1024]{1,0:T(8,128)(2,1)S(1)} %add_convert_fusion.5), channel_id=1, source_target_pairs={{0,8},{8,16},{16,24},{1,9},{9,17},{17,25},{2,10},{10,18},{18,26},{... | collective-permute-start | bytes 786440 | tf_op jit(solution)/shard_map/ppermute | solution.py:19
  111.4 5.2 %collective-permute-done.14 = bf16[128,1024]{1,0:T(8,128)(2,1)S(1)} collective-permute-done((bf16[128,1024]{1,0:T(8,128)(2,1)S(1)}, bf16[128,1024]{1,0:T(8,128)(2,1)S(1)}, u32[]{:S(2)}, u32[]{:S(2)}) %collective-permute-start.14) | collective-permute-done | bytes 262176 | tf_op jit(solution)/shard_map/ppermute | solution.py:651
  125.4 5.0 %section_forward.9 = (bf16[256,1024]{1,0:T(8,128)(2,1)}, bf16[128,1024]{1,0:T(8,128)(2,1)}, f32[128,1024]{1,0:T(8,128)}, bf16[128,1024]{1,0:T(8,128)(2,1)}) custom-call(s32[3]{0:T(128)} %get-tuple-element.125.where, bf16[2,256,1024]{2,1,0:T(8,128)(2,1)} %bitcast.81, f32[256,1280]{1,0:T(8,128)} %get-tuple-element.63.refs_9_.refs_0_, ...), custom_call_target="tpu_custom_call" | custom-call | flops 4294967296 | bytes 16777216 | tf_op jit(solution)/shard_map/section_forward/pallas_call | solution.py:156
  134.2 9.6 %collective-permute-start.18 = (f32[8,256]{1,0:T(8,128)S(1)}, f32[8,256]{1,0:T(8,128)S(1)}, u32[]{:S(2)}, u32[]{:S(2)}) collective-permute-start(f32[8,256]{1,0:T(8,128)S(1)} %copy-done.31), channel_id=1, source_target_pairs={{0,8},{4,12},{8,16},{12,20},{16,24},{20,28},{24,0},{28,4},{1,9},{5... | collective-permute-start | bytes 24584 | tf_op jit(solution)/shard_map/ppermute | solution.py:628
  161.2 5.3 %collective-permute-start.45 = (bf16[128,1024]{1,0:T(8,128)(2,1)S(1)}, bf16[128,1024]{1,0:T(8,128)(2,1)S(1)}, u32[]{:S(2)}, u32[]{:S(2)}) collective-permute-start(bf16[128,1024]{1,0:T(8,128)(2,1)S(1)} %add_convert_fusion.1), channel_id=1, source_target_pairs={{8,24},{9,25},{10,26},{11,27},{12,28},{13,29},{14,30},{15,31}} | collective-permute-start | bytes 786440 | tf_op jit(solution)/shard_map/ppermute | solution.py:700
  168.6 9.1 %collective-permute-done.45 = bf16[128,1024]{1,0:T(8,128)(2,1)S(1)} collective-permute-done((bf16[128,1024]{1,0:T(8,128)(2,1)S(1)}, bf16[128,1024]{1,0:T(8,128)(2,1)S(1)}, u32[]{:S(2)}, u32[]{:S(2)}) %collective-permute-start.45) | collective-permute-done | bytes 262176 | tf_op jit(solution)/shard_map/ppermute | solution.py:700
  202.0 5.2 %section_backward.4 = (bf16[128,1024]{1,0:T(8,128)(2,1)}, f32[128,1024]{1,0:T(8,128)}, bf16[128,1024]{1,0:T(8,128)(2,1)}) custom-call(s32[3]{0:T(128)} %get-tuple-element.124.where, bf16[256,1024]{1,0:T(8,128)(2,1)} %get-tuple-element.79.refs_0_.refs_6_, bf16[256,1024]{1,0:T(8,128)(2,1)} %get-tuple-element.80.refs_1_.refs_7_, bf16[128,1024]{1,0:T(8,128)(2,1)} %copy-done.7, ...), custom_call_target="tpu_custom_call" | custom-call | flops 6442450944 | bytes 16777216 | tf_op jit(solution)/shard_map/section_backward/pallas_call | solution.py:232
  209.6 11.6 %collective-permute-start.41 = (bf16[128,1024]{1,0:T(8,128)(2,1)S(1)}, bf16[128,1024]{1,0:T(8,128)(2,1)S(1)}, u32[]{:S(2)}, u32[]{:S(2)}) collective-permute-start(bf16[128,1024]{1,0:T(8,128)(2,1)S(1)} %add_convert_fusion.3), channel_id=1, source_target_pairs={{8,24},{9,25},{10,26},{11,27},{12,28},{13,29},{14,30},{15,31}} | collective-permute-start | bytes 786440 | tf_op jit(solution)/shard_map/ppermute | solution.py:700
  227.0 5.5 %collective-permute-done.41 = bf16[128,1024]{1,0:T(8,128)(2,1)S(1)} collective-permute-done((bf16[128,1024]{1,0:T(8,128)(2,1)S(1)}, bf16[128,1024]{1,0:T(8,128)(2,1)S(1)}, u32[]{:S(2)}, u32[]{:S(2)}) %collective-permute-start.41) | collective-permute-done | bytes 262176 | tf_op jit(solution)/shard_map/ppermute | solution.py:700
  251.7 13.0 %collective-permute-done.52.refs_8_ = bf16[128,1024]{1,0:T(8,128)(2,1)S(1)} collective-permute-done((bf16[128,1024]{1,0:T(8,128)(2,1)S(1)}, bf16[128,1024]{1,0:T(8,128)(2,1)S(1)}, u32[]{:S(2)}, u32[]{:S(2)}) %collective-permute-start.52) | collective-permute-done | bytes 262176 | tf_op jit(solution)/shard_map/ppermute | solution.py:19
  272.5 12.5 %section_backward.6 = (bf16[128,1024]{1,0:T(8,128)(2,1)}, f32[128,1024]{1,0:T(8,128)}, bf16[128,1024]{1,0:T(8,128)(2,1)}) custom-call(s32[3]{0:T(128)} %get-tuple-element.122.where, f32[1,512]{1,0:T(1,128)} %copy-done.46, f32[1,512]{1,0:T(1,128)} %copy-done.49, f32[1,512]{1,0:T(1,128)} %copy-done.50, f32[1,512]{1,0:T(1,128)} %copy-done.51, ...), custom_call_target="tpu_custom_call" | custom-call | flops 6442450944 | bytes 16777216 | tf_op jit(solution)/shard_map/section_backward/pallas_call | solution.py:232
  292.6 8.4 %collective-permute-done.58.refs_5_ = bf16[128,1024]{1,0:T(8,128)(2,1)S(1)} collective-permute-done((bf16[128,1024]{1,0:T(8,128)(2,1)S(1)}, bf16[128,1024]{1,0:T(8,128)(2,1)S(1)}, u32[]{:S(2)}, u32[]{:S(2)}) %collective-permute-start.58) | collective-permute-done | bytes 262176 | tf_op jit(solution)/shard_map/ppermute | solution.py:19
  304.1 12.7 %section_backward.7 = (bf16[128,1024]{1,0:T(8,128)(2,1)}, f32[128,1024]{1,0:T(8,128)}, bf16[128,1024]{1,0:T(8,128)(2,1)}) custom-call(s32[3]{0:T(128)} %get-tuple-element.104.where, bf16[4,2,128,1024]{3,2,1,0:T(8,128)(2,1)} %bitcast.62, bf16[4,2,128,1024]{3,2,1,0:T(8,128)(2,1)} %copy-done, bf16[256,1024]{1,0:T(8,128)(2,1)} %get-tuple-element.84.refs_0_.refs_2_, ...), custom_call_target="tpu_custom_call" | custom-call | flops 6442450944 | bytes 16777216 | tf_op jit(solution)/shard_map/section_backward/pallas_call | solution.py:232
  323.3 8.4 %collective-permute-done.62 = bf16[128,1024]{1,0:T(8,128)(2,1)S(1)} collective-permute-done((bf16[128,1024]{1,0:T(8,128)(2,1)S(1)}, bf16[128,1024]{1,0:T(8,128)(2,1)S(1)}, u32[]{:S(2)}, u32[]{:S(2)}) %collective-permute-start.62) | collective-permute-done | bytes 262176 | tf_op jit(solution)/shard_map/ppermute | solution.py:19
  335.1 27.1 %all-gather.15.cloned.1.call-done = bf16[512,1024]{1,0:T(8,128)(2,1)} async-done(((bf16[128,1024]{1,0:T(8,128)(2,1)}), bf16[512,1024]{1,0:T(8,128)(2,1)}) %all-gather.15.cloned.1.call-update) | async-done | bytes 1048592 | tf_op jit(solution)/shard_map/all_gather | solution.py:620
  363.1 15.7 %unit_grads.1 = f32[256,1280]{1,0:T(8,128)} custom-call(s32[2]{0:T(128)} %pad_add_fusion.12.where, bf16[4,2,128,1024]{3,2,1,0:T(8,128)(2,1)} %bitcast.63, bf16[4,2,128,1024]{3,2,1,0:T(8,128)(2,1)} %bitcast.64, bf16[4,2,128,1024]{3,2,1,0:T(8,128)(2,1)} %bitcast.65, bf16[4,2,128,1024]{3,2,1,0:T(8,128)(2,1)} %bitcast.66, bf16[4,2,128,1024]{3,2,1,0:T(8,128)(2,1)} %bitcast.67, ...), custom_call_target="tpu_custom_call" | custom-call | flops 6710886400 | bytes 7864320 | tf_op jit(solution)/shard_map/unit_grads/pallas_call | solution.py:453
  378.8 12.3 %all-gather.13.cloned.1.call-done = bf16[512,1024]{1,0:T(8,128)(2,1)} async-done(((bf16[128,1024]{1,0:T(8,128)(2,1)}), bf16[512,1024]{1,0:T(8,128)(2,1)}) %all-gather.13.cloned.1.call-update) | async-done | bytes 1048592 | tf_op jit(solution)/shard_map/all_gather | solution.py:620
  391.9 18.7 %weight_grads.4 = (f32[256,4096]{1,0:T(8,128)}, f32[4096,256]{1,0:T(8,128)}) custom-call(s32[1]{0:T(128)} %bitcast.18.where, bf16[4,2,128,1024]{3,2,1,0:T(8,128)(2,1)} %bitcast.95, bf16[4,2,128,1024]{3,2,1,0:T(8,128)(2,1)} %bitcast.96, bf16[4,2,128,1024]{3,2,1,0:T(8,128)(2,1)} %bitcast.97, bf16[4,2,128,1024]{3,2,1,0:T(8,128)(2,1)} %bitcast.98, ...), custom_call_target="tpu_custom_call" | custom-call | flops 10737418240 | bytes 33554432 | tf_op jit(solution)/shard_map/weight_grads/pallas_call | solution.py:532
  411.6 19.9 %weight_grads.5 = (f32[256,4096]{1,0:T(8,128)}, f32[4096,256]{1,0:T(8,128)}) custom-call(s32[1]{0:T(128)} %bitcast.18.where, bf16[4,2,128,1024]{3,2,1,0:T(8,128)(2,1)} %collective-permute-done.38.refs_5_.refs_0_.refs_1_.refs_2_.refs_3_, ...), custom_call_target="tpu_custom_call", output_to_operand_aliasing={{0}: (11, {}), {1}: (12, {})} | custom-call | flops 10737418240 | bytes 33554432 | tf_op jit(solution)/shard_map/weight_grads/pallas_call | solution.py:532
  431.5 19.9 %weight_grads.6 = (f32[256,4096]{1,0:T(8,128)}, f32[4096,256]{1,0:T(8,128)}) custom-call(s32[1]{0:T(128)} %bitcast.18.where, bf16[4,2,128,1024]{3,2,1,0:T(8,128)(2,1)} %bitcast.99, bf16[4,2,128,1024]{3,2,1,0:T(8,128)(2,1)} %bitcast.100, bf16[4,2,128,1024]{3,2,1,0:T(8,128)(2,1)} %bitcast.101, ...), custom_call_target="tpu_custom_call", output_to_operand_aliasing={{0}: (11, {}), {1}: (12, {})} | custom-call | flops 10737418240 | bytes 33554432 | tf_op jit(solution)/shard_map/weight_grads/pallas_call | solution.py:532
  452.4 19.9 %weight_grads.7 = (f32[256,4096]{1,0:T(8,128)}, f32[4096,256]{1,0:T(8,128)}) custom-call(s32[1]{0:T(128)} %bitcast.18.where, bf16[4,2,128,1024]{3,2,1,0:T(8,128)(2,1)} %collective-permute-done.38.refs_5_.refs_0_.refs_1_.refs_2_.refs_3_, ...), custom_call_target="tpu_custom_call", output_to_operand_aliasing={{0}: (11, {}), {1}: (12, {})} | custom-call | flops 10737418240 | bytes 33554432 | tf_op jit(solution)/shard_map/weight_grads/pallas_call | solution.py:532
  (319 shorter events, 175.3 us)
Async XLA Ops:
  7.2 229.8 %all-gather.9.cloned.1.call-start = ((), (), s32[]{:S(2)}) async-start(), calls=%async_computation | async-start | bytes 2621440 | tf_op jit(solution)/shard_map/all_gather | solution.py:620
  16.4 14.0 %collective-permute-start.4 = (bf16[128,1024]{1,0:T(8,128)(2,1)S(1)}, bf16[128,1024]{1,0:T(8,128)(2,1)S(1)}, u32[]{:S(2)}, u32[]{:S(2)}) collective-permute-start(bf16[128,1024]{1,0:T(8,128)(2,1)S(1)} %add_convert_fusion.8), channel_id=1, source_target_pairs={{0,8},{8,16},{16,24},{1,9},{9,17},{17,25},{2,10},{10,18},{18,26},{... | collective-permute-start | bytes 786440 | tf_op jit(solution)/shard_map/ppermute | solution.py:19
  49.4 11.5 %collective-permute-start = (s32[4,640]{1,0:T(4,128)S(1)}, s32[4,640]{1,0:T(4,128)S(1)}, u32[]{:S(2)}, u32[]{:S(2)}) collective-permute-start(s32[4,640]{1,0:T(4,128)S(1)} %pad_add_fusion), channel_id=1, source_target_pairs={{0,1},{1,2},{2,3},{3,0},{4,5},{5,6},{6,7},{7,4},{8,9},{9,10},{10,1... | collective-permute-start | bytes 30728 | tf_op jit(solution)/shard_map/ppermute | solution.py:603
  50.7 22.3 %collective-permute-start.1 = (s32[4,640]{1,0:T(4,128)S(1)}, s32[4,640]{1,0:T(4,128)S(1)}, u32[]{:S(2)}, u32[]{:S(2)}) collective-permute-start(s32[4,640]{1,0:T(4,128)S(1)} %pad_add_fusion), channel_id=1, source_target_pairs={{0,2},{1,3},{2,0},{3,1},{4,6},{5,7},{6,4},{7,5},{8,10},{9,11},{10,... | collective-permute-start | bytes 30728 | tf_op jit(solution)/shard_map/ppermute | solution.py:603
  51.8 27.9 %collective-permute-start.2 = (s32[4,640]{1,0:T(4,128)S(1)}, s32[4,640]{1,0:T(4,128)S(1)}, u32[]{:S(2)}, u32[]{:S(2)}) collective-permute-start(s32[4,640]{1,0:T(4,128)S(1)} %pad_add_fusion), channel_id=1, source_target_pairs={{0,3},{1,0},{2,1},{3,2},{4,7},{5,4},{6,5},{7,6},{8,11},{9,8},{10,9... | collective-permute-start | bytes 30728 | tf_op jit(solution)/shard_map/ppermute | solution.py:603
  98.9 12.5 %collective-permute-start.13 = (bf16[128,1024]{1,0:T(8,128)(2,1)S(1)}, bf16[128,1024]{1,0:T(8,128)(2,1)S(1)}, u32[]{:S(2)}, u32[]{:S(2)}) collective-permute-start(bf16[128,1024]{1,0:T(8,128)(2,1)S(1)} %add_convert_fusion.5), channel_id=1, source_target_pairs={{24,16},{25,17},{26,18},{27,19},{28,20},{29,21},{30,22},{31,23}} | collective-permute-start | bytes 786440 | tf_op jit(solution)/shard_map/ppermute | solution.py:651
  99.6 17.0 %collective-permute-start.14 = (bf16[128,1024]{1,0:T(8,128)(2,1)S(1)}, bf16[128,1024]{1,0:T(8,128)(2,1)S(1)}, u32[]{:S(2)}, u32[]{:S(2)}) collective-permute-start(bf16[128,1024]{1,0:T(8,128)(2,1)S(1)} %add_convert_fusion.5), channel_id=1, source_target_pairs={{24,8},{25,9},{26,10},{27,11},{28,12},{29,13},{30,14},{31,15}} | collective-permute-start | bytes 786440 | tf_op jit(solution)/shard_map/ppermute | solution.py:651
  100.9 15.7 %collective-permute-start.15 = (bf16[128,1024]{1,0:T(8,128)(2,1)S(1)}, bf16[128,1024]{1,0:T(8,128)(2,1)S(1)}, u32[]{:S(2)}, u32[]{:S(2)}) collective-permute-start(bf16[128,1024]{1,0:T(8,128)(2,1)S(1)} %add_convert_fusion.5), channel_id=1, source_target_pairs={{24,0},{25,1},{26,2},{27,3},{28,4},{29,5},{30,6},{31,7}} | collective-permute-start | bytes 786440 | tf_op jit(solution)/shard_map/ppermute | solution.py:651
  101.6 16.3 %collective-permute-start.24 = (bf16[128,1024]{1,0:T(8,128)(2,1)S(1)}, bf16[128,1024]{1,0:T(8,128)(2,1)S(1)}, u32[]{:S(2)}, u32[]{:S(2)}) collective-permute-start(bf16[128,1024]{1,0:T(8,128)(2,1)S(1)} %add_convert_fusion.5), channel_id=1, source_target_pairs={{0,8},{8,16},{16,24},{1,9},{9,17},{17,25},{2,10},{10,18},{18,26},{... | collective-permute-start | bytes 786440 | tf_op jit(solution)/shard_map/ppermute | solution.py:19
  131.4 139.3 %all-gather.11.cloned.1.call-start = ((), (), s32[]{:S(2)}) async-start(), calls=%async_computation.1 | async-start | bytes 2621440 | tf_op jit(solution)/shard_map/all_gather | solution.py:620
  131.5 25.2 %collective-permute-start.26 = (bf16[128,1024]{1,0:T(8,128)(2,1)S(1)}, bf16[128,1024]{1,0:T(8,128)(2,1)S(1)}, u32[]{:S(2)}, u32[]{:S(2)}) collective-permute-start(bf16[128,1024]{1,0:T(8,128)(2,1)S(1)} %copy-done.55), channel_id=1, source_target_pairs={{0,4},{4,0},{1,5},{5,1},{2,6},{6,2},{3,7},{7,3},{8,12},{12,8},{9,1... | collective-permute-start | bytes 786440 | tf_op jit(solution)/shard_map/ppermute | solution.py:23
  131.9 11.9 %collective-permute-start.17 = (f32[8,256]{1,0:T(8,128)S(1)}, f32[8,256]{1,0:T(8,128)S(1)}, u32[]{:S(2)}, u32[]{:S(2)}) collective-permute-start(f32[8,256]{1,0:T(8,128)S(1)} %copy-done.31), channel_id=1, source_target_pairs={{0,4},{4,8},{8,12},{12,16},{16,20},{20,24},{24,28},{28,0},{1,5},{5... | collective-permute-start | bytes 24584 | tf_op jit(solution)/shard_map/ppermute | solution.py:628
  161.2 16.5 %collective-permute-start.45 = (bf16[128,1024]{1,0:T(8,128)(2,1)S(1)}, bf16[128,1024]{1,0:T(8,128)(2,1)S(1)}, u32[]{:S(2)}, u32[]{:S(2)}) collective-permute-start(bf16[128,1024]{1,0:T(8,128)(2,1)S(1)} %add_convert_fusion.1), channel_id=1, source_target_pairs={{8,24},{9,25},{10,26},{11,27},{12,28},{13,29},{14,30},{15,31}} | collective-permute-start | bytes 786440 | tf_op jit(solution)/shard_map/ppermute | solution.py:700
  178.3 23.0 %collective-permute-start.47 = (bf16[128,1024]{1,0:T(8,128)(2,1)S(1)}, bf16[128,1024]{1,0:T(8,128)(2,1)S(1)}, u32[]{:S(2)}, u32[]{:S(2)}) collective-permute-start(bf16[128,1024]{1,0:T(8,128)(2,1)S(1)} %fusion.65.refs_2_), channel_id=1, source_target_pairs={{0,4},{4,0},{1,5},{5,1},{2,6},{6,2},{3,7},{7,3},{8,12},{12,8},{9,1... | collective-permute-start | bytes 786440 | tf_op jit(solution)/shard_map/ppermute | solution.py:23
  193.5 168.7 %all-gather.15.cloned.1.call-start = ((), (), s32[]{:S(2)}) async-start(), calls=%async_computation.3 | async-start | bytes 1310720 | tf_op jit(solution)/shard_map/all_gather | solution.py:620
  207.2 14.7 %collective-permute-start.48 = (bf16[128,1024]{1,0:T(8,128)(2,1)}, bf16[128,1024]{1,0:T(8,128)(2,1)S(1)}, u32[]{:S(2)}, u32[]{:S(2)}) collective-permute-start(bf16[128,1024]{1,0:T(8,128)(2,1)} %get-tuple-element.83), channel_id=1, source_target_pairs={{0,4},{4,0},{1,5},{5,1},{2,6},{6,2},{3,7},{7,3},{8,12},{12,8},{9,1... | collective-permute-start | bytes 786440 | tf_op jit(solution)/shard_map/ppermute | solution.py:23
  208.9 18.1 %collective-permute-start.40 = (bf16[128,1024]{1,0:T(8,128)(2,1)S(1)}, bf16[128,1024]{1,0:T(8,128)(2,1)S(1)}, u32[]{:S(2)}, u32[]{:S(2)}) collective-permute-start(bf16[128,1024]{1,0:T(8,128)(2,1)S(1)} %add_convert_fusion.3), channel_id=1, source_target_pairs={{0,24},{1,25},{2,26},{3,27},{4,28},{5,29},{6,30},{7,31}} | collective-permute-start | bytes 786440 | tf_op jit(solution)/shard_map/ppermute | solution.py:700
  209.6 22.9 %collective-permute-start.41 = (bf16[128,1024]{1,0:T(8,128)(2,1)S(1)}, bf16[128,1024]{1,0:T(8,128)(2,1)S(1)}, u32[]{:S(2)}, u32[]{:S(2)}) collective-permute-start(bf16[128,1024]{1,0:T(8,128)(2,1)S(1)} %add_convert_fusion.3), channel_id=1, source_target_pairs={{8,24},{9,25},{10,26},{11,27},{12,28},{13,29},{14,30},{15,31}} | collective-permute-start | bytes 786440 | tf_op jit(solution)/shard_map/ppermute | solution.py:700
  236.9 34.9 %collective-permute-start.38 = (bf16[4,2,128,1024]{3,2,1,0:T(8,128)(2,1)}, bf16[4,2,128,1024]{3,2,1,0:T(8,128)(2,1)}, u32[]{:S(2)}, u32[]{:S(2)}) collective-permute-start(bf16[4,2,128,1024]{3,2,1,0:T(8,128)(2,1)} %bitcast.93), channel_id=1, source_target_pairs={{0,4},{4,0},{1,5},{5,1},{2,6},{6,2},{3,7},{7,3},{8,12},{12,8},{9,1... | collective-permute-start | bytes 6291464 | tf_op jit(solution)/shard_map/ppermute | solution.py:23
  248.4 16.3 %collective-permute-start.52 = (bf16[128,1024]{1,0:T(8,128)(2,1)S(1)}, bf16[128,1024]{1,0:T(8,128)(2,1)S(1)}, u32[]{:S(2)}, u32[]{:S(2)}) collective-permute-start(bf16[128,1024]{1,0:T(8,128)(2,1)S(1)} %fusion.52), channel_id=1, source_target_pairs={{8,0},{16,8},{24,16},{9,1},{17,9},{25,17},{10,2},{18,10},{26,18},{... | collective-permute-start | bytes 786440 | tf_op jit(solution)/shard_map/ppermute | solution.py:19
  270.8 31.4 %collective-permute-start.59 = (bf16[4,2,128,1024]{3,2,1,0:T(8,128)(2,1)}, bf16[4,2,128,1024]{3,2,1,0:T(8,128)(2,1)S(1)}, u32[]{:S(2)}, u32[]{:S(2)}) collective-permute-start(bf16[4,2,128,1024]{3,2,1,0:T(8,128)(2,1)} %bitcast.61), channel_id=1, source_target_pairs={{0,4},{4,0},{1,5},{5,1},{2,6},{6,2},{3,7},{7,3},{8,12},{12,8},{9,1... | collective-permute-start | bytes 6291464 | tf_op jit(solution)/shard_map/ppermute | solution.py:23
  332.6 58.5 %all-gather.13.cloned.1.call-start = ((), (), s32[]{:S(2)}) async-start(), calls=%async_computation.2 | async-start | bytes 1310720 | tf_op jit(solution)/shard_map/all_gather | solution.py:620
  362.2 48.5 %collective-permute-start.64 = (bf16[4,128,1024]{2,1,0:T(8,128)(2,1)}, bf16[4,128,1024]{2,1,0:T(8,128)(2,1)S(1)}, u32[]{:S(2)}, u32[]{:S(2)}) collective-permute-start(bf16[4,128,1024]{2,1,0:T(8,128)(2,1)} %bitcast.108), channel_id=1, source_target_pairs={{0,4},{4,0},{1,5},{5,1},{2,6},{6,2},{3,7},{7,3},{8,12},{12,8},{9,1... | collective-permute-start | bytes 3145736 | tf_op jit(solution)/shard_map/ppermute | solution.py:23
  391.1 60.4 %collective-permute-start.63 = (bf16[4,128,1024]{2,1,0:T(8,128)(2,1)}, bf16[4,128,1024]{2,1,0:T(8,128)(2,1)S(1)}, u32[]{:S(2)}, u32[]{:S(2)}) collective-permute-start(bf16[4,128,1024]{2,1,0:T(8,128)(2,1)} %bitcast.103), channel_id=1, source_target_pairs={{0,4},{4,0},{1,5},{5,1},{2,6},{6,2},{3,7},{7,3},{8,12},{12,8},{9,1... | collective-permute-start | bytes 3145736 | tf_op jit(solution)/shard_map/ppermute | solution.py:23
  (104 other events, 573.8 us)
Sparse Core Ops, SparseCore 0:
  131.6 54.2 all-gather.8
  193.6 45.3 all-gather.10
  332.7 29.4 all-gather.14
  363.6 27.4 all-gather.12

commit v7 on v6

--- a/solution.py
+++ b/solution.py
@@ -7,7 +7,7 @@
 from jax.sharding import PartitionSpec as P
 
 CHUNKS = 2
-VMEM_MIB = 58
+VMEM_MIB = 60
 BF16 = jnp.bfloat16
 F32 = jnp.float32
 MIB = 1024 * 1024
@@ -111,23 +111,35 @@
     return pl.BlockSpec(shape, lambda *_: (0,) * len(shape))
 
 
-def forward_kernel(halves, has_arrived, ties, where, own, *refs):
+def keep_live(live, arrived, before, after):
+    for came, old, new in zip(arrived, before, after):
+        new[...] = jnp.where(live, came[...], old[...])
+
+
+def forward_kernel(halves, stage, ties, where, *refs):
     refs = refs[ties:]
-    if has_arrived:
+    if stage == 0:
+        own, refs = refs[0], refs[1:]
+    else:
         arrived, refs = refs[:halves], refs[halves:]
-    live = where[2] == 1
-    w_in, w_out, rows_out, mine_out, keep, *send, whole, normed, total = refs
+        before, refs = refs[:halves], refs[halves:]
+    w_in, w_out, refs = refs[0], refs[1], refs[2:]
+    after, refs = refs[:halves], refs[halves:]
+    keep, *send, whole, normed, total = refs
     step = pl.program_id(0)
+    live = where[0] == stage
 
     @pl.when(step == 0)
     def _():
-        rows = own[...]
-        if has_arrived:
-            rows = jnp.where(where[0] == 0, rows, gathered(arrived, where[1]))
-        rows_out[...] = rows
-        whole[...] = rows
-        mine_out[...] = part_of(whole, where[1], halves)
-        normed[...] = normalised(rows)
+        if stage == 0:
+            whole[...] = own[...]
+            after[0][...] = part_of(whole, where[1], halves)
+            if halves == 2:
+                after[1][...] = part_of(whole, 1 - where[1], halves)
+        else:
+            whole[...] = gathered(arrived, where[1])
+            keep_live(live, arrived, before, after)
+        normed[...] = normalised(whole[...])
         total[...] = jnp.zeros_like(total)
 
     @pl.when(live)
@@ -147,23 +159,28 @@
             keep[...] = total[...]
 
 
-def forward_section(where, text, at, halves, arrived, w_in, w_out, ties):
+def forward_section(where, stage, halves, text, at, arrived, before, w_in, w_out, ties):
     _, rows, width = text.shape
     hidden = w_in.shape[1]
     tile = tile_of(hidden, 1024)
     full, part = (rows, width), (rows // halves, width)
-    shapes = [(full, BF16), (part, BF16), (part, F32)] + [(part, BF16)] * (halves - 1)
+    shapes = [(part, BF16)] * halves + [(part, F32)] + [(part, BF16)] * (halves - 1)
+    if stage == 0:
+        operands = [text]
+        specs = [pl.BlockSpec((None, rows, width), lambda j, s: (at, 0, 0))]
+    else:
+        operands = [*arrived, *before]
+        specs = [whole_spec(part)] * len(operands)
     return pl.pallas_call(
-        functools.partial(forward_kernel, halves, bool(arrived), len(ties)),
+        functools.partial(forward_kernel, halves, stage, len(ties)),
         grid_spec=pltpu.PrefetchScalarGridSpec(
             num_scalar_prefetch=1,
             grid=(hidden // tile,),
-            in_specs=[
-                pl.BlockSpec((None, rows, width), lambda j, s: (at, 0, 0)),
-                *[pl.BlockSpec(memory_space=pl.ANY)] * len(ties),
-                *[whole_spec(part)] * len(arrived),
-                pl.BlockSpec((width, tile), lambda j, s: (0, j * s[2])),
-                pl.BlockSpec((tile, width), lambda j, s: (j * s[2], 0)),
+            in_specs=[pl.BlockSpec(memory_space=pl.ANY)] * len(ties)
+            + specs
+            + [
+                pl.BlockSpec((width, tile), lambda j, s: (0, jnp.where(s[0] == stage, j, 0))),
+                pl.BlockSpec((tile, width), lambda j, s: (jnp.where(s[0] == stage, j, 0), 0)),
             ],
             out_specs=[whole_spec(shape) for shape, _ in shapes],
             scratch_shapes=[pltpu.VMEM(full, BF16), pltpu.VMEM(full, BF16), pltpu.VMEM(full, F32)],
@@ -176,7 +193,7 @@
             transcendentals=rows * hidden,
         ),
         name="section_forward",
-    )(where, text, *ties, *arrived, w_in, w_out)
+    )(where, *ties, *operands, w_in, w_out)
 
 
 def total_of(pieces):
@@ -190,20 +207,22 @@
     return (grads.astype(F32) + norm_back(rows, total_of(pieces))).astype(BF16)
 
 
-def backward_kernel(owners, halves, ties, where, *refs):
+def backward_kernel(halves, owner, old, ties, where, *refs):
     refs = refs[ties:]
-    live = where[2] == 1
-    stashed, refs = refs[: len(owners)], refs[len(owners) :]
+    stash, refs = refs[:halves], refs[halves:]
     arrived, refs = refs[:halves], refs[halves:]
-    w_in, w_out, mine_rows, keep, *send, rows, grads, normed, total = refs
+    before, refs = refs[:old], refs[old:]
+    w_in, w_out, refs = refs[0], refs[1], refs[2:]
+    after, refs = refs[:halves], refs[halves:]
+    keep, *send, grads, normed, total = refs
     step = pl.program_id(0)
+    live = where[0] == owner
 
     @pl.when(step == 0)
     def _():
-        rows[...] = chosen(where[0], [(at, ref[...]) for at, ref in zip(owners, stashed)])
         grads[...] = gathered(arrived, where[1])
-        mine_rows[...] = part_of(rows, where[1], halves)
-        normed[...] = normalised(rows[...])
+        keep_live(live, arrived, before if old else arrived, after)
+        normed[...] = normalised(gathered(stash, where[1]))
         total[...] = jnp.zeros_like(total)
 
     @pl.when(live)
@@ -223,36 +242,61 @@
             keep[...] = total[...]
 
 
-def backward_section(where, halves, options, arrived, w_in, w_out, ties):
+def backward_section(where, owner, stash, arrived, before, w_in, w_out, ties):
     width, hidden = w_in.shape
-    rows = options[0][1].shape[0]
+    halves = len(stash)
+    part = stash[0].shape
+    full = (part[0] * halves, width)
     tile = tile_of(hidden, 1024)
-    full, part = (rows, width), (rows // halves, width)
-    shapes = [(part, BF16), (part, F32)] + [(part, BF16)] * (halves - 1)
+    shapes = [(part, BF16)] * halves + [(part, F32)] + [(part, BF16)] * (halves - 1)
+    operands = [*stash, *arrived, *before]
     return pl.pallas_call(
-        functools.partial(backward_kernel, tuple(at for at, _ in options), halves, len(ties)),
+        functools.partial(backward_kernel, halves, owner, len(before), len(ties)),
         grid_spec=pltpu.PrefetchScalarGridSpec(
             num_scalar_prefetch=1,
             grid=(hidden // tile,),
             in_specs=[pl.BlockSpec(memory_space=pl.ANY)] * len(ties)
-            + [whole_spec(full)] * len(options)
-            + [whole_spec(part)] * halves
+            + [whole_spec(part)] * len(operands)
             + [
-                pl.BlockSpec((width, tile), lambda j, s: (0, j * s[2])),
-                pl.BlockSpec((tile, width), lambda j, s: (j * s[2], 0)),
+                pl.BlockSpec((width, tile), lambda j, s: (0, jnp.where(s[0] == owner, j, 0))),
+                pl.BlockSpec((tile, width), lambda j, s: (jnp.where(s[0] == owner, j, 0), 0)),
             ],
             out_specs=[whole_spec(shape) for shape, _ in shapes],
-            scratch_shapes=[pltpu.VMEM(full, BF16)] * 3 + [pltpu.VMEM(full, F32)],
+            scratch_shapes=[pltpu.VMEM(full, BF16)] * 2 + [pltpu.VMEM(full, F32)],
         ),
         out_shape=[jax.ShapeDtypeStruct(*shape) for shape in shapes],
         compiler_params=params(VMEM_MIB),
         cost_estimate=cost(
-            flops=6 * rows * width * hidden,
+            flops=6 * full[0] * width * hidden,
             bytes_accessed=4 * width * hidden,
-            transcendentals=rows * hidden,
+            transcendentals=full[0] * hidden,
         ),
         name="section_backward",
-    )(where, *ties, *[option for _, option in options], *arrived, w_in, w_out)
+    )(where, *ties, *operands, w_in, w_out)
+
+
+def pick_kernel(halves, owner, ties, where, *refs):
+    refs = refs[ties:]
+    arrived, before, after = refs[:halves], refs[halves : 2 * halves], refs[2 * halves :]
+    keep_live(where[0] == owner, arrived, before, after)
+
+
+def pick(where, owner, arrived, before, ties):
+    halves = len(arrived)
+    part = arrived[0].shape
+    return pl.pallas_call(
+        functools.partial(pick_kernel, halves, owner, len(ties)),
+        grid_spec=pltpu.PrefetchScalarGridSpec(
+            num_scalar_prefetch=1,
+            grid=(1,),
+            in_specs=[pl.BlockSpec(memory_space=pl.ANY)] * len(ties)
+            + [whole_spec(part)] * (2 * halves),
+            out_specs=[whole_spec(part)] * halves,
+        ),
+        out_shape=[jax.ShapeDtypeStruct(part, BF16)] * halves,
+        compiler_params=params(VMEM_MIB),
+        name="pick_grads",
+    )(where, *ties, *arrived, *before)
 
 
 def row_table(rows):
@@ -268,15 +312,18 @@
     return jnp.broadcast_to(row, (128, row.shape[1])).T
 
 
-def logits_kernel(halves, where, *refs):
-    final, refs = refs[:halves], refs[halves:]
+def logits_kernel(halves, chunks, where, *refs):
+    finals, refs = refs[: halves * chunks], refs[halves * chunks :]
     w_unit, counts, logits, stats, normed, peak, total, target = refs
     step = pl.program_id(0)
     lanes = peak.shape[1]
 
     @pl.when(step == 0)
     def _():
-        normed[...] = normalised(gathered(final, where[1]))
+        rows = normed.shape[0] // chunks
+        for at in range(chunks):
+            final = finals[at * halves : (at + 1) * halves]
+            normed[at * rows : (at + 1) * rows, :] = normalised(gathered(final, where[1]))
         peak[...] = jnp.full_like(peak, -1e30)
         total[...] = jnp.zeros_like(total)
         target[...] = jnp.zeros_like(target)
@@ -309,22 +356,22 @@
         stats[...] = row_table([as_row(top), as_row(mass), as_row(summed)])
 
 
-def head_logits(where, final, w_unit, counts, at):
-    halves = len(final)
-    half, width = final[0].shape
-    rows = half * halves
+def head_logits(where, finals, w_unit, counts):
+    halves, chunks = len(finals[0]), len(finals)
+    half, width = finals[0][0].shape
+    rows = half * halves * chunks
     vocab = w_unit.shape[1]
     lanes = 128 if vocab % 128 == 0 else vocab
     tile = tile_of(vocab, 640)
     return pl.pallas_call(
-        functools.partial(logits_kernel, halves),
+        functools.partial(logits_kernel, halves, chunks),
         grid_spec=pltpu.PrefetchScalarGridSpec(
             num_scalar_prefetch=1,
             grid=(vocab // tile,),
             in_specs=[
-                *[whole_spec((half, width))] * halves,
+                *[whole_spec((half, width))] * (halves * chunks),
                 pl.BlockSpec((width, tile), lambda t, s: (0, t)),
-                pl.BlockSpec((None, rows, tile), lambda t, s: (at, 0, t)),
+                pl.BlockSpec((rows, tile), lambda t, s: (0, t)),
             ],
             out_specs=[
                 pl.BlockSpec((rows, tile), lambda t, s: (0, t)),
@@ -343,12 +390,12 @@
             transcendentals=rows * vocab,
         ),
         name="head_logits",
-    )(where, *final, w_unit, counts)
-
-
-def head_grads_kernel(denom, halves, tables, where, *refs):
+    )(where, *[half for final in finals for half in final], w_unit, counts)
+
+
+def head_grads_kernel(denom, halves, chunks, tables, where, *refs):
     stats, refs = refs[:tables], refs[tables:]
-    lengths, logits, counts, w_unit, keep, *send, results, shift, total = refs
+    lengths, logits, counts, w_unit, *parts, results, shift, total = refs
     step = pl.program_id(0)
 
     @pl.when(step == 0)
@@ -374,29 +421,36 @@
 
     @pl.when(step == pl.num_programs(0) - 1)
     def _():
-        if send:
-            keep[...] = part_of(total, where[1], 2)
-            send[0][...] = part_of(total, 1 - where[1], 2).astype(send[0].dtype)
-        else:
-            keep[...] = total[...]
-
-
-def head_grads(where, halves, stats, lengths, logits, counts, at, w_unit, denom):
+        half = total.shape[0] // (chunks * halves)
+        for at in range(chunks):
+            base = at * halves * half
+            mine, theirs = base, base
+            if halves == 2:
+                mine, theirs = base + where[1] * half, base + (1 - where[1]) * half
+                out = parts[chunks + at]
+                out[...] = total[pl.ds(pl.multiple_of(theirs, half), half), :].astype(out.dtype)
+                parts[at][...] = total[pl.ds(pl.multiple_of(mine, half), half), :]
+            else:
+                parts[at][...] = total[base : base + half, :]
+
+
+def head_grads(where, halves, chunks, stats, lengths, logits, counts, w_unit, denom):
     rows, vocab = logits.shape
     width = w_unit.shape[0]
     tile = tile_of(vocab, 640)
-    part = (rows // halves, width)
-    shapes = [(part, F32)] + [(part, BF16)] * (halves - 1) + [((8, rows), F32)]
+    part = (rows // (halves * chunks), width)
+    shapes = [(part, F32)] * chunks + [(part, BF16)] * (chunks * (halves - 1))
+    shapes += [((8, rows), F32)]
     return pl.pallas_call(
-        functools.partial(head_grads_kernel, denom, halves, len(stats)),
+        functools.partial(head_grads_kernel, denom, halves, chunks, len(stats)),
         grid_spec=pltpu.PrefetchScalarGridSpec(
             num_scalar_prefetch=1,
             grid=(vocab // tile,),
             in_specs=[
                 *[whole_spec((8, rows))] * len(stats),
-                pl.BlockSpec((None, 1, rows), lambda t, s: (at, 0, 0)),
+                whole_spec((1, rows)),
                 pl.BlockSpec((rows, tile), lambda t, s: (0, t)),
-                pl.BlockSpec((None, rows, tile), lambda t, s: (at, 0, t)),
+                pl.BlockSpec((rows, tile), lambda t, s: (0, t)),
                 pl.BlockSpec((width, tile), lambda t, s: (0, t)),
             ],
             out_specs=[whole_spec(shape) for shape, _ in shapes],
@@ -512,10 +566,12 @@
     width, hidden = w_in.shape
     tile = tile_of(hidden, 512)
     blocks = len(g_parts)
-    count = g_parts[0][0].shape[1]
+    count = g_parts[0][0].shape[-2]
     rows = blocks * count
-    in_specs = [pl.BlockSpec((None, None, count, width), index) for _, index in x_parts]
-    in_specs += [pl.BlockSpec((None, count, width), index) for _, index in g_parts]
+    in_specs = [
+        pl.BlockSpec((None,) * (array.ndim - 2) + (count, width), index)
+        for array, index in (*x_parts, *g_parts)
+    ]
     in_specs += [
         pl.BlockSpec((width, tile), lambda j, s: (0, j)),
         pl.BlockSpec((tile, width), lambda j, s: (j, 0)),
@@ -580,10 +636,7 @@
     pair = mp_size == 2
     halves = 2 if pair else 1
     chunks = CHUNKS
-    def place(live_at):
-        live = (live_at >= 0) & (live_at < chunks)
-        return jnp.stack([seg, mp_at, jnp.asarray(live, jnp.int32)])
-
+    where = jnp.stack([seg, mp_at])
     first = w_in[0]
     second = w_out[0]
     rows = micro * row_count // chunks
@@ -592,7 +645,7 @@
     unit_count = unit_targets.shape[1]
     denom = float(micro * unit_count * dp_size)
     lengths = durations[:, 0, :]
-    length_f = lengths.astype(F32).reshape(chunks, 1, rows)
+    length_f = lengths.astype(F32).reshape(1, micro * row_count)
     ends = jnp.cumsum(lengths, axis=-1)
     own_ids = (seg * mp_size + mp_at) * vocab_part + jnp.arange(vocab_part, dtype=jnp.int32)
 
@@ -607,7 +660,6 @@
         unit_counts(packed[:, unit_count:], packed[:, :unit_count], own_ids)
         for packed in around(jnp.concatenate([unit_targets, ends], axis=1))
     ]
-    head_counts = unit_hits[0].reshape(chunks, rows, vocab_part)
     unit_hits = [hits.reshape(micro * row_count, vocab_part) for hits in unit_hits]
 
     def both(part):
@@ -629,122 +681,60 @@
             for k in range(1, count)
         ]
 
-    stash, x_halves, grads, finals, results = [], [], [], [], []
-    sums = None
-    x_gathered = None
-    f_hop = b_hop = None
-
-    def x_parts(at, side):
-        return [
-            (x_gathered[side], lambda j, s, k=k: (k, at, 0, 0)) for k in range(dp_size)
+    every = range(chunks)
+    stash = [None] * chunks
+    hops = [None] * chunks
+    for stage in range(segments):
+        for b in every:
+            arrived = []
+            if stage > 0:
+                arrived = both(lax.ppermute(hops[b], "segment", [(stage - 1, stage)]))
+            ties = unit_hits if stage == min(2, last) and b == 0 else []
+            outs = forward_section(
+                where, stage, halves, text, b, arrived, stash[b], first, second, ties
+            )
+            stash[b], keep, send = outs[:halves], outs[halves], outs[halves + 1 :]
+            pieces = reduced(keep, send)
+            hops[b] = total_of(pieces if pair else [stash[b][0], *pieces]).astype(BF16)
+    x_gathered = gathered_rows(jnp.stack([stash[b][0] for b in every]))
+
+    finals = []
+    for b in every:
+        options = [(last, hops[b])]
+        options += [
+            (to, lax.ppermute(hops[b], "segment", [(last, to)])) for to in range(last)
         ]
-
-    clocks = 2 * segments + chunks - 1
-    for clock in range(clocks):
-        f_out = b_out = None
-        f_ties, b_ties = [], []
-        head_at = clock - segments
-        if 0 <= head_at < chunks:
-            final = chosen(
-                seg,
-                [(last, f_hop)]
-                + [(to, lax.ppermute(f_hop, "segment", [(last, to)])) for to in range(last)],
+        finals.append(both(chosen(seg, options)))
+    logits, stats = head_logits(where, finals, w_unit, unit_hits[0])
+    *parts, result = head_grads(
+        where, halves, chunks, all_tables(stats), length_f, logits, unit_hits[0], w_unit, denom
+    )
+    loss = (jnp.sum(result[1, :]) / denom)[None]
+    shifts = around(result[0:1, :])
+    unit_rows = gathered_rows(jnp.stack([final[0] for final in finals]))
+    for b in every:
+        dnorm = total_of(reduced(parts[b], parts[chunks + b : chunks + b + 1])).astype(BF16)
+        dnorm = total_of(
+            [dnorm] + [lax.ppermute(dnorm, "segment", [(j, last)]) for j in range(last)]
+        ).astype(BF16)
+        hops[b] = norm_back(finals[b][0], dnorm.astype(F32)).astype(BF16)
+
+    grads = [[] for _ in every]
+    for stage in range(last):
+        owner = last - stage
+        for b in every:
+            came = hops[b]
+            if stage > 0:
+                came = lax.ppermute(came, "segment", [(owner + 1, owner)])
+            ties = []
+            if b == 0 and stage == last - 1:
+                ties = [*shifts, *x_gathered, *unit_rows]
+            outs = backward_section(
+                where, owner, stash[b], both(came), grads[b], first, second, ties
             )
-            finals.append(final)
-            logits, stats = head_logits(place(0), both(final), w_unit, head_counts, head_at)
-            f_ties = [logits]
-        if clock < segments + chunks - 1:
-            arrived = [] if clock == 0 else both(shifted(f_hop, "segment", 1))
-            if clock == segments - 1:
-                f_ties = unit_hits
-            rows_in, mine, keep, *send = forward_section(
-                place(clock - seg),
-                text,
-                min(clock, chunks - 1),
-                halves,
-                arrived,
-                first,
-                second,
-                f_ties,
-            )
-            stash.append(rows_in)
-            x_halves.append(mine)
-            pieces = reduced(keep, send)
-            f_out = total_of(pieces if pair else [mine, *pieces]).astype(BF16)
-        if clock == segments + chunks - 2:
-            x_half = jnp.stack(
-                [
-                    chosen(seg, [(s, x_halves[b + s]) for s in range(segments)])
-                    for b in range(chunks)
-                ]
-            )
-            x_gathered = gathered_rows(x_half)
-        if clock >= segments:
-            arrived = None if head_at == 0 else shifted(b_hop, "segment", -1)
-            if head_at < chunks:
-                keep, *send, result = head_grads(
-                    place(0),
-                    halves,
-                    all_tables(stats),
-                    length_f,
-                    logits,
-                    head_counts,
-                    head_at,
-                    w_unit,
-                    denom,
-                )
-                results.append(result)
-                dnorm = total_of(reduced(keep, send)).astype(BF16)
-                dnorm = total_of(
-                    [dnorm]
-                    + [lax.ppermute(dnorm, "segment", [(j, last)]) for j in range(last)]
-                ).astype(BF16)
-                grad_final = norm_back(final, dnorm.astype(F32)).astype(BF16)
-                arrived = (
-                    grad_final if arrived is None else jnp.where(seg == last, grad_final, arrived)
-                )
-                if head_at == chunks - 1:
-                    unit_rows = gathered_rows(jnp.stack(finals))
-                    shifts = around(
-                        jnp.concatenate([result[0:1, :] for result in results], axis=1)
-                    )
-            grads.append(arrived)
-            if clock < clocks - 1:
-                options = []
-                for other in range(segments):
-                    stage = clock - 2 * segments + 1 + 2 * other
-                    if 0 <= stage < len(stash):
-                        options.append((other, stash[stage]))
-                if clock == clocks - 3:
-                    b_ties = [*shifts, *x_gathered]
-                if clock == clocks - 2:
-                    b_ties = unit_rows
-                mine, keep, *send = backward_section(
-                    place(head_at - last + seg),
-                    halves,
-                    options,
-                    both(arrived),
-                    first,
-                    second,
-                    b_ties,
-                )
-                b_out = finish_backward(mine, arrived, reduced(keep, send))
-        if clock >= 2 * segments - 1:
-            at = clock - 2 * segments + 1
-            mine = chosen(seg, [(s, grads[at + last - s]) for s in range(segments)])
-            for side, source in enumerate(gathered_rows(mine)):
-                sums = weight_grads(
-                    dp_at[None],
-                    x_parts(at, side),
-                    [(source, lambda j, s, k=k: (k, 0, 0)) for k in range(dp_size)],
-                    first,
-                    second,
-                    sums,
-                    width // dp_size,
-                )
-        f_hop, b_hop = f_out, b_out
-
-    loss = (sum(jnp.sum(result[1, :]) for result in results) / denom)[None]
+            grads[b], keep, send = outs[:halves], outs[halves], outs[halves + 1 :]
+            hops[b] = finish_backward(stash[b][0], came, reduced(keep, send))
+
     unit_parts = [
         (
             source,
@@ -758,6 +748,37 @@
     sum_unit = unit_grads(
         jnp.stack([dp_at, mp_at]), unit_parts, shifts, unit_hits, w_unit, denom, width // dp_size
     )
+    for b in every:
+        arrived = both(lax.ppermute(hops[b], "segment", [(1, 0)]))
+        grads[b] = pick(where, 0, arrived, grads[b], [sum_unit] if b == 0 else [])
+    share = width // dp_size
+    sums = weight_grads(
+        dp_at[None],
+        [(half, lambda j, s: (0, 0)) for b in every for half in stash[b]],
+        [(half, lambda j, s: (0, 0)) for b in every for half in grads[b]],
+        first,
+        second,
+        None,
+        share,
+    )
+    for b in every:
+        sources = gathered_rows(grads[b][0])
+        others = [(side, k) for side in range(halves) for k in range(1, dp_size)]
+        sums = weight_grads(
+            dp_at[None],
+            [
+                (x_gathered[side], lambda j, s, k=k: (lax.rem(s[0] + k, dp_size), b, 0, 0))
+                for side, k in others
+            ],
+            [
+                (sources[side], lambda j, s, k=k: (lax.rem(s[0] + k, dp_size), 0, 0))
+                for side, k in others
+            ],
+            first,
+            second,
+            sums,
+            share,
+        )
     return (loss, sums[0][None], sums[1][None], sum_unit)
 
 

time: 489 us -> 525 us (1.074)
  waiting for transfers between devices: 125 us -> 176 us
  starting transfers between devices: 97.4 us -> 73.1 us
  Pallas kernels: 186 us -> 199 us
  other arithmetic: 32.1 us -> 22.5 us
    ppermute x14 -> x18, waiting for transfers between devices: 54.6 us -> 116 us  [the longest x4 46.2 us: on_device(): came = lax.ppermute(came, 'segment', [(owner + 1, owner)])]
    pallas_call x13 -> x18, Pallas kernels: 91.5 us -> 115 us  [the longest x8 50.2 us: forward_section(): pl.pallas_call(functools.partial(forward_kernel, halves, stage, len(ties)...]
    ppermute x6, starting transfers between devices: 19.6 us -> 7.49 us  [on_device(): lax.ppermute(dnorm, 'segment', [(j, last)])]
    ppermute x14 -> x18, starting transfers between devices: 31.4 us -> 19.4 us  [the longest x6 6.89 us: on_device(): arrived = both(lax.ppermute(hops[b], 'segment', [(stage - 1, stage)]))]
    pallas_call x4 -> x3, Pallas kernels: 78.4 us -> 67.6 us  [weight_grads(): pl.pallas_call(functools.partial(weight_kernel, blocks, adding, share), g...]
    all_gather x4, waiting for transfers between devices: 39.4 us -> 32.3 us  [gathered_rows(): came = lax.all_gather(mine, 'dp')]
    ppermute x14 -> x7, starting transfers between devices: 22.2 us -> 17.4 us  [all_tables(): lax.ppermute(table, ('segment', 'mp'), [(i, (i + k) % count) for i in ran...]
    unnamed x118 -> x152, local copies, waits for them, and re-layouts: 10.3 us -> 14 us
  transfers between devices with their start and end apart: 69 -> 77, of which waited for: 27 -> 24; matrix products, arithmetic and copies ran while one was open for 7% -> 7% of each run, Pallas kernels for 27% -> 31%
where the time goes in v7:
time: 525 us; the launch traced here: 515 us
  Pallas kernels  199 us (38%)
  waiting for transfers between devices  176 us (34%)
  starting transfers between devices  73.1 us (14%)
  other arithmetic  22.5 us (4%)
  between operations  17.1 us (3%)
  local copies, waits for them, and re-layouts  14 us (3%)
  matrix products  12.8 us (2%)
    pallas_call x3, Pallas kernels, weight_grads(): pl.pallas_call(functools.partial(weight_kernel, blocks, adding, share), g...  67.6 us
    pallas_call x8, Pallas kernels, forward_section(): pl.pallas_call(functools.partial(forward_kernel, halves, stage, len(ties)...  50.2 us
    pallas_call x6, Pallas kernels, backward_section(): pl.pallas_call(functools.partial(backward_kernel, halves, owner, len(befo...  46.5 us
    ppermute x4, waiting for transfers between devices, on_device(): came = lax.ppermute(came, 'segment', [(owner + 1, owner)])  46.2 us
    ppermute x6, waiting for transfers between devices, on_device(): lax.ppermute(hops[b], 'segment', [(last, to)])  45 us
    all_gather x4, waiting for transfers between devices, gathered_rows(): came = lax.all_gather(mine, 'dp')  32.3 us
    ppermute x36, starting transfers between devices, swapped(): return lax.ppermute(block, 'mp', [(0, 1), (1, 0)])  19.8 us
    ppermute x6, waiting for transfers between devices, on_device(): arrived = both(lax.ppermute(hops[b], 'segment', [(stage - 1, stage)]))  19.5 us
  transfers between devices with their start and end apart: 77, of which 24 were waited for; matrix products, arithmetic and copies ran while one was open for 7% of the time, Pallas kernels for 31%

profile of v7, /device:TPU:11, one launch (start us, length us, event | category | flops | bytes accessed | tf_op | source)
XLA Modules:
  0.0 514.6 jit_solution(17199565375403416741)
XLA Ops:
  30.8 16.9 %collective-permute-done.18.refs_0_ = bf16[128,1024]{1,0:T(8,128)(2,1)S(1)} collective-permute-done((bf16[128,1024]{1,0:T(8,128)(2,1)S(1)}, bf16[128,1024]{1,0:T(8,128)(2,1)S(1)}, u32[]{:S(2)}, u32[]{:S(2)}) %collective-permute-start.18) | collective-permute-done | bytes 262176 | tf_op jit(solution)/shard_map/ppermute | solution.py:691
  55.0 10.8 %section_forward.13 = (bf16[128,1024]{1,0:T(8,128)(2,1)}, bf16[128,1024]{1,0:T(8,128)(2,1)}, f32[128,1024]{1,0:T(8,128)}, bf16[128,1024]{1,0:T(8,128)(2,1)}) custom-call(s32[2]{0:T(128)} %pad_add_fusion.1.where, bf16[128,1024]{1,0:T(8,128)(2,1)} %copy-done.33, bf16[128,1024]{1,0:T(8,128)(2,1)} %copy-done.39, bf16[128,1024]{1,0:T(8,128)(2,1)} %get-tuple-element.93.refs_2_, ...), custom_call_target="tpu_custom_call" | custom-call | flops 4294967296 | bytes 16777216 | tf_op jit(solution)/shard_map/section_forward/pallas_call | solution.py:174
  66.6 11.0 %section_forward.9 = (bf16[128,1024]{1,0:T(8,128)(2,1)}, bf16[128,1024]{1,0:T(8,128)(2,1)}, f32[128,1024]{1,0:T(8,128)}, bf16[128,1024]{1,0:T(8,128)(2,1)}) custom-call(s32[2]{0:T(128)} %pad_add_fusion.1.where, bf16[128,1024]{1,0:T(8,128)(2,1)} %copy-done.34, bf16[128,1024]{1,0:T(8,128)(2,1)} %copy-done.40, bf16[128,1024]{1,0:T(8,128)(2,1)} %get-tuple-element.79.refs_2_, ...), custom_call_target="tpu_custom_call" | custom-call | flops 4294967296 | bytes 16777216 | tf_op jit(solution)/shard_map/section_forward/pallas_call | solution.py:174
  98.0 4.9 section_forward.10
  114.7 4.9 section_forward.11
  127.8 40.5 %collective-permute-done.28 = bf16[128,1024]{1,0:T(8,128)(2,1)S(1)} collective-permute-done((bf16[128,1024]{1,0:T(8,128)(2,1)S(1)}, bf16[128,1024]{1,0:T(8,128)(2,1)S(1)}, u32[]{:S(2)}, u32[]{:S(2)}) %collective-permute-start.28) | collective-permute-done | bytes 262176 | tf_op jit(solution)/shard_map/ppermute | solution.py:705
  176.6 6.9 %head_logits.1 = (f32[512,1280]{1,0:T(8,128)}, f32[8,512]{1,0:T(8,128)}) custom-call(s32[2]{0:T(128)} %pad_add_fusion.1.where, bf16[128,1024]{1,0:T(8,128)(2,1)} %copy-done.11, bf16[128,1024]{1,0:T(8,128)(2,1)} %copy-done.48, bf16[128,1024]{1,0:T(8,128)(2,1)} %copy-done.9, bf16[128,1024]{1,0:T(8,128)(2,1)} %copy-done.46, bf16[1024,1280]{1,0:T(8,128)(2,1)} %refs_24_.1, ...), custom_call_target="tpu_custom_call" | custom-call | flops 1342177280 | bytes 6553600 | tf_op jit(solution)/shard_map/head_logits/pallas_call | solution.py:366
  183.5 6.0 %collective-permute-start.31 = (f32[8,512]{1,0:T(8,128)}, f32[8,512]{1,0:T(8,128)S(1)}, u32[]{:S(2)}, u32[]{:S(2)}) collective-permute-start(f32[8,512]{1,0:T(8,128)} %get-tuple-element.105.refs_0_), channel_id=1, source_target_pairs={{0,4},{4,8},{8,12},{12,16},{16,20},{20,24},{24,28},{28,0},{1,5},{5... | collective-permute-start | bytes 49160 | tf_op jit(solution)/shard_map/ppermute | solution.py:680
  205.9 6.5 %head_grads.1 = (f32[128,1024]{1,0:T(8,128)}, f32[128,1024]{1,0:T(8,128)}, bf16[128,1024]{1,0:T(8,128)(2,1)}, bf16[128,1024]{1,0:T(8,128)(2,1)}, f32[8,512]{1,0:T(8,128)}) custom-call(s32[2]{0:T(128)} %pad_add_fusion.1.where, f32[8,512]{1,0:T(8,128)} %get-tuple-element.105.refs_0_, f32[8,512]{1,0:T(8,128)} %copy-done.56, f32[8,512]{1,0:T(8,128)} %copy-done.57, ...), custom_call_target="tpu_custom_call" | custom-call | flops 1342177280 | bytes 6553600 | tf_op jit(solution)/shard_map/head_grads/pallas_call | solution.py:444
  223.9 11.3 %collective-permute-done.60 = bf16[128,1024]{1,0:T(8,128)(2,1)S(1)} collective-permute-done((bf16[128,1024]{1,0:T(8,128)(2,1)S(1)}, bf16[128,1024]{1,0:T(8,128)(2,1)S(1)}, u32[]{:S(2)}, u32[]{:S(2)}) %collective-permute-start.60) | collective-permute-done | bytes 262176 | tf_op jit(solution)/shard_map/ppermute | solution.py:718
  248.3 4.9 section_backward.6
  257.5 5.2 %all-gather.13.cloned.1.call-done = bf16[8,128,1024]{2,1,0:T(8,128)(2,1)} async-done(((bf16[2,128,1024]{2,1,0:T(8,128)(2,1)}), bf16[8,128,1024]{2,1,0:T(8,128)(2,1)}) %all-gather.13.cloned.1.call-update) | async-done | bytes 2097168 | tf_op jit(solution)/shard_map/all_gather | solution.py:672
  264.3 5.0 section_backward.10
  270.0 5.1 section_backward.7
  284.9 40.6 %collective-permute-done.67.refs_10_ = bf16[128,1024]{1,0:T(8,128)(2,1)S(1)} collective-permute-done((bf16[128,1024]{1,0:T(8,128)(2,1)S(1)}, bf16[128,1024]{1,0:T(8,128)(2,1)S(1)}, u32[]{:S(2)}, u32[]{:S(2)}) %collective-permute-start.67) | collective-permute-done | bytes 262176 | tf_op jit(solution)/shard_map/ppermute | solution.py:728
  330.3 12.8 %section_backward.11 = (bf16[128,1024]{1,0:T(8,128)(2,1)}, bf16[128,1024]{1,0:T(8,128)(2,1)}, f32[128,1024]{1,0:T(8,128)}, bf16[128,1024]{1,0:T(8,128)(2,1)}) custom-call(s32[2]{0:T(128)} %pad_add_fusion.1.where, f32[1,512]{1,0:T(1,128)} %copy-done.55, f32[1,512]{1,0:T(1,128)} %copy-done.64, f32[1,512]{1,0:T(1,128)} %copy-done.65, f32[1,512]{1,0:T(1,128)} %copy-done.66, ...), custom_call_target="tpu_custom_call" | custom-call | flops 6442450944 | bytes 16777216 | tf_op jit(solution)/shard_map/section_backward/pallas_call | solution.py:253
  350.6 5.6 %collective-permute-done.48.refs_2_ = bf16[128,1024]{1,0:T(8,128)(2,1)S(1)} collective-permute-done((bf16[128,1024]{1,0:T(8,128)(2,1)S(1)}, bf16[128,1024]{1,0:T(8,128)(2,1)S(1)}, u32[]{:S(2)}, u32[]{:S(2)}) %collective-permute-start.48) | collective-permute-done | bytes 262176 | tf_op jit(solution)/shard_map/ppermute | solution.py:728
  357.1 15.7 %unit_grads.1.refs_0_ = f32[256,1280]{1,0:T(8,128)} custom-call(s32[2]{0:T(128)} %pad_add_fusion.2.where, bf16[4,2,128,1024]{3,2,1,0:T(8,128)(2,1)} %bitcast.60, bf16[4,2,128,1024]{3,2,1,0:T(8,128)(2,1)} %bitcast.61, bf16[4,2,128,1024]{3,2,1,0:T(8,128)(2,1)} %bitcast.62, bf16[4,2,128,1024]{3,2,1,0:T(8,128)(2,1)} %bitcast.63, ...), custom_call_target="tpu_custom_call" | custom-call | flops 6710886400 | bytes 7864320 | tf_op jit(solution)/shard_map/unit_grads/pallas_call | solution.py:507
  377.0 13.8 %section_backward.8 = (bf16[128,1024]{1,0:T(8,128)(2,1)}, bf16[128,1024]{1,0:T(8,128)(2,1)}, f32[128,1024]{1,0:T(8,128)}, bf16[128,1024]{1,0:T(8,128)(2,1)}) custom-call(s32[2]{0:T(128)} %pad_add_fusion.1.where, bf16[128,1024]{1,0:T(8,128)(2,1)} %get-tuple-element.109.refs_0_.refs_2_, bf16[128,1024]{1,0:T(8,128)(2,1)} %get-tuple-element.112.refs_1_.refs_3_, ...), custom_call_target="tpu_custom_call" | custom-call | flops 6442450944 | bytes 16777216 | tf_op jit(solution)/shard_map/section_backward/pallas_call | solution.py:253
  396.8 5.4 %collective-permute-done.51.refs_0_ = bf16[128,1024]{1,0:T(8,128)(2,1)S(1)} collective-permute-done((bf16[128,1024]{1,0:T(8,128)(2,1)S(1)}, bf16[128,1024]{1,0:T(8,128)(2,1)S(1)}, u32[]{:S(2)}, u32[]{:S(2)}) %collective-permute-start.51) | collective-permute-done | bytes 262176 | tf_op jit(solution)/shard_map/ppermute | solution.py:752
  408.7 27.1 %all-gather.11.cloned.1.call-done = bf16[512,1024]{1,0:T(8,128)(2,1)} async-done(((bf16[128,1024]{1,0:T(8,128)(2,1)}), bf16[512,1024]{1,0:T(8,128)(2,1)}) %all-gather.11.cloned.1.call-update) | async-done | bytes 1048592 | tf_op jit(solution)/shard_map/all_gather | solution.py:672
  436.8 18.7 %weight_grads.3 = (f32[256,4096]{1,0:T(8,128)}, f32[4096,256]{1,0:T(8,128)}) custom-call(s32[1]{0:T(128)} %bitcast.12.where, bf16[128,1024]{1,0:T(8,128)(2,1)} %get-tuple-element.108.refs_0_.refs_8_, bf16[128,1024]{1,0:T(8,128)(2,1)} %get-tuple-element.128.refs_1_.refs_9_, bf16[128,1024]{1,0:T(8,128)(2,1)} %get-tuple-element.109.refs_0_.refs_2_, ...), custom_call_target="tpu_custom_call" | custom-call | flops 10737418240 | bytes 33554432 | tf_op jit(solution)/shard_map/weight_grads/pallas_call | solution.py:588
  456.5 24.5 %weight_grads.4 = (f32[256,4096]{1,0:T(8,128)}, f32[4096,256]{1,0:T(8,128)}) custom-call(s32[1]{0:T(128)} %bitcast.12.where, bf16[4,2,128,1024]{3,2,1,0:T(8,128)(2,1)} %bitcast.86, bf16[4,2,128,1024]{3,2,1,0:T(8,128)(2,1)} %bitcast.87, bf16[4,2,128,1024]{3,2,1,0:T(8,128)(2,1)} %bitcast.88, ...), custom_call_target="tpu_custom_call", output_to_operand_aliasing={{0}: (15, {}), {1}: (16, {})} | custom-call | flops 16106127360 | bytes 33554432 | tf_op jit(solution)/shard_map/weight_grads/pallas_call | solution.py:588
  482.0 24.5 %weight_grads.5 = (f32[256,4096]{1,0:T(8,128)}, f32[4096,256]{1,0:T(8,128)}) custom-call(s32[1]{0:T(128)} %bitcast.12.where, bf16[4,2,128,1024]{3,2,1,0:T(8,128)(2,1)} %bitcast.89, bf16[4,2,128,1024]{3,2,1,0:T(8,128)(2,1)} %bitcast.90, bf16[4,2,128,1024]{3,2,1,0:T(8,128)(2,1)} %bitcast.91, ...), custom_call_target="tpu_custom_call", output_to_operand_aliasing={{0}: (15, {}), {1}: (16, {})} | custom-call | flops 16106127360 | bytes 33554432 | tf_op jit(solution)/shard_map/weight_grads/pallas_call | solution.py:588
  (374 shorter events, 169.2 us)
Async XLA Ops:
  7.2 249.9 %all-gather.9.cloned.1.call-start = ((), (), s32[]{:S(2)}) async-start(), calls=%async_computation | async-start | bytes 2621440 | tf_op jit(solution)/shard_map/all_gather | solution.py:672
  8.9 18.7 %collective-permute-start = (s32[4,640]{1,0:T(4,128)S(1)}, s32[4,640]{1,0:T(4,128)S(1)}, u32[]{:S(2)}, u32[]{:S(2)}) collective-permute-start(s32[4,640]{1,0:T(4,128)S(1)} %pad_add_fusion), channel_id=1, source_target_pairs={{0,1},{1,2},{2,3},{3,0},{4,5},{5,6},{6,7},{7,4},{8,9},{9,10},{10,1... | collective-permute-start | bytes 30728 | tf_op jit(solution)/shard_map/ppermute | solution.py:656
  10.2 19.2 %collective-permute-start.1 = (s32[4,640]{1,0:T(4,128)S(1)}, s32[4,640]{1,0:T(4,128)S(1)}, u32[]{:S(2)}, u32[]{:S(2)}) collective-permute-start(s32[4,640]{1,0:T(4,128)S(1)} %pad_add_fusion), channel_id=1, source_target_pairs={{0,2},{1,3},{2,0},{3,1},{4,6},{5,7},{6,4},{7,5},{8,10},{9,11},{10,... | collective-permute-start | bytes 30728 | tf_op jit(solution)/shard_map/ppermute | solution.py:656
  11.2 71.6 %collective-permute-start.2 = (s32[4,640]{1,0:T(4,128)S(1)}, s32[4,640]{1,0:T(4,128)S(1)}, u32[]{:S(2)}, u32[]{:S(2)}) collective-permute-start(s32[4,640]{1,0:T(4,128)S(1)} %pad_add_fusion), channel_id=1, source_target_pairs={{0,3},{1,0},{2,1},{3,2},{4,7},{5,4},{6,5},{7,6},{8,11},{9,8},{10,9... | collective-permute-start | bytes 30728 | tf_op jit(solution)/shard_map/ppermute | solution.py:656
  27.7 20.0 %collective-permute-start.18 = (bf16[128,1024]{1,0:T(8,128)(2,1)S(1)}, bf16[128,1024]{1,0:T(8,128)(2,1)S(1)}, u32[]{:S(2)}, u32[]{:S(2)}) collective-permute-start(bf16[128,1024]{1,0:T(8,128)(2,1)S(1)} %add_convert_fusion.7), channel_id=1, source_target_pairs={{0,8},{1,9},{2,10},{3,11},{4,12},{5,13},{6,14},{7,15}} | collective-permute-start | bytes 786440 | tf_op jit(solution)/shard_map/ppermute | solution.py:691
  29.5 23.8 %collective-permute-start.4 = (bf16[128,1024]{1,0:T(8,128)(2,1)S(1)}, bf16[128,1024]{1,0:T(8,128)(2,1)S(1)}, u32[]{:S(2)}, u32[]{:S(2)}) collective-permute-start(bf16[128,1024]{1,0:T(8,128)(2,1)S(1)} %add_convert_fusion.11), channel_id=1, source_target_pairs={{0,8},{1,9},{2,10},{3,11},{4,12},{5,13},{6,14},{7,15}} | collective-permute-start | bytes 786440 | tf_op jit(solution)/shard_map/ppermute | solution.py:691
  121.5 141.2 %all-gather.13.cloned.1.call-start = ((), (), s32[]{:S(2)}) async-start(), calls=%async_computation.2 | async-start | bytes 2621440 | tf_op jit(solution)/shard_map/all_gather | solution.py:672
  122.5 45.8 %collective-permute-start.28 = (bf16[128,1024]{1,0:T(8,128)(2,1)S(1)}, bf16[128,1024]{1,0:T(8,128)(2,1)S(1)}, u32[]{:S(2)}, u32[]{:S(2)}) collective-permute-start(bf16[128,1024]{1,0:T(8,128)(2,1)S(1)} %add_convert_fusion.4), channel_id=1, source_target_pairs={{24,8},{25,9},{26,10},{27,11},{28,12},{29,13},{30,14},{31,15}} | collective-permute-start | bytes 786440 | tf_op jit(solution)/shard_map/ppermute | solution.py:705
  123.8 44.5 %collective-permute-start.29 = (bf16[128,1024]{1,0:T(8,128)(2,1)S(1)}, bf16[128,1024]{1,0:T(8,128)(2,1)S(1)}, u32[]{:S(2)}, u32[]{:S(2)}) collective-permute-start(bf16[128,1024]{1,0:T(8,128)(2,1)S(1)} %add_convert_fusion.4), channel_id=1, source_target_pairs={{24,0},{25,1},{26,2},{27,3},{28,4},{29,5},{30,6},{31,7}} | collective-permute-start | bytes 786440 | tf_op jit(solution)/shard_map/ppermute | solution.py:705
  124.6 44.8 %collective-permute-start.13 = (bf16[128,1024]{1,0:T(8,128)(2,1)S(1)}, bf16[128,1024]{1,0:T(8,128)(2,1)S(1)}, u32[]{:S(2)}, u32[]{:S(2)}) collective-permute-start(bf16[128,1024]{1,0:T(8,128)(2,1)S(1)} %add_convert_fusion.8), channel_id=1, source_target_pairs={{24,16},{25,17},{26,18},{27,19},{28,20},{29,21},{30,22},{31,23}} | collective-permute-start | bytes 786440 | tf_op jit(solution)/shard_map/ppermute | solution.py:705
  125.3 48.7 %collective-permute-start.14 = (bf16[128,1024]{1,0:T(8,128)(2,1)S(1)}, bf16[128,1024]{1,0:T(8,128)(2,1)S(1)}, u32[]{:S(2)}, u32[]{:S(2)}) collective-permute-start(bf16[128,1024]{1,0:T(8,128)(2,1)S(1)} %add_convert_fusion.8), channel_id=1, source_target_pairs={{24,8},{25,9},{26,10},{27,11},{28,12},{29,13},{30,14},{31,15}} | collective-permute-start | bytes 786440 | tf_op jit(solution)/shard_map/ppermute | solution.py:705
  126.6 47.4 %collective-permute-start.15 = (bf16[128,1024]{1,0:T(8,128)(2,1)S(1)}, bf16[128,1024]{1,0:T(8,128)(2,1)S(1)}, u32[]{:S(2)}, u32[]{:S(2)}) collective-permute-start(bf16[128,1024]{1,0:T(8,128)(2,1)S(1)} %add_convert_fusion.8), channel_id=1, source_target_pairs={{24,0},{25,1},{26,2},{27,3},{28,4},{29,5},{30,6},{31,7}} | collective-permute-start | bytes 786440 | tf_op jit(solution)/shard_map/ppermute | solution.py:705
  216.0 19.1 %collective-permute-start.60 = (bf16[128,1024]{1,0:T(8,128)(2,1)S(1)}, bf16[128,1024]{1,0:T(8,128)(2,1)S(1)}, u32[]{:S(2)}, u32[]{:S(2)}) collective-permute-start(bf16[128,1024]{1,0:T(8,128)(2,1)S(1)} %add_convert_fusion.1), channel_id=1, source_target_pairs={{8,24},{9,25},{10,26},{11,27},{12,28},{13,29},{14,30},{15,31}} | collective-permute-start | bytes 786440 | tf_op jit(solution)/shard_map/ppermute | solution.py:718
  219.9 187.8 %all-gather.15.cloned.1.call-start = ((), (), s32[]{:S(2)}) async-start(), calls=%async_computation.3 | async-start | bytes 1310720 | tf_op jit(solution)/shard_map/all_gather | solution.py:672
  220.7 20.1 %collective-permute-start.41 = (bf16[128,1024]{1,0:T(8,128)(2,1)S(1)}, bf16[128,1024]{1,0:T(8,128)(2,1)S(1)}, u32[]{:S(2)}, u32[]{:S(2)}) collective-permute-start(bf16[128,1024]{1,0:T(8,128)(2,1)S(1)} %add_convert_fusion.3), channel_id=1, source_target_pairs={{8,24},{9,25},{10,26},{11,27},{12,28},{13,29},{14,30},{15,31}} | collective-permute-start | bytes 786440 | tf_op jit(solution)/shard_map/ppermute | solution.py:718
  257.1 71.8 %collective-permute-start.38 = (bf16[4,2,128,1024]{3,2,1,0:T(8,128)(2,1)}, bf16[4,2,128,1024]{3,2,1,0:T(8,128)(2,1)}, u32[]{:S(2)}, u32[]{:S(2)}) collective-permute-start(bf16[4,2,128,1024]{3,2,1,0:T(8,128)(2,1)} %bitcast.84), channel_id=1, source_target_pairs={{0,4},{4,0},{1,5},{5,1},{2,6},{6,2},{3,7},{7,3},{8,12},{12,8},{9,1... | collective-permute-start | bytes 6291464 | tf_op jit(solution)/shard_map/ppermute | solution.py:23
  262.6 66.3 %collective-permute-start.54 = (bf16[4,2,128,1024]{3,2,1,0:T(8,128)(2,1)}, bf16[4,2,128,1024]{3,2,1,0:T(8,128)(2,1)S(1)}, u32[]{:S(2)}, u32[]{:S(2)}) collective-permute-start(bf16[4,2,128,1024]{3,2,1,0:T(8,128)(2,1)} %bitcast.58), channel_id=1, source_target_pairs={{0,4},{4,0},{1,5},{5,1},{2,6},{6,2},{3,7},{7,3},{8,12},{12,8},{9,1... | collective-permute-start | bytes 6291464 | tf_op jit(solution)/shard_map/ppermute | solution.py:23
  278.2 47.3 %collective-permute-start.67 = (bf16[128,1024]{1,0:T(8,128)(2,1)S(1)}, bf16[128,1024]{1,0:T(8,128)(2,1)S(1)}, u32[]{:S(2)}, u32[]{:S(2)}) collective-permute-start(bf16[128,1024]{1,0:T(8,128)(2,1)S(1)} %fusion.75), channel_id=1, source_target_pairs={{16,8},{17,9},{18,10},{19,11},{20,12},{21,13},{22,14},{23,15}} | collective-permute-start | bytes 786440 | tf_op jit(solution)/shard_map/ppermute | solution.py:728
  280.9 45.5 %collective-permute-start.55 = (f32[1,512]{1,0:T(1,128)S(1)}, f32[1,512]{1,0:T(1,128)S(1)}, u32[]{:S(2)}, u32[]{:S(2)}) collective-permute-start(f32[1,512]{1,0:T(1,128)S(1)} %get-tuple-element.158.refs_16_.refs_0_), channel_id=1, source_target_pairs={{0,1},{1,2},{2,3},{3,0},{4,5},{5,6},{6,7},{7,4},{8,9},{9,10},{10,1... | collective-permute-start | bytes 6152 | tf_op jit(solution)/shard_map/ppermute | solution.py:656
  282.4 45.1 %collective-permute-start.56 = (f32[1,512]{1,0:T(1,128)S(1)}, f32[1,512]{1,0:T(1,128)S(1)}, u32[]{:S(2)}, u32[]{:S(2)}) collective-permute-start(f32[1,512]{1,0:T(1,128)S(1)} %get-tuple-element.158.refs_16_.refs_0_), channel_id=1, source_target_pairs={{0,2},{1,3},{2,0},{3,1},{4,6},{5,7},{6,4},{7,5},{8,10},{9,11},{10,... | collective-permute-start | bytes 6152 | tf_op jit(solution)/shard_map/ppermute | solution.py:656
  356.2 20.1 %collective-permute-start.49 = (bf16[128,1024]{1,0:T(8,128)(2,1)S(1)}, bf16[128,1024]{1,0:T(8,128)(2,1)S(1)}, u32[]{:S(2)}, u32[]{:S(2)}) collective-permute-start(bf16[128,1024]{1,0:T(8,128)(2,1)S(1)} %collective-permute-done.48.refs_2_), channel_id=1, source_target_pairs={{0,4},{4,0},{1,5},{5,1},{2,6},{6,2},{3,7},{7,3},{8,12},{12,8},{9,1... | collective-permute-start | bytes 786440 | tf_op jit(solution)/shard_map/ppermute | solution.py:23
  376.3 59.6 %all-gather.11.cloned.1.call-start = ((), (), s32[]{:S(2)}) async-start(), calls=%async_computation.1 | async-start | bytes 1310720 | tf_op jit(solution)/shard_map/all_gather | solution.py:672
  407.6 47.8 %collective-permute-start.72 = (bf16[4,128,1024]{2,1,0:T(8,128)(2,1)}, bf16[4,128,1024]{2,1,0:T(8,128)(2,1)S(1)}, u32[]{:S(2)}, u32[]{:S(2)}) collective-permute-start(bf16[4,128,1024]{2,1,0:T(8,128)(2,1)} %bitcast.93), channel_id=1, source_target_pairs={{0,4},{4,0},{1,5},{5,1},{2,6},{6,2},{3,7},{7,3},{8,12},{12,8},{9,1... | collective-permute-start | bytes 3145736 | tf_op jit(solution)/shard_map/ppermute | solution.py:23
  435.9 45.1 %collective-permute-start.53 = (bf16[4,128,1024]{2,1,0:T(8,128)(2,1)}, bf16[4,128,1024]{2,1,0:T(8,128)(2,1)S(1)}, u32[]{:S(2)}, u32[]{:S(2)}) collective-permute-start(bf16[4,128,1024]{2,1,0:T(8,128)(2,1)} %bitcast.97), channel_id=1, source_target_pairs={{0,4},{4,0},{1,5},{5,1},{2,6},{6,2},{3,7},{7,3},{8,12},{12,8},{9,1... | collective-permute-start | bytes 3145736 | tf_op jit(solution)/shard_map/ppermute | solution.py:23
  (130 other events, 946.2 us)
Sparse Core Ops, SparseCore 0:
  121.6 78.5 all-gather.8
  220.0 42.5 all-gather.12
  376.4 27.1 all-gather.14
  407.7 28.1 all-gather.10

commit v8 on v7

--- a/solution.py
+++ b/solution.py
@@ -477,12 +477,8 @@
 
     @pl.when(pl.program_id(0) == 0)
     def _():
-        for ref, (base, theirs) in zip(x_refs, blocks):
-            side = 0
-            if theirs is not None:
-                side = 1 - where[1] if theirs else where[1]
-            place = pl.ds(pl.multiple_of(base + side * half, half), half)
-            normed[place, :] = normalised(ref[...])
+        for ref, base in zip(x_refs, blocks):
+            normed[base : base + half, :] = normalised(ref[...])
         columns = pl.ds(pl.multiple_of(where[0] * share, share), share)
         normed_t[...] = normed[:, columns].astype(F32).T.astype(BF16)
         for shift, column in zip(shifts, columns_of):
@@ -500,7 +496,7 @@
 def unit_grads(where, x_parts, shifts, counts, w_unit, denom, share):
     width, vocab = w_unit.shape
     tile = tile_of(vocab, 256)
-    half = x_parts[0][0].shape[2]
+    half = x_parts[0][0].shape[-2]
     rows = shifts[0].shape[1]
     tables = len(shifts)
     blocks = tuple(block for _, _, block in x_parts)
@@ -509,7 +505,7 @@
         grid_spec=pltpu.PrefetchScalarGridSpec(
             num_scalar_prefetch=1,
             grid=(vocab // tile,),
-            in_specs=[pl.BlockSpec((None, None, half, width), index) for _, index, _ in x_parts]
+            in_specs=[pl.BlockSpec((None, None, None, half, width), index) for _, index, _ in x_parts]
             + [whole_spec((1, rows))] * tables
             + [pl.BlockSpec((rows, tile), lambda j, s: (0, j))] * tables
             + [pl.BlockSpec((width, tile), lambda j, s: (0, j))],
@@ -669,8 +665,10 @@
         return [keep, swapped(send[0])] if pair else [lax.psum(keep, "mp")]
 
     def gathered_rows(mine):
-        came = lax.all_gather(mine, "dp")
-        return [came, swapped(came)] if pair else [came]
+        if pair:
+            came = lax.all_gather(mine, ("mp", "dp"))
+            return came.reshape(mp_size, dp_size, *mine.shape)
+        return lax.all_gather(mine, "dp")[None]
 
     def all_tables(table):
         if not pair:
@@ -689,7 +687,7 @@
             arrived = []
             if stage > 0:
                 arrived = both(lax.ppermute(hops[b], "segment", [(stage - 1, stage)]))
-            ties = unit_hits if stage == min(2, last) and b == 0 else []
+            ties = [hops[b - 1], *unit_hits[stage : stage + 1]] if b > 0 else []
             outs = forward_section(
                 where, stage, halves, text, b, arrived, stash[b], first, second, ties
             )
@@ -726,9 +724,7 @@
             came = hops[b]
             if stage > 0:
                 came = lax.ppermute(came, "segment", [(owner + 1, owner)])
-            ties = []
-            if b == 0 and stage == last - 1:
-                ties = [*shifts, *x_gathered, *unit_rows]
+            ties = [hops[b - 1]] if b > 0 else []
             outs = backward_section(
                 where, owner, stash[b], both(came), grads[b], first, second, ties
             )
@@ -737,48 +733,45 @@
 
     unit_parts = [
         (
-            source,
-            lambda j, s, k=k, b=b: (lax.rem(s[0] + dp_size - k, dp_size), b, 0, 0),
-            ((k * chunks + b) * rows, bool(at) if pair else None),
+            unit_rows,
+            lambda j, s, side=side, k=k, b=b: (side, lax.rem(s[0] + dp_size - k, dp_size), b, 0, 0),
+            (k * micro * row_count + b * rows + side * (rows // halves)),
         )
-        for at, source in enumerate(unit_rows)
+        for side in range(halves)
         for k in range(dp_size)
-        for b in range(chunks)
+        for b in every
     ]
     sum_unit = unit_grads(
-        jnp.stack([dp_at, mp_at]), unit_parts, shifts, unit_hits, w_unit, denom, width // dp_size
+        dp_at[None], unit_parts, shifts, unit_hits, w_unit, denom, width // dp_size
     )
+    share = width // dp_size
+    sums = None
+    sources = [None] * chunks
+
+    def own_parts(halves_of):
+        return [(half, lambda j, s: (0, 0)) for half in halves_of]
+
+    def other_parts(array, tail):
+        return [
+            (array, lambda j, s, side=side, k=k: (side, lax.rem(s[0] + k, dp_size), *tail, 0, 0))
+            for side in range(halves)
+            for k in range(1, dp_size)
+        ]
+
+    def weight_step(x_parts, g_parts, sums):
+        return weight_grads(dp_at[None], x_parts, g_parts, first, second, sums, share)
+
+    waiting = ([], [])
     for b in every:
         arrived = both(lax.ppermute(hops[b], "segment", [(1, 0)]))
-        grads[b] = pick(where, 0, arrived, grads[b], [sum_unit] if b == 0 else [])
-    share = width // dp_size
-    sums = weight_grads(
-        dp_at[None],
-        [(half, lambda j, s: (0, 0)) for b in every for half in stash[b]],
-        [(half, lambda j, s: (0, 0)) for b in every for half in grads[b]],
-        first,
-        second,
-        None,
-        share,
-    )
-    for b in every:
-        sources = gathered_rows(grads[b][0])
-        others = [(side, k) for side in range(halves) for k in range(1, dp_size)]
-        sums = weight_grads(
-            dp_at[None],
-            [
-                (x_gathered[side], lambda j, s, k=k: (lax.rem(s[0] + k, dp_size), b, 0, 0))
-                for side, k in others
-            ],
-            [
-                (sources[side], lambda j, s, k=k: (lax.rem(s[0] + k, dp_size), 0, 0))
-                for side, k in others
-            ],
-            first,
-            second,
-            sums,
-            share,
-        )
+        ties = [sum_unit, sums[0]] if b == 1 else []
+        grads[b] = pick(where, 0, arrived, grads[b], ties)
+        source = gathered_rows(grads[b][0])
+        x_parts = own_parts(stash[b]) + waiting[0]
+        g_parts = own_parts(grads[b]) + waiting[1]
+        sums = weight_step(x_parts, g_parts, sums)
+        waiting = (other_parts(x_gathered, (b,)), other_parts(source, ()))
+    sums = weight_step(*waiting, sums)
     return (loss, sums[0][None], sums[1][None], sum_unit)
 
 

time: 525 us -> 455 us (0.87)
  waiting for transfers between devices: 176 us -> 91 us
  starting transfers between devices: 73.1 us -> 86.5 us
    all_gather x4, waiting for transfers between devices: 32.3 us -> 0.08 us  [gathered_rows(): came = lax.all_gather(mine, ('mp', 'dp'))]
    ppermute x4, waiting for transfers between devices: 46.2 us -> 24.7 us  [on_device(): came = lax.ppermute(came, 'segment', [(owner + 1, owner)])]
    ppermute x6, waiting for transfers between devices: 45 us -> 25.7 us  [on_device(): lax.ppermute(hops[b], 'segment', [(last, to)])]
    ppermute x6, starting transfers between devices: 7.49 us -> 19.1 us  [on_device(): lax.ppermute(dnorm, 'segment', [(j, last)])]
    ppermute x6, waiting for transfers between devices: 19.5 us -> 8.38 us  [on_device(): arrived = both(lax.ppermute(hops[b], 'segment', [(stage - 1, stage)]))]
    unnamed x152 -> x150, local copies, waits for them, and re-layouts: 14 us -> 12.2 us
    ppermute x36 -> x32, starting transfers between devices: 19.8 us -> 19.7 us  [swapped(): return lax.ppermute(block, 'mp', [(0, 1), (1, 0)])]
  transfers between devices with their start and end apart: 77 -> 73, of which waited for: 24 -> 20; matrix products, arithmetic and copies ran while one was open for 7% -> 8% of each run, Pallas kernels for 31% -> 38%
where the time goes in v8:
time: 455 us; the launch traced here: 446 us
  Pallas kernels  202 us (44%)
  waiting for transfers between devices  91 us (20%)
  starting transfers between devices  86.5 us (19%)
  other arithmetic  24.8 us (5%)
  between operations  17.1 us (4%)
  matrix products  12.9 us (3%)
  local copies, waits for them, and re-layouts  12.2 us (3%)
    pallas_call x3, Pallas kernels, weight_grads(): pl.pallas_call(functools.partial(weight_kernel, blocks, adding, share), g...  70.9 us
    pallas_call x8, Pallas kernels, forward_section(): pl.pallas_call(functools.partial(forward_kernel, halves, stage, len(ties)...  50.2 us
    pallas_call x6, Pallas kernels, backward_section(): pl.pallas_call(functools.partial(backward_kernel, halves, owner, len(befo...  46.7 us
    ppermute x6, waiting for transfers between devices, on_device(): lax.ppermute(hops[b], 'segment', [(last, to)])  25.7 us
    ppermute x4, waiting for transfers between devices, on_device(): came = lax.ppermute(came, 'segment', [(owner + 1, owner)])  24.7 us
    ppermute x32, starting transfers between devices, swapped(): return lax.ppermute(block, 'mp', [(0, 1), (1, 0)])  19.7 us
    ppermute x6, starting transfers between devices, on_device(): lax.ppermute(dnorm, 'segment', [(j, last)])  19.1 us
    ppermute x6, waiting for transfers between devices, on_device(): lax.ppermute(dnorm, 'segment', [(j, last)])  17 us
  transfers between devices with their start and end apart: 73, of which 20 were waited for; matrix products, arithmetic and copies ran while one was open for 8% of the time, Pallas kernels for 38%

profile of v8, /device:TPU:11, one launch (start us, length us, event | category | flops | bytes accessed | tf_op | source)
XLA Modules:
  0.0 446.1 jit_solution(8114133831192133198)
XLA Ops:
  23.2 8.4 %collective-permute-done.1.refs_0_ = bf16[128,1024]{1,0:T(8,128)(2,1)S(1)} collective-permute-done((bf16[128,1024]{1,0:T(8,128)(2,1)S(1)}, bf16[128,1024]{1,0:T(8,128)(2,1)S(1)}, u32[]{:S(2)}, u32[]{:S(2)}) %collective-permute-start.1) | collective-permute-done | bytes 262176 | tf_op jit(solution)/shard_map/ppermute | solution.py:689
  37.8 10.8 %section_forward.9 = (bf16[128,1024]{1,0:T(8,128)(2,1)}, bf16[128,1024]{1,0:T(8,128)(2,1)}, f32[128,1024]{1,0:T(8,128)}, bf16[128,1024]{1,0:T(8,128)(2,1)}) custom-call(s32[2]{0:T(128)} %pad_add_fusion.1.where, bf16[128,1024]{1,0:T(8,128)(2,1)} %copy-done.33, bf16[128,1024]{1,0:T(8,128)(2,1)} %copy-done.34, bf16[128,1024]{1,0:T(8,128)(2,1)} %get-tuple-element.79.refs_2_, ...), custom_call_target="tpu_custom_call" | custom-call | flops 4294967296 | bytes 16777216 | tf_op jit(solution)/shard_map/section_forward/pallas_call | solution.py:174
  55.7 10.8 %section_forward.13 = (bf16[128,1024]{1,0:T(8,128)(2,1)}, bf16[128,1024]{1,0:T(8,128)(2,1)}, f32[128,1024]{1,0:T(8,128)}, bf16[128,1024]{1,0:T(8,128)(2,1)}) custom-call(s32[2]{0:T(128)} %pad_add_fusion.1.where, bf16[128,1024]{1,0:T(8,128)(2,1)} %copy-done.17, bf16[512,1280]{1,0:T(8,128)(2,1)} %bitcast.101, bf16[128,1024]{1,0:T(8,128)(2,1)} %copy-done.30, ...), custom_call_target="tpu_custom_call" | custom-call | flops 4294967296 | bytes 16777216 | tf_op jit(solution)/shard_map/section_forward/pallas_call | solution.py:174
  119.2 20.3 %collective-permute-done.11 = bf16[128,1024]{1,0:T(8,128)(2,1)S(1)} collective-permute-done((bf16[128,1024]{1,0:T(8,128)(2,1)S(1)}, bf16[128,1024]{1,0:T(8,128)(2,1)S(1)}, u32[]{:S(2)}, u32[]{:S(2)}) %collective-permute-start.11) | collective-permute-done | bytes 262176 | tf_op jit(solution)/shard_map/ppermute | solution.py:703
  139.7 5.4 %collective-permute-done.28 = bf16[128,1024]{1,0:T(8,128)(2,1)S(1)} collective-permute-done((bf16[128,1024]{1,0:T(8,128)(2,1)S(1)}, bf16[128,1024]{1,0:T(8,128)(2,1)S(1)}, u32[]{:S(2)}, u32[]{:S(2)}) %collective-permute-start.28) | collective-permute-done | bytes 262176 | tf_op jit(solution)/shard_map/ppermute | solution.py:703
  150.0 6.8 %head_logits.1 = (f32[512,1280]{1,0:T(8,128)}, f32[8,512]{1,0:T(8,128)}) custom-call(s32[2]{0:T(128)} %pad_add_fusion.1.where, bf16[128,1024]{1,0:T(8,128)(2,1)} %copy-done.10, bf16[128,1024]{1,0:T(8,128)(2,1)} %copy-done.40, bf16[128,1024]{1,0:T(8,128)(2,1)} %copy-done.8, bf16[128,1024]{1,0:T(8,128)(2,1)} %copy-done.41, bf16[1024,1280]{1,0:T(8,128)(2,1)} %refs_24_.1, ...), custom_call_target="tpu_custom_call" | custom-call | flops 1342177280 | bytes 6553600 | tf_op jit(solution)/shard_map/head_logits/pallas_call | solution.py:366
  157.2 5.7 %collective-permute-start.36 = (f32[8,512]{1,0:T(8,128)}, f32[8,512]{1,0:T(8,128)S(1)}, u32[]{:S(2)}, u32[]{:S(2)}) collective-permute-start(f32[8,512]{1,0:T(8,128)} %get-tuple-element.105.refs_0_), channel_id=1, source_target_pairs={{0,24},{4,28},{8,0},{12,4},{16,8},{20,12},{24,16},{28,20},{1,25},{... | collective-permute-start | bytes 49160 | tf_op jit(solution)/shard_map/ppermute | solution.py:678
  162.9 7.0 %collective-permute-start.35 = (f32[8,512]{1,0:T(8,128)}, f32[8,512]{1,0:T(8,128)S(1)}, u32[]{:S(2)}, u32[]{:S(2)}) collective-permute-start(f32[8,512]{1,0:T(8,128)} %get-tuple-element.105.refs_0_), channel_id=1, source_target_pairs={{0,20},{4,24},{8,28},{12,0},{16,4},{20,8},{24,12},{28,16},{1,21},{... | collective-permute-start | bytes 49160 | tf_op jit(solution)/shard_map/ppermute | solution.py:678
  175.0 6.5 %head_grads.1 = (f32[128,1024]{1,0:T(8,128)}, f32[128,1024]{1,0:T(8,128)}, bf16[128,1024]{1,0:T(8,128)(2,1)}, bf16[128,1024]{1,0:T(8,128)(2,1)}, f32[8,512]{1,0:T(8,128)}) custom-call(s32[2]{0:T(128)} %pad_add_fusion.1.where, f32[8,512]{1,0:T(8,128)} %get-tuple-element.105.refs_0_, f32[8,512]{1,0:T(8,128)} %copy-done.61, f32[8,512]{1,0:T(8,128)} %copy-done.60, ...), custom_call_target="tpu_custom_call" | custom-call | flops 1342177280 | bytes 6553600 | tf_op jit(solution)/shard_map/head_grads/pallas_call | solution.py:444
  190.7 10.1 %collective-permute-done.43 = bf16[128,1024]{1,0:T(8,128)(2,1)S(1)} collective-permute-done((bf16[128,1024]{1,0:T(8,128)(2,1)S(1)}, bf16[128,1024]{1,0:T(8,128)(2,1)S(1)}, u32[]{:S(2)}, u32[]{:S(2)}) %collective-permute-start.43) | collective-permute-done | bytes 262176 | tf_op jit(solution)/shard_map/ppermute | solution.py:716
  210.5 13.6 %collective-permute-start.57 = (bf16[128,1024]{1,0:T(8,128)(2,1)S(1)}, bf16[128,1024]{1,0:T(8,128)(2,1)S(1)}, u32[]{:S(2)}, u32[]{:S(2)}) collective-permute-start(bf16[128,1024]{1,0:T(8,128)(2,1)S(1)} %add_convert_fusion.1), channel_id=1, source_target_pairs={{8,24},{9,25},{10,26},{11,27},{12,28},{13,29},{14,30},{15,31}} | collective-permute-start | bytes 786440 | tf_op jit(solution)/shard_map/ppermute | solution.py:716
  228.4 6.9 %collective-permute-done.57 = bf16[128,1024]{1,0:T(8,128)(2,1)S(1)} collective-permute-done((bf16[128,1024]{1,0:T(8,128)(2,1)S(1)}, bf16[128,1024]{1,0:T(8,128)(2,1)S(1)}, u32[]{:S(2)}, u32[]{:S(2)}) %collective-permute-start.57) | collective-permute-done | bytes 262176 | tf_op jit(solution)/shard_map/ppermute | solution.py:716
  238.5 5.1 %section_backward.7 = (bf16[128,1024]{1,0:T(8,128)(2,1)}, bf16[128,1024]{1,0:T(8,128)(2,1)}, f32[128,1024]{1,0:T(8,128)}, bf16[128,1024]{1,0:T(8,128)(2,1)}) custom-call(s32[2]{0:T(128)} %pad_add_fusion.1.where, bf16[128,1024]{1,0:T(8,128)(2,1)} %get-tuple-element.108.refs_0_, bf16[128,1024]{1,0:T(8,128)(2,1)} %get-tuple-element.110.refs_1_, ...), custom_call_target="tpu_custom_call" | custom-call | flops 6442450944 | bytes 16777216 | tf_op jit(solution)/shard_map/section_backward/pallas_call | solution.py:253
  244.8 4.9 %section_backward.9 = (bf16[128,1024]{1,0:T(8,128)(2,1)}, bf16[128,1024]{1,0:T(8,128)(2,1)}, f32[128,1024]{1,0:T(8,128)}, bf16[128,1024]{1,0:T(8,128)(2,1)}) custom-call(s32[2]{0:T(128)} %pad_add_fusion.1.where, bf16[128,1024]{1,0:T(8,128)(2,1)} %copy-done.47, bf16[128,1024]{1,0:T(8,128)(2,1)} %get-tuple-element.109.refs_1_.refs_0_, ...), custom_call_target="tpu_custom_call" | custom-call | flops 6442450944 | bytes 16777216 | tf_op jit(solution)/shard_map/section_backward/pallas_call | solution.py:253
  251.9 15.8 %collective-permute-done.50.refs_2_ = bf16[128,1024]{1,0:T(8,128)(2,1)S(1)} collective-permute-done((bf16[128,1024]{1,0:T(8,128)(2,1)S(1)}, bf16[128,1024]{1,0:T(8,128)(2,1)S(1)}, u32[]{:S(2)}, u32[]{:S(2)}) %collective-permute-start.50) | collective-permute-done | bytes 262176 | tf_op jit(solution)/shard_map/ppermute | solution.py:726
  270.5 13.8 %section_backward.8 = (bf16[128,1024]{1,0:T(8,128)(2,1)}, bf16[128,1024]{1,0:T(8,128)(2,1)}, f32[128,1024]{1,0:T(8,128)}, bf16[128,1024]{1,0:T(8,128)(2,1)}) custom-call(s32[2]{0:T(128)} %pad_add_fusion.1.where, bf16[128,1024]{1,0:T(8,128)(2,1)} %get-tuple-element.108.refs_0_, bf16[128,1024]{1,0:T(8,128)(2,1)} %get-tuple-element.110.refs_1_, ...), custom_call_target="tpu_custom_call" | custom-call | flops 6442450944 | bytes 16777216 | tf_op jit(solution)/shard_map/section_backward/pallas_call | solution.py:253
  289.5 5.1 %collective-permute-done.53.refs_0_ = bf16[128,1024]{1,0:T(8,128)(2,1)S(1)} collective-permute-done((bf16[128,1024]{1,0:T(8,128)(2,1)S(1)}, bf16[128,1024]{1,0:T(8,128)(2,1)S(1)}, u32[]{:S(2)}, u32[]{:S(2)}) %collective-permute-start.53) | collective-permute-done | bytes 262176 | tf_op jit(solution)/shard_map/ppermute | solution.py:766
  296.3 5.1 %section_backward.10 = (bf16[128,1024]{1,0:T(8,128)(2,1)}, bf16[128,1024]{1,0:T(8,128)(2,1)}, f32[128,1024]{1,0:T(8,128)}, bf16[128,1024]{1,0:T(8,128)(2,1)}) custom-call(s32[2]{0:T(128)} %pad_add_fusion.1.where, bf16[128,1024]{1,0:T(8,128)(2,1)} %copy-done.43, bf16[128,1024]{1,0:T(8,128)(2,1)} %get-tuple-element.109.refs_1_.refs_0_, ...), custom_call_target="tpu_custom_call" | custom-call | flops 6442450944 | bytes 16777216 | tf_op jit(solution)/shard_map/section_backward/pallas_call | solution.py:253
  309.0 8.9 %collective-permute-done.64.refs_3_ = bf16[128,1024]{1,0:T(8,128)(2,1)S(1)} collective-permute-done((bf16[128,1024]{1,0:T(8,128)(2,1)S(1)}, bf16[128,1024]{1,0:T(8,128)(2,1)S(1)}, u32[]{:S(2)}, u32[]{:S(2)}) %collective-permute-start.64) | collective-permute-done | bytes 262176 | tf_op jit(solution)/shard_map/ppermute | solution.py:726
  321.1 12.9 %section_backward.11 = (bf16[128,1024]{1,0:T(8,128)(2,1)}, bf16[128,1024]{1,0:T(8,128)(2,1)}, f32[128,1024]{1,0:T(8,128)}, bf16[128,1024]{1,0:T(8,128)(2,1)}) custom-call(s32[2]{0:T(128)} %pad_add_fusion.1.where, bf16[128,1024]{1,0:T(8,128)(2,1)} %copy-done.42, bf16[128,1024]{1,0:T(8,128)(2,1)} %get-tuple-element.109.refs_1_.refs_0_, ...), custom_call_target="tpu_custom_call" | custom-call | flops 6442450944 | bytes 16777216 | tf_op jit(solution)/shard_map/section_backward/pallas_call | solution.py:253
  346.1 15.2 %weight_grads.3 = (f32[256,4096]{1,0:T(8,128)}, f32[4096,256]{1,0:T(8,128)}) custom-call(s32[1]{0:T(128)} %bitcast.12.where, bf16[128,1024]{1,0:T(8,128)(2,1)} %get-tuple-element.108.refs_0_, bf16[128,1024]{1,0:T(8,128)(2,1)} %get-tuple-element.110.refs_1_, bf16[128,1024]{1,0:T(8,128)(2,1)} %get-tuple-element.125.refs_2_, ...), custom_call_target="tpu_custom_call" | custom-call | flops 5368709120 | bytes 33554432 | tf_op jit(solution)/shard_map/weight_grads/pallas_call | solution.py:584
  363.0 15.1 %unit_grads.1.refs_0_ = f32[256,1280]{1,0:T(8,128)} custom-call(s32[1]{0:T(128)} %bitcast.12.where, bf16[2,4,2,128,1024]{4,3,2,1,0:T(8,128)(2,1)} %bitcast.24, bf16[2,4,2,128,1024]{4,3,2,1,0:T(8,128)(2,1)} %bitcast.25, bf16[2,4,2,128,1024]{4,3,2,1,0:T(8,128)(2,1)} %bitcast.26, bf16[2,4,2,128,1024]{4,3,2,1,0:T(8,128)(2,1)} %bitcast.27, ...), custom_call_target="tpu_custom_call" | custom-call | flops 6710886400 | bytes 7864320 | tf_op jit(solution)/shard_map/unit_grads/pallas_call | solution.py:503
  382.3 31.0 %weight_grads.4 = (f32[256,4096]{1,0:T(8,128)}, f32[4096,256]{1,0:T(8,128)}) custom-call(s32[1]{0:T(128)} %bitcast.12.where, bf16[128,1024]{1,0:T(8,128)(2,1)} %get-tuple-element.109.refs_1_.refs_0_, bf16[128,1024]{1,0:T(8,128)(2,1)} %get-tuple-element.130.refs_2_.refs_1_, ...), custom_call_target="tpu_custom_call", output_to_operand_aliasing={{0}: (19, {}), {1}: (20, {})} | custom-call | flops 21474836480 | bytes 33554432 | tf_op jit(solution)/shard_map/weight_grads/pallas_call | solution.py:584
  413.3 24.8 %weight_grads.5 = (f32[256,4096]{1,0:T(8,128)}, f32[4096,256]{1,0:T(8,128)}) custom-call(s32[1]{0:T(128)} %bitcast.12.where, bf16[2,4,2,128,1024]{4,3,2,1,0:T(8,128)(2,1)} %bitcast.80, bf16[2,4,2,128,1024]{4,3,2,1,0:T(8,128)(2,1)} %bitcast.81, bf16[2,4,2,128,1024]{4,3,2,1,0:T(8,128)(2,1)} %bitcast.82, ...), custom_call_target="tpu_custom_call", output_to_operand_aliasing={{0}: (15, {}), {1}: (16, {})} | custom-call | flops 16106127360 | bytes 33554432 | tf_op jit(solution)/shard_map/weight_grads/pallas_call | solution.py:584
  (362 shorter events, 158.9 us)
Async XLA Ops:
  7.2 355.3 %all-gather.11.cloned.1.call-start = ((), (), s32[]{:S(2)}) async-start(), calls=%async_computation.1 | async-start | bytes 4718592 | tf_op jit(solution)/shard_map/all_gather | solution.py:669
  17.3 14.3 %collective-permute-start.1 = (bf16[128,1024]{1,0:T(8,128)(2,1)S(1)}, bf16[128,1024]{1,0:T(8,128)(2,1)S(1)}, u32[]{:S(2)}, u32[]{:S(2)}) collective-permute-start(bf16[128,1024]{1,0:T(8,128)(2,1)S(1)} %add_convert_fusion.11.refs_0_), channel_id=1, source_target_pairs={{0,8},{1,9},{2,10},{3,11},{4,12},{5,13},{6,14},{7,15}} | collective-permute-start | bytes 786440 | tf_op jit(solution)/shard_map/ppermute | solution.py:689
  35.8 14.4 %collective-permute-start.18 = (bf16[128,1024]{1,0:T(8,128)(2,1)S(1)}, bf16[128,1024]{1,0:T(8,128)(2,1)S(1)}, u32[]{:S(2)}, u32[]{:S(2)}) collective-permute-start(bf16[128,1024]{1,0:T(8,128)(2,1)S(1)} %add_convert_fusion.7), channel_id=1, source_target_pairs={{0,8},{1,9},{2,10},{3,11},{4,12},{5,13},{6,14},{7,15}} | collective-permute-start | bytes 786440 | tf_op jit(solution)/shard_map/ppermute | solution.py:689
  113.4 26.1 %collective-permute-start.11 = (bf16[128,1024]{1,0:T(8,128)(2,1)S(1)}, bf16[128,1024]{1,0:T(8,128)(2,1)S(1)}, u32[]{:S(2)}, u32[]{:S(2)}) collective-permute-start(bf16[128,1024]{1,0:T(8,128)(2,1)S(1)} %copy-done.12), channel_id=1, source_target_pairs={{24,8},{25,9},{26,10},{27,11},{28,12},{29,13},{30,14},{31,15}} | collective-permute-start | bytes 786440 | tf_op jit(solution)/shard_map/ppermute | solution.py:703
  114.7 24.8 %collective-permute-start.10 = (bf16[128,1024]{1,0:T(8,128)(2,1)S(1)}, bf16[128,1024]{1,0:T(8,128)(2,1)S(1)}, u32[]{:S(2)}, u32[]{:S(2)}) collective-permute-start(bf16[128,1024]{1,0:T(8,128)(2,1)S(1)} %copy-done.12), channel_id=1, source_target_pairs={{24,16},{25,17},{26,18},{27,19},{28,20},{29,21},{30,22},{31,23}} | collective-permute-start | bytes 786440 | tf_op jit(solution)/shard_map/ppermute | solution.py:703
  116.5 23.3 %collective-permute-start.29 = (bf16[128,1024]{1,0:T(8,128)(2,1)S(1)}, bf16[128,1024]{1,0:T(8,128)(2,1)S(1)}, u32[]{:S(2)}, u32[]{:S(2)}) collective-permute-start(bf16[128,1024]{1,0:T(8,128)(2,1)S(1)} %add_convert_fusion.4), channel_id=1, source_target_pairs={{24,0},{25,1},{26,2},{27,3},{28,4},{29,5},{30,6},{31,7}} | collective-permute-start | bytes 786440 | tf_op jit(solution)/shard_map/ppermute | solution.py:703
  117.2 28.0 %collective-permute-start.28 = (bf16[128,1024]{1,0:T(8,128)(2,1)S(1)}, bf16[128,1024]{1,0:T(8,128)(2,1)S(1)}, u32[]{:S(2)}, u32[]{:S(2)}) collective-permute-start(bf16[128,1024]{1,0:T(8,128)(2,1)S(1)} %add_convert_fusion.4), channel_id=1, source_target_pairs={{24,8},{25,9},{26,10},{27,11},{28,12},{29,13},{30,14},{31,15}} | collective-permute-start | bytes 786440 | tf_op jit(solution)/shard_map/ppermute | solution.py:703
  118.5 26.6 %collective-permute-start.27 = (bf16[128,1024]{1,0:T(8,128)(2,1)S(1)}, bf16[128,1024]{1,0:T(8,128)(2,1)S(1)}, u32[]{:S(2)}, u32[]{:S(2)}) collective-permute-start(bf16[128,1024]{1,0:T(8,128)(2,1)S(1)} %add_convert_fusion.4), channel_id=1, source_target_pairs={{24,16},{25,17},{26,18},{27,19},{28,20},{29,21},{30,22},{31,23}} | collective-permute-start | bytes 786440 | tf_op jit(solution)/shard_map/ppermute | solution.py:703
  146.3 235.9 %all-gather.9.cloned.1.call-start = ((), (), s32[]{:S(2)}) async-start(), calls=%async_computation | async-start | bytes 4718592 | tf_op jit(solution)/shard_map/all_gather | solution.py:669
  156.8 13.8 %collective-permute-start.37 = (f32[8,512]{1,0:T(8,128)}, f32[8,512]{1,0:T(8,128)S(1)}, u32[]{:S(2)}, u32[]{:S(2)}) collective-permute-start(f32[8,512]{1,0:T(8,128)} %get-tuple-element.105.refs_0_), channel_id=1, source_target_pairs={{0,28},{4,0},{8,4},{12,8},{16,12},{20,16},{24,20},{28,24},{1,29},{... | collective-permute-start | bytes 49160 | tf_op jit(solution)/shard_map/ppermute | solution.py:678
  157.2 14.7 %collective-permute-start.36 = (f32[8,512]{1,0:T(8,128)}, f32[8,512]{1,0:T(8,128)S(1)}, u32[]{:S(2)}, u32[]{:S(2)}) collective-permute-start(f32[8,512]{1,0:T(8,128)} %get-tuple-element.105.refs_0_), channel_id=1, source_target_pairs={{0,24},{4,28},{8,0},{12,4},{16,8},{20,12},{24,16},{28,20},{1,25},{... | collective-permute-start | bytes 49160 | tf_op jit(solution)/shard_map/ppermute | solution.py:678
  187.1 13.6 %collective-permute-start.43 = (bf16[128,1024]{1,0:T(8,128)(2,1)S(1)}, bf16[128,1024]{1,0:T(8,128)(2,1)S(1)}, u32[]{:S(2)}, u32[]{:S(2)}) collective-permute-start(bf16[128,1024]{1,0:T(8,128)(2,1)S(1)} %add_convert_fusion.3), channel_id=1, source_target_pairs={{8,24},{9,25},{10,26},{11,27},{12,28},{13,29},{14,30},{15,31}} | collective-permute-start | bytes 786440 | tf_op jit(solution)/shard_map/ppermute | solution.py:716
  203.5 178.8 %all-gather.15.cloned.1.call-start = ((), (), s32[]{:S(2)}) async-start(), calls=%async_computation.3 | async-start | bytes 2359296 | tf_op jit(solution)/shard_map/all_gather | solution.py:669
  209.4 15.5 %collective-permute-start.46 = (bf16[128,1024]{1,0:T(8,128)(2,1)}, bf16[128,1024]{1,0:T(8,128)(2,1)S(1)}, u32[]{:S(2)}, u32[]{:S(2)}) collective-permute-start(bf16[128,1024]{1,0:T(8,128)(2,1)} %get-tuple-element.114), channel_id=1, source_target_pairs={{0,4},{4,0},{1,5},{5,1},{2,6},{6,2},{3,7},{7,3},{8,12},{12,8},{9,1... | collective-permute-start | bytes 786440 | tf_op jit(solution)/shard_map/ppermute | solution.py:23
  209.9 18.6 %collective-permute-start.58 = (bf16[128,1024]{1,0:T(8,128)(2,1)S(1)}, bf16[128,1024]{1,0:T(8,128)(2,1)S(1)}, u32[]{:S(2)}, u32[]{:S(2)}) collective-permute-start(bf16[128,1024]{1,0:T(8,128)(2,1)S(1)} %add_convert_fusion.1), channel_id=1, source_target_pairs={{16,24},{17,25},{18,26},{19,27},{20,28},{21,29},{22,30},{23,31}} | collective-permute-start | bytes 786440 | tf_op jit(solution)/shard_map/ppermute | solution.py:716
  210.5 24.8 %collective-permute-start.57 = (bf16[128,1024]{1,0:T(8,128)(2,1)S(1)}, bf16[128,1024]{1,0:T(8,128)(2,1)S(1)}, u32[]{:S(2)}, u32[]{:S(2)}) collective-permute-start(bf16[128,1024]{1,0:T(8,128)(2,1)S(1)} %add_convert_fusion.1), channel_id=1, source_target_pairs={{8,24},{9,25},{10,26},{11,27},{12,28},{13,29},{14,30},{15,31}} | collective-permute-start | bytes 786440 | tf_op jit(solution)/shard_map/ppermute | solution.py:716
  249.7 19.0 %collective-permute-start.60 = (bf16[128,1024]{1,0:T(8,128)(2,1)}, bf16[128,1024]{1,0:T(8,128)(2,1)S(1)}, u32[]{:S(2)}, u32[]{:S(2)}) collective-permute-start(bf16[128,1024]{1,0:T(8,128)(2,1)} %get-tuple-element.132), channel_id=1, source_target_pairs={{0,4},{4,0},{1,5},{5,1},{2,6},{6,2},{3,7},{7,3},{8,12},{12,8},{9,1... | collective-permute-start | bytes 786440 | tf_op jit(solution)/shard_map/ppermute | solution.py:23
  250.5 17.2 %collective-permute-start.50 = (bf16[128,1024]{1,0:T(8,128)(2,1)S(1)}, bf16[128,1024]{1,0:T(8,128)(2,1)S(1)}, u32[]{:S(2)}, u32[]{:S(2)}) collective-permute-start(bf16[128,1024]{1,0:T(8,128)(2,1)S(1)} %fusion.55.refs_0_), channel_id=1, source_target_pairs={{16,8},{17,9},{18,10},{19,11},{20,12},{21,13},{22,14},{23,15}} | collective-permute-start | bytes 786440 | tf_op jit(solution)/shard_map/ppermute | solution.py:726
  304.9 108.3 %all-gather.13.cloned.1.call-start = ((), (), s32[]{:S(2)}) async-start(), calls=%async_computation.2 | async-start | bytes 2359296 | tf_op jit(solution)/shard_map/all_gather | solution.py:669
  335.8 26.6 %collective-permute-start.40 = (f32[1,512]{1,0:T(1,128)S(1)}, f32[1,512]{1,0:T(1,128)S(1)}, u32[]{:S(2)}, u32[]{:S(2)}) collective-permute-start(f32[1,512]{1,0:T(1,128)S(1)} %get-tuple-element.158.refs_16_), channel_id=1, source_target_pairs={{0,3},{1,0},{2,1},{3,2},{4,7},{5,4},{6,5},{7,6},{8,11},{9,8},{10,9... | collective-permute-start | bytes 6152 | tf_op jit(solution)/shard_map/ppermute | solution.py:652
  337.6 24.8 %collective-permute-start.39 = (f32[1,512]{1,0:T(1,128)S(1)}, f32[1,512]{1,0:T(1,128)S(1)}, u32[]{:S(2)}, u32[]{:S(2)}) collective-permute-start(f32[1,512]{1,0:T(1,128)S(1)} %get-tuple-element.158.refs_16_), channel_id=1, source_target_pairs={{0,2},{1,3},{2,0},{3,1},{4,6},{5,7},{6,4},{7,5},{8,10},{9,11},{10,... | collective-permute-start | bytes 6152 | tf_op jit(solution)/shard_map/ppermute | solution.py:652
  339.8 22.6 %collective-permute-start.38 = (f32[1,512]{1,0:T(1,128)S(1)}, f32[1,512]{1,0:T(1,128)S(1)}, u32[]{:S(2)}, u32[]{:S(2)}) collective-permute-start(f32[1,512]{1,0:T(1,128)S(1)} %get-tuple-element.158.refs_16_), channel_id=1, source_target_pairs={{0,1},{1,2},{2,3},{3,0},{4,5},{5,6},{6,7},{7,4},{8,9},{9,10},{10,1... | collective-permute-start | bytes 6152 | tf_op jit(solution)/shard_map/ppermute | solution.py:652
  344.8 16.5 %collective-permute-start.67 = (bf16[128,1024]{1,0:T(8,128)(2,1)S(1)}, bf16[128,1024]{1,0:T(8,128)(2,1)S(1)}, u32[]{:S(2)}, u32[]{:S(2)}) collective-permute-start(bf16[128,1024]{1,0:T(8,128)(2,1)S(1)} %fusion.80), channel_id=1, source_target_pairs={{8,0},{9,1},{10,2},{11,3},{12,4},{13,5},{14,6},{15,7}} | collective-permute-start | bytes 786440 | tf_op jit(solution)/shard_map/ppermute | solution.py:766
  361.3 16.8 %collective-permute-start.68 = (bf16[128,1024]{1,0:T(8,128)(2,1)S(1)}, bf16[128,1024]{1,0:T(8,128)(2,1)S(1)}, u32[]{:S(2)}, u32[]{:S(2)}) collective-permute-start(bf16[128,1024]{1,0:T(8,128)(2,1)S(1)} %collective-permute-done.67.refs_2_), channel_id=1, source_target_pairs={{0,4},{4,0},{1,5},{5,1},{2,6},{6,2},{3,7},{7,3},{8,12},{12,8},{9,1... | collective-permute-start | bytes 786440 | tf_op jit(solution)/shard_map/ppermute | solution.py:23
  (124 other events, 736.1 us)
Sparse Core Ops, SparseCore 0:
  146.4 57.8 all-gather.10
  205.9 47.0 all-gather.8
  305.1 32.1 all-gather.14
  381.7 27.4 all-gather.12
